TPU v7x, 32 devices: a whole 2x2x4 slice. The times are simulated.
32 devices in a mesh: seq: 4 (over z), ctx: 8 (over y, x, core).
Axes of the slice: x: 2, y: 2, z: 4, core: 2. Of those that a mesh axis runs over, the one named last changes fastest.
Arguments:
- queries: bfloat16 [4096, 2048], P(('seq', 'ctx')), parts along dimension 0, may hold values from -6 to 6
- key_rows: bfloat16 [4096, 2048], P(('seq', 'ctx')), parts along dimension 0, may hold values from -6 to 6
- values: bfloat16 [4096, 2048], P(('seq', 'ctx')), parts along dimension 0, may hold values from -6 to 6
- out_grad: bfloat16 [4096, 2048], P(('seq', 'ctx')), parts along dimension 0, may hold values from -0.016479492 to 0.016479492
- feature_map: bfloat16 [16, 128, 128], replicated, may hold values from -0.5 to 0.5
Outputs:
- query_grad: bfloat16 [4096, 2048], P(('seq', 'ctx')), parts along dimension 0
- key_grad: bfloat16 [4096, 2048], P(('seq', 'ctx')), parts along dimension 0
- value_grad: bfloat16 [4096, 2048], P(('seq', 'ctx')), parts along dimension 0
- map_grad: float32 [64, 128, 128], P('seq'), parts along dimension 0
There are 4 independent parts, one for each index of `seq`. A program takes and returns all parts, laid end to end along the dimension named above; an argument that names none is the same for every part. Nothing has to cross between parts.
All inputs are finite; a program needn't handle non-finite values.
Results may differ from a plain program's by a relative error of at most 0.033.
Values may be sent and summed in bfloat16 or wider, within the bound.
No kernel may reach another device: no remote copies, remote signals or barrier semaphores. Data moves between devices by JAX's collectives and lax.ppermute only.
A program may use at most 128 MiB of HBM per device.

v0:
```python
import math

import jax
import jax.numpy as jnp
from jax import lax
from jax.sharding import PartitionSpec as P


def carried_in(part, axis, combine, identity, reverse):
    count = lax.axis_size(axis)
    place = lax.axis_index(axis)
    ahead = count - 1 - place if reverse else place
    gathered = lax.all_gather(part, axis)
    state = jnp.zeros_like(part) + jnp.asarray(identity, part.dtype)

    def one(turn, state):
        source = count - 1 - turn if reverse else turn
        return combine(state, lax.dynamic_index_in_dim(gathered, source, 0, False))

    return lax.fori_loop(0, ahead, one, state)


def add_states(earlier, later):
    return earlier + later


def per_device(queries, key_rows, values, out_grad, feature_map):
    f32 = jnp.float32
    bf16 = jnp.bfloat16
    length_dev = queries.shape[0]
    heads_count = feature_map.shape[0]
    head_size = feature_map.shape[1]
    shape_heads = (length_dev, heads_count, head_size)
    query_h = queries.reshape(shape_heads)
    key_h = key_rows.reshape(shape_heads)
    value_h = values.reshape(shape_heads)
    grad_h = out_grad.reshape(shape_heads)
    query_feat = jnp.einsum(
        "thd,hde->the", query_h, feature_map, preferred_element_type=f32
    ).astype(bf16)
    key_feat = jnp.einsum("thd,hde->the", key_h, feature_map, preferred_element_type=f32).astype(
        bf16
    )
    key_state = jnp.einsum("the,thv->hev", key_feat, value_h, preferred_element_type=f32).astype(
        bf16
    )
    grad_state = jnp.einsum("the,thv->hev", query_feat, grad_h, preferred_element_type=f32).astype(
        bf16
    )
    zeros_state = jnp.zeros_like(key_state)
    prefix = carried_in(key_state, "ctx", add_states, zeros_state, False).astype(f32)
    suffix = carried_in(grad_state, "ctx", add_states, zeros_state, True).astype(f32)
    prefix = prefix.astype(bf16)
    suffix = suffix.astype(bf16)
    rows_idx = lax.broadcasted_iota(jnp.int32, (length_dev, length_dev), 0)
    cols_idx = lax.broadcasted_iota(jnp.int32, (length_dev, length_dev), 1)
    causal = rows_idx >= cols_idx
    scores = jnp.einsum("the,she->hts", query_feat, key_feat, preferred_element_type=f32)
    scores = jnp.where(causal, scores, 0.0).astype(bf16)
    mixing = jnp.einsum("thv,shv->hts", grad_h, value_h, preferred_element_type=f32)
    mixing = jnp.where(causal, mixing, 0.0).astype(bf16)
    feat_qgrad = (
        jnp.einsum("hts,she->the", mixing, key_feat, preferred_element_type=f32)
        + jnp.einsum("thv,hev->the", grad_h, prefix, preferred_element_type=f32)
    ).astype(bf16)
    feat_kgrad = (
        jnp.einsum("hts,the->she", mixing, query_feat, preferred_element_type=f32)
        + jnp.einsum("shv,hev->she", value_h, suffix, preferred_element_type=f32)
    ).astype(bf16)
    value_grad = jnp.einsum(
        "hts,thv->shv", scores, grad_h, preferred_element_type=f32
    ) + jnp.einsum("she,hev->shv", key_feat, suffix, preferred_element_type=f32)
    query_grad = jnp.einsum("the,hde->thd", feat_qgrad, feature_map, preferred_element_type=f32)
    key_grad = jnp.einsum("the,hde->thd", feat_kgrad, feature_map, preferred_element_type=f32)
    local_grad = jnp.einsum(
        "thd,the->hde", query_h, feat_qgrad, preferred_element_type=f32
    ) + jnp.einsum("thd,the->hde", key_h, feat_kgrad, preferred_element_type=f32)
    local_grad = local_grad.astype(bf16).astype(f32)
    map_grad = lax.psum(local_grad.astype(jnp.bfloat16), "ctx").astype(jnp.float32) / math.sqrt(
        length_dev * lax.axis_size("ctx")
    )
    flat_shape = (length_dev, heads_count * head_size)
    return (
        query_grad.reshape(flat_shape).astype(bf16),
        key_grad.reshape(flat_shape).astype(bf16),
        value_grad.reshape(flat_shape).astype(bf16),
        map_grad,
    )


def solution(mesh):
    placed = (
        P(("seq", "ctx"), None),
        P(("seq", "ctx"), None),
        P(("seq", "ctx"), None),
        P(("seq", "ctx"), None),
        P(),
    )
    return jax.shard_map(
        per_device,
        mesh=mesh,
        in_specs=placed,
        out_specs=(
            P(("seq", "ctx"), None),
            P(("seq", "ctx"), None),
            P(("seq", "ctx"), None),
            P("seq", None, None),
        ),
        check_vma=False,
    )
```

profile of v0, /device:TPU:0, one launch (start us, length us, event | category | flops | bytes accessed | tf_op | source)
XLA Modules:
  0.0 168.9 jit_solution(15054660292216451872)
XLA Ops:
  7.2 0.0 copy-start
  7.2 0.0 copy-start.1
  7.2 0.0 copy-start.2
  7.2 0.0 all-gather.5.cloned.1.call-start
  7.2 1.1 copy-done
  8.4 1.6 fusion.10
  9.9 2.1 %convolution_convert_fusion.4 = bf16[16,128,128]{2,1,0:T(8,128)(2,1)} fusion(bf16[128,16,128]{0,2,1:T(8,128)(2,1)S(1)} %fusion.10, bf16[128,2048]{1,0:T(8,128)(2,1)} %param.11), kind=kOutput, calls=%fused_computation.14 | convolution fusion | flops 67371008 | bytes 1572864 | tf_op jit(solution)/shard_map/the,thv->hev/dot_general | solution.py:44
  12.1 0.0 all-gather.5.cloned.1.call-update
  12.1 0.0 all-gather.7.cloned.1.call-start
  12.1 1.3 copy.57
  13.5 0.0 copy-done.2
  13.5 0.5 fusion.11
  14.0 1.3 convolution_convert_fusion.2
  15.3 0.0 all-gather.7.cloned.1.call-update
  15.3 0.0 all-reduce.2.cloned.1.call-start
  15.4 0.0 copy-done.1
  15.4 0.5 fusion.1
  15.9 1.4 fusion.30
  17.3 1.4 fusion.31
  18.7 33.0 %all-gather.5.cloned.1.call-done = bf16[128,128,128]{2,1,0:T(8,128)(2,1)} async-done(((bf16[16,128,128]{2,1,0:T(8,128)(2,1)}), bf16[128,128,128]{2,1,0:T(8,128)(2,1)}) %all-gather.5.cloned.1.call-update) | async-done | bytes 4194320 | tf_op jit(solution)/shard_map/all_gather | solution.py:13
  51.7 0.1 broadcast_in_dim.17.clone
  51.8 1.5 fusion.9
  53.3 0.3 convolution_convert_fusion.1
  53.6 1.0 copy.47
  54.6 2.3 %fusion.12 = f32[16,128,128]{2,1,0:T(8,128)} fusion(bf16[128,16,128]{0,2,1:T(8,128)(2,1)S(1)} %fusion.9, bf16[128,2048]{1,0:T(8,128)(2,1)} %param.9), kind=kOutput, calls=%fused_computation.28 | convolution fusion | flops 67108864 | bytes 2097152 | tf_op jit(solution)/shard_map/thd,the->hde/dot_general | solution.py:75
  56.9 33.9 %all-gather.7.cloned.1.call-done = bf16[128,128,128]{2,1,0:T(8,128)(2,1)} async-done(((bf16[16,128,128]{2,1,0:T(8,128)(2,1)}), bf16[128,128,128]{2,1,0:T(8,128)(2,1)}) %all-gather.7.cloned.1.call-update) | async-done | bytes 4194320 | tf_op jit(solution)/shard_map/all_gather | solution.py:13
  90.9 0.1 broadcast_in_dim.17.clone.1
  91.0 8.1 %while.23 = (s32[]{:T(128)}, bf16[16,128,128]{2,1,0:T(8,128)(2,1)S(1)}, s32[]{:T(128)}, bf16[8,16,128,128]{3,2,1,0:T(8,128)(2,1)}, s32[]{:T(128)}, /*index=5*/s32[]{:T(128)}, s32[]{:T(128)}, s32[]{:T(128)}) while((s32[]{:T(128)}, bf16[16,128,128]{2,1,0:T(8,128)(2,1)S(1)}, s32[]{:T(128)}, bf16[8,16,128,128]{3,2,1,0:T(8,128)(2,1)}, s32[]{:T(128)}, ...), condition=%wide.region_3.4_spmd, body=%wide.region_2.3_spmd.sunk | while | flops 262150 | bytes 1573007 | solution.py:20
  91.0 1.1 bitcast_add_fusion.5
  92.2 1.1 bitcast_add_fusion.5
  93.3 1.1 bitcast_add_fusion.5
  94.5 1.1 bitcast_add_fusion.5
  95.6 1.1 bitcast_add_fusion.5
  96.8 1.1 bitcast_add_fusion.5
  97.9 1.1 bitcast_add_fusion.5
  99.1 1.3 convolution_bitcast_fusion.1
  100.4 1.9 %fusion.8 = bf16[128,16,128]{0,2,1:T(8,128)(2,1)S(1)} fusion(f32[16,128,128]{2,1,0:T(8,128)} %fusion.31, bf16[16,128,128]{2,1,0:T(8,128)(2,1)S(1)} %get-tuple-element.84, bf16[128,2048]{1,0:T(8,128)(2,1)} %param.11), kind=kOutput, calls=%fused_computation.23 | convolution fusion | flops 67633152 | bytes 2621440 | tf_op jit(solution)/shard_map/shv,hev->she/dot_general | solution.py:68
  102.3 0.3 convolution_convert_fusion
  102.6 1.0 copy.48
  103.6 2.5 %fusion.7 = bf16[16,128,128]{1,2,0:T(8,128)(2,1)} fusion(f32[16,128,128]{2,1,0:T(8,128)} %fusion.12, bf16[128,16,128]{0,2,1:T(8,128)(2,1)S(1)} %fusion.8, bf16[128,2048]{1,0:T(8,128)(2,1)} %param.10), kind=kOutput, calls=%fused_computation.22 | convolution fusion | flops 67633152 | bytes 2621440 | tf_op jit(solution)/shard_map/thd,the->hde/dot_general | solution.py:77
  106.1 0.0 all-reduce.2.cloned.1.call-update
  106.1 1.7 %fusion.6 = bf16[128,16,128]{0,2,1:T(8,128)(2,1)S(1)} fusion(f32[128,16,128]{0,2,1:T(8,128)} %convolution_bitcast_fusion.1, bf16[128,16,128]{0,2,1:T(8,128)(2,1)S(1)} %bitcast.104, bf16[128,16,128]{0,2,1:T(8,128)(2,1)S(1)} %fusion.11, bf16[128,16,128]{0,2,1:T(8,128)(2,1)S(1)} %fusion.10, pred[128,128]{1,0:T(8,128)(4,1)S(1)} %iota_compare_fusion), kind=kOutput, calls=%fused_computation.21 | convolution fusion | flops 135266304 | bytes 3162112 | tf_op jit(solution)/shard_map/hts,thv->shv/dot_general | solution.py:70
  107.8 1.0 copy.49
  108.8 51.1 %all-reduce.2.cloned.1.call-done = bf16[16,128,128]{1,2,0:T(8,128)(2,1)} async-done(((bf16[16,128,128]{1,2,0:T(8,128)(2,1)}), bf16[16,128,128]{1,2,0:T(8,128)(2,1)}) %all-reduce.2.cloned.1.call-update) | async-done | bytes 524304 | tf_op jit(solution)/shard_map/psum | solution.py:79
  159.9 1.1 convert_multiply_fusion
  161.0 1.3 copy.50
  (2 shorter events, 0.0 us)
Async XLA Ops:
  7.2 1.2 copy-start
  7.2 8.2 %copy-start.1 = (bf16[128,2048]{1,0:T(8,128)(2,1)S(1)}, bf16[128,2048]{1,0:T(8,128)(2,1)}, u32[]{:S(2)}) copy-start(bf16[128,2048]{1,0:T(8,128)(2,1)} %param.11) | copy-start | bytes 1572868
  7.2 6.3 %copy-start.2 = (bf16[128,2048]{1,0:T(8,128)(2,1)S(1)}, bf16[128,2048]{1,0:T(8,128)(2,1)}, u32[]{:S(2)}) copy-start(bf16[128,2048]{1,0:T(8,128)(2,1)} %param.9) | copy-start | bytes 1572868
  7.2 44.5 %all-gather.5.cloned.1.call-start = ((), (), s32[]{:S(2)}) async-start(), calls=%async_computation.1 | async-start | bytes 4718592 | tf_op jit(solution)/shard_map/all_gather | solution.py:13
  12.1 78.8 %all-gather.7.cloned.1.call-start = ((), (), s32[]{:S(2)}) async-start(), calls=%async_computation.2 | async-start | bytes 4718592 | tf_op jit(solution)/shard_map/all_gather | solution.py:13
  15.3 144.6 %all-reduce.2.cloned.1.call-start = ((), (), s32[]{:S(2)}) async-start(), calls=%async_computation | async-start | bytes 1048576 | tf_op jit(solution)/shard_map/psum | solution.py:79
Sparse Core Ops, SparseCore 0:
  12.2 39.4 all-gather.4
  54.1 36.7 all-gather.6
  106.2 53.6 all-reduce.1
where the time goes:
time: 170 us; the launch traced here: 169 us
  waiting for transfers between devices  118 us (69%)
  matrix products  20.6 us (12%)
  between operations  13.9 us (8%)
  other arithmetic  9.1 us (5%)
  local copies, waits for them, and re-layouts  6.98 us (4%)
    all_gather x2, waiting for transfers between devices, carried_in(): gathered = lax.all_gather(part, axis)  66.9 us
    psum x1, waiting for transfers between devices, per_device(): lax.psum(local_grad.astype(jnp.bfloat16), 'ctx').astype(jnp.float32)  51.1 us
    add x7, other arithmetic, add_states(): return earlier + later  7.94 us
    unnamed x10, local copies, waits for them, and re-layouts  5.48 us
  transfers between devices with their start and end apart: 3, of which 3 were waited for; matrix products, arithmetic and copies ran while one was open for 9% of the time, Pallas kernels for 0%

commit v1 on v0

v1 whole, which is shorter than its diff:
```python
import functools
import math

import jax
import jax.numpy as jnp
from jax import lax
from jax.experimental import pallas as pl
from jax.experimental.pallas import tpu as pltpu
from jax.sharding import PartitionSpec as P

F32 = jnp.float32
BF16 = jnp.bfloat16
VMEM = pl.BlockSpec(memory_space=pltpu.VMEM)
PARAMS = pltpu.CompilerParams(vmem_limit_bytes=8 * 2**20)
GROUPS = 4
EXTRA = 16


def dot_nn(a, b):
    return lax.dot_general(a, b, (((1,), (0,)), ((), ())), preferred_element_type=F32)


def dot_nt(a, b):
    return lax.dot_general(a, b, (((1,), (1,)), ((), ())), preferred_element_type=F32)


def dot_tn(a, b):
    return lax.dot_general(a, b, (((0,), (0,)), ((), ())), preferred_element_type=F32)


def call(body, outs, *operands):
    return pl.pallas_call(
        body,
        out_shape=[jax.ShapeDtypeStruct(shape, dtype) for shape, dtype in outs],
        in_specs=[VMEM] * len(operands),
        out_specs=[VMEM] * len(outs),
        compiler_params=PARAMS,
    )(*operands)


def place():
    me = lax.axis_index("ctx")
    return lax.rem(me, 2), lax.div(me, 2)


def head_of(half, chip, apart, i, per_owner):
    return half * (GROUPS * per_owner) + (chip ^ apart) * per_owner + i


def columns(head, size):
    return pl.ds(pl.multiple_of(head * size, size), size)


def triangle(size):
    rows = lax.broadcasted_iota(jnp.int32, (size, size), 0)
    cols = lax.broadcasted_iota(jnp.int32, (size, size), 1)
    return rows, cols


def states_body(mine, per_owner, q, k, v, g, *outs):
    out = outs[0]
    size = out.shape[-1]
    core, chip = place()
    half = core if mine else 1 - core
    for apart in range(GROUPS):
        for i in range(per_owner):
            at = columns(head_of(half, chip, apart, i, per_owner), size)
            early = dot_tn(k[:, at], v[:, at]).astype(BF16)
            late = dot_tn(q[:, at], g[:, at]).astype(BF16)
            out[apart, 0, i] = early
            out[apart, 1, i] = late
            if mine:
                outs[1][apart, i] = jnp.where(core == 0, early, late)


def add_body(own, other, *outs):
    for apart in range(GROUPS):
        outs[apart][...] = (own[apart].astype(F32) + other[apart].astype(F32)).astype(BF16)


def local_body(per_owner, q, k, v, g, own_c, send_c, part_q):
    size = own_c.shape[-1]
    core, chip = place()
    rows, cols = triangle(q.shape[0])
    causal = rows >= cols
    for which, out in ((1, send_c), (0, own_c)):
        half = core if which == 0 else 1 - core
        for apart in range(GROUPS):
            for i in range(per_owner):
                at = columns(head_of(half, chip, apart, i, per_owner), size)
                mixing = jnp.where(causal, dot_nt(g[:, at], v[:, at]), 0.0).astype(BF16)
                mixed = dot_nn(mixing, k[:, at])
                part_q[which, apart, i] = mixed
                out[apart, i] = dot_tn(q[:, at], mixed.astype(BF16)).astype(BF16)


def local_rest_body(per_owner, q, k, v, g, w, part_k, part_v, key_w, gram):
    size = w.shape[-1]
    core, chip = place()
    rows, cols = triangle(q.shape[0])
    causal = rows >= cols
    for which in (0, 1):
        half = core if which == 0 else 1 - core
        for apart in range(GROUPS):
            for i in range(per_owner):
                head = head_of(half, chip, apart, i, per_owner)
                at = columns(head, size)
                mixing = jnp.where(causal, dot_nt(g[:, at], v[:, at]), 0.0).astype(BF16)
                part_k[which, apart, i] = dot_tn(mixing, q[:, at])
                square = dot_nt(w[head], w[head]).astype(BF16)
                gram[which, apart, i] = square
                keyed = dot_nn(k[:, at], square).astype(BF16)
                key_w[which, apart, i] = keyed
                scores = jnp.where(causal, dot_nt(q[:, at], keyed), 0.0).astype(BF16)
                part_v[which, apart, i] = dot_tn(scores, g[:, at])


def pack(first, second):
    size = first.shape[0]
    rows, cols = triangle(size)
    both = jnp.where(rows >= cols, first, second)
    diagonal = jnp.sum(jnp.where(rows == cols, second, 0.0), axis=0, keepdims=True)
    return both, jnp.broadcast_to(diagonal, (EXTRA, size))


def pack_body(per_owner, own, other, own_c, other_c, *outs):
    size = own_c.shape[-1]
    core, _ = place()
    last = core == 1
    for apart in range(GROUPS):
        for pair in range(per_owner // 2):
            sums = []
            for i in (2 * pair, 2 * pair + 1):
                early = jnp.where(last, other[apart, 0, i], own[apart, 0, i])
                late = jnp.where(last, own[apart, 1, i], other[apart, 1, i])
                total = dot_nt(late, early)
                total += own_c[apart, i].astype(F32) + other_c[apart, i].astype(F32)
                sums.append(total + total.T)
            both, diagonal = pack(*sums)
            outs[apart][pair, :size] = both.astype(BF16)
            outs[apart][pair, size:] = diagonal.astype(BF16)


def carry_body(*refs):
    parts, outs = refs[:GROUPS], refs[GROUPS:]
    _, chip = place()
    early = [part[0].astype(F32) for part in parts]
    late = [part[1].astype(F32) for part in parts]
    for to in range(GROUPS):
        prefix = jnp.zeros_like(early[0])
        suffix = jnp.zeros_like(early[0])
        for apart in range(GROUPS):
            if apart == to:
                continue
            before = (chip ^ apart) < (chip ^ to)
            prefix += jnp.where(before, early[apart], 0.0)
            suffix += jnp.where(before, 0.0, late[apart])
        outs[to][0] = prefix.astype(BF16)
        outs[to][1] = suffix.astype(BF16)


def cross_body(per_owner, *refs):
    parts, carried, packed = refs[:GROUPS], refs[GROUPS : 2 * GROUPS], refs[2 * GROUPS : 3 * GROUPS]
    out = refs[3 * GROUPS]
    size = out.shape[-1]
    for pair in range(per_owner // 2):
        sums = []
        for i in (2 * pair, 2 * pair + 1):
            total = dot_nt(parts[0][1, i], carried[0][0, i])
            for apart in range(1, GROUPS):
                total += dot_nt(parts[apart][1, i], carried[apart][0, i])
            sums.append(total + total.T)
        both, diagonal = pack(*sums)
        for apart in range(GROUPS):
            both += packed[apart][pair, :size].astype(F32)
            diagonal += packed[apart][pair, size:].astype(F32)
        out[pair, :size] = both.astype(BF16)
        out[pair, size:] = diagonal.astype(BF16)


def final_body(per_owner, *refs):
    q, k, v, g, key_w, gram, part_q, part_k, part_v, other, extra = refs[:11]
    carried = refs[11 : 11 + 2 * GROUPS]
    query_grad, key_grad, value_grad = refs[11 + 2 * GROUPS :]
    size = gram.shape[-1]
    core, chip = place()
    for which in (0, 1):
        half = core if which == 0 else 1 - core
        for apart in range(GROUPS):
            for i in range(per_owner):
                at = columns(head_of(half, chip, apart, i, per_owner), size)
                state = carried[which * GROUPS + apart]
                if which == 0:
                    near_early, near_late = other[apart, 0, i], other[apart, 1, i]
                else:
                    near_early = near_late = extra[apart, i]
                prefix = state[0, i].astype(F32)
                prefix += jnp.where(core == 1, near_early.astype(F32), 0.0)
                suffix = state[1, i].astype(F32)
                suffix += jnp.where(core == 0, near_late.astype(F32), 0.0)
                prefix = prefix.astype(BF16)
                suffix = suffix.astype(BF16)
                square = gram[which, apart, i]
                raw_q = (part_q[which, apart, i] + dot_nt(g[:, at], prefix)).astype(BF16)
                query_grad[:, at] = dot_nn(raw_q, square).astype(BF16)
                raw_k = (part_k[which, apart, i] + dot_nt(v[:, at], suffix)).astype(BF16)
                key_grad[:, at] = dot_nn(raw_k, square).astype(BF16)
                whole = part_v[which, apart, i] + dot_nn(key_w[which, apart, i], suffix)
                value_grad[:, at] = whole.astype(BF16)


def map_body(per_owner, scale, w, *refs):
    packed, out = refs[: 2 * GROUPS], refs[2 * GROUPS]
    size = w.shape[-1]
    core, chip = place()
    rows, cols = triangle(size)
    for which in (0, 1):
        half = core if which == 0 else 1 - core
        for apart in range(GROUPS):
            for pair in range(per_owner // 2):
                ref = packed[which * GROUPS + apart]
                both = ref[pair, :size].astype(F32)
                diagonal = ref[pair, size:][:1].astype(F32)
                turned = both.T
                first = jnp.where(rows >= cols, both, turned)
                second = jnp.where(rows < cols, both, turned)
                second = jnp.where(rows == cols, diagonal, second)
                for i, whole in ((2 * pair, first), (2 * pair + 1, second)):
                    head = head_of(half, chip, apart, i, per_owner)
                    out[head] = dot_nn(whole.astype(BF16), w[head]) * scale


def swap(x, apart):
    count = lax.axis_size("ctx")
    return lax.ppermute(x, "ctx", [(i, i ^ apart) for i in range(count)])


def paired(q, k, v, g, w):
    rows, width = q.shape
    heads, size = w.shape[0], w.shape[-1]
    per_owner = heads // (2 * GROUPS)
    pairs = per_owner // 2
    length = rows * lax.axis_size("ctx")
    block = (size, size)
    both_shape = (GROUPS, 2, per_owner) + block
    one_shape = (GROUPS, per_owner) + block
    state_shape = (2, per_owner) + block
    pack_shape = (pairs, size + EXTRA, size)
    all_shape = (2, GROUPS, per_owner) + block
    bind = functools.partial

    (send,) = call(bind(states_body, False, per_owner), [(both_shape, BF16)], q, k, v, g)
    other = swap(send, 1)
    own, extra = call(
        bind(states_body, True, per_owner), [(both_shape, BF16), (one_shape, BF16)], q, k, v, g
    )
    chip_states = call(add_body, [(state_shape, BF16)] * GROUPS, own, other)
    parts = [chip_states[0]] + [swap(chip_states[j], 2 * j) for j in range(1, GROUPS)]
    extra = swap(extra, 1)

    own_c, send_c, part_q = call(
        bind(local_body, per_owner),
        [(one_shape, BF16), (one_shape, BF16), (all_shape, F32)],
        q, k, v, g,
    )
    other_c = swap(send_c, 1)
    chip_c = call(
        bind(pack_body, per_owner), [(pack_shape, BF16)] * GROUPS, own, other, own_c, other_c
    )
    packed = [chip_c[0]] + [swap(chip_c[j], 2 * j) for j in range(1, GROUPS)]
    part_k, part_v, key_w, gram = call(
        bind(local_rest_body, per_owner),
        [(all_shape, F32), (all_shape, F32), (all_shape, BF16), (all_shape, BF16)],
        q, k, v, g, w,
    )

    carried = call(carry_body, [(state_shape, BF16)] * GROUPS, *parts)
    near = [carried[0]] + [swap(carried[j], 2 * j) for j in range(1, GROUPS)]
    far = [swap(x, 1) for x in near]
    (total,) = call(
        bind(cross_body, per_owner), [(pack_shape, BF16)], *parts, *carried, *packed
    )
    near_map = [total] + [swap(total, 2 * j) for j in range(1, GROUPS)]
    far_map = [swap(x, 1) for x in near_map]
    grads = call(
        bind(final_body, per_owner),
        [((rows, width), BF16)] * 3,
        q, k, v, g, key_w, gram, part_q, part_k, part_v, other, extra, *near, *far,
    )
    (map_grad,) = call(
        bind(map_body, per_owner, 1.0 / math.sqrt(length)),
        [((heads,) + block, F32)],
        w, *near_map, *far_map,
    )
    return (*grads, map_grad)


def gathered(q, k, v, g, w):
    rows, width = q.shape
    heads, size = w.shape[0], w.shape[-1]
    count = lax.axis_size("ctx")
    me = lax.axis_index("ctx")
    q, k, v, g = (x.reshape(rows, heads, size) for x in (q, k, v, g))

    def mul(spec, a, b):
        return jnp.einsum(spec, a, b, preferred_element_type=F32)

    query_feat = mul("thd,hde->the", q, w).astype(BF16)
    key_feat = mul("thd,hde->the", k, w).astype(BF16)
    key_state = mul("the,thv->hev", key_feat, v).astype(BF16)
    grad_state = mul("the,thv->hev", query_feat, g).astype(BF16)
    index = jnp.arange(count).reshape(count, 1, 1, 1)
    keys = lax.all_gather(key_state, "ctx").astype(F32)
    prefix = jnp.sum(jnp.where(index < me, keys, 0.0), 0).astype(BF16)
    grads = lax.all_gather(grad_state, "ctx").astype(F32)
    suffix = jnp.sum(jnp.where(index > me, grads, 0.0), 0).astype(BF16)
    row, col = triangle(rows)
    causal = row >= col
    scores = jnp.where(causal, mul("the,she->hts", query_feat, key_feat), 0.0).astype(BF16)
    mixing = jnp.where(causal, mul("thv,shv->hts", g, v), 0.0).astype(BF16)
    feat_q = mul("hts,she->the", mixing, key_feat) + mul("thv,hev->the", g, prefix)
    feat_k = mul("hts,the->she", mixing, query_feat) + mul("shv,hev->she", v, suffix)
    feat_q, feat_k = feat_q.astype(BF16), feat_k.astype(BF16)
    value_grad = mul("hts,thv->shv", scores, g) + mul("she,hev->shv", key_feat, suffix)
    query_grad = mul("the,hde->thd", feat_q, w)
    key_grad = mul("the,hde->thd", feat_k, w)
    local = mul("thd,the->hde", q, feat_q) + mul("thd,the->hde", k, feat_k)
    map_grad = lax.psum(local.astype(BF16).astype(F32), "ctx") / math.sqrt(rows * count)
    flat = (rows, width)
    return (
        query_grad.reshape(flat).astype(BF16),
        key_grad.reshape(flat).astype(BF16),
        value_grad.reshape(flat).astype(BF16),
        map_grad,
    )


def per_device(queries, key_rows, values, out_grad, feature_map):
    fits = lax.axis_size("ctx") == 2 * GROUPS and feature_map.shape[0] % (4 * GROUPS) == 0
    plan = paired if fits else gathered
    return plan(queries, key_rows, values, out_grad, feature_map)


def solution(mesh):
    rows = P(("seq", "ctx"), None)
    return jax.shard_map(
        per_device,
        mesh=mesh,
        in_specs=(rows, rows, rows, rows, P()),
        out_specs=(rows, rows, rows, P("seq", None, None)),
        check_vma=False,
    )
```

time: 170 us -> 53.4 us (0.31)
  waiting for transfers between devices: 118 us -> 8.05 us
  Pallas kernels: 0 us -> 21.8 us
  matrix products: 20.6 us -> 0 us
  starting transfers between devices: 0.12 us -> 18.2 us
  between operations: 13.9 us -> 0.78 us
  other arithmetic: 9.1 us -> 0 us
  local copies, waits for them, and re-layouts: 6.98 us -> 4.18 us
    all_gather x2 -> x0, waiting for transfers between devices: 66.9 us -> none  [carried_in(): gathered = lax.all_gather(part, axis)]
    psum x1 -> x0, waiting for transfers between devices: 51.1 us -> none  [per_device(): lax.psum(local_grad.astype(jnp.bfloat16), 'ctx').astype(jnp.float32)]
    pallas_call x0 -> x10, Pallas kernels: none -> 21.8 us  [call(): pl.pallas_call(body, out_shape=[jax.ShapeDtypeStruct(shape, dtype) for sh...]
    dot_general x15 -> x0, matrix products: 20.6 us -> none  [the longest x1 2.48 us: per_device(): jnp.einsum('thd,the->hde', key_h, feat_kgrad, preferred_element_type=f32)]
    ppermute x0 -> x23, starting transfers between devices: none -> 18.2 us  [swap(): return lax.ppermute(x, 'ctx', [(i, i ^ apart) for i in range(count)])]
    ppermute x0 -> x23, waiting for transfers between devices: none -> 8.05 us  [swap(): return lax.ppermute(x, 'ctx', [(i, i ^ apart) for i in range(count)])]
    add x7 -> x0, other arithmetic: 7.94 us -> none  [add_states(): return earlier + later]
    unnamed x10 -> x18, local copies, waits for them, and re-layouts: 5.48 us -> 4.18 us
  transfers between devices with their start and end apart: 3 -> 23, of which waited for: 3 -> 10; matrix products, arithmetic and copies ran while one was open for 9% -> 0% of each run, Pallas kernels for 0% -> 31%
where the time goes in v1:
time: 53.4 us; the launch traced here: 53.1 us
  Pallas kernels  21.8 us (41%)
  starting transfers between devices  18.2 us (34%)
  waiting for transfers between devices  8.05 us (15%)
  local copies, waits for them, and re-layouts  4.18 us (8%)
  between operations  0.78 us (1%)
    pallas_call x10, Pallas kernels, call(): pl.pallas_call(body, out_shape=[jax.ShapeDtypeStruct(shape, dtype) for sh...  21.8 us
    ppermute x23, starting transfers between devices, swap(): return lax.ppermute(x, 'ctx', [(i, i ^ apart) for i in range(count)])  18.2 us
    ppermute x23, waiting for transfers between devices, swap(): return lax.ppermute(x, 'ctx', [(i, i ^ apart) for i in range(count)])  8.05 us
    unnamed x18, local copies, waits for them, and re-layouts  4.18 us
  transfers between devices with their start and end apart: 23, of which 10 were waited for; matrix products, arithmetic and copies ran while one was open for 0% of the time, Pallas kernels for 31%

profile of v1, /device:TPU:0, one launch (start us, length us, event | category | flops | bytes accessed | tf_op | source)
XLA Modules:
  0.0 53.1 jit_solution(18022526782019858060)
XLA Ops:
  0.6 0.0 copy-start
  0.6 1.0 %copy-done = bf16[128,2048]{1,0:T(8,128)(2,1)S(1)} copy-done((bf16[128,2048]{1,0:T(8,128)(2,1)S(1)}, bf16[128,2048]{1,0:T(8,128)(2,1)}, u32[]{:S(2)}) %copy-start) | copy-done | bytes 524312
  1.7 1.0 %copy-done.2 = bf16[128,2048]{1,0:T(8,128)(2,1)S(1)} copy-done((bf16[128,2048]{1,0:T(8,128)(2,1)S(1)}, bf16[128,2048]{1,0:T(8,128)(2,1)}, u32[]{:S(2)}) %copy-start.2) | copy-done | bytes 524312
  2.7 1.0 %copy-done.4 = bf16[128,2048]{1,0:T(8,128)(2,1)S(1)} copy-done((bf16[128,2048]{1,0:T(8,128)(2,1)S(1)}, bf16[128,2048]{1,0:T(8,128)(2,1)}, u32[]{:S(2)}) %copy-start.4) | copy-done | bytes 524312
  3.8 1.0 %copy-done.6 = bf16[128,2048]{1,0:T(8,128)(2,1)S(1)} copy-done((bf16[128,2048]{1,0:T(8,128)(2,1)S(1)}, bf16[128,2048]{1,0:T(8,128)(2,1)}, u32[]{:S(2)}) %copy-start.6) | copy-done | bytes 524312
  4.8 0.5 shard_map.86
  5.3 0.5 collective-permute-start
  5.8 2.7 %shard_map.85 = (bf16[4,2,128,128]{3,2,1,0:T(8,128)(2,1)S(1)}, bf16[4,2,128,128]{3,2,1,0:T(8,128)(2,1)S(1)}, f32[2,4,2,128,128]{4,3,2,1,0:T(8,128)S(1)}) custom-call(bf16[128,2048]{1,0:T(8,128)(2,1)S(1)} %copy-done, bf16[128,2048]{1,0:T(8,128)(2,1)S(1)} %copy-done.2, bf16[128,2048]{1,0:T(8,128)(2,1)S(1)} %copy-done.4, bf16[128,2048]{1,0:T(8,128)(2,1)S(1)} %copy-done.6), custom_call_target="tpu_custom_call" | custom-call | tf_op jit(solution)/shard_map/pallas_call | solution.py:32
  8.5 0.1 collective-permute-start.12
  8.6 0.5 shard_map.87
  9.1 0.0 collective-permute-done.other.refs_9_
  9.1 0.1 shard_map.88
  9.3 3.0 %collective-permute-start.2 = (bf16[2,2,128,128]{3,2,1,0:T(8,128)(2,1)S(1)}, bf16[2,2,128,128]{3,2,1,0:T(8,128)(2,1)S(1)}, u32[]{:S(2)}, u32[]{:S(2)}) collective-permute-start(bf16[2,2,128,128]{3,2,1,0:T(8,128)(2,1)S(1)} %get-tuple-element.36), channel_id=1, source_target_pairs={{0,2},{1,3},{2,0},{3,1},{4,6},{5,7},{6,4},{7,5},{8,10},{9,11},{10,... | collective-permute-start | bytes 393224 | tf_op jit(solution)/shard_map/ppermute | solution.py:235
  12.3 1.5 %collective-permute-start.3 = (bf16[2,2,128,128]{3,2,1,0:T(8,128)(2,1)S(1)}, bf16[2,2,128,128]{3,2,1,0:T(8,128)(2,1)S(1)}, u32[]{:S(2)}, u32[]{:S(2)}) collective-permute-start(bf16[2,2,128,128]{3,2,1,0:T(8,128)(2,1)S(1)} %get-tuple-element.37), channel_id=1, source_target_pairs={{0,4},{1,5},{2,6},{3,7},{4,0},{5,1},{6,2},{7,3},{8,12},{9,13},{10,... | collective-permute-start | bytes 393224 | tf_op jit(solution)/shard_map/ppermute | solution.py:235
  13.8 0.0 collective-permute-start.4
  13.8 0.4 shard_map.91
  14.2 2.0 %collective-permute-start.13 = (bf16[1,144,128]{2,1,0:T(8,128)(2,1)S(1)}, bf16[1,144,128]{2,1,0:T(8,128)(2,1)S(1)}, u32[]{:S(2)}, u32[]{:S(2)}) collective-permute-start(bf16[1,144,128]{2,1,0:T(8,128)(2,1)S(1)} %get-tuple-element.49), channel_id=1, source_target_pairs={{0,2},{1,3},{2,0},{3,1},{4,6},{5,7},{6,4},{7,5},{8,10},{9,11},{10,... | collective-permute-start | bytes 110600 | tf_op jit(solution)/shard_map/ppermute | solution.py:235
  16.3 1.5 %collective-permute-start.14 = (bf16[1,144,128]{2,1,0:T(8,128)(2,1)S(1)}, bf16[1,144,128]{2,1,0:T(8,128)(2,1)S(1)}, u32[]{:S(2)}, u32[]{:S(2)}) collective-permute-start(bf16[1,144,128]{2,1,0:T(8,128)(2,1)S(1)} %get-tuple-element.50), channel_id=1, source_target_pairs={{0,4},{1,5},{2,6},{3,7},{4,0},{5,1},{6,2},{7,3},{8,12},{9,13},{10,... | collective-permute-start | bytes 110600 | tf_op jit(solution)/shard_map/ppermute | solution.py:235
  17.8 1.8 %collective-permute-start.15 = (bf16[1,144,128]{2,1,0:T(8,128)(2,1)S(1)}, bf16[1,144,128]{2,1,0:T(8,128)(2,1)S(1)}, u32[]{:S(2)}, u32[]{:S(2)}) collective-permute-start(bf16[1,144,128]{2,1,0:T(8,128)(2,1)S(1)} %get-tuple-element.51), channel_id=1, source_target_pairs={{0,6},{1,7},{2,4},{3,5},{4,2},{5,3},{6,0},{7,1},{8,14},{9,15},{10,... | collective-permute-start | bytes 110600 | tf_op jit(solution)/shard_map/ppermute | solution.py:235
  19.6 0.5 collective-permute-done.3.refs_2_
  20.1 0.8 %collective-permute-done.4.refs_3_ = bf16[2,2,128,128]{3,2,1,0:T(8,128)(2,1)S(1)} collective-permute-done((bf16[2,2,128,128]{3,2,1,0:T(8,128)(2,1)S(1)}, bf16[2,2,128,128]{3,2,1,0:T(8,128)(2,1)S(1)}, u32[]{:S(2)}, u32[]{:S(2)}) %collective-permute-start.4) | collective-permute-done | bytes 131104 | tf_op jit(solution)/shard_map/ppermute | solution.py:235
  20.9 0.2 shard_map.89
  21.1 0.0 collective-permute-done.13.refs_9_
  21.1 0.3 collective-permute-done.14.refs_10_
  21.4 1.2 %collective-permute-done.15.refs_11_ = bf16[1,144,128]{2,1,0:T(8,128)(2,1)S(1)} collective-permute-done((bf16[1,144,128]{2,1,0:T(8,128)(2,1)S(1)}, bf16[1,144,128]{2,1,0:T(8,128)(2,1)S(1)}, u32[]{:S(2)}, u32[]{:S(2)}) %collective-permute-start.15) | collective-permute-done | bytes 36896 | tf_op jit(solution)/shard_map/ppermute | solution.py:235
  22.6 0.4 shard_map.92.refs_0_
  23.1 0.1 collective-permute-start.19
  23.1 1.9 %collective-permute-start.18 = (bf16[1,144,128]{2,1,0:T(8,128)(2,1)S(1)}, bf16[1,144,128]{2,1,0:T(8,128)(2,1)S(1)}, u32[]{:S(2)}, u32[]{:S(2)}) collective-permute-start(bf16[1,144,128]{2,1,0:T(8,128)(2,1)S(1)} %shard_map.92.refs_0_), channel_id=1, source_target_pairs={{0,6},{1,7},{2,4},{3,5},{4,2},{5,3},{6,0},{7,1},{8,14},{9,15},{10,... | collective-permute-start | bytes 110600 | tf_op jit(solution)/shard_map/ppermute | solution.py:235
  25.0 0.5 collective-permute-start.17
  25.5 1.2 %collective-permute-start.16 = (bf16[1,144,128]{2,1,0:T(8,128)(2,1)S(1)}, bf16[1,144,128]{2,1,0:T(8,128)(2,1)S(1)}, u32[]{:S(2)}, u32[]{:S(2)}) collective-permute-start(bf16[1,144,128]{2,1,0:T(8,128)(2,1)S(1)} %shard_map.92.refs_0_), channel_id=1, source_target_pairs={{0,2},{1,3},{2,0},{3,1},{4,6},{5,7},{6,4},{7,5},{8,10},{9,11},{10,... | collective-permute-start | bytes 110600 | tf_op jit(solution)/shard_map/ppermute | solution.py:235
  26.7 0.0 collective-permute-start.1
  26.7 0.0 collective-permute-done.19.refs_4_
  26.7 0.8 %collective-permute-start.5 = (bf16[2,2,128,128]{3,2,1,0:T(8,128)(2,1)S(1)}, bf16[2,2,128,128]{3,2,1,0:T(8,128)(2,1)S(1)}, u32[]{:S(2)}, u32[]{:S(2)}) collective-permute-start(bf16[2,2,128,128]{3,2,1,0:T(8,128)(2,1)S(1)} %get-tuple-element.40.refs_5_), channel_id=1, source_target_pairs={{0,2},{1,3},{2,0},{3,1},{4,6},{5,7},{6,4},{7,5},{8,10},{9,11},{10,... | collective-permute-start | bytes 393224 | tf_op jit(solution)/shard_map/ppermute | solution.py:235
  27.5 0.6 %collective-permute-done.18.refs_3_ = bf16[1,144,128]{2,1,0:T(8,128)(2,1)S(1)} collective-permute-done((bf16[1,144,128]{2,1,0:T(8,128)(2,1)S(1)}, bf16[1,144,128]{2,1,0:T(8,128)(2,1)S(1)}, u32[]{:S(2)}, u32[]{:S(2)}) %collective-permute-start.18) | collective-permute-done | bytes 36896 | tf_op jit(solution)/shard_map/ppermute | solution.py:235
  28.1 1.0 %collective-permute-start.6 = (bf16[2,2,128,128]{3,2,1,0:T(8,128)(2,1)S(1)}, bf16[2,2,128,128]{3,2,1,0:T(8,128)(2,1)S(1)}, u32[]{:S(2)}, u32[]{:S(2)}) collective-permute-start(bf16[2,2,128,128]{3,2,1,0:T(8,128)(2,1)S(1)} %get-tuple-element.41.refs_6_), channel_id=1, source_target_pairs={{0,4},{1,5},{2,6},{3,7},{4,0},{5,1},{6,2},{7,3},{8,12},{9,13},{10,... | collective-permute-start | bytes 393224 | tf_op jit(solution)/shard_map/ppermute | solution.py:235
  29.1 1.4 %collective-permute-start.7 = (bf16[2,2,128,128]{3,2,1,0:T(8,128)(2,1)S(1)}, bf16[2,2,128,128]{3,2,1,0:T(8,128)(2,1)S(1)}, u32[]{:S(2)}, u32[]{:S(2)}) collective-permute-start(bf16[2,2,128,128]{3,2,1,0:T(8,128)(2,1)S(1)} %get-tuple-element.42.refs_7_), channel_id=1, source_target_pairs={{0,6},{1,7},{2,4},{3,5},{4,2},{5,3},{6,0},{7,1},{8,14},{9,15},{10,... | collective-permute-start | bytes 393224 | tf_op jit(solution)/shard_map/ppermute | solution.py:235
  30.5 1.2 %collective-permute-done.22.refs_7_ = bf16[1,144,128]{2,1,0:T(8,128)(2,1)S(1)} collective-permute-done((bf16[1,144,128]{2,1,0:T(8,128)(2,1)S(1)}, bf16[1,144,128]{2,1,0:T(8,128)(2,1)S(1)}, u32[]{:S(2)}, u32[]{:S(2)}) %collective-permute-start.22) | collective-permute-done | bytes 36896 | tf_op jit(solution)/shard_map/ppermute | solution.py:235
  31.7 0.2 collective-permute-start.21
  31.8 1.1 %collective-permute-done.21.refs_6_ = bf16[1,144,128]{2,1,0:T(8,128)(2,1)S(1)} collective-permute-done((bf16[1,144,128]{2,1,0:T(8,128)(2,1)S(1)}, bf16[1,144,128]{2,1,0:T(8,128)(2,1)S(1)}, u32[]{:S(2)}, u32[]{:S(2)}) %collective-permute-start.21) | collective-permute-done | bytes 36896 | tf_op jit(solution)/shard_map/ppermute | solution.py:235
  32.9 0.2 collective-permute-start.20
  33.1 1.1 %collective-permute-done.20.refs_5_ = bf16[1,144,128]{2,1,0:T(8,128)(2,1)S(1)} collective-permute-done((bf16[1,144,128]{2,1,0:T(8,128)(2,1)S(1)}, bf16[1,144,128]{2,1,0:T(8,128)(2,1)S(1)}, u32[]{:S(2)}, u32[]{:S(2)}) %collective-permute-start.20) | collective-permute-done | bytes 36896 | tf_op jit(solution)/shard_map/ppermute | solution.py:235
  34.1 0.2 collective-permute-start.8
  34.3 0.3 collective-permute-start.9
  34.6 0.4 collective-permute-done.6.refs_13_
  35.0 0.9 %collective-permute-done.7.refs_14_ = bf16[2,2,128,128]{3,2,1,0:T(8,128)(2,1)S(1)} collective-permute-done((bf16[2,2,128,128]{3,2,1,0:T(8,128)(2,1)S(1)}, bf16[2,2,128,128]{3,2,1,0:T(8,128)(2,1)S(1)}, u32[]{:S(2)}, u32[]{:S(2)}) %collective-permute-start.7) | collective-permute-done | bytes 131104 | tf_op jit(solution)/shard_map/ppermute | solution.py:235
  36.0 11.3 %shard_map.84 = (f32[2,4,2,128,128]{4,3,2,1,0:T(8,128)S(1)}, f32[2,4,2,128,128]{4,3,2,1,0:T(8,128)S(1)}, bf16[2,4,2,128,128]{4,3,2,1,0:T(8,128)(2,1)S(1)}, bf16[2,4,2,128,128]{4,3,2,1,0:T(8,128)(2,1)S(1)}) custom-call(bf16[128,2048]{1,0:T(8,128)(2,1)S(1)} %copy-done.1, bf16[128,2048]{1,0:T(8,128)(2,1)S(1)} %copy-done.3, bf16[128,2048]{1,0:T(8,128)(2,1)S(1)} %copy-done.5, ...), custom_call_target="tpu_custom_call" | custom-call | tf_op jit(solution)/shard_map/pallas_call | solution.py:32
  47.3 1.3 %shard_map.93 = f32[16,128,128]{2,1,0:T(8,128)} custom-call(bf16[16,128,128]{2,1,0:T(8,128)(2,1)S(1)} %copy-done.8, bf16[1,144,128]{2,1,0:T(8,128)(2,1)S(1)} %shard_map.92.refs_0_, bf16[1,144,128]{2,1,0:T(8,128)(2,1)S(1)} %collective-permute-done.16.refs_1_, bf16[1,144,128]{2,1,0:T(8,128)(2,1)S(1)} %collective-permute-done.17.refs_2_, ...), custom_call_target="tpu_custom_call" | custom-call | tf_op jit(solution)/shard_map/pallas_call | solution.py:32
  48.7 4.3 %shard_map.90 = (bf16[128,2048]{1,0:T(8,128)(2,1)}, bf16[128,2048]{1,0:T(8,128)(2,1)}, bf16[128,2048]{1,0:T(8,128)(2,1)}) custom-call(bf16[128,2048]{1,0:T(8,128)(2,1)S(1)} %copy-done.1, bf16[128,2048]{1,0:T(8,128)(2,1)S(1)} %copy-done.3, bf16[128,2048]{1,0:T(8,128)(2,1)S(1)} %copy-done.5, bf16[128,2048]{1,0:T(8,128)(2,1)S(1)} %copy-done.7, ...), custom_call_target="tpu_custom_call" | custom-call | tf_op jit(solution)/shard_map/pallas_call | solution.py:32
  (26 shorter events, 0.1 us)
Async XLA Ops:
  0.6 1.0 %copy-start = (bf16[128,2048]{1,0:T(8,128)(2,1)S(1)}, bf16[128,2048]{1,0:T(8,128)(2,1)}, u32[]{:S(2)}) copy-start(bf16[128,2048]{1,0:T(8,128)(2,1)} %refs_0_.1) | copy-start | bytes 1572868
  1.7 1.0 %copy-start.2 = (bf16[128,2048]{1,0:T(8,128)(2,1)S(1)}, bf16[128,2048]{1,0:T(8,128)(2,1)}, u32[]{:S(2)}) copy-start(bf16[128,2048]{1,0:T(8,128)(2,1)} %refs_1_.1) | copy-start | bytes 1572868
  2.7 1.0 %copy-start.4 = (bf16[128,2048]{1,0:T(8,128)(2,1)S(1)}, bf16[128,2048]{1,0:T(8,128)(2,1)}, u32[]{:S(2)}) copy-start(bf16[128,2048]{1,0:T(8,128)(2,1)} %refs_2_.1) | copy-start | bytes 1572868
  3.8 1.0 %copy-start.6 = (bf16[128,2048]{1,0:T(8,128)(2,1)S(1)}, bf16[128,2048]{1,0:T(8,128)(2,1)}, u32[]{:S(2)}) copy-start(bf16[128,2048]{1,0:T(8,128)(2,1)} %refs_3_.1) | copy-start | bytes 1572868
  5.3 3.9 %collective-permute-start = (bf16[4,2,2,128,128]{4,3,2,1,0:T(8,128)(2,1)S(1)}, bf16[4,2,2,128,128]{4,3,2,1,0:T(8,128)(2,1)S(1)}, u32[]{:S(2)}, u32[]{:S(2)}) collective-permute-start(bf16[4,2,2,128,128]{4,3,2,1,0:T(8,128)(2,1)S(1)} %shard_map.86), channel_id=1, source_target_pairs={{0,1},{1,0},{2,3},{3,2},{4,5},{5,4},{6,7},{7,6},{8,9},{9,8},{10,11... | collective-permute-start | bytes 1572872 | tf_op jit(solution)/shard_map/ppermute | solution.py:235
  8.5 5.3 %collective-permute-start.12 = (bf16[4,2,128,128]{3,2,1,0:T(8,128)(2,1)S(1)}, bf16[4,2,128,128]{3,2,1,0:T(8,128)(2,1)S(1)}, u32[]{:S(2)}, u32[]{:S(2)}) collective-permute-start(bf16[4,2,128,128]{3,2,1,0:T(8,128)(2,1)S(1)} %get-tuple-element.47), channel_id=1, source_target_pairs={{0,1},{1,0},{2,3},{3,2},{4,5},{5,4},{6,7},{7,6},{8,9},{9,8},{10,11... | collective-permute-start | bytes 786440 | tf_op jit(solution)/shard_map/ppermute | solution.py:235
  9.3 8.5 %collective-permute-start.2 = (bf16[2,2,128,128]{3,2,1,0:T(8,128)(2,1)S(1)}, bf16[2,2,128,128]{3,2,1,0:T(8,128)(2,1)S(1)}, u32[]{:S(2)}, u32[]{:S(2)}) collective-permute-start(bf16[2,2,128,128]{3,2,1,0:T(8,128)(2,1)S(1)} %get-tuple-element.36), channel_id=1, source_target_pairs={{0,2},{1,3},{2,0},{3,1},{4,6},{5,7},{6,4},{7,5},{8,10},{9,11},{10,... | collective-permute-start | bytes 393224 | tf_op jit(solution)/shard_map/ppermute | solution.py:235
  12.3 7.8 %collective-permute-start.3 = (bf16[2,2,128,128]{3,2,1,0:T(8,128)(2,1)S(1)}, bf16[2,2,128,128]{3,2,1,0:T(8,128)(2,1)S(1)}, u32[]{:S(2)}, u32[]{:S(2)}) collective-permute-start(bf16[2,2,128,128]{3,2,1,0:T(8,128)(2,1)S(1)} %get-tuple-element.37), channel_id=1, source_target_pairs={{0,4},{1,5},{2,6},{3,7},{4,0},{5,1},{6,2},{7,3},{8,12},{9,13},{10,... | collective-permute-start | bytes 393224 | tf_op jit(solution)/shard_map/ppermute | solution.py:235
  13.8 7.1 %collective-permute-start.4 = (bf16[2,2,128,128]{3,2,1,0:T(8,128)(2,1)S(1)}, bf16[2,2,128,128]{3,2,1,0:T(8,128)(2,1)S(1)}, u32[]{:S(2)}, u32[]{:S(2)}) collective-permute-start(bf16[2,2,128,128]{3,2,1,0:T(8,128)(2,1)S(1)} %get-tuple-element.38), channel_id=1, source_target_pairs={{0,6},{1,7},{2,4},{3,5},{4,2},{5,3},{6,0},{7,1},{8,14},{9,15},{10,... | collective-permute-start | bytes 393224 | tf_op jit(solution)/shard_map/ppermute | solution.py:235
  13.8 22.2 %copy-start.7 = (bf16[128,2048]{1,0:T(8,128)(2,1)S(1)}, bf16[128,2048]{1,0:T(8,128)(2,1)}, u32[]{:S(2)}) copy-start(bf16[128,2048]{1,0:T(8,128)(2,1)} %refs_3_.1) | copy-start | bytes 1572868
  13.8 22.2 %copy-start.8 = (bf16[16,128,128]{2,1,0:T(8,128)(2,1)S(1)}, bf16[16,128,128]{2,1,0:T(8,128)(2,1)}, u32[]{:S(2)}) copy-start(bf16[16,128,128]{2,1,0:T(8,128)(2,1)} %w.3) | copy-start | bytes 1572868
  14.2 6.9 %collective-permute-start.13 = (bf16[1,144,128]{2,1,0:T(8,128)(2,1)S(1)}, bf16[1,144,128]{2,1,0:T(8,128)(2,1)S(1)}, u32[]{:S(2)}, u32[]{:S(2)}) collective-permute-start(bf16[1,144,128]{2,1,0:T(8,128)(2,1)S(1)} %get-tuple-element.49), channel_id=1, source_target_pairs={{0,2},{1,3},{2,0},{3,1},{4,6},{5,7},{6,4},{7,5},{8,10},{9,11},{10,... | collective-permute-start | bytes 110600 | tf_op jit(solution)/shard_map/ppermute | solution.py:235
  16.3 5.2 %collective-permute-start.14 = (bf16[1,144,128]{2,1,0:T(8,128)(2,1)S(1)}, bf16[1,144,128]{2,1,0:T(8,128)(2,1)S(1)}, u32[]{:S(2)}, u32[]{:S(2)}) collective-permute-start(bf16[1,144,128]{2,1,0:T(8,128)(2,1)S(1)} %get-tuple-element.50), channel_id=1, source_target_pairs={{0,4},{1,5},{2,6},{3,7},{4,0},{5,1},{6,2},{7,3},{8,12},{9,13},{10,... | collective-permute-start | bytes 110600 | tf_op jit(solution)/shard_map/ppermute | solution.py:235
  17.8 4.9 %collective-permute-start.15 = (bf16[1,144,128]{2,1,0:T(8,128)(2,1)S(1)}, bf16[1,144,128]{2,1,0:T(8,128)(2,1)S(1)}, u32[]{:S(2)}, u32[]{:S(2)}) collective-permute-start(bf16[1,144,128]{2,1,0:T(8,128)(2,1)S(1)} %get-tuple-element.51), channel_id=1, source_target_pairs={{0,6},{1,7},{2,4},{3,5},{4,2},{5,3},{6,0},{7,1},{8,14},{9,15},{10,... | collective-permute-start | bytes 110600 | tf_op jit(solution)/shard_map/ppermute | solution.py:235
  20.9 15.1 %copy-start.5 = (bf16[128,2048]{1,0:T(8,128)(2,1)S(1)}, bf16[128,2048]{1,0:T(8,128)(2,1)}, u32[]{:S(2)}) copy-start(bf16[128,2048]{1,0:T(8,128)(2,1)} %refs_2_.1) | copy-start | bytes 1572868
  22.6 13.4 %copy-start.1 = (bf16[128,2048]{1,0:T(8,128)(2,1)S(1)}, bf16[128,2048]{1,0:T(8,128)(2,1)}, u32[]{:S(2)}) copy-start(bf16[128,2048]{1,0:T(8,128)(2,1)} %refs_0_.1) | copy-start | bytes 1572868
  22.6 13.4 %copy-start.3 = (bf16[128,2048]{1,0:T(8,128)(2,1)S(1)}, bf16[128,2048]{1,0:T(8,128)(2,1)}, u32[]{:S(2)}) copy-start(bf16[128,2048]{1,0:T(8,128)(2,1)} %refs_1_.1) | copy-start | bytes 1572868
  23.1 3.6 %collective-permute-start.19 = (bf16[1,144,128]{2,1,0:T(8,128)(2,1)S(1)}, bf16[1,144,128]{2,1,0:T(8,128)(2,1)S(1)}, u32[]{:S(2)}, u32[]{:S(2)}) collective-permute-start(bf16[1,144,128]{2,1,0:T(8,128)(2,1)S(1)} %shard_map.92.refs_0_), channel_id=1, source_target_pairs={{0,1},{1,0},{2,3},{3,2},{4,5},{5,4},{6,7},{7,6},{8,9},{9,8},{10,11... | collective-permute-start | bytes 110600 | tf_op jit(solution)/shard_map/ppermute | solution.py:235
  23.1 5.0 %collective-permute-start.18 = (bf16[1,144,128]{2,1,0:T(8,128)(2,1)S(1)}, bf16[1,144,128]{2,1,0:T(8,128)(2,1)S(1)}, u32[]{:S(2)}, u32[]{:S(2)}) collective-permute-start(bf16[1,144,128]{2,1,0:T(8,128)(2,1)S(1)} %shard_map.92.refs_0_), channel_id=1, source_target_pairs={{0,6},{1,7},{2,4},{3,5},{4,2},{5,3},{6,0},{7,1},{8,14},{9,15},{10,... | collective-permute-start | bytes 110600 | tf_op jit(solution)/shard_map/ppermute | solution.py:235
  25.0 4.1 %collective-permute-start.17 = (bf16[1,144,128]{2,1,0:T(8,128)(2,1)S(1)}, bf16[1,144,128]{2,1,0:T(8,128)(2,1)S(1)}, u32[]{:S(2)}, u32[]{:S(2)}) collective-permute-start(bf16[1,144,128]{2,1,0:T(8,128)(2,1)S(1)} %shard_map.92.refs_0_), channel_id=1, source_target_pairs={{0,4},{1,5},{2,6},{3,7},{4,0},{5,1},{6,2},{7,3},{8,12},{9,13},{10,... | collective-permute-start | bytes 110600 | tf_op jit(solution)/shard_map/ppermute | solution.py:235
  25.5 5.0 %collective-permute-start.16 = (bf16[1,144,128]{2,1,0:T(8,128)(2,1)S(1)}, bf16[1,144,128]{2,1,0:T(8,128)(2,1)S(1)}, u32[]{:S(2)}, u32[]{:S(2)}) collective-permute-start(bf16[1,144,128]{2,1,0:T(8,128)(2,1)S(1)} %shard_map.92.refs_0_), channel_id=1, source_target_pairs={{0,2},{1,3},{2,0},{3,1},{4,6},{5,7},{6,4},{7,5},{8,10},{9,11},{10,... | collective-permute-start | bytes 110600 | tf_op jit(solution)/shard_map/ppermute | solution.py:235
  26.7 22.0 %collective-permute-start.1 = (bf16[4,2,128,128]{3,2,1,0:T(8,128)(2,1)S(1)}, bf16[4,2,128,128]{3,2,1,0:T(8,128)(2,1)S(1)}, u32[]{:S(2)}, u32[]{:S(2)}) collective-permute-start(bf16[4,2,128,128]{3,2,1,0:T(8,128)(2,1)S(1)} %get-tuple-element.33), channel_id=1, source_target_pairs={{0,1},{1,0},{2,3},{3,2},{4,5},{5,4},{6,7},{7,6},{8,9},{9,8},{10,11... | collective-permute-start | bytes 786440 | tf_op jit(solution)/shard_map/ppermute | solution.py:235
  26.7 7.6 %collective-permute-start.5 = (bf16[2,2,128,128]{3,2,1,0:T(8,128)(2,1)S(1)}, bf16[2,2,128,128]{3,2,1,0:T(8,128)(2,1)S(1)}, u32[]{:S(2)}, u32[]{:S(2)}) collective-permute-start(bf16[2,2,128,128]{3,2,1,0:T(8,128)(2,1)S(1)} %get-tuple-element.40.refs_5_), channel_id=1, source_target_pairs={{0,2},{1,3},{2,0},{3,1},{4,6},{5,7},{6,4},{7,5},{8,10},{9,11},{10,... | collective-permute-start | bytes 393224 | tf_op jit(solution)/shard_map/ppermute | solution.py:235
  28.1 7.0 %collective-permute-start.6 = (bf16[2,2,128,128]{3,2,1,0:T(8,128)(2,1)S(1)}, bf16[2,2,128,128]{3,2,1,0:T(8,128)(2,1)S(1)}, u32[]{:S(2)}, u32[]{:S(2)}) collective-permute-start(bf16[2,2,128,128]{3,2,1,0:T(8,128)(2,1)S(1)} %get-tuple-element.41.refs_6_), channel_id=1, source_target_pairs={{0,4},{1,5},{2,6},{3,7},{4,0},{5,1},{6,2},{7,3},{8,12},{9,13},{10,... | collective-permute-start | bytes 393224 | tf_op jit(solution)/shard_map/ppermute | solution.py:235
  29.1 6.9 %collective-permute-start.7 = (bf16[2,2,128,128]{3,2,1,0:T(8,128)(2,1)S(1)}, bf16[2,2,128,128]{3,2,1,0:T(8,128)(2,1)S(1)}, u32[]{:S(2)}, u32[]{:S(2)}) collective-permute-start(bf16[2,2,128,128]{3,2,1,0:T(8,128)(2,1)S(1)} %get-tuple-element.42.refs_7_), channel_id=1, source_target_pairs={{0,6},{1,7},{2,4},{3,5},{4,2},{5,3},{6,0},{7,1},{8,14},{9,15},{10,... | collective-permute-start | bytes 393224 | tf_op jit(solution)/shard_map/ppermute | solution.py:235
  30.5 1.2 %collective-permute-start.22 = (bf16[1,144,128]{2,1,0:T(8,128)(2,1)S(1)}, bf16[1,144,128]{2,1,0:T(8,128)(2,1)S(1)}, u32[]{:S(2)}, u32[]{:S(2)}) collective-permute-start(bf16[1,144,128]{2,1,0:T(8,128)(2,1)S(1)} %collective-permute-done.18.refs_3_), channel_id=1, source_target_pairs={{0,1},{1,0},{2,3},{3,2},{4,5},{5,4},{6,7},{7,6},{8,9},{9,8},{10,11... | collective-permute-start | bytes 110600 | tf_op jit(solution)/shard_map/ppermute | solution.py:235
  31.7 1.2 %collective-permute-start.21 = (bf16[1,144,128]{2,1,0:T(8,128)(2,1)S(1)}, bf16[1,144,128]{2,1,0:T(8,128)(2,1)S(1)}, u32[]{:S(2)}, u32[]{:S(2)}) collective-permute-start(bf16[1,144,128]{2,1,0:T(8,128)(2,1)S(1)} %collective-permute-done.17.refs_2_), channel_id=1, source_target_pairs={{0,1},{1,0},{2,3},{3,2},{4,5},{5,4},{6,7},{7,6},{8,9},{9,8},{10,11... | collective-permute-start | bytes 110600 | tf_op jit(solution)/shard_map/ppermute | solution.py:235
  32.9 1.2 %collective-permute-start.20 = (bf16[1,144,128]{2,1,0:T(8,128)(2,1)S(1)}, bf16[1,144,128]{2,1,0:T(8,128)(2,1)S(1)}, u32[]{:S(2)}, u32[]{:S(2)}) collective-permute-start(bf16[1,144,128]{2,1,0:T(8,128)(2,1)S(1)} %collective-permute-done.16.refs_1_), channel_id=1, source_target_pairs={{0,1},{1,0},{2,3},{3,2},{4,5},{5,4},{6,7},{7,6},{8,9},{9,8},{10,11... | collective-permute-start | bytes 110600 | tf_op jit(solution)/shard_map/ppermute | solution.py:235
  34.1 14.6 %collective-permute-start.8 = (bf16[2,2,128,128]{3,2,1,0:T(8,128)(2,1)S(1)}, bf16[2,2,128,128]{3,2,1,0:T(8,128)(2,1)S(1)}, u32[]{:S(2)}, u32[]{:S(2)}) collective-permute-start(bf16[2,2,128,128]{3,2,1,0:T(8,128)(2,1)S(1)} %get-tuple-element.39.refs_11_.refs_4_), channel_id=1, source_target_pairs={{0,1},{1,0},{2,3},{3,2},{4,5},{5,4},{6,7},{7,6},{8,9},{9,8},{10,11... | collective-permute-start | bytes 393224 | tf_op jit(solution)/shard_map/ppermute | solution.py:235
  34.3 14.4 %collective-permute-start.9 = (bf16[2,2,128,128]{3,2,1,0:T(8,128)(2,1)S(1)}, bf16[2,2,128,128]{3,2,1,0:T(8,128)(2,1)S(1)}, u32[]{:S(2)}, u32[]{:S(2)}) collective-permute-start(bf16[2,2,128,128]{3,2,1,0:T(8,128)(2,1)S(1)} %collective-permute-done.5.refs_12_), channel_id=1, source_target_pairs={{0,1},{1,0},{2,3},{3,2},{4,5},{5,4},{6,7},{7,6},{8,9},{9,8},{10,11... | collective-permute-start | bytes 393224 | tf_op jit(solution)/shard_map/ppermute | solution.py:235
  35.0 13.6 %collective-permute-start.10 = (bf16[2,2,128,128]{3,2,1,0:T(8,128)(2,1)S(1)}, bf16[2,2,128,128]{3,2,1,0:T(8,128)(2,1)S(1)}, u32[]{:S(2)}, u32[]{:S(2)}) collective-permute-start(bf16[2,2,128,128]{3,2,1,0:T(8,128)(2,1)S(1)} %collective-permute-done.6.refs_13_), channel_id=1, source_target_pairs={{0,1},{1,0},{2,3},{3,2},{4,5},{5,4},{6,7},{7,6},{8,9},{9,8},{10,11... | collective-permute-start | bytes 393224 | tf_op jit(solution)/shard_map/ppermute | solution.py:235
  36.0 12.7 %collective-permute-start.11 = (bf16[2,2,128,128]{3,2,1,0:T(8,128)(2,1)S(1)}, bf16[2,2,128,128]{3,2,1,0:T(8,128)(2,1)S(1)}, u32[]{:S(2)}, u32[]{:S(2)}) collective-permute-start(bf16[2,2,128,128]{3,2,1,0:T(8,128)(2,1)S(1)} %collective-permute-done.7.refs_14_), channel_id=1, source_target_pairs={{0,1},{1,0},{2,3},{3,2},{4,5},{5,4},{6,7},{7,6},{8,9},{9,8},{10,11... | collective-permute-start | bytes 393224 | tf_op jit(solution)/shard_map/ppermute | solution.py:235

commit v2 on v1

v2 whole, which is shorter than its diff:
```python
import functools
import math

import jax
import jax.numpy as jnp
from jax import lax
from jax.experimental import pallas as pl
from jax.experimental.pallas import tpu as pltpu
from jax.sharding import PartitionSpec as P

F32 = jnp.float32
BF16 = jnp.bfloat16
VMEM = pl.BlockSpec(memory_space=pltpu.VMEM)
HBM = pl.BlockSpec(memory_space=pltpu.HBM)
ANY = pl.BlockSpec(memory_space=pl.ANY)
GROUPS = 4
EXTRA = 16


def dot_nn(a, b):
    return lax.dot_general(a, b, (((1,), (0,)), ((), ())), preferred_element_type=F32)


def dot_nt(a, b):
    return lax.dot_general(a, b, (((1,), (1,)), ((), ())), preferred_element_type=F32)


def dot_tn(a, b):
    return lax.dot_general(a, b, (((0,), (0,)), ((), ())), preferred_element_type=F32)


def call(body, outs, operands, cost, after=(), scratch=(), in_spec=VMEM, out_specs=None, aliases=None):
    count = len(operands)

    def run(*refs):
        return body(*refs[:count], *refs[count + len(after) :])

    return pl.pallas_call(
        run,
        out_shape=[jax.ShapeDtypeStruct(shape, dtype) for shape, dtype in outs],
        in_specs=[in_spec] * count + [ANY] * len(after),
        out_specs=out_specs or [VMEM] * len(outs),
        scratch_shapes=list(scratch),
        input_output_aliases=aliases or {},
        cost_estimate=pl.CostEstimate(
            flops=int(cost * 1.15e9), bytes_accessed=0, transcendentals=0
        ),
        compiler_params=pltpu.CompilerParams(vmem_limit_bytes=16 * 2**20),
    )(*operands, *after)


def place():
    me = lax.axis_index("ctx")
    return lax.rem(me, 2), lax.div(me, 2)


def owned(half, chip, per_owner):
    base = half * (GROUPS * per_owner)
    return [
        (apart, i, base + (chip ^ apart) * per_owner + i)
        for apart in range(GROUPS)
        for i in range(per_owner)
    ]


def columns(head, size):
    return pl.ds(pl.multiple_of(head * size, size), size)


def triangle(size):
    rows = lax.broadcasted_iota(jnp.int32, (size, size), 0)
    cols = lax.broadcasted_iota(jnp.int32, (size, size), 1)
    return rows, cols


def load_body(per_owner, q, k, v, g, q_here, k_here, v_here, g_here, send, sems):
    size = send.shape[-1]
    half_width = q.shape[1] // 2
    core, chip = place()
    pairs = ((k, k_here), (v, v_here), (q, q_here), (g, g_here))
    copies = []
    for turn, half in enumerate((1 - core, core)):
        at = columns(half, half_width)
        for n, (source, target) in enumerate(pairs):
            copy = pltpu.make_async_copy(source.at[:, at], target.at[:, at], sems.at[turn, n])
            copy.start()
            copies.append(copy)
    heads = owned(1 - core, chip, per_owner)
    ats = [columns(head, size) for _, _, head in heads]
    for kind, (left, right) in enumerate(((k_here, v_here), (q_here, g_here))):
        copies[2 * kind].wait()
        copies[2 * kind + 1].wait()
        states = [dot_tn(left[:, at], right[:, at]) for at in ats]
        for (apart, i, _), state in zip(heads, states):
            send[apart, kind, i] = state.astype(BF16)
    for copy in copies[4:]:
        copy.wait()


def mixed_keys(q, k, v, g, ats):
    rows, cols = triangle(q.shape[0])
    mixing = [dot_nt(g[:, at], v[:, at]) for at in ats]
    mixing = [jnp.where(rows >= cols, x, 0.0).astype(BF16) for x in mixing]
    return [dot_nn(x, k[:, at]) for x, at in zip(mixing, ats)]


def near_body(per_owner, q, k, v, g, own, extra_c, part_q):
    size = own.shape[-1]
    core, chip = place()
    heads = owned(core, chip, per_owner)
    ats = [columns(head, size) for _, _, head in heads]
    early = [dot_tn(k[:, at], v[:, at]).astype(BF16) for at in ats]
    late = [dot_tn(q[:, at], g[:, at]).astype(BF16) for at in ats]
    for n, (apart, i, _) in enumerate(heads):
        own[apart, 0, i] = early[n]
        own[apart, 1, i] = late[n]
        extra_c[0, apart, i] = jnp.where(core == 0, early[n], late[n])
    heads = owned(1 - core, chip, per_owner)
    ats = [columns(head, size) for _, _, head in heads]
    mixed = mixed_keys(q, k, v, g, ats)
    cross = [dot_tn(q[:, at], x.astype(BF16)) for x, at in zip(mixed, ats)]
    for n, (apart, i, _) in enumerate(heads):
        part_q[apart, i] = mixed[n]
        extra_c[1, apart, i] = cross[n].astype(BF16)


def add_body(own, other, *outs):
    for apart in range(GROUPS):
        outs[apart][...] = (own[apart].astype(F32) + other[apart].astype(F32)).astype(BF16)


def own_body(per_owner, q, k, v, g, own_c, part_q):
    size = own_c.shape[-1]
    core, chip = place()
    heads = owned(core, chip, per_owner)
    ats = [columns(head, size) for _, _, head in heads]
    mixed = mixed_keys(q, k, v, g, ats)
    cross = [dot_tn(q[:, at], x.astype(BF16)) for x, at in zip(mixed, ats)]
    for n, (apart, i, _) in enumerate(heads):
        part_q[apart, i] = mixed[n]
        own_c[apart, i] = cross[n].astype(BF16)


def rest_body(per_owner, q, k, v, g, w, part_k, part_v, key_w, gram):
    size = w.shape[-1]
    core, chip = place()
    rows, cols = triangle(q.shape[0])
    later = cols >= rows
    for which, half in enumerate((core, 1 - core)):
        heads = owned(half, chip, per_owner)
        ats = [columns(head, size) for _, _, head in heads]
        square = [dot_nt(w[head], w[head]).astype(BF16) for _, _, head in heads]
        mixing = [dot_nt(v[:, at], g[:, at]) for at in ats]
        mixing = [jnp.where(later, x, 0.0).astype(BF16) for x in mixing]
        keyed = [dot_nn(k[:, at], x).astype(BF16) for x, at in zip(square, ats)]
        mixed = [dot_nn(x, q[:, at]) for x, at in zip(mixing, ats)]
        scores = [dot_nt(x, q[:, at]) for x, at in zip(keyed, ats)]
        scores = [jnp.where(later, x, 0.0).astype(BF16) for x in scores]
        scored = [dot_nn(x, g[:, at]) for x, at in zip(scores, ats)]
        for n, (apart, i, _) in enumerate(heads):
            gram[which, apart, i] = square[n]
            key_w[which, apart, i] = keyed[n]
            part_k[which, apart, i] = mixed[n]
            part_v[which, apart, i] = scored[n]


def pack(first, second):
    size = first.shape[0]
    rows, cols = triangle(size)
    both = jnp.where(rows >= cols, first, second)
    diagonal = jnp.sum(jnp.where(rows == cols, second, 0.0), axis=0, keepdims=True)
    return both, jnp.broadcast_to(diagonal, (EXTRA, size))


def pack_body(per_owner, own, other, own_c, extra_c, *outs):
    size = own_c.shape[-1]
    core, _ = place()
    last = core == 1
    totals = []
    for apart in range(GROUPS):
        for i in range(per_owner):
            early = jnp.where(last, other[apart, 0, i], own[apart, 0, i])
            late = jnp.where(last, own[apart, 1, i], other[apart, 1, i])
            totals.append(dot_nt(late, early))
    for apart in range(GROUPS):
        for pair in range(per_owner // 2):
            sums = []
            for i in (2 * pair, 2 * pair + 1):
                total = totals[apart * per_owner + i]
                total += own_c[apart, i].astype(F32) + extra_c[1, apart, i].astype(F32)
                sums.append(total + total.T)
            both, diagonal = pack(*sums)
            outs[apart][pair, :size] = both.astype(BF16)
            outs[apart][pair, size:] = diagonal.astype(BF16)


def owner_body(per_owner, *refs):
    parts, packed, outs = refs[:GROUPS], refs[GROUPS : 2 * GROUPS], refs[2 * GROUPS :]
    size = outs[0].shape[-1]
    _, chip = place()
    turns = []
    for i in range(per_owner):
        early = [part[0, i].astype(F32) for part in parts]
        late = [part[1, i].astype(F32) for part in parts]
        cross = None
        for to in range(GROUPS):
            prefix = jnp.zeros_like(early[0])
            suffix = jnp.zeros_like(early[0])
            for apart in range(GROUPS):
                if apart == to:
                    continue
                before = (chip ^ apart) < (chip ^ to)
                prefix += jnp.where(before, early[apart], 0.0)
                suffix += jnp.where(before, 0.0, late[apart])
            prefix = prefix.astype(BF16)
            outs[to][i * size : (i + 1) * size] = prefix
            outs[to][(per_owner + i) * size : (per_owner + i + 1) * size] = suffix.astype(BF16)
            product = dot_nt(parts[to][1, i], prefix)
            cross = product if cross is None else cross + product
        turns.append(cross + cross.T)
    for pair in range(per_owner // 2):
        both, diagonal = pack(turns[2 * pair], turns[2 * pair + 1])
        for apart in range(GROUPS):
            both += packed[apart][pair, :size].astype(F32)
            diagonal += packed[apart][pair, size:].astype(F32)
        start = 2 * per_owner * size + pair * (size + EXTRA)
        for to in range(GROUPS):
            outs[to][start : start + size] = both.astype(BF16)
            outs[to][start + size : start + size + EXTRA] = diagonal.astype(BF16)


def tail_body(which, per_owner, scale, *refs):
    q, k, v, g, w, key_w, gram, part_q, part_k, part_v, near = refs[:11]
    carried = refs[11 : 11 + GROUPS]
    outs = refs[-9:-5]
    here = refs[-5:-1]
    sems = refs[-1]
    query_here, key_here, value_here, map_here = here
    size = gram.shape[-1]
    core, chip = place()
    half = 1 - core if which else core
    heads = owned(half, chip, per_owner)
    ats = [columns(head, size) for _, _, head in heads]
    slots = [columns((chip ^ apart) * per_owner + i, size) for apart, i, _ in heads]
    prefix, suffix = [], []
    for apart, i, _ in heads:
        if which:
            early = late = near[0, apart, i]
        else:
            early, late = near[apart, 0, i], near[apart, 1, i]
        before = carried[apart][i * size : (i + 1) * size].astype(F32)
        after = carried[apart][(per_owner + i) * size : (per_owner + i + 1) * size].astype(F32)
        prefix.append((before + jnp.where(core == 1, early.astype(F32), 0.0)).astype(BF16))
        suffix.append((after + jnp.where(core == 0, late.astype(F32), 0.0)).astype(BF16))
    raw_q = [dot_nt(g[:, at], x) for x, at in zip(prefix, ats)]
    raw_k = [dot_nt(v[:, at], x) for x, at in zip(suffix, ats)]
    raw_v = [dot_nn(key_w[which, a, i], x) for x, (a, i, _) in zip(suffix, heads)]
    raw_q = [(part_q[a, i] + x).astype(BF16) for x, (a, i, _) in zip(raw_q, heads)]
    raw_k = [(part_k[which, a, i] + x).astype(BF16) for x, (a, i, _) in zip(raw_k, heads)]
    for n, (a, i, _) in enumerate(heads):
        value_here[:, slots[n]] = (part_v[which, a, i] + raw_v[n]).astype(BF16)
    done_q = [dot_nn(x, gram[which, a, i]) for x, (a, i, _) in zip(raw_q, heads)]
    done_k = [dot_nn(x, gram[which, a, i]) for x, (a, i, _) in zip(raw_k, heads)]
    for n, slot in enumerate(slots):
        query_here[:, slot] = done_q[n].astype(BF16)
        key_here[:, slot] = done_k[n].astype(BF16)
    span = columns(half, q.shape[1] // 2)
    copies = [
        pltpu.make_async_copy(here[n], outs[n].at[:, span], sems.at[n]) for n in range(3)
    ]
    for copy in copies:
        copy.start()
    rows, cols = triangle(size)
    for apart in range(GROUPS):
        for pair in range(per_owner // 2):
            start = 2 * per_owner * size + pair * (size + EXTRA)
            both = carried[apart][start : start + size].astype(F32)
            diagonal = carried[apart][start + size : start + size + EXTRA][:1].astype(F32)
            turned = both.T
            first = jnp.where(rows >= cols, both, turned)
            second = jnp.where(rows < cols, both, turned)
            second = jnp.where(rows == cols, diagonal, second)
            for i, whole in ((2 * pair, first), (2 * pair + 1, second)):
                slot = (chip ^ apart) * per_owner + i
                head = half * (GROUPS * per_owner) + slot
                map_here[slot] = dot_nn(whole.astype(BF16), w[head]) * scale
    count = GROUPS * per_owner
    copies.append(
        pltpu.make_async_copy(map_here, outs[3].at[pl.ds(half * count, count)], sems.at[3])
    )
    copies[-1].start()
    for copy in copies:
        copy.wait()


def swap(x, apart):
    count = lax.axis_size("ctx")
    return lax.ppermute(x, "ctx", [(i, i ^ apart) for i in range(count)])


def paired(q, k, v, g, w):
    rows, width = q.shape
    heads, size = w.shape[0], w.shape[-1]
    per_owner = heads // (2 * GROUPS)
    length = rows * lax.axis_size("ctx")
    block = (size, size)
    one = (GROUPS, per_owner) + block
    both = (GROUPS, 2, per_owner) + block
    twice = (2,) + one
    state = (2, per_owner) + block
    pack_shape = (per_owner // 2, size + EXTRA, size)
    payload = (2 * per_owner * size + (per_owner // 2) * (size + EXTRA), size)
    bind = functools.partial

    *here, send = call(
        bind(load_body, per_owner),
        [((rows, width), BF16)] * 4 + [(both, BF16)],
        (q, k, v, g),
        2.0,
        in_spec=HBM,
        scratch=[pltpu.SemaphoreType.DMA((2, 4))],
    )
    other = swap(send, 1)
    own, extra_c, part_q1 = call(
        bind(near_body, per_owner), [(both, BF16), (twice, BF16), (one, F32)], here, 1.4
    )
    chip_states = call(add_body, [(state, BF16)] * GROUPS, (own, other), 0.2)
    parts = [chip_states[0]] + [swap(chip_states[j], 2 * j) for j in range(1, GROUPS)]
    extra_c = swap(extra_c, 1)
    own_c, part_q0 = call(
        bind(own_body, per_owner),
        [(one, BF16), (one, F32)],
        here,
        1.0,
        after=chip_states[:1],
    )
    chip_c = call(
        bind(pack_body, per_owner),
        [(pack_shape, BF16)] * GROUPS,
        (own, other, own_c, extra_c),
        0.4,
    )
    packed = [chip_c[0]] + [swap(chip_c[j], 2 * j) for j in range(1, GROUPS)]
    part_k, part_v, key_w, gram = call(
        bind(rest_body, per_owner),
        [(twice, F32), (twice, F32), (twice, BF16), (twice, BF16)],
        (*here, w),
        1.8,
        after=chip_c[:1],
    )
    carried = call(
        bind(owner_body, per_owner),
        [(payload, BF16)] * GROUPS,
        (*parts, *packed),
        0.5,
        after=(gram,),
    )
    near = [carried[0]] + [swap(carried[j], 2 * j) for j in range(1, GROUPS)]
    far = [swap(x, 1) for x in near]
    outs = [((rows, width), BF16)] * 3 + [((heads,) + block, F32)]
    scale = 1.0 / math.sqrt(length)

    def tail(which, part_q, other_states, payloads, before):
        return call(
            bind(tail_body, which, per_owner, scale),
            outs,
            (*here, w, key_w, gram, part_q, part_k, part_v, other_states, *payloads),
            1.6,
            after=before,
            scratch=[pltpu.VMEM((rows, width // 2), BF16)] * 3
            + [pltpu.VMEM((heads // 2,) + block, F32), pltpu.SemaphoreType.DMA((4,))],
            out_specs=[HBM] * 4,
            aliases={11 + GROUPS + n: n for n in range(len(before))},
        )

    first = tail(0, part_q0, other, near, ())
    return tuple(tail(1, part_q1, extra_c, far, tuple(first)))


def gathered(q, k, v, g, w):
    rows, width = q.shape
    heads, size = w.shape[0], w.shape[-1]
    count = lax.axis_size("ctx")
    me = lax.axis_index("ctx")
    q, k, v, g = (x.reshape(rows, heads, size) for x in (q, k, v, g))

    def mul(spec, a, b):
        return jnp.einsum(spec, a, b, preferred_element_type=F32)

    query_feat = mul("thd,hde->the", q, w).astype(BF16)
    key_feat = mul("thd,hde->the", k, w).astype(BF16)
    key_state = mul("the,thv->hev", key_feat, v).astype(BF16)
    grad_state = mul("the,thv->hev", query_feat, g).astype(BF16)
    index = jnp.arange(count).reshape(count, 1, 1, 1)
    keys = lax.all_gather(key_state, "ctx").astype(F32)
    prefix = jnp.sum(jnp.where(index < me, keys, 0.0), 0).astype(BF16)
    grads = lax.all_gather(grad_state, "ctx").astype(F32)
    suffix = jnp.sum(jnp.where(index > me, grads, 0.0), 0).astype(BF16)
    row, col = triangle(rows)
    causal = row >= col
    scores = jnp.where(causal, mul("the,she->hts", query_feat, key_feat), 0.0).astype(BF16)
    mixing = jnp.where(causal, mul("thv,shv->hts", g, v), 0.0).astype(BF16)
    feat_q = mul("hts,she->the", mixing, key_feat) + mul("thv,hev->the", g, prefix)
    feat_k = mul("hts,the->she", mixing, query_feat) + mul("shv,hev->she", v, suffix)
    feat_q, feat_k = feat_q.astype(BF16), feat_k.astype(BF16)
    value_grad = mul("hts,thv->shv", scores, g) + mul("she,hev->shv", key_feat, suffix)
    query_grad = mul("the,hde->thd", feat_q, w)
    key_grad = mul("the,hde->thd", feat_k, w)
    local = mul("thd,the->hde", q, feat_q) + mul("thd,the->hde", k, feat_k)
    map_grad = lax.psum(local.astype(BF16).astype(F32), "ctx") / math.sqrt(rows * count)
    flat = (rows, width)
    return (
        query_grad.reshape(flat).astype(BF16),
        key_grad.reshape(flat).astype(BF16),
        value_grad.reshape(flat).astype(BF16),
        map_grad,
    )


def per_device(queries, key_rows, values, out_grad, feature_map):
    fits = lax.axis_size("ctx") == 2 * GROUPS and feature_map.shape[0] % (4 * GROUPS) == 0
    plan = paired if fits else gathered
    return plan(queries, key_rows, values, out_grad, feature_map)


def solution(mesh):
    rows = P(("seq", "ctx"), None)
    return jax.shard_map(
        per_device,
        mesh=mesh,
        in_specs=(rows, rows, rows, rows, P()),
        out_specs=(rows, rows, rows, P("seq", None, None)),
        check_vma=False,
    )
```

time: 53.4 us -> 38 us (0.71)
  Pallas kernels: 21.8 us -> 9.06 us
  starting transfers between devices: 18.2 us -> 12.6 us
  waiting for transfers between devices: 8.05 us -> 11 us
    pallas_call x10 -> x9, Pallas kernels: 21.8 us -> 9.06 us  [call(): pl.pallas_call(run, out_shape=[jax.ShapeDtypeStruct(shape, dtype) for sha...]
    ppermute x23 -> x15, starting transfers between devices: 18.2 us -> 12.6 us  [swap(): return lax.ppermute(x, 'ctx', [(i, i ^ apart) for i in range(count)])]
    ppermute x23 -> x15, waiting for transfers between devices: 8.05 us -> 11 us  [swap(): return lax.ppermute(x, 'ctx', [(i, i ^ apart) for i in range(count)])]
    unnamed x18 -> x10, local copies, waits for them, and re-layouts: 4.18 us -> 4.16 us
  transfers between devices with their start and end apart: 23 -> 15, of which waited for: 10 -> 5; matrix products, arithmetic and copies ran while one was open for 0% -> 0% of each run, Pallas kernels for 31% -> 14%
where the time goes in v2:
time: 38 us; the launch traced here: 37.7 us
  starting transfers between devices  12.6 us (33%)
  waiting for transfers between devices  11 us (29%)
  Pallas kernels  9.06 us (24%)
  local copies, waits for them, and re-layouts  4.16 us (11%)
  between operations  0.74 us (2%)
    ppermute x15, starting transfers between devices, swap(): return lax.ppermute(x, 'ctx', [(i, i ^ apart) for i in range(count)])  12.6 us
    ppermute x15, waiting for transfers between devices, swap(): return lax.ppermute(x, 'ctx', [(i, i ^ apart) for i in range(count)])  11 us
    pallas_call x9, Pallas kernels, call(): pl.pallas_call(run, out_shape=[jax.ShapeDtypeStruct(shape, dtype) for sha...  9.06 us
    unnamed x10, local copies, waits for them, and re-layouts  4.16 us
  transfers between devices with their start and end apart: 15, of which 5 were waited for; matrix products, arithmetic and copies ran while one was open for 0% of the time, Pallas kernels for 14%

profile of v2, /device:TPU:0, one launch (start us, length us, event | category | flops | bytes accessed | tf_op | source)
XLA Modules:
  0.0 37.7 jit_solution(6175309274362086323)
XLA Ops:
  0.6 0.0 copy-start.1
  0.6 1.0 %copy-done.1 = bf16[128,2048]{1,0:T(8,128)(2,1)S(1)} copy-done((bf16[128,2048]{1,0:T(8,128)(2,1)S(1)}, bf16[128,2048]{1,0:T(8,128)(2,1)}, u32[]{:S(2)}) %copy-start.1) | copy-done | bytes 524312
  1.7 0.0 copy-start.2
  1.7 1.0 %copy-done.2 = bf16[128,2048]{1,0:T(8,128)(2,1)S(1)} copy-done((bf16[128,2048]{1,0:T(8,128)(2,1)S(1)}, bf16[128,2048]{1,0:T(8,128)(2,1)}, u32[]{:S(2)}) %copy-start.2) | copy-done | bytes 524312
  2.7 0.0 copy-start.3
  2.7 1.0 %copy-done.3 = bf16[128,2048]{1,0:T(8,128)(2,1)S(1)} copy-done((bf16[128,2048]{1,0:T(8,128)(2,1)S(1)}, bf16[128,2048]{1,0:T(8,128)(2,1)}, u32[]{:S(2)}) %copy-start.3) | copy-done | bytes 524312
  3.8 0.0 copy-start.4
  3.8 1.0 %copy-done.4 = bf16[128,2048]{1,0:T(8,128)(2,1)S(1)} copy-done((bf16[128,2048]{1,0:T(8,128)(2,1)S(1)}, bf16[128,2048]{1,0:T(8,128)(2,1)}, u32[]{:S(2)}) %copy-start.4) | copy-done | bytes 524312
  4.8 0.8 %shard_map.84 = (bf16[128,2048]{1,0:T(8,128)(2,1)S(1)}, bf16[128,2048]{1,0:T(8,128)(2,1)S(1)}, bf16[128,2048]{1,0:T(8,128)(2,1)S(1)}, bf16[128,2048]{1,0:T(8,128)(2,1)S(1)}, bf16[4,2,2,128,128]{4,3,2,1,0:T(8,128)(2,1)S(1)}) custom-call(bf16[128,2048]{1,0:T(8,128)(2,1)S(1)} %copy-done.1, bf16[128,2048]{1,0:T(8,128)(2,1)S(1)} %copy-done.2, ...), custom_call_target="tpu_custom_call" | custom-call | flops 2300000000 | tf_op jit(solution)/shard_map/pallas_call | solution.py:38
  5.6 0.5 %collective-permute-start = (bf16[4,2,2,128,128]{4,3,2,1,0:T(8,128)(2,1)S(1)}, bf16[4,2,2,128,128]{4,3,2,1,0:T(8,128)(2,1)S(1)}, u32[]{:S(2)}, u32[]{:S(2)}) collective-permute-start(bf16[4,2,2,128,128]{4,3,2,1,0:T(8,128)(2,1)S(1)} %get-tuple-element.39), channel_id=1, source_target_pairs={{0,1},{1,0},{2,3},{3,2},{4,5},{5,4},{6,7},{7,6},{8,9},{9,8},{10,11... | collective-permute-start | bytes 1572872 | tf_op jit(solution)/shard_map/ppermute | solution.py:298
  6.1 1.0 %shard_map.85 = (bf16[4,2,2,128,128]{4,3,2,1,0:T(8,128)(2,1)S(1)}, bf16[2,4,2,128,128]{4,3,2,1,0:T(8,128)(2,1)S(1)}, f32[4,2,128,128]{3,2,1,0:T(8,128)S(1)}) custom-call(bf16[128,2048]{1,0:T(8,128)(2,1)S(1)} %get-tuple-element.34.refs_0_, bf16[128,2048]{1,0:T(8,128)(2,1)S(1)} %get-tuple-element.35.refs_1_, bf16[128,2048]{1,0:T(8,128)(2,1)S(1)} %get-tuple-element.36.refs_2_, ...), custom_call_target="tpu_custom_call" | custom-call | flops 1610000000 | tf_op jit(solution)/shard_map/pallas_call | solution.py:38
  7.1 0.1 collective-permute-start.1
  7.2 0.5 %collective-permute-done.refs_1_.refs_10_ = bf16[4,2,2,128,128]{4,3,2,1,0:T(8,128)(2,1)S(1)} collective-permute-done((bf16[4,2,2,128,128]{4,3,2,1,0:T(8,128)(2,1)S(1)}, bf16[4,2,2,128,128]{4,3,2,1,0:T(8,128)(2,1)S(1)}, u32[]{:S(2)}, u32[]{:S(2)}) %collective-permute-start) | collective-permute-done | bytes 524320 | tf_op jit(solution)/shard_map/ppermute | solution.py:298
  7.7 0.1 shard_map.86
  7.8 0.6 %shard_map.87 = (bf16[4,2,128,128]{3,2,1,0:T(8,128)(2,1)S(1)}, f32[4,2,128,128]{3,2,1,0:T(8,128)S(1)}) custom-call(bf16[128,2048]{1,0:T(8,128)(2,1)S(1)} %get-tuple-element.34.refs_0_, bf16[128,2048]{1,0:T(8,128)(2,1)S(1)} %get-tuple-element.35.refs_1_, bf16[128,2048]{1,0:T(8,128)(2,1)S(1)} %get-tuple-element.36.refs_2_, ...), custom_call_target="tpu_custom_call" | custom-call | flops 1150000000 | tf_op jit(solution)/shard_map/pallas_call | solution.py:38
  8.5 0.6 %collective-permute-done.1.refs_3_.refs_10_ = bf16[2,4,2,128,128]{4,3,2,1,0:T(8,128)(2,1)S(1)} collective-permute-done((bf16[2,4,2,128,128]{4,3,2,1,0:T(8,128)(2,1)S(1)}, bf16[2,4,2,128,128]{4,3,2,1,0:T(8,128)(2,1)S(1)}, u32[]{:S(2)}, u32[]{:S(2)}) %collective-permute-start.1) | collective-permute-done | bytes 524320 | tf_op jit(solution)/shard_map/ppermute | solution.py:298
  9.1 0.4 %shard_map.88 = (bf16[1,144,128]{2,1,0:T(8,128)(2,1)S(1)}, bf16[1,144,128]{2,1,0:T(8,128)(2,1)S(1)}, bf16[1,144,128]{2,1,0:T(8,128)(2,1)S(1)}, bf16[1,144,128]{2,1,0:T(8,128)(2,1)S(1)}) custom-call(bf16[4,2,2,128,128]{4,3,2,1,0:T(8,128)(2,1)S(1)} %get-tuple-element.38.refs_0_, bf16[4,2,2,128,128]{4,3,2,1,0:T(8,128)(2,1)S(1)} %collective-permute-done.refs_1_.refs_10_, ...), custom_call_target="tpu_custom_call" | custom-call | flops 460000000 | tf_op jit(solution)/shard_map/pallas_call | solution.py:38
  9.5 2.7 %collective-permute-start.5 = (bf16[1,144,128]{2,1,0:T(8,128)(2,1)S(1)}, bf16[1,144,128]{2,1,0:T(8,128)(2,1)S(1)}, u32[]{:S(2)}, u32[]{:S(2)}) collective-permute-start(bf16[1,144,128]{2,1,0:T(8,128)(2,1)S(1)} %get-tuple-element.52), channel_id=1, source_target_pairs={{0,2},{1,3},{2,0},{3,1},{4,6},{5,7},{6,4},{7,5},{8,10},{9,11},{10,... | collective-permute-start | bytes 110600 | tf_op jit(solution)/shard_map/ppermute | solution.py:298
  12.2 0.1 collective-permute-start.2
  12.3 2.0 %collective-permute-start.3 = (bf16[2,2,128,128]{3,2,1,0:T(8,128)(2,1)S(1)}, bf16[2,2,128,128]{3,2,1,0:T(8,128)(2,1)S(1)}, u32[]{:S(2)}, u32[]{:S(2)}) collective-permute-start(bf16[2,2,128,128]{3,2,1,0:T(8,128)(2,1)S(1)} %get-tuple-element.50), channel_id=1, source_target_pairs={{0,4},{1,5},{2,6},{3,7},{4,0},{5,1},{6,2},{7,3},{8,12},{9,13},{10,... | collective-permute-start | bytes 393224 | tf_op jit(solution)/shard_map/ppermute | solution.py:298
  14.3 1.4 %collective-permute-start.4 = (bf16[2,2,128,128]{3,2,1,0:T(8,128)(2,1)S(1)}, bf16[2,2,128,128]{3,2,1,0:T(8,128)(2,1)S(1)}, u32[]{:S(2)}, u32[]{:S(2)}) collective-permute-start(bf16[2,2,128,128]{3,2,1,0:T(8,128)(2,1)S(1)} %get-tuple-element.51), channel_id=1, source_target_pairs={{0,6},{1,7},{2,4},{3,5},{4,2},{5,3},{6,0},{7,1},{8,14},{9,15},{10,... | collective-permute-start | bytes 393224 | tf_op jit(solution)/shard_map/ppermute | solution.py:298
  15.7 1.5 %collective-permute-start.6 = (bf16[1,144,128]{2,1,0:T(8,128)(2,1)S(1)}, bf16[1,144,128]{2,1,0:T(8,128)(2,1)S(1)}, u32[]{:S(2)}, u32[]{:S(2)}) collective-permute-start(bf16[1,144,128]{2,1,0:T(8,128)(2,1)S(1)} %get-tuple-element.53), channel_id=1, source_target_pairs={{0,4},{1,5},{2,6},{3,7},{4,0},{5,1},{6,2},{7,3},{8,12},{9,13},{10,... | collective-permute-start | bytes 110600 | tf_op jit(solution)/shard_map/ppermute | solution.py:298
  17.2 0.0 collective-permute-done.5.refs_5_
  17.2 0.2 collective-permute-start.7
  17.5 0.0 copy-done
  17.5 1.8 %shard_map.89 = (f32[2,4,2,128,128]{4,3,2,1,0:T(8,128)S(1)}, f32[2,4,2,128,128]{4,3,2,1,0:T(8,128)S(1)}, bf16[2,4,2,128,128]{4,3,2,1,0:T(8,128)(2,1)S(1)}, bf16[2,4,2,128,128]{4,3,2,1,0:T(8,128)(2,1)S(1)}) custom-call(bf16[128,2048]{1,0:T(8,128)(2,1)S(1)} %get-tuple-element.34.refs_0_, bf16[128,2048]{1,0:T(8,128)(2,1)S(1)} %get-tuple-element.35.refs_1_, ...), custom_call_target="tpu_custom_call" | custom-call | flops 2070000000 | tf_op jit(solution)/shard_map/pallas_call | solution.py:38
  19.3 3.2 %collective-permute-done.6.refs_6_ = bf16[1,144,128]{2,1,0:T(8,128)(2,1)S(1)} collective-permute-done((bf16[1,144,128]{2,1,0:T(8,128)(2,1)S(1)}, bf16[1,144,128]{2,1,0:T(8,128)(2,1)S(1)}, u32[]{:S(2)}, u32[]{:S(2)}) %collective-permute-start.6) | collective-permute-done | bytes 36896 | tf_op jit(solution)/shard_map/ppermute | solution.py:298
  22.5 0.0 collective-permute-done.7.refs_7_
  22.5 0.0 collective-permute-done.2.refs_1_
  22.5 0.0 collective-permute-done.3.refs_2_
  22.5 0.0 collective-permute-done.4.refs_3_
  22.5 0.5 %shard_map.90 = (bf16[656,128]{1,0:T(8,128)(2,1)S(1)}, bf16[656,128]{1,0:T(8,128)(2,1)S(1)}, bf16[656,128]{1,0:T(8,128)(2,1)S(1)}, bf16[656,128]{1,0:T(8,128)(2,1)S(1)}) custom-call(bf16[2,2,128,128]{3,2,1,0:T(8,128)(2,1)S(1)} %get-tuple-element.40.refs_4_.refs_0_, bf16[2,2,128,128]{3,2,1,0:T(8,128)(2,1)S(1)} %collective-permute-done.2.refs_1_, ...), custom_call_target="tpu_custom_call" | custom-call | flops 575000000 | tf_op jit(solution)/shard_map/pallas_call | solution.py:38
  23.1 1.4 %collective-permute-start.9 = (bf16[656,128]{1,0:T(8,128)(2,1)S(1)}, bf16[656,128]{1,0:T(8,128)(2,1)S(1)}, u32[]{:S(2)}, u32[]{:S(2)}) collective-permute-start(bf16[656,128]{1,0:T(8,128)(2,1)S(1)} %get-tuple-element.56), channel_id=1, source_target_pairs={{0,2},{1,3},{2,0},{3,1},{4,6},{5,7},{6,4},{7,5},{8,10},{9,11},{10,... | collective-permute-start | bytes 503816 | tf_op jit(solution)/shard_map/ppermute | solution.py:298
  24.4 1.5 %collective-permute-start.11 = (bf16[656,128]{1,0:T(8,128)(2,1)S(1)}, bf16[656,128]{1,0:T(8,128)(2,1)S(1)}, u32[]{:S(2)}, u32[]{:S(2)}) collective-permute-start(bf16[656,128]{1,0:T(8,128)(2,1)S(1)} %get-tuple-element.57), channel_id=1, source_target_pairs={{0,4},{1,5},{2,6},{3,7},{4,0},{5,1},{6,2},{7,3},{8,12},{9,13},{10,... | collective-permute-start | bytes 503816 | tf_op jit(solution)/shard_map/ppermute | solution.py:298
  26.0 0.6 %collective-permute-start.13 = (bf16[656,128]{1,0:T(8,128)(2,1)S(1)}, bf16[656,128]{1,0:T(8,128)(2,1)S(1)}, u32[]{:S(2)}, u32[]{:S(2)}) collective-permute-start(bf16[656,128]{1,0:T(8,128)(2,1)S(1)} %get-tuple-element.58), channel_id=1, source_target_pairs={{0,6},{1,7},{2,4},{3,5},{4,2},{5,3},{6,0},{7,1},{8,14},{9,15},{10,... | collective-permute-start | bytes 503816 | tf_op jit(solution)/shard_map/ppermute | solution.py:298
  26.6 0.0 collective-permute-start.8
  26.6 3.3 %collective-permute-done.9.refs_12_ = bf16[656,128]{1,0:T(8,128)(2,1)S(1)} collective-permute-done((bf16[656,128]{1,0:T(8,128)(2,1)S(1)}, bf16[656,128]{1,0:T(8,128)(2,1)S(1)}, u32[]{:S(2)}, u32[]{:S(2)}) %collective-permute-start.9) | collective-permute-done | bytes 167968 | tf_op jit(solution)/shard_map/ppermute | solution.py:298
  29.9 0.0 collective-permute-start.10
  29.9 3.4 %collective-permute-done.11.refs_13_ = bf16[656,128]{1,0:T(8,128)(2,1)S(1)} collective-permute-done((bf16[656,128]{1,0:T(8,128)(2,1)S(1)}, bf16[656,128]{1,0:T(8,128)(2,1)S(1)}, u32[]{:S(2)}, u32[]{:S(2)}) %collective-permute-start.11) | collective-permute-done | bytes 167968 | tf_op jit(solution)/shard_map/ppermute | solution.py:298
  33.3 0.0 collective-permute-start.12
  33.3 0.0 collective-permute-done.13.refs_14_
  33.3 0.5 %collective-permute-start.14 = (bf16[656,128]{1,0:T(8,128)(2,1)S(1)}, bf16[656,128]{1,0:T(8,128)(2,1)S(1)}, u32[]{:S(2)}, u32[]{:S(2)}) collective-permute-start(bf16[656,128]{1,0:T(8,128)(2,1)S(1)} %collective-permute-done.13.refs_14_), channel_id=1, source_target_pairs={{0,1},{1,0},{2,3},{3,2},{4,5},{5,4},{6,7},{7,6},{8,9},{9,8},{10,11... | collective-permute-start | bytes 503816 | tf_op jit(solution)/shard_map/ppermute | solution.py:298
  33.8 1.9 %shard_map.91 = (bf16[128,2048]{1,0:T(8,128)(2,1)}, bf16[128,2048]{1,0:T(8,128)(2,1)}, bf16[128,2048]{1,0:T(8,128)(2,1)}, f32[16,128,128]{2,1,0:T(8,128)}) custom-call(bf16[128,2048]{1,0:T(8,128)(2,1)S(1)} %get-tuple-element.34.refs_0_, bf16[128,2048]{1,0:T(8,128)(2,1)S(1)} %get-tuple-element.35.refs_1_, bf16[128,2048]{1,0:T(8,128)(2,1)S(1)} %get-tuple-element.36.refs_2_, ...), custom_call_target="tpu_custom_call" | custom-call | flops 1840000000 | tf_op jit(solution)/shard_map/pallas_call | solution.py:38
  35.7 0.0 collective-permute-done.8.refs_11_
  35.7 0.0 collective-permute-done.10.refs_12_
  35.7 0.0 collective-permute-done.12.refs_13_
  35.7 0.0 collective-permute-done.14.refs_14_
  35.8 1.9 %shard_map.92 = (bf16[128,2048]{1,0:T(8,128)(2,1)}, bf16[128,2048]{1,0:T(8,128)(2,1)}, bf16[128,2048]{1,0:T(8,128)(2,1)}, f32[16,128,128]{2,1,0:T(8,128)}) custom-call(bf16[128,2048]{1,0:T(8,128)(2,1)S(1)} %get-tuple-element.34.refs_0_, ...), custom_call_target="tpu_custom_call", output_to_operand_aliasing={{0}: (15, {}), {1}: (16, {}), {2}: (17, {}), {3}: (18, {})} | custom-call | flops 1840000000 | tf_op jit(solution)/shard_map/pallas_call | solution.py:38
  (1 shorter events, 0.0 us)
Async XLA Ops:
  0.6 1.0 %copy-start.1 = (bf16[128,2048]{1,0:T(8,128)(2,1)S(1)}, bf16[128,2048]{1,0:T(8,128)(2,1)}, u32[]{:S(2)}) copy-start(bf16[128,2048]{1,0:T(8,128)(2,1)} %refs_0_.1) | copy-start | bytes 1572868
  1.7 1.0 %copy-start.2 = (bf16[128,2048]{1,0:T(8,128)(2,1)S(1)}, bf16[128,2048]{1,0:T(8,128)(2,1)}, u32[]{:S(2)}) copy-start(bf16[128,2048]{1,0:T(8,128)(2,1)} %refs_1_.1) | copy-start | bytes 1572868
  2.7 1.0 %copy-start.3 = (bf16[128,2048]{1,0:T(8,128)(2,1)S(1)}, bf16[128,2048]{1,0:T(8,128)(2,1)}, u32[]{:S(2)}) copy-start(bf16[128,2048]{1,0:T(8,128)(2,1)} %refs_2_.1) | copy-start | bytes 1572868
  3.8 1.0 %copy-start.4 = (bf16[128,2048]{1,0:T(8,128)(2,1)S(1)}, bf16[128,2048]{1,0:T(8,128)(2,1)}, u32[]{:S(2)}) copy-start(bf16[128,2048]{1,0:T(8,128)(2,1)} %refs_3_.1) | copy-start | bytes 1572868
  5.6 2.1 %collective-permute-start = (bf16[4,2,2,128,128]{4,3,2,1,0:T(8,128)(2,1)S(1)}, bf16[4,2,2,128,128]{4,3,2,1,0:T(8,128)(2,1)S(1)}, u32[]{:S(2)}, u32[]{:S(2)}) collective-permute-start(bf16[4,2,2,128,128]{4,3,2,1,0:T(8,128)(2,1)S(1)} %get-tuple-element.39), channel_id=1, source_target_pairs={{0,1},{1,0},{2,3},{3,2},{4,5},{5,4},{6,7},{7,6},{8,9},{9,8},{10,11... | collective-permute-start | bytes 1572872 | tf_op jit(solution)/shard_map/ppermute | solution.py:298
  7.1 2.0 %collective-permute-start.1 = (bf16[2,4,2,128,128]{4,3,2,1,0:T(8,128)(2,1)S(1)}, bf16[2,4,2,128,128]{4,3,2,1,0:T(8,128)(2,1)S(1)}, u32[]{:S(2)}, u32[]{:S(2)}) collective-permute-start(bf16[2,4,2,128,128]{4,3,2,1,0:T(8,128)(2,1)S(1)} %get-tuple-element.42), channel_id=1, source_target_pairs={{0,1},{1,0},{2,3},{3,2},{4,5},{5,4},{6,7},{7,6},{8,9},{9,8},{10,11... | collective-permute-start | bytes 1572872 | tf_op jit(solution)/shard_map/ppermute | solution.py:298
  9.1 8.4 %copy-start = (bf16[16,128,128]{2,1,0:T(8,128)(2,1)S(1)}, bf16[16,128,128]{2,1,0:T(8,128)(2,1)}, u32[]{:S(2)}) copy-start(bf16[16,128,128]{2,1,0:T(8,128)(2,1)} %refs_4_.5) | copy-start | bytes 1572868
  9.5 7.7 %collective-permute-start.5 = (bf16[1,144,128]{2,1,0:T(8,128)(2,1)S(1)}, bf16[1,144,128]{2,1,0:T(8,128)(2,1)S(1)}, u32[]{:S(2)}, u32[]{:S(2)}) collective-permute-start(bf16[1,144,128]{2,1,0:T(8,128)(2,1)S(1)} %get-tuple-element.52), channel_id=1, source_target_pairs={{0,2},{1,3},{2,0},{3,1},{4,6},{5,7},{6,4},{7,5},{8,10},{9,11},{10,... | collective-permute-start | bytes 110600 | tf_op jit(solution)/shard_map/ppermute | solution.py:298
  12.2 10.3 %collective-permute-start.2 = (bf16[2,2,128,128]{3,2,1,0:T(8,128)(2,1)S(1)}, bf16[2,2,128,128]{3,2,1,0:T(8,128)(2,1)S(1)}, u32[]{:S(2)}, u32[]{:S(2)}) collective-permute-start(bf16[2,2,128,128]{3,2,1,0:T(8,128)(2,1)S(1)} %get-tuple-element.49), channel_id=1, source_target_pairs={{0,2},{1,3},{2,0},{3,1},{4,6},{5,7},{6,4},{7,5},{8,10},{9,11},{10,... | collective-permute-start | bytes 393224 | tf_op jit(solution)/shard_map/ppermute | solution.py:298
  12.3 10.2 %collective-permute-start.3 = (bf16[2,2,128,128]{3,2,1,0:T(8,128)(2,1)S(1)}, bf16[2,2,128,128]{3,2,1,0:T(8,128)(2,1)S(1)}, u32[]{:S(2)}, u32[]{:S(2)}) collective-permute-start(bf16[2,2,128,128]{3,2,1,0:T(8,128)(2,1)S(1)} %get-tuple-element.50), channel_id=1, source_target_pairs={{0,4},{1,5},{2,6},{3,7},{4,0},{5,1},{6,2},{7,3},{8,12},{9,13},{10,... | collective-permute-start | bytes 393224 | tf_op jit(solution)/shard_map/ppermute | solution.py:298
  14.3 8.3 %collective-permute-start.4 = (bf16[2,2,128,128]{3,2,1,0:T(8,128)(2,1)S(1)}, bf16[2,2,128,128]{3,2,1,0:T(8,128)(2,1)S(1)}, u32[]{:S(2)}, u32[]{:S(2)}) collective-permute-start(bf16[2,2,128,128]{3,2,1,0:T(8,128)(2,1)S(1)} %get-tuple-element.51), channel_id=1, source_target_pairs={{0,6},{1,7},{2,4},{3,5},{4,2},{5,3},{6,0},{7,1},{8,14},{9,15},{10,... | collective-permute-start | bytes 393224 | tf_op jit(solution)/shard_map/ppermute | solution.py:298
  15.7 6.8 %collective-permute-start.6 = (bf16[1,144,128]{2,1,0:T(8,128)(2,1)S(1)}, bf16[1,144,128]{2,1,0:T(8,128)(2,1)S(1)}, u32[]{:S(2)}, u32[]{:S(2)}) collective-permute-start(bf16[1,144,128]{2,1,0:T(8,128)(2,1)S(1)} %get-tuple-element.53), channel_id=1, source_target_pairs={{0,4},{1,5},{2,6},{3,7},{4,0},{5,1},{6,2},{7,3},{8,12},{9,13},{10,... | collective-permute-start | bytes 110600 | tf_op jit(solution)/shard_map/ppermute | solution.py:298
  17.2 5.3 %collective-permute-start.7 = (bf16[1,144,128]{2,1,0:T(8,128)(2,1)S(1)}, bf16[1,144,128]{2,1,0:T(8,128)(2,1)S(1)}, u32[]{:S(2)}, u32[]{:S(2)}) collective-permute-start(bf16[1,144,128]{2,1,0:T(8,128)(2,1)S(1)} %get-tuple-element.54), channel_id=1, source_target_pairs={{0,6},{1,7},{2,4},{3,5},{4,2},{5,3},{6,0},{7,1},{8,14},{9,15},{10,... | collective-permute-start | bytes 110600 | tf_op jit(solution)/shard_map/ppermute | solution.py:298
  23.1 6.9 %collective-permute-start.9 = (bf16[656,128]{1,0:T(8,128)(2,1)S(1)}, bf16[656,128]{1,0:T(8,128)(2,1)S(1)}, u32[]{:S(2)}, u32[]{:S(2)}) collective-permute-start(bf16[656,128]{1,0:T(8,128)(2,1)S(1)} %get-tuple-element.56), channel_id=1, source_target_pairs={{0,2},{1,3},{2,0},{3,1},{4,6},{5,7},{6,4},{7,5},{8,10},{9,11},{10,... | collective-permute-start | bytes 503816 | tf_op jit(solution)/shard_map/ppermute | solution.py:298
  24.4 8.9 %collective-permute-start.11 = (bf16[656,128]{1,0:T(8,128)(2,1)S(1)}, bf16[656,128]{1,0:T(8,128)(2,1)S(1)}, u32[]{:S(2)}, u32[]{:S(2)}) collective-permute-start(bf16[656,128]{1,0:T(8,128)(2,1)S(1)} %get-tuple-element.57), channel_id=1, source_target_pairs={{0,4},{1,5},{2,6},{3,7},{4,0},{5,1},{6,2},{7,3},{8,12},{9,13},{10,... | collective-permute-start | bytes 503816 | tf_op jit(solution)/shard_map/ppermute | solution.py:298
  26.0 7.4 %collective-permute-start.13 = (bf16[656,128]{1,0:T(8,128)(2,1)S(1)}, bf16[656,128]{1,0:T(8,128)(2,1)S(1)}, u32[]{:S(2)}, u32[]{:S(2)}) collective-permute-start(bf16[656,128]{1,0:T(8,128)(2,1)S(1)} %get-tuple-element.58), channel_id=1, source_target_pairs={{0,6},{1,7},{2,4},{3,5},{4,2},{5,3},{6,0},{7,1},{8,14},{9,15},{10,... | collective-permute-start | bytes 503816 | tf_op jit(solution)/shard_map/ppermute | solution.py:298
  26.6 9.1 %collective-permute-start.8 = (bf16[656,128]{1,0:T(8,128)(2,1)S(1)}, bf16[656,128]{1,0:T(8,128)(2,1)S(1)}, u32[]{:S(2)}, u32[]{:S(2)}) collective-permute-start(bf16[656,128]{1,0:T(8,128)(2,1)S(1)} %get-tuple-element.55.refs_11_), channel_id=1, source_target_pairs={{0,1},{1,0},{2,3},{3,2},{4,5},{5,4},{6,7},{7,6},{8,9},{9,8},{10,11... | collective-permute-start | bytes 503816 | tf_op jit(solution)/shard_map/ppermute | solution.py:298
  29.9 5.8 %collective-permute-start.10 = (bf16[656,128]{1,0:T(8,128)(2,1)S(1)}, bf16[656,128]{1,0:T(8,128)(2,1)S(1)}, u32[]{:S(2)}, u32[]{:S(2)}) collective-permute-start(bf16[656,128]{1,0:T(8,128)(2,1)S(1)} %collective-permute-done.9.refs_12_), channel_id=1, source_target_pairs={{0,1},{1,0},{2,3},{3,2},{4,5},{5,4},{6,7},{7,6},{8,9},{9,8},{10,11... | collective-permute-start | bytes 503816 | tf_op jit(solution)/shard_map/ppermute | solution.py:298
  33.3 2.4 %collective-permute-start.12 = (bf16[656,128]{1,0:T(8,128)(2,1)S(1)}, bf16[656,128]{1,0:T(8,128)(2,1)S(1)}, u32[]{:S(2)}, u32[]{:S(2)}) collective-permute-start(bf16[656,128]{1,0:T(8,128)(2,1)S(1)} %collective-permute-done.11.refs_13_), channel_id=1, source_target_pairs={{0,1},{1,0},{2,3},{3,2},{4,5},{5,4},{6,7},{7,6},{8,9},{9,8},{10,11... | collective-permute-start | bytes 503816 | tf_op jit(solution)/shard_map/ppermute | solution.py:298
  33.3 2.4 %collective-permute-start.14 = (bf16[656,128]{1,0:T(8,128)(2,1)S(1)}, bf16[656,128]{1,0:T(8,128)(2,1)S(1)}, u32[]{:S(2)}, u32[]{:S(2)}) collective-permute-start(bf16[656,128]{1,0:T(8,128)(2,1)S(1)} %collective-permute-done.13.refs_14_), channel_id=1, source_target_pairs={{0,1},{1,0},{2,3},{3,2},{4,5},{5,4},{6,7},{7,6},{8,9},{9,8},{10,11... | collective-permute-start | bytes 503816 | tf_op jit(solution)/shard_map/ppermute | solution.py:298

commit v3 on v2

--- a/solution.py
+++ b/solution.py
@@ -73,8 +73,7 @@
     return rows, cols
 
 
-def load_body(per_owner, q, k, v, g, q_here, k_here, v_here, g_here, send, sems):
-    size = send.shape[-1]
+def load_body(per_owner, q, k, v, g, q_here, k_here, v_here, g_here, send, part_q, sems):
     half_width = q.shape[1] // 2
     core, chip = place()
     pairs = ((k, k_here), (v, v_here), (q, q_here), (g, g_here))
@@ -85,60 +84,71 @@
             copy = pltpu.make_async_copy(source.at[:, at], target.at[:, at], sems.at[turn, n])
             copy.start()
             copies.append(copy)
-    heads = owned(1 - core, chip, per_owner)
-    ats = [columns(head, size) for _, _, head in heads]
-    for kind, (left, right) in enumerate(((k_here, v_here), (q_here, g_here))):
-        copies[2 * kind].wait()
-        copies[2 * kind + 1].wait()
-        states = [dot_tn(left[:, at], right[:, at]) for at in ats]
-        for (apart, i, _), state in zip(heads, states):
-            send[apart, kind, i] = state.astype(BF16)
+    for copy in copies[:4]:
+        copy.wait()
+    half_states(owned(1 - core, chip, per_owner), q_here, k_here, v_here, g_here, send, part_q)
     for copy in copies[4:]:
         copy.wait()
 
 
-def mixed_keys(q, k, v, g, ats):
+def half_states(heads, q, k, v, g, out, part_q):
+    size = out.shape[-1]
     rows, cols = triangle(q.shape[0])
+    ats = [columns(head, size) for _, _, head in heads]
     mixing = [dot_nt(g[:, at], v[:, at]) for at in ats]
     mixing = [jnp.where(rows >= cols, x, 0.0).astype(BF16) for x in mixing]
-    return [dot_nn(x, k[:, at]) for x, at in zip(mixing, ats)]
-
-
-def near_body(per_owner, q, k, v, g, own, extra_c, part_q):
-    size = own.shape[-1]
-    core, chip = place()
-    heads = owned(core, chip, per_owner)
-    ats = [columns(head, size) for _, _, head in heads]
-    early = [dot_tn(k[:, at], v[:, at]).astype(BF16) for at in ats]
-    late = [dot_tn(q[:, at], g[:, at]).astype(BF16) for at in ats]
-    for n, (apart, i, _) in enumerate(heads):
-        own[apart, 0, i] = early[n]
-        own[apart, 1, i] = late[n]
-        extra_c[0, apart, i] = jnp.where(core == 0, early[n], late[n])
-    heads = owned(1 - core, chip, per_owner)
-    ats = [columns(head, size) for _, _, head in heads]
-    mixed = mixed_keys(q, k, v, g, ats)
+    mixed = [dot_nn(x, k[:, at]) for x, at in zip(mixing, ats)]
+    early = [dot_tn(k[:, at], v[:, at]) for at in ats]
+    late = [dot_tn(q[:, at], g[:, at]) for at in ats]
     cross = [dot_tn(q[:, at], x.astype(BF16)) for x, at in zip(mixed, ats)]
     for n, (apart, i, _) in enumerate(heads):
         part_q[apart, i] = mixed[n]
-        extra_c[1, apart, i] = cross[n].astype(BF16)
-
-
-def add_body(own, other, *outs):
-    for apart in range(GROUPS):
-        outs[apart][...] = (own[apart].astype(F32) + other[apart].astype(F32)).astype(BF16)
-
-
-def own_body(per_owner, q, k, v, g, own_c, part_q):
-    size = own_c.shape[-1]
+        for kind, states in enumerate((early, late, cross)):
+            out[apart, kind, i] = states[n].astype(BF16)
+
+
+def near_body(per_owner, q, k, v, g, own, extra, part_q):
     core, chip = place()
     heads = owned(core, chip, per_owner)
-    ats = [columns(head, size) for _, _, head in heads]
-    mixed = mixed_keys(q, k, v, g, ats)
-    cross = [dot_tn(q[:, at], x.astype(BF16)) for x, at in zip(mixed, ats)]
-    for n, (apart, i, _) in enumerate(heads):
-        part_q[apart, i] = mixed[n]
-        own_c[apart, i] = cross[n].astype(BF16)
+    half_states(heads, q, k, v, g, own, part_q)
+    for apart, i, _ in heads:
+        extra[apart, i] = jnp.where(core == 0, own[apart, 0, i], own[apart, 1, i])
+
+
+def pack(first, second):
+    size = first.shape[0]
+    rows, cols = triangle(size)
+    both = jnp.where(rows >= cols, first, second)
+    diagonal = jnp.sum(jnp.where(rows == cols, second, 0.0), axis=0, keepdims=True)
+    return both, jnp.broadcast_to(diagonal, (EXTRA, size))
+
+
+def join_body(per_owner, own, other, *outs):
+    size = own.shape[-1]
+    core, _ = place()
+    last = core == 1
+    totals = []
+    for apart in range(GROUPS):
+        for i in range(per_owner):
+            early = jnp.where(last, other[apart, 0, i], own[apart, 0, i])
+            late = jnp.where(last, own[apart, 1, i], other[apart, 1, i])
+            totals.append(dot_nt(late, early))
+    for apart in range(GROUPS):
+        for kind in range(2):
+            for i in range(per_owner):
+                start = (kind * per_owner + i) * size
+                total = own[apart, kind, i].astype(F32) + other[apart, kind, i].astype(F32)
+                outs[apart][start : start + size] = total.astype(BF16)
+        for pair in range(per_owner // 2):
+            sums = []
+            for i in (2 * pair, 2 * pair + 1):
+                total = totals[apart * per_owner + i]
+                total += own[apart, 2, i].astype(F32) + other[apart, 2, i].astype(F32)
+                sums.append(total + total.T)
+            both, diagonal = pack(*sums)
+            start = 2 * per_owner * size + pair * (size + EXTRA)
+            outs[apart][start : start + size] = both.astype(BF16)
+            outs[apart][start + size : start + size + EXTRA] = diagonal.astype(BF16)
 
 
 def rest_body(per_owner, q, k, v, g, w, part_k, part_v, key_w, gram):
@@ -164,44 +174,16 @@
             part_v[which, apart, i] = scored[n]
 
 
-def pack(first, second):
-    size = first.shape[0]
-    rows, cols = triangle(size)
-    both = jnp.where(rows >= cols, first, second)
-    diagonal = jnp.sum(jnp.where(rows == cols, second, 0.0), axis=0, keepdims=True)
-    return both, jnp.broadcast_to(diagonal, (EXTRA, size))
-
-
-def pack_body(per_owner, own, other, own_c, extra_c, *outs):
-    size = own_c.shape[-1]
-    core, _ = place()
-    last = core == 1
-    totals = []
-    for apart in range(GROUPS):
-        for i in range(per_owner):
-            early = jnp.where(last, other[apart, 0, i], own[apart, 0, i])
-            late = jnp.where(last, own[apart, 1, i], other[apart, 1, i])
-            totals.append(dot_nt(late, early))
-    for apart in range(GROUPS):
-        for pair in range(per_owner // 2):
-            sums = []
-            for i in (2 * pair, 2 * pair + 1):
-                total = totals[apart * per_owner + i]
-                total += own_c[apart, i].astype(F32) + extra_c[1, apart, i].astype(F32)
-                sums.append(total + total.T)
-            both, diagonal = pack(*sums)
-            outs[apart][pair, :size] = both.astype(BF16)
-            outs[apart][pair, size:] = diagonal.astype(BF16)
-
-
 def owner_body(per_owner, *refs):
-    parts, packed, outs = refs[:GROUPS], refs[GROUPS : 2 * GROUPS], refs[2 * GROUPS :]
+    parts, outs = refs[:GROUPS], refs[GROUPS:]
     size = outs[0].shape[-1]
     _, chip = place()
     turns = []
     for i in range(per_owner):
-        early = [part[0, i].astype(F32) for part in parts]
-        late = [part[1, i].astype(F32) for part in parts]
+        ahead = slice(i * size, (i + 1) * size)
+        behind = slice((per_owner + i) * size, (per_owner + i + 1) * size)
+        early = [part[ahead].astype(F32) for part in parts]
+        late = [part[behind].astype(F32) for part in parts]
         cross = None
         for to in range(GROUPS):
             prefix = jnp.zeros_like(early[0])
@@ -213,20 +195,20 @@
                 prefix += jnp.where(before, early[apart], 0.0)
                 suffix += jnp.where(before, 0.0, late[apart])
             prefix = prefix.astype(BF16)
-            outs[to][i * size : (i + 1) * size] = prefix
-            outs[to][(per_owner + i) * size : (per_owner + i + 1) * size] = suffix.astype(BF16)
-            product = dot_nt(parts[to][1, i], prefix)
+            outs[to][ahead] = prefix
+            outs[to][behind] = suffix.astype(BF16)
+            product = dot_nt(parts[to][behind], prefix)
             cross = product if cross is None else cross + product
         turns.append(cross + cross.T)
     for pair in range(per_owner // 2):
         both, diagonal = pack(turns[2 * pair], turns[2 * pair + 1])
-        for apart in range(GROUPS):
-            both += packed[apart][pair, :size].astype(F32)
-            diagonal += packed[apart][pair, size:].astype(F32)
         start = 2 * per_owner * size + pair * (size + EXTRA)
-        for to in range(GROUPS):
-            outs[to][start : start + size] = both.astype(BF16)
-            outs[to][start + size : start + size + EXTRA] = diagonal.astype(BF16)
+        for part in parts:
+            both += part[start : start + size].astype(F32)
+            diagonal += part[start + size : start + size + EXTRA].astype(F32)
+        for out in outs:
+            out[start : start + size] = both.astype(BF16)
+            out[start + size : start + size + EXTRA] = diagonal.astype(BF16)
 
 
 def tail_body(which, per_owner, scale, *refs):
@@ -245,7 +227,7 @@
     prefix, suffix = [], []
     for apart, i, _ in heads:
         if which:
-            early = late = near[0, apart, i]
+            early = late = near[apart, i]
         else:
             early, late = near[apart, 0, i], near[apart, 1, i]
         before = carried[apart][i * size : (i + 1) * size].astype(F32)
@@ -305,55 +287,35 @@
     length = rows * lax.axis_size("ctx")
     block = (size, size)
     one = (GROUPS, per_owner) + block
-    both = (GROUPS, 2, per_owner) + block
+    triple = (GROUPS, 3, per_owner) + block
     twice = (2,) + one
-    state = (2, per_owner) + block
-    pack_shape = (per_owner // 2, size + EXTRA, size)
     payload = (2 * per_owner * size + (per_owner // 2) * (size + EXTRA), size)
     bind = functools.partial
 
-    *here, send = call(
+    *here, send, part_q1 = call(
         bind(load_body, per_owner),
-        [((rows, width), BF16)] * 4 + [(both, BF16)],
-        (q, k, v, g),
+        [((rows, width), BF16)] * 4 + [(triple, BF16), (one, F32)],
+        [pltpu.with_memory_space_constraint(x, pltpu.HBM) for x in (q, k, v, g)],
         2.0,
         in_spec=HBM,
         scratch=[pltpu.SemaphoreType.DMA((2, 4))],
     )
     other = swap(send, 1)
-    own, extra_c, part_q1 = call(
-        bind(near_body, per_owner), [(both, BF16), (twice, BF16), (one, F32)], here, 1.4
-    )
-    chip_states = call(add_body, [(state, BF16)] * GROUPS, (own, other), 0.2)
-    parts = [chip_states[0]] + [swap(chip_states[j], 2 * j) for j in range(1, GROUPS)]
-    extra_c = swap(extra_c, 1)
-    own_c, part_q0 = call(
-        bind(own_body, per_owner),
-        [(one, BF16), (one, F32)],
-        here,
-        1.0,
-        after=chip_states[:1],
-    )
-    chip_c = call(
-        bind(pack_body, per_owner),
-        [(pack_shape, BF16)] * GROUPS,
-        (own, other, own_c, extra_c),
-        0.4,
-    )
-    packed = [chip_c[0]] + [swap(chip_c[j], 2 * j) for j in range(1, GROUPS)]
+    own, extra, part_q0 = call(
+        bind(near_body, per_owner), [(triple, BF16), (one, BF16), (one, F32)], here, 1.0
+    )
+    chip_sums = call(bind(join_body, per_owner), [(payload, BF16)] * GROUPS, (own, other), 0.5)
+    parts = [chip_sums[0]] + [swap(chip_sums[j], 2 * j) for j in range(1, GROUPS)]
+    extra = swap(extra, 1)
     part_k, part_v, key_w, gram = call(
         bind(rest_body, per_owner),
         [(twice, F32), (twice, F32), (twice, BF16), (twice, BF16)],
         (*here, w),
         1.8,
-        after=chip_c[:1],
+        after=chip_sums[:1],
     )
     carried = call(
-        bind(owner_body, per_owner),
-        [(payload, BF16)] * GROUPS,
-        (*parts, *packed),
-        0.5,
-        after=(gram,),
+        bind(owner_body, per_owner), [(payload, BF16)] * GROUPS, parts, 0.5, after=(gram,)
     )
     near = [carried[0]] + [swap(carried[j], 2 * j) for j in range(1, GROUPS)]
     far = [swap(x, 1) for x in near]
@@ -374,7 +336,7 @@
         )
 
     first = tail(0, part_q0, other, near, ())
-    return tuple(tail(1, part_q1, extra_c, far, tuple(first)))
+    return tuple(tail(1, part_q1, extra, far, tuple(first)))
 
 
 def gathered(q, k, v, g, w):

time: 38 us -> 33.2 us (0.87)
  local copies, waits for them, and re-layouts: 4.16 us -> 0.01 us
  starting transfers between devices: 12.6 us -> 9.55 us
  waiting for transfers between devices: 11 us -> 13.6 us
    unnamed x10 -> x2, local copies, waits for them, and re-layouts: 4.16 us -> 0.01 us
    ppermute x15 -> x12, starting transfers between devices: 12.6 us -> 9.55 us  [swap(): return lax.ppermute(x, 'ctx', [(i, i ^ apart) for i in range(count)])]
    ppermute x15 -> x12, waiting for transfers between devices: 11 us -> 13.6 us  [swap(): return lax.ppermute(x, 'ctx', [(i, i ^ apart) for i in range(count)])]
    pallas_call x9 -> x7, Pallas kernels: 9.06 us -> 9.26 us  [call(): pl.pallas_call(run, out_shape=[jax.ShapeDtypeStruct(shape, dtype) for sha...]
  transfers between devices with their start and end apart: 15 -> 12, of which waited for: 5 -> 5; matrix products, arithmetic and copies ran while one was open for 0% -> 0% of each run, Pallas kernels for 14% -> 13%
where the time goes in v3:
time: 33.2 us; the launch traced here: 33.1 us
  waiting for transfers between devices  13.6 us (41%)
  starting transfers between devices  9.55 us (29%)
  Pallas kernels  9.26 us (28%)
  between operations  0.71 us (2%)
    ppermute x12, waiting for transfers between devices, swap(): return lax.ppermute(x, 'ctx', [(i, i ^ apart) for i in range(count)])  13.6 us
    ppermute x12, starting transfers between devices, swap(): return lax.ppermute(x, 'ctx', [(i, i ^ apart) for i in range(count)])  9.55 us
    pallas_call x7, Pallas kernels, call(): pl.pallas_call(run, out_shape=[jax.ShapeDtypeStruct(shape, dtype) for sha...  9.26 us
  transfers between devices with their start and end apart: 12, of which 5 were waited for; matrix products, arithmetic and copies ran while one was open for 0% of the time, Pallas kernels for 13%

profile of v3, /device:TPU:0, one launch (start us, length us, event | category | flops | bytes accessed | tf_op | source)
XLA Modules:
  0.0 33.1 jit_solution(13937787571295755007)
XLA Ops:
  0.6 2.0 %shard_map.84 = (bf16[128,2048]{1,0:T(8,128)(2,1)S(1)}, bf16[128,2048]{1,0:T(8,128)(2,1)S(1)}, bf16[128,2048]{1,0:T(8,128)(2,1)S(1)}, bf16[128,2048]{1,0:T(8,128...) custom-call(bf16[128,2048]{1,0:T(8,128)(2,1)} %refs_0_.1, ...), custom_call_target="tpu_custom_call" | custom-call | flops 2300000000 | tf_op jit(solution)/shard_map/pallas_call | solution.py:38
  2.6 0.5 %collective-permute-start = (bf16[4,3,2,128,128]{4,3,2,1,0:T(8,128)(2,1)S(1)}, bf16[4,3,2,128,128]{4,3,2,1,0:T(8,128)(2,1)S(1)}, u32[]{:S(2)}, u32[]{:S(2)}) collective-permute-start(bf16[4,3,2,128,128]{4,3,2,1,0:T(8,128)(2,1)S(1)} %get-tuple-element.34), channel_id=1, source_target_pairs={{0,1},{1,0},{2,3},{3,2},{4,5},{5,4},{6,7},{7,6},{8,9},{9,8},{10,11... | collective-permute-start | bytes 2359304 | tf_op jit(solution)/shard_map/ppermute | solution.py:280
  3.1 0.7 %shard_map.85 = (bf16[4,3,2,128,128]{4,3,2,1,0:T(8,128)(2,1)S(1)}, bf16[4,2,128,128]{3,2,1,0:T(8,128)(2,1)S(1)}, f32[4,2,128,128]{3,2,1,0:T(8,128)S(1)}) custom-call(bf16[128,2048]{1,0:T(8,128)(2,1)S(1)} %get-tuple-element.29.refs_0_, bf16[128,2048]{1,0:T(8,128)(2,1)S(1)} %get-tuple-element.30.refs_1_, bf16[128,2048]{1,0:T(8,128)(2,1)S(1)} %get-tuple-element.31.refs_2_, ...), custom_call_target="tpu_custom_call" | custom-call | flops 1150000000 | tf_op jit(solution)/shard_map/pallas_call | solution.py:38
  3.9 1.2 %collective-permute-done.refs_1_.refs_10_ = bf16[4,3,2,128,128]{4,3,2,1,0:T(8,128)(2,1)S(1)} collective-permute-done((bf16[4,3,2,128,128]{4,3,2,1,0:T(8,128)(2,1)S(1)}, bf16[4,3,2,128,128]{4,3,2,1,0:T(8,128)(2,1)S(1)}, u32[]{:S(2)}, u32[]{:S(2)}) %collective-permute-start) | collective-permute-done | bytes 786464 | tf_op jit(solution)/shard_map/ppermute | solution.py:280
  5.0 0.0 copy-start
  5.0 0.5 %shard_map.86 = (bf16[656,128]{1,0:T(8,128)(2,1)S(1)}, bf16[656,128]{1,0:T(8,128)(2,1)S(1)}, bf16[656,128]{1,0:T(8,128)(2,1)S(1)}, bf16[656,128]{1,0:T(8,128)(2,1)S(1)}) custom-call(bf16[4,3,2,128,128]{4,3,2,1,0:T(8,128)(2,1)S(1)} %get-tuple-element.33.refs_0_, bf16[4,3,2,128,128]{4,3,2,1,0:T(8,128)(2,1)S(1)} %collective-permute-done.refs_1_.refs_10_), custom_call_target="tpu_custom_call" | custom-call | flops 575000000 | tf_op jit(solution)/shard_map/pallas_call | solution.py:38
  5.5 2.9 %collective-permute-start.2 = (bf16[656,128]{1,0:T(8,128)(2,1)S(1)}, bf16[656,128]{1,0:T(8,128)(2,1)S(1)}, u32[]{:S(2)}, u32[]{:S(2)}) collective-permute-start(bf16[656,128]{1,0:T(8,128)(2,1)S(1)} %get-tuple-element.42), channel_id=1, source_target_pairs={{0,2},{1,3},{2,0},{3,1},{4,6},{5,7},{6,4},{7,5},{8,10},{9,11},{10,... | collective-permute-start | bytes 503816 | tf_op jit(solution)/shard_map/ppermute | solution.py:280
  8.4 1.5 %collective-permute-start.3 = (bf16[656,128]{1,0:T(8,128)(2,1)S(1)}, bf16[656,128]{1,0:T(8,128)(2,1)S(1)}, u32[]{:S(2)}, u32[]{:S(2)}) collective-permute-start(bf16[656,128]{1,0:T(8,128)(2,1)S(1)} %get-tuple-element.43), channel_id=1, source_target_pairs={{0,4},{1,5},{2,6},{3,7},{4,0},{5,1},{6,2},{7,3},{8,12},{9,13},{10,... | collective-permute-start | bytes 503816 | tf_op jit(solution)/shard_map/ppermute | solution.py:280
  10.0 0.0 collective-permute-start.4
  10.0 0.0 copy-done
  10.0 1.8 %shard_map.87 = (f32[2,4,2,128,128]{4,3,2,1,0:T(8,128)S(1)}, f32[2,4,2,128,128]{4,3,2,1,0:T(8,128)S(1)}, bf16[2,4,2,128,128]{4,3,2,1,0:T(8,128)(2,1)S(1)}, bf16[2,4,2,128,128]{4,3,2,1,0:T(8,128)(2,1)S(1)}) custom-call(bf16[128,2048]{1,0:T(8,128)(2,1)S(1)} %get-tuple-element.29.refs_0_, bf16[128,2048]{1,0:T(8,128)(2,1)S(1)} %get-tuple-element.30.refs_1_, ...), custom_call_target="tpu_custom_call" | custom-call | flops 2070000000 | tf_op jit(solution)/shard_map/pallas_call | solution.py:38
  11.8 1.7 %collective-permute-done.2.refs_1_ = bf16[656,128]{1,0:T(8,128)(2,1)S(1)} collective-permute-done((bf16[656,128]{1,0:T(8,128)(2,1)S(1)}, bf16[656,128]{1,0:T(8,128)(2,1)S(1)}, u32[]{:S(2)}, u32[]{:S(2)}) %collective-permute-start.2) | collective-permute-done | bytes 167968 | tf_op jit(solution)/shard_map/ppermute | solution.py:280
  13.5 4.6 %collective-permute-done.3.refs_2_ = bf16[656,128]{1,0:T(8,128)(2,1)S(1)} collective-permute-done((bf16[656,128]{1,0:T(8,128)(2,1)S(1)}, bf16[656,128]{1,0:T(8,128)(2,1)S(1)}, u32[]{:S(2)}, u32[]{:S(2)}) %collective-permute-start.3) | collective-permute-done | bytes 167968 | tf_op jit(solution)/shard_map/ppermute | solution.py:280
  18.1 0.0 collective-permute-done.4.refs_3_
  18.1 0.5 %shard_map.88 = (bf16[656,128]{1,0:T(8,128)(2,1)S(1)}, bf16[656,128]{1,0:T(8,128)(2,1)S(1)}, bf16[656,128]{1,0:T(8,128)(2,1)S(1)}, bf16[656,128]{1,0:T(8,128)(2,1)S(1)}) custom-call(bf16[656,128]{1,0:T(8,128)(2,1)S(1)} %get-tuple-element.35.refs_5_.refs_0_, bf16[656,128]{1,0:T(8,128)(2,1)S(1)} %collective-permute-done.2.refs_1_, ...), custom_call_target="tpu_custom_call" | custom-call | flops 575000000 | tf_op jit(solution)/shard_map/pallas_call | solution.py:38
  18.6 1.3 %collective-permute-start.6 = (bf16[656,128]{1,0:T(8,128)(2,1)S(1)}, bf16[656,128]{1,0:T(8,128)(2,1)S(1)}, u32[]{:S(2)}, u32[]{:S(2)}) collective-permute-start(bf16[656,128]{1,0:T(8,128)(2,1)S(1)} %get-tuple-element.46), channel_id=1, source_target_pairs={{0,2},{1,3},{2,0},{3,1},{4,6},{5,7},{6,4},{7,5},{8,10},{9,11},{10,... | collective-permute-start | bytes 503816 | tf_op jit(solution)/shard_map/ppermute | solution.py:280
  19.9 0.8 %collective-permute-start.8 = (bf16[656,128]{1,0:T(8,128)(2,1)S(1)}, bf16[656,128]{1,0:T(8,128)(2,1)S(1)}, u32[]{:S(2)}, u32[]{:S(2)}) collective-permute-start(bf16[656,128]{1,0:T(8,128)(2,1)S(1)} %get-tuple-element.47), channel_id=1, source_target_pairs={{0,4},{1,5},{2,6},{3,7},{4,0},{5,1},{6,2},{7,3},{8,12},{9,13},{10,... | collective-permute-start | bytes 503816 | tf_op jit(solution)/shard_map/ppermute | solution.py:280
  20.8 1.4 %collective-permute-start.10 = (bf16[656,128]{1,0:T(8,128)(2,1)S(1)}, bf16[656,128]{1,0:T(8,128)(2,1)S(1)}, u32[]{:S(2)}, u32[]{:S(2)}) collective-permute-start(bf16[656,128]{1,0:T(8,128)(2,1)S(1)} %get-tuple-element.48), channel_id=1, source_target_pairs={{0,6},{1,7},{2,4},{3,5},{4,2},{5,3},{6,0},{7,1},{8,14},{9,15},{10,... | collective-permute-start | bytes 503816 | tf_op jit(solution)/shard_map/ppermute | solution.py:280
  22.2 0.0 collective-permute-start.1
  22.2 0.5 %collective-permute-start.5 = (bf16[656,128]{1,0:T(8,128)(2,1)S(1)}, bf16[656,128]{1,0:T(8,128)(2,1)S(1)}, u32[]{:S(2)}, u32[]{:S(2)}) collective-permute-start(bf16[656,128]{1,0:T(8,128)(2,1)S(1)} %get-tuple-element.45.refs_11_), channel_id=1, source_target_pairs={{0,1},{1,0},{2,3},{3,2},{4,5},{5,4},{6,7},{7,6},{8,9},{9,8},{10,11... | collective-permute-start | bytes 503816 | tf_op jit(solution)/shard_map/ppermute | solution.py:280
  22.7 2.8 %collective-permute-done.6.refs_12_ = bf16[656,128]{1,0:T(8,128)(2,1)S(1)} collective-permute-done((bf16[656,128]{1,0:T(8,128)(2,1)S(1)}, bf16[656,128]{1,0:T(8,128)(2,1)S(1)}, u32[]{:S(2)}, u32[]{:S(2)}) %collective-permute-start.6) | collective-permute-done | bytes 167968 | tf_op jit(solution)/shard_map/ppermute | solution.py:280
  25.5 0.0 collective-permute-start.7
  25.5 3.3 %collective-permute-done.8.refs_13_ = bf16[656,128]{1,0:T(8,128)(2,1)S(1)} collective-permute-done((bf16[656,128]{1,0:T(8,128)(2,1)S(1)}, bf16[656,128]{1,0:T(8,128)(2,1)S(1)}, u32[]{:S(2)}, u32[]{:S(2)}) %collective-permute-start.8) | collective-permute-done | bytes 167968 | tf_op jit(solution)/shard_map/ppermute | solution.py:280
  28.7 0.0 collective-permute-start.9
  28.7 0.0 collective-permute-done.10.refs_14_
  28.7 0.5 %collective-permute-start.11 = (bf16[656,128]{1,0:T(8,128)(2,1)S(1)}, bf16[656,128]{1,0:T(8,128)(2,1)S(1)}, u32[]{:S(2)}, u32[]{:S(2)}) collective-permute-start(bf16[656,128]{1,0:T(8,128)(2,1)S(1)} %collective-permute-done.10.refs_14_), channel_id=1, source_target_pairs={{0,1},{1,0},{2,3},{3,2},{4,5},{5,4},{6,7},{7,6},{8,9},{9,8},{10,11... | collective-permute-start | bytes 503816 | tf_op jit(solution)/shard_map/ppermute | solution.py:280
  29.3 1.9 %shard_map.89 = (bf16[128,2048]{1,0:T(8,128)(2,1)}, bf16[128,2048]{1,0:T(8,128)(2,1)}, bf16[128,2048]{1,0:T(8,128)(2,1)}, f32[16,128,128]{2,1,0:T(8,128)}) custom-call(bf16[128,2048]{1,0:T(8,128)(2,1)S(1)} %get-tuple-element.29.refs_0_, bf16[128,2048]{1,0:T(8,128)(2,1)S(1)} %get-tuple-element.30.refs_1_, bf16[128,2048]{1,0:T(8,128)(2,1)S(1)} %get-tuple-element.31.refs_2_, ...), custom_call_target="tpu_custom_call" | custom-call | flops 1840000000 | tf_op jit(solution)/shard_map/pallas_call | solution.py:38
  31.2 0.0 collective-permute-done.1.refs_10_
  31.2 0.0 collective-permute-done.5.refs_11_
  31.2 0.0 collective-permute-done.7.refs_12_
  31.2 0.0 collective-permute-done.9.refs_13_
  31.2 0.0 collective-permute-done.11.refs_14_
  31.2 1.9 %shard_map.90 = (bf16[128,2048]{1,0:T(8,128)(2,1)}, bf16[128,2048]{1,0:T(8,128)(2,1)}, bf16[128,2048]{1,0:T(8,128)(2,1)}, f32[16,128,128]{2,1,0:T(8,128)}) custom-call(bf16[128,2048]{1,0:T(8,128)(2,1)S(1)} %get-tuple-element.29.refs_0_, ...), custom_call_target="tpu_custom_call", output_to_operand_aliasing={{0}: (15, {}), {1}: (16, {}), {2}: (17, {}), {3}: (18, {})} | custom-call | flops 1840000000 | tf_op jit(solution)/shard_map/pallas_call | solution.py:38
Async XLA Ops:
  2.6 2.4 %collective-permute-start = (bf16[4,3,2,128,128]{4,3,2,1,0:T(8,128)(2,1)S(1)}, bf16[4,3,2,128,128]{4,3,2,1,0:T(8,128)(2,1)S(1)}, u32[]{:S(2)}, u32[]{:S(2)}) collective-permute-start(bf16[4,3,2,128,128]{4,3,2,1,0:T(8,128)(2,1)S(1)} %get-tuple-element.34), channel_id=1, source_target_pairs={{0,1},{1,0},{2,3},{3,2},{4,5},{5,4},{6,7},{7,6},{8,9},{9,8},{10,11... | collective-permute-start | bytes 2359304 | tf_op jit(solution)/shard_map/ppermute | solution.py:280
  5.0 4.9 %copy-start = (bf16[16,128,128]{2,1,0:T(8,128)(2,1)S(1)}, bf16[16,128,128]{2,1,0:T(8,128)(2,1)}, u32[]{:S(2)}) copy-start(bf16[16,128,128]{2,1,0:T(8,128)(2,1)} %refs_4_.5) | copy-start | bytes 1572868
  5.5 8.0 %collective-permute-start.2 = (bf16[656,128]{1,0:T(8,128)(2,1)S(1)}, bf16[656,128]{1,0:T(8,128)(2,1)S(1)}, u32[]{:S(2)}, u32[]{:S(2)}) collective-permute-start(bf16[656,128]{1,0:T(8,128)(2,1)S(1)} %get-tuple-element.42), channel_id=1, source_target_pairs={{0,2},{1,3},{2,0},{3,1},{4,6},{5,7},{6,4},{7,5},{8,10},{9,11},{10,... | collective-permute-start | bytes 503816 | tf_op jit(solution)/shard_map/ppermute | solution.py:280
  8.4 9.6 %collective-permute-start.3 = (bf16[656,128]{1,0:T(8,128)(2,1)S(1)}, bf16[656,128]{1,0:T(8,128)(2,1)S(1)}, u32[]{:S(2)}, u32[]{:S(2)}) collective-permute-start(bf16[656,128]{1,0:T(8,128)(2,1)S(1)} %get-tuple-element.43), channel_id=1, source_target_pairs={{0,4},{1,5},{2,6},{3,7},{4,0},{5,1},{6,2},{7,3},{8,12},{9,13},{10,... | collective-permute-start | bytes 503816 | tf_op jit(solution)/shard_map/ppermute | solution.py:280
  10.0 8.1 %collective-permute-start.4 = (bf16[656,128]{1,0:T(8,128)(2,1)S(1)}, bf16[656,128]{1,0:T(8,128)(2,1)S(1)}, u32[]{:S(2)}, u32[]{:S(2)}) collective-permute-start(bf16[656,128]{1,0:T(8,128)(2,1)S(1)} %get-tuple-element.44), channel_id=1, source_target_pairs={{0,6},{1,7},{2,4},{3,5},{4,2},{5,3},{6,0},{7,1},{8,14},{9,15},{10,... | collective-permute-start | bytes 503816 | tf_op jit(solution)/shard_map/ppermute | solution.py:280
  18.6 6.8 %collective-permute-start.6 = (bf16[656,128]{1,0:T(8,128)(2,1)S(1)}, bf16[656,128]{1,0:T(8,128)(2,1)S(1)}, u32[]{:S(2)}, u32[]{:S(2)}) collective-permute-start(bf16[656,128]{1,0:T(8,128)(2,1)S(1)} %get-tuple-element.46), channel_id=1, source_target_pairs={{0,2},{1,3},{2,0},{3,1},{4,6},{5,7},{6,4},{7,5},{8,10},{9,11},{10,... | collective-permute-start | bytes 503816 | tf_op jit(solution)/shard_map/ppermute | solution.py:280
  19.9 8.8 %collective-permute-start.8 = (bf16[656,128]{1,0:T(8,128)(2,1)S(1)}, bf16[656,128]{1,0:T(8,128)(2,1)S(1)}, u32[]{:S(2)}, u32[]{:S(2)}) collective-permute-start(bf16[656,128]{1,0:T(8,128)(2,1)S(1)} %get-tuple-element.47), channel_id=1, source_target_pairs={{0,4},{1,5},{2,6},{3,7},{4,0},{5,1},{6,2},{7,3},{8,12},{9,13},{10,... | collective-permute-start | bytes 503816 | tf_op jit(solution)/shard_map/ppermute | solution.py:280
  20.8 8.0 %collective-permute-start.10 = (bf16[656,128]{1,0:T(8,128)(2,1)S(1)}, bf16[656,128]{1,0:T(8,128)(2,1)S(1)}, u32[]{:S(2)}, u32[]{:S(2)}) collective-permute-start(bf16[656,128]{1,0:T(8,128)(2,1)S(1)} %get-tuple-element.48), channel_id=1, source_target_pairs={{0,6},{1,7},{2,4},{3,5},{4,2},{5,3},{6,0},{7,1},{8,14},{9,15},{10,... | collective-permute-start | bytes 503816 | tf_op jit(solution)/shard_map/ppermute | solution.py:280
  22.2 9.0 %collective-permute-start.1 = (bf16[4,2,128,128]{3,2,1,0:T(8,128)(2,1)S(1)}, bf16[4,2,128,128]{3,2,1,0:T(8,128)(2,1)S(1)}, u32[]{:S(2)}, u32[]{:S(2)}) collective-permute-start(bf16[4,2,128,128]{3,2,1,0:T(8,128)(2,1)S(1)} %get-tuple-element.41), channel_id=1, source_target_pairs={{0,1},{1,0},{2,3},{3,2},{4,5},{5,4},{6,7},{7,6},{8,9},{9,8},{10,11... | collective-permute-start | bytes 786440 | tf_op jit(solution)/shard_map/ppermute | solution.py:280
  22.2 9.0 %collective-permute-start.5 = (bf16[656,128]{1,0:T(8,128)(2,1)S(1)}, bf16[656,128]{1,0:T(8,128)(2,1)S(1)}, u32[]{:S(2)}, u32[]{:S(2)}) collective-permute-start(bf16[656,128]{1,0:T(8,128)(2,1)S(1)} %get-tuple-element.45.refs_11_), channel_id=1, source_target_pairs={{0,1},{1,0},{2,3},{3,2},{4,5},{5,4},{6,7},{7,6},{8,9},{9,8},{10,11... | collective-permute-start | bytes 503816 | tf_op jit(solution)/shard_map/ppermute | solution.py:280
  25.5 5.7 %collective-permute-start.7 = (bf16[656,128]{1,0:T(8,128)(2,1)S(1)}, bf16[656,128]{1,0:T(8,128)(2,1)S(1)}, u32[]{:S(2)}, u32[]{:S(2)}) collective-permute-start(bf16[656,128]{1,0:T(8,128)(2,1)S(1)} %collective-permute-done.6.refs_12_), channel_id=1, source_target_pairs={{0,1},{1,0},{2,3},{3,2},{4,5},{5,4},{6,7},{7,6},{8,9},{9,8},{10,11... | collective-permute-start | bytes 503816 | tf_op jit(solution)/shard_map/ppermute | solution.py:280
  28.7 2.4 %collective-permute-start.9 = (bf16[656,128]{1,0:T(8,128)(2,1)S(1)}, bf16[656,128]{1,0:T(8,128)(2,1)S(1)}, u32[]{:S(2)}, u32[]{:S(2)}) collective-permute-start(bf16[656,128]{1,0:T(8,128)(2,1)S(1)} %collective-permute-done.8.refs_13_), channel_id=1, source_target_pairs={{0,1},{1,0},{2,3},{3,2},{4,5},{5,4},{6,7},{7,6},{8,9},{9,8},{10,11... | collective-permute-start | bytes 503816 | tf_op jit(solution)/shard_map/ppermute | solution.py:280
  28.7 2.4 %collective-permute-start.11 = (bf16[656,128]{1,0:T(8,128)(2,1)S(1)}, bf16[656,128]{1,0:T(8,128)(2,1)S(1)}, u32[]{:S(2)}, u32[]{:S(2)}) collective-permute-start(bf16[656,128]{1,0:T(8,128)(2,1)S(1)} %collective-permute-done.10.refs_14_), channel_id=1, source_target_pairs={{0,1},{1,0},{2,3},{3,2},{4,5},{5,4},{6,7},{7,6},{8,9},{9,8},{10,11... | collective-permute-start | bytes 503816 | tf_op jit(solution)/shard_map/ppermute | solution.py:280

commit v4 on v3

--- a/solution.py
+++ b/solution.py
@@ -14,6 +14,7 @@
 HBM = pl.BlockSpec(memory_space=pltpu.HBM)
 ANY = pl.BlockSpec(memory_space=pl.ANY)
 GROUPS = 4
+FIRST = 0
 EXTRA = 16
 
 
@@ -29,7 +30,9 @@
     return lax.dot_general(a, b, (((0,), (0,)), ((), ())), preferred_element_type=F32)
 
 
-def call(body, outs, operands, cost, after=(), scratch=(), in_spec=VMEM, out_specs=None, aliases=None):
+def call(
+    body, outs, operands, cost, after=(), scratch=(), in_spec=VMEM, out_specs=None, aliases=None, in_after=ANY
+):
     count = len(operands)
 
     def run(*refs):
@@ -38,7 +41,7 @@
     return pl.pallas_call(
         run,
         out_shape=[jax.ShapeDtypeStruct(shape, dtype) for shape, dtype in outs],
-        in_specs=[in_spec] * count + [ANY] * len(after),
+        in_specs=[in_spec] * count + [in_after] * len(after),
         out_specs=out_specs or [VMEM] * len(outs),
         scratch_shapes=list(scratch),
         input_output_aliases=aliases or {},
@@ -119,7 +122,8 @@
     size = first.shape[0]
     rows, cols = triangle(size)
     both = jnp.where(rows >= cols, first, second)
-    diagonal = jnp.sum(jnp.where(rows == cols, second, 0.0), axis=0, keepdims=True)
+    both += jnp.where(rows <= cols, first, second).T
+    diagonal = 2.0 * jnp.sum(jnp.where(rows == cols, second, 0.0), axis=0, keepdims=True)
     return both, jnp.broadcast_to(diagonal, (EXTRA, size))
 
 
@@ -143,15 +147,30 @@
             sums = []
             for i in (2 * pair, 2 * pair + 1):
                 total = totals[apart * per_owner + i]
-                total += own[apart, 2, i].astype(F32) + other[apart, 2, i].astype(F32)
-                sums.append(total + total.T)
+                sums.append(total + own[apart, 2, i].astype(F32) + other[apart, 2, i].astype(F32))
             both, diagonal = pack(*sums)
             start = 2 * per_owner * size + pair * (size + EXTRA)
             outs[apart][start : start + size] = both.astype(BF16)
             outs[apart][start + size : start + size + EXTRA] = diagonal.astype(BF16)
 
 
-def rest_body(per_owner, q, k, v, g, w, part_k, part_v, key_w, gram):
+def rest_first_body(per_owner, *refs):
+    core, _ = place()
+
+    @pl.when(core == FIRST)
+    def _():
+        rest(per_owner, *refs)
+
+
+def rest_second_body(per_owner, *refs):
+    core, _ = place()
+
+    @pl.when(core != FIRST)
+    def _():
+        rest(per_owner, *refs[:5], *refs[-4:])
+
+
+def rest(per_owner, q, k, v, g, w, part_k, part_v, key_w, gram):
     size = w.shape[-1]
     core, chip = place()
     rows, cols = triangle(q.shape[0])
@@ -199,7 +218,7 @@
             outs[to][behind] = suffix.astype(BF16)
             product = dot_nt(parts[to][behind], prefix)
             cross = product if cross is None else cross + product
-        turns.append(cross + cross.T)
+        turns.append(cross)
     for pair in range(per_owner // 2):
         both, diagonal = pack(turns[2 * pair], turns[2 * pair + 1])
         start = 2 * per_owner * size + pair * (size + EXTRA)
@@ -305,15 +324,24 @@
         bind(near_body, per_owner), [(triple, BF16), (one, BF16), (one, F32)], here, 1.0
     )
     chip_sums = call(bind(join_body, per_owner), [(payload, BF16)] * GROUPS, (own, other), 0.5)
+    locals_ = [(twice, F32), (twice, F32), (twice, BF16), (twice, BF16)]
+    local = list(
+        call(bind(rest_first_body, per_owner), locals_, (*here, w), 1.8, after=chip_sums[:1])
+    )
+    held = lax.optimization_barrier((*chip_sums, local[0]))
+    chip_sums, local[0] = list(held[:GROUPS]), held[GROUPS]
     parts = [chip_sums[0]] + [swap(chip_sums[j], 2 * j) for j in range(1, GROUPS)]
     extra = swap(extra, 1)
-    part_k, part_v, key_w, gram = call(
-        bind(rest_body, per_owner),
-        [(twice, F32), (twice, F32), (twice, BF16), (twice, BF16)],
+    local = call(
+        bind(rest_second_body, per_owner),
+        locals_,
         (*here, w),
         1.8,
-        after=chip_sums[:1],
-    )
+        after=tuple(local),
+        aliases={5 + n: n for n in range(4)},
+        in_after=VMEM,
+    )
+    part_k, part_v, key_w, gram = local
     carried = call(
         bind(owner_body, per_owner), [(payload, BF16)] * GROUPS, parts, 0.5, after=(gram,)
     )

time: 33.2 us -> 31.6 us (0.952)
  waiting for transfers between devices: 13.6 us -> 11.8 us
  local copies, waits for them, and re-layouts: 0.01 us -> 0.51 us
  starting transfers between devices: 9.55 us -> 9.05 us
    ppermute x12, waiting for transfers between devices: 13.6 us -> 11.8 us  [swap(): return lax.ppermute(x, 'ctx', [(i, i ^ apart) for i in range(count)])]
    ppermute x12, starting transfers between devices: 9.55 us -> 9.05 us  [swap(): return lax.ppermute(x, 'ctx', [(i, i ^ apart) for i in range(count)])]
    unnamed x2, local copies, waits for them, and re-layouts: 0.01 us -> 0.51 us
    pallas_call x7 -> x8, Pallas kernels: 9.26 us -> 9.27 us  [call(): pl.pallas_call(run, out_shape=[jax.ShapeDtypeStruct(shape, dtype) for sha...]
  transfers between devices with their start and end apart: 12 -> 12, of which waited for: 5 -> 6; matrix products, arithmetic and copies ran while one was open for 0% -> 0% of each run, Pallas kernels for 13% -> 8%
where the time goes in v4:
time: 31.6 us; the launch traced here: 31.4 us
  waiting for transfers between devices  11.8 us (37%)
  Pallas kernels  9.27 us (29%)
  starting transfers between devices  9.05 us (29%)
  between operations  0.71 us (2%)
  local copies, waits for them, and re-layouts  0.51 us (2%)
    ppermute x12, waiting for transfers between devices, swap(): return lax.ppermute(x, 'ctx', [(i, i ^ apart) for i in range(count)])  11.8 us
    pallas_call x8, Pallas kernels, call(): pl.pallas_call(run, out_shape=[jax.ShapeDtypeStruct(shape, dtype) for sha...  9.27 us
    ppermute x12, starting transfers between devices, swap(): return lax.ppermute(x, 'ctx', [(i, i ^ apart) for i in range(count)])  9.05 us
  transfers between devices with their start and end apart: 12, of which 6 were waited for; matrix products, arithmetic and copies ran while one was open for 0% of the time, Pallas kernels for 8%

profile of v4, /device:TPU:0, one launch (start us, length us, event | category | flops | bytes accessed | tf_op | source)
XLA Modules:
  0.0 31.4 jit_solution(11445018780898508724)
XLA Ops:
  0.6 2.0 %shard_map.84 = (bf16[128,2048]{1,0:T(8,128)(2,1)S(1)}, bf16[128,2048]{1,0:T(8,128)(2,1)S(1)}, bf16[128,2048]{1,0:T(8,128)(2,1)S(1)}, bf16[128,2048]{1,0:T(8,128...) custom-call(bf16[128,2048]{1,0:T(8,128)(2,1)} %refs_0_.1, ...), custom_call_target="tpu_custom_call" | custom-call | flops 2300000000 | tf_op jit(solution)/shard_map/pallas_call | solution.py:41
  2.6 0.5 %collective-permute-start = (bf16[4,3,2,128,128]{4,3,2,1,0:T(8,128)(2,1)S(1)}, bf16[4,3,2,128,128]{4,3,2,1,0:T(8,128)(2,1)S(1)}, u32[]{:S(2)}, u32[]{:S(2)}) collective-permute-start(bf16[4,3,2,128,128]{4,3,2,1,0:T(8,128)(2,1)S(1)} %get-tuple-element.43), channel_id=1, source_target_pairs={{0,1},{1,0},{2,3},{3,2},{4,5},{5,4},{6,7},{7,6},{8,9},{9,8},{10,11... | collective-permute-start | bytes 2359304 | tf_op jit(solution)/shard_map/ppermute | solution.py:299
  3.1 0.7 %shard_map.85 = (bf16[4,3,2,128,128]{4,3,2,1,0:T(8,128)(2,1)S(1)}, bf16[4,2,128,128]{3,2,1,0:T(8,128)(2,1)S(1)}, f32[4,2,128,128]{3,2,1,0:T(8,128)S(1)}) custom-call(bf16[128,2048]{1,0:T(8,128)(2,1)S(1)} %get-tuple-element.38.refs_0_, bf16[128,2048]{1,0:T(8,128)(2,1)S(1)} %get-tuple-element.39.refs_1_, bf16[128,2048]{1,0:T(8,128)(2,1)S(1)} %get-tuple-element.40.refs_2_, ...), custom_call_target="tpu_custom_call" | custom-call | flops 1150000000 | tf_op jit(solution)/shard_map/pallas_call | solution.py:41
  3.9 1.2 %collective-permute-done.refs_1_.refs_10_ = bf16[4,3,2,128,128]{4,3,2,1,0:T(8,128)(2,1)S(1)} collective-permute-done((bf16[4,3,2,128,128]{4,3,2,1,0:T(8,128)(2,1)S(1)}, bf16[4,3,2,128,128]{4,3,2,1,0:T(8,128)(2,1)S(1)}, u32[]{:S(2)}, u32[]{:S(2)}) %collective-permute-start) | collective-permute-done | bytes 786464 | tf_op jit(solution)/shard_map/ppermute | solution.py:299
  5.0 0.0 copy-start
  5.0 0.5 %shard_map.86 = (bf16[656,128]{1,0:T(8,128)(2,1)S(1)}, bf16[656,128]{1,0:T(8,128)(2,1)S(1)}, bf16[656,128]{1,0:T(8,128)(2,1)S(1)}, bf16[656,128]{1,0:T(8,128)(2,1)S(1)}) custom-call(bf16[4,3,2,128,128]{4,3,2,1,0:T(8,128)(2,1)S(1)} %get-tuple-element.42.refs_0_, bf16[4,3,2,128,128]{4,3,2,1,0:T(8,128)(2,1)S(1)} %collective-permute-done.refs_1_.refs_10_), custom_call_target="tpu_custom_call" | custom-call | flops 575000000 | tf_op jit(solution)/shard_map/pallas_call | solution.py:41
  5.6 0.5 %copy-done = bf16[16,128,128]{2,1,0:T(8,128)(2,1)S(1)} copy-done((bf16[16,128,128]{2,1,0:T(8,128)(2,1)S(1)}, bf16[16,128,128]{2,1,0:T(8,128)(2,1)}, u32[]{:S(2)}) %copy-start) | copy-done | bytes 524312
  6.1 1.8 %shard_map.87 = (f32[2,4,2,128,128]{4,3,2,1,0:T(8,128)S(1)}, f32[2,4,2,128,128]{4,3,2,1,0:T(8,128)S(1)}, bf16[2,4,2,128,128]{4,3,2,1,0:T(8,128)(2,1)S(1)}, bf16[2,4,2,128,128]{4,3,2,1,0:T(8,128)(2,1)S(1)}) custom-call(bf16[128,2048]{1,0:T(8,128)(2,1)S(1)} %get-tuple-element.38.refs_0_, bf16[128,2048]{1,0:T(8,128)(2,1)S(1)} %get-tuple-element.39.refs_1_, ...), custom_call_target="tpu_custom_call" | custom-call | flops 2070000000 | tf_op jit(solution)/shard_map/pallas_call | solution.py:41
  7.9 2.9 %collective-permute-start.2 = (bf16[656,128]{1,0:T(8,128)(2,1)S(1)}, bf16[656,128]{1,0:T(8,128)(2,1)S(1)}, u32[]{:S(2)}, u32[]{:S(2)}) collective-permute-start(bf16[656,128]{1,0:T(8,128)(2,1)S(1)} %get-tuple-element.60), channel_id=1, source_target_pairs={{0,2},{1,3},{2,0},{3,1},{4,6},{5,7},{6,4},{7,5},{8,10},{9,11},{10,... | collective-permute-start | bytes 503816 | tf_op jit(solution)/shard_map/ppermute | solution.py:299
  10.8 1.5 %collective-permute-start.3 = (bf16[656,128]{1,0:T(8,128)(2,1)S(1)}, bf16[656,128]{1,0:T(8,128)(2,1)S(1)}, u32[]{:S(2)}, u32[]{:S(2)}) collective-permute-start(bf16[656,128]{1,0:T(8,128)(2,1)S(1)} %get-tuple-element.61), channel_id=1, source_target_pairs={{0,4},{1,5},{2,6},{3,7},{4,0},{5,1},{6,2},{7,3},{8,12},{9,13},{10,... | collective-permute-start | bytes 503816 | tf_op jit(solution)/shard_map/ppermute | solution.py:299
  12.3 0.0 collective-permute-start.4
  12.3 3.4 %collective-permute-done.2.refs_1_ = bf16[656,128]{1,0:T(8,128)(2,1)S(1)} collective-permute-done((bf16[656,128]{1,0:T(8,128)(2,1)S(1)}, bf16[656,128]{1,0:T(8,128)(2,1)S(1)}, u32[]{:S(2)}, u32[]{:S(2)}) %collective-permute-start.2) | collective-permute-done | bytes 167968 | tf_op jit(solution)/shard_map/ppermute | solution.py:299
  15.7 3.5 %collective-permute-done.3.refs_2_ = bf16[656,128]{1,0:T(8,128)(2,1)S(1)} collective-permute-done((bf16[656,128]{1,0:T(8,128)(2,1)S(1)}, bf16[656,128]{1,0:T(8,128)(2,1)S(1)}, u32[]{:S(2)}, u32[]{:S(2)}) %collective-permute-start.3) | collective-permute-done | bytes 167968 | tf_op jit(solution)/shard_map/ppermute | solution.py:299
  19.2 0.0 collective-permute-done.4.refs_3_
  19.2 0.5 %shard_map.89 = (bf16[656,128]{1,0:T(8,128)(2,1)S(1)}, bf16[656,128]{1,0:T(8,128)(2,1)S(1)}, bf16[656,128]{1,0:T(8,128)(2,1)S(1)}, bf16[656,128]{1,0:T(8,128)(2,1)S(1)}) custom-call(bf16[656,128]{1,0:T(8,128)(2,1)S(1)} %get-tuple-element.59.refs_5_.refs_0_, bf16[656,128]{1,0:T(8,128)(2,1)S(1)} %collective-permute-done.2.refs_1_, ...), custom_call_target="tpu_custom_call" | custom-call | flops 575000000 | tf_op jit(solution)/shard_map/pallas_call | solution.py:41
  19.7 0.7 %collective-permute-start.6 = (bf16[656,128]{1,0:T(8,128)(2,1)S(1)}, bf16[656,128]{1,0:T(8,128)(2,1)S(1)}, u32[]{:S(2)}, u32[]{:S(2)}) collective-permute-start(bf16[656,128]{1,0:T(8,128)(2,1)S(1)} %get-tuple-element.64), channel_id=1, source_target_pairs={{0,2},{1,3},{2,0},{3,1},{4,6},{5,7},{6,4},{7,5},{8,10},{9,11},{10,... | collective-permute-start | bytes 503816 | tf_op jit(solution)/shard_map/ppermute | solution.py:299
  20.4 0.8 %collective-permute-start.8 = (bf16[656,128]{1,0:T(8,128)(2,1)S(1)}, bf16[656,128]{1,0:T(8,128)(2,1)S(1)}, u32[]{:S(2)}, u32[]{:S(2)}) collective-permute-start(bf16[656,128]{1,0:T(8,128)(2,1)S(1)} %get-tuple-element.65), channel_id=1, source_target_pairs={{0,4},{1,5},{2,6},{3,7},{4,0},{5,1},{6,2},{7,3},{8,12},{9,13},{10,... | collective-permute-start | bytes 503816 | tf_op jit(solution)/shard_map/ppermute | solution.py:299
  21.2 2.0 %collective-permute-start.10 = (bf16[656,128]{1,0:T(8,128)(2,1)S(1)}, bf16[656,128]{1,0:T(8,128)(2,1)S(1)}, u32[]{:S(2)}, u32[]{:S(2)}) collective-permute-start(bf16[656,128]{1,0:T(8,128)(2,1)S(1)} %get-tuple-element.66), channel_id=1, source_target_pairs={{0,6},{1,7},{2,4},{3,5},{4,2},{5,3},{6,0},{7,1},{8,14},{9,15},{10,... | collective-permute-start | bytes 503816 | tf_op jit(solution)/shard_map/ppermute | solution.py:299
  23.3 0.0 collective-permute-start.1
  23.3 0.5 %collective-permute-start.5 = (bf16[656,128]{1,0:T(8,128)(2,1)S(1)}, bf16[656,128]{1,0:T(8,128)(2,1)S(1)}, u32[]{:S(2)}, u32[]{:S(2)}) collective-permute-start(bf16[656,128]{1,0:T(8,128)(2,1)S(1)} %get-tuple-element.63.refs_11_), channel_id=1, source_target_pairs={{0,1},{1,0},{2,3},{3,2},{4,5},{5,4},{6,7},{7,6},{8,9},{9,8},{10,11... | collective-permute-start | bytes 503816 | tf_op jit(solution)/shard_map/ppermute | solution.py:299
  23.8 1.4 %collective-permute-done.6.refs_12_ = bf16[656,128]{1,0:T(8,128)(2,1)S(1)} collective-permute-done((bf16[656,128]{1,0:T(8,128)(2,1)S(1)}, bf16[656,128]{1,0:T(8,128)(2,1)S(1)}, u32[]{:S(2)}, u32[]{:S(2)}) %collective-permute-start.6) | collective-permute-done | bytes 167968 | tf_op jit(solution)/shard_map/ppermute | solution.py:299
  25.2 0.0 collective-permute-start.7
  25.2 0.5 %collective-permute-done.8.refs_13_ = bf16[656,128]{1,0:T(8,128)(2,1)S(1)} collective-permute-done((bf16[656,128]{1,0:T(8,128)(2,1)S(1)}, bf16[656,128]{1,0:T(8,128)(2,1)S(1)}, u32[]{:S(2)}, u32[]{:S(2)}) %collective-permute-start.8) | collective-permute-done | bytes 167968 | tf_op jit(solution)/shard_map/ppermute | solution.py:299
  25.8 0.0 collective-permute-start.9
  25.8 1.8 %collective-permute-done.10.refs_14_ = bf16[656,128]{1,0:T(8,128)(2,1)S(1)} collective-permute-done((bf16[656,128]{1,0:T(8,128)(2,1)S(1)}, bf16[656,128]{1,0:T(8,128)(2,1)S(1)}, u32[]{:S(2)}, u32[]{:S(2)}) %collective-permute-start.10) | collective-permute-done | bytes 167968 | tf_op jit(solution)/shard_map/ppermute | solution.py:299
  27.6 0.0 collective-permute-start.11
  27.6 1.9 %shard_map.90 = (bf16[128,2048]{1,0:T(8,128)(2,1)}, bf16[128,2048]{1,0:T(8,128)(2,1)}, bf16[128,2048]{1,0:T(8,128)(2,1)}, f32[16,128,128]{2,1,0:T(8,128)}) custom-call(bf16[128,2048]{1,0:T(8,128)(2,1)S(1)} %get-tuple-element.38.refs_0_, bf16[128,2048]{1,0:T(8,128)(2,1)S(1)} %get-tuple-element.39.refs_1_, bf16[128,2048]{1,0:T(8,128)(2,1)S(1)} %get-tuple-element.40.refs_2_, ...), custom_call_target="tpu_custom_call" | custom-call | flops 1840000000 | tf_op jit(solution)/shard_map/pallas_call | solution.py:41
  29.5 0.0 collective-permute-done.1.refs_10_
  29.5 0.0 collective-permute-done.5.refs_11_
  29.5 0.0 collective-permute-done.7.refs_12_
  29.5 0.0 collective-permute-done.9.refs_13_
  29.5 0.0 collective-permute-done.11.refs_14_
  29.5 1.9 %shard_map.91 = (bf16[128,2048]{1,0:T(8,128)(2,1)}, bf16[128,2048]{1,0:T(8,128)(2,1)}, bf16[128,2048]{1,0:T(8,128)(2,1)}, f32[16,128,128]{2,1,0:T(8,128)}) custom-call(bf16[128,2048]{1,0:T(8,128)(2,1)S(1)} %get-tuple-element.38.refs_0_, ...), custom_call_target="tpu_custom_call", output_to_operand_aliasing={{0}: (15, {}), {1}: (16, {}), {2}: (17, {}), {3}: (18, {})} | custom-call | flops 1840000000 | tf_op jit(solution)/shard_map/pallas_call | solution.py:41
  (1 shorter events, 0.0 us)
Async XLA Ops:
  2.6 2.4 %collective-permute-start = (bf16[4,3,2,128,128]{4,3,2,1,0:T(8,128)(2,1)S(1)}, bf16[4,3,2,128,128]{4,3,2,1,0:T(8,128)(2,1)S(1)}, u32[]{:S(2)}, u32[]{:S(2)}) collective-permute-start(bf16[4,3,2,128,128]{4,3,2,1,0:T(8,128)(2,1)S(1)} %get-tuple-element.43), channel_id=1, source_target_pairs={{0,1},{1,0},{2,3},{3,2},{4,5},{5,4},{6,7},{7,6},{8,9},{9,8},{10,11... | collective-permute-start | bytes 2359304 | tf_op jit(solution)/shard_map/ppermute | solution.py:299
  5.0 1.0 %copy-start = (bf16[16,128,128]{2,1,0:T(8,128)(2,1)S(1)}, bf16[16,128,128]{2,1,0:T(8,128)(2,1)}, u32[]{:S(2)}) copy-start(bf16[16,128,128]{2,1,0:T(8,128)(2,1)} %refs_4_.7) | copy-start | bytes 1572868
  7.9 7.8 %collective-permute-start.2 = (bf16[656,128]{1,0:T(8,128)(2,1)S(1)}, bf16[656,128]{1,0:T(8,128)(2,1)S(1)}, u32[]{:S(2)}, u32[]{:S(2)}) collective-permute-start(bf16[656,128]{1,0:T(8,128)(2,1)S(1)} %get-tuple-element.60), channel_id=1, source_target_pairs={{0,2},{1,3},{2,0},{3,1},{4,6},{5,7},{6,4},{7,5},{8,10},{9,11},{10,... | collective-permute-start | bytes 503816 | tf_op jit(solution)/shard_map/ppermute | solution.py:299
  10.8 8.4 %collective-permute-start.3 = (bf16[656,128]{1,0:T(8,128)(2,1)S(1)}, bf16[656,128]{1,0:T(8,128)(2,1)S(1)}, u32[]{:S(2)}, u32[]{:S(2)}) collective-permute-start(bf16[656,128]{1,0:T(8,128)(2,1)S(1)} %get-tuple-element.61), channel_id=1, source_target_pairs={{0,4},{1,5},{2,6},{3,7},{4,0},{5,1},{6,2},{7,3},{8,12},{9,13},{10,... | collective-permute-start | bytes 503816 | tf_op jit(solution)/shard_map/ppermute | solution.py:299
  12.3 6.9 %collective-permute-start.4 = (bf16[656,128]{1,0:T(8,128)(2,1)S(1)}, bf16[656,128]{1,0:T(8,128)(2,1)S(1)}, u32[]{:S(2)}, u32[]{:S(2)}) collective-permute-start(bf16[656,128]{1,0:T(8,128)(2,1)S(1)} %get-tuple-element.62), channel_id=1, source_target_pairs={{0,6},{1,7},{2,4},{3,5},{4,2},{5,3},{6,0},{7,1},{8,14},{9,15},{10,... | collective-permute-start | bytes 503816 | tf_op jit(solution)/shard_map/ppermute | solution.py:299
  19.7 5.5 %collective-permute-start.6 = (bf16[656,128]{1,0:T(8,128)(2,1)S(1)}, bf16[656,128]{1,0:T(8,128)(2,1)S(1)}, u32[]{:S(2)}, u32[]{:S(2)}) collective-permute-start(bf16[656,128]{1,0:T(8,128)(2,1)S(1)} %get-tuple-element.64), channel_id=1, source_target_pairs={{0,2},{1,3},{2,0},{3,1},{4,6},{5,7},{6,4},{7,5},{8,10},{9,11},{10,... | collective-permute-start | bytes 503816 | tf_op jit(solution)/shard_map/ppermute | solution.py:299
  20.4 5.4 %collective-permute-start.8 = (bf16[656,128]{1,0:T(8,128)(2,1)S(1)}, bf16[656,128]{1,0:T(8,128)(2,1)S(1)}, u32[]{:S(2)}, u32[]{:S(2)}) collective-permute-start(bf16[656,128]{1,0:T(8,128)(2,1)S(1)} %get-tuple-element.65), channel_id=1, source_target_pairs={{0,4},{1,5},{2,6},{3,7},{4,0},{5,1},{6,2},{7,3},{8,12},{9,13},{10,... | collective-permute-start | bytes 503816 | tf_op jit(solution)/shard_map/ppermute | solution.py:299
  21.2 6.3 %collective-permute-start.10 = (bf16[656,128]{1,0:T(8,128)(2,1)S(1)}, bf16[656,128]{1,0:T(8,128)(2,1)S(1)}, u32[]{:S(2)}, u32[]{:S(2)}) collective-permute-start(bf16[656,128]{1,0:T(8,128)(2,1)S(1)} %get-tuple-element.66), channel_id=1, source_target_pairs={{0,6},{1,7},{2,4},{3,5},{4,2},{5,3},{6,0},{7,1},{8,14},{9,15},{10,... | collective-permute-start | bytes 503816 | tf_op jit(solution)/shard_map/ppermute | solution.py:299
  23.3 6.2 %collective-permute-start.1 = (bf16[4,2,128,128]{3,2,1,0:T(8,128)(2,1)S(1)}, bf16[4,2,128,128]{3,2,1,0:T(8,128)(2,1)S(1)}, u32[]{:S(2)}, u32[]{:S(2)}) collective-permute-start(bf16[4,2,128,128]{3,2,1,0:T(8,128)(2,1)S(1)} %get-tuple-element.58), channel_id=1, source_target_pairs={{0,1},{1,0},{2,3},{3,2},{4,5},{5,4},{6,7},{7,6},{8,9},{9,8},{10,11... | collective-permute-start | bytes 786440 | tf_op jit(solution)/shard_map/ppermute | solution.py:299
  23.3 6.2 %collective-permute-start.5 = (bf16[656,128]{1,0:T(8,128)(2,1)S(1)}, bf16[656,128]{1,0:T(8,128)(2,1)S(1)}, u32[]{:S(2)}, u32[]{:S(2)}) collective-permute-start(bf16[656,128]{1,0:T(8,128)(2,1)S(1)} %get-tuple-element.63.refs_11_), channel_id=1, source_target_pairs={{0,1},{1,0},{2,3},{3,2},{4,5},{5,4},{6,7},{7,6},{8,9},{9,8},{10,11... | collective-permute-start | bytes 503816 | tf_op jit(solution)/shard_map/ppermute | solution.py:299
  25.2 4.2 %collective-permute-start.7 = (bf16[656,128]{1,0:T(8,128)(2,1)S(1)}, bf16[656,128]{1,0:T(8,128)(2,1)S(1)}, u32[]{:S(2)}, u32[]{:S(2)}) collective-permute-start(bf16[656,128]{1,0:T(8,128)(2,1)S(1)} %collective-permute-done.6.refs_12_), channel_id=1, source_target_pairs={{0,1},{1,0},{2,3},{3,2},{4,5},{5,4},{6,7},{7,6},{8,9},{9,8},{10,11... | collective-permute-start | bytes 503816 | tf_op jit(solution)/shard_map/ppermute | solution.py:299
  25.8 3.7 %collective-permute-start.9 = (bf16[656,128]{1,0:T(8,128)(2,1)S(1)}, bf16[656,128]{1,0:T(8,128)(2,1)S(1)}, u32[]{:S(2)}, u32[]{:S(2)}) collective-permute-start(bf16[656,128]{1,0:T(8,128)(2,1)S(1)} %collective-permute-done.8.refs_13_), channel_id=1, source_target_pairs={{0,1},{1,0},{2,3},{3,2},{4,5},{5,4},{6,7},{7,6},{8,9},{9,8},{10,11... | collective-permute-start | bytes 503816 | tf_op jit(solution)/shard_map/ppermute | solution.py:299
  27.6 1.9 %collective-permute-start.11 = (bf16[656,128]{1,0:T(8,128)(2,1)S(1)}, bf16[656,128]{1,0:T(8,128)(2,1)S(1)}, u32[]{:S(2)}, u32[]{:S(2)}) collective-permute-start(bf16[656,128]{1,0:T(8,128)(2,1)S(1)} %collective-permute-done.10.refs_14_), channel_id=1, source_target_pairs={{0,1},{1,0},{2,3},{3,2},{4,5},{5,4},{6,7},{7,6},{8,9},{9,8},{10,11... | collective-permute-start | bytes 503816 | tf_op jit(solution)/shard_map/ppermute | solution.py:299

commit v5 on v4

--- a/solution.py
+++ b/solution.py
@@ -31,7 +31,7 @@
 
 
 def call(
-    body, outs, operands, cost, after=(), scratch=(), in_spec=VMEM, out_specs=None, aliases=None, in_after=ANY
+    body, outs, operands, cost, after=(), scratch=(), in_spec=None, out_specs=None, aliases=None, in_after=ANY
 ):
     count = len(operands)
 
@@ -41,7 +41,7 @@
     return pl.pallas_call(
         run,
         out_shape=[jax.ShapeDtypeStruct(shape, dtype) for shape, dtype in outs],
-        in_specs=[in_spec] * count + [in_after] * len(after),
+        in_specs=(in_spec or [VMEM] * count) + [in_after] * len(after),
         out_specs=out_specs or [VMEM] * len(outs),
         scratch_shapes=list(scratch),
         input_output_aliases=aliases or {},
@@ -110,12 +110,15 @@
             out[apart, kind, i] = states[n].astype(BF16)
 
 
-def near_body(per_owner, q, k, v, g, own, extra, part_q):
+def near_body(per_owner, q, k, v, g, w, own, extra, part_q, w_here, sem):
     core, chip = place()
+    copy = pltpu.make_async_copy(w, w_here, sem)
+    copy.start()
     heads = owned(core, chip, per_owner)
     half_states(heads, q, k, v, g, own, part_q)
     for apart, i, _ in heads:
         extra[apart, i] = jnp.where(core == 0, own[apart, 0, i], own[apart, 1, i])
+    copy.wait()
 
 
 def pack(first, second):
@@ -141,8 +144,7 @@
         for kind in range(2):
             for i in range(per_owner):
                 start = (kind * per_owner + i) * size
-                total = own[apart, kind, i].astype(F32) + other[apart, kind, i].astype(F32)
-                outs[apart][start : start + size] = total.astype(BF16)
+                outs[apart][start : start + size] = own[apart, kind, i] + other[apart, kind, i]
         for pair in range(per_owner // 2):
             sums = []
             for i in (2 * pair, 2 * pair + 1):
@@ -230,13 +232,10 @@
             out[start + size : start + size + EXTRA] = diagonal.astype(BF16)
 
 
-def tail_body(which, per_owner, scale, *refs):
+def finish(which, per_owner, refs, outs):
     q, k, v, g, w, key_w, gram, part_q, part_k, part_v, near = refs[:11]
-    carried = refs[11 : 11 + GROUPS]
-    outs = refs[-9:-5]
-    here = refs[-5:-1]
-    sems = refs[-1]
-    query_here, key_here, value_here, map_here = here
+    carried = refs[11:]
+    query_here, key_here, value_here = outs
     size = gram.shape[-1]
     core, chip = place()
     half = 1 - core if which else core
@@ -249,10 +248,10 @@
             early = late = near[apart, i]
         else:
             early, late = near[apart, 0, i], near[apart, 1, i]
-        before = carried[apart][i * size : (i + 1) * size].astype(F32)
-        after = carried[apart][(per_owner + i) * size : (per_owner + i + 1) * size].astype(F32)
-        prefix.append((before + jnp.where(core == 1, early.astype(F32), 0.0)).astype(BF16))
-        suffix.append((after + jnp.where(core == 0, late.astype(F32), 0.0)).astype(BF16))
+        before = carried[apart][i * size : (i + 1) * size]
+        after = carried[apart][(per_owner + i) * size : (per_owner + i + 1) * size]
+        prefix.append(before + jnp.where(core == 1, early, jnp.zeros_like(early)))
+        suffix.append(after + jnp.where(core == 0, late, jnp.zeros_like(late)))
     raw_q = [dot_nt(g[:, at], x) for x, at in zip(prefix, ats)]
     raw_k = [dot_nt(v[:, at], x) for x, at in zip(suffix, ats)]
     raw_v = [dot_nn(key_w[which, a, i], x) for x, (a, i, _) in zip(suffix, heads)]
@@ -265,12 +264,12 @@
     for n, slot in enumerate(slots):
         query_here[:, slot] = done_q[n].astype(BF16)
         key_here[:, slot] = done_k[n].astype(BF16)
-    span = columns(half, q.shape[1] // 2)
-    copies = [
-        pltpu.make_async_copy(here[n], outs[n].at[:, span], sems.at[n]) for n in range(3)
-    ]
-    for copy in copies:
-        copy.start()
+
+
+def maps(which, per_owner, scale, w, carried, out):
+    size = w.shape[-1]
+    core, chip = place()
+    half = 1 - core if which else core
     rows, cols = triangle(size)
     for apart in range(GROUPS):
         for pair in range(per_owner // 2):
@@ -284,12 +283,34 @@
             for i, whole in ((2 * pair, first), (2 * pair + 1, second)):
                 slot = (chip ^ apart) * per_owner + i
                 head = half * (GROUPS * per_owner) + slot
-                map_here[slot] = dot_nn(whole.astype(BF16), w[head]) * scale
-    count = GROUPS * per_owner
-    copies.append(
-        pltpu.make_async_copy(map_here, outs[3].at[pl.ds(half * count, count)], sems.at[3])
-    )
-    copies[-1].start()
+                out[slot] = dot_nn(whole.astype(BF16), w[head]) * scale
+
+
+def tail_near_body(per_owner, scale, *refs):
+    operands, outs = refs[: 11 + GROUPS], refs[11 + GROUPS :]
+    maps(0, per_owner, scale, operands[4], operands[11:], outs[3])
+    finish(0, per_owner, operands, outs[:3])
+
+
+def tail_far_body(per_owner, scale, *refs):
+    operands, near = refs[: 11 + GROUPS], refs[11 + GROUPS : 15 + GROUPS]
+    outs, here, sems = refs[-9:-5], refs[-5:-1], refs[-1]
+    core, _ = place()
+    width = here[0].shape[1]
+    count = here[3].shape[0]
+    copies = []
+
+    def leave(n, half, source):
+        to = outs[n].at[pl.ds(half * count, count)] if n == 3 else outs[n].at[:, columns(half, width)]
+        copies.append(pltpu.make_async_copy(source, to, sems.at[len(copies)]))
+        copies[-1].start()
+
+    for n in range(4):
+        leave(n, core, near[n])
+    maps(1, per_owner, scale, operands[4], operands[11:], here[3])
+    finish(1, per_owner, operands, here[:3])
+    for n in range(4):
+        leave(n, 1 - core, here[n])
     for copy in copies:
         copy.wait()
 
@@ -316,12 +337,17 @@
         [((rows, width), BF16)] * 4 + [(triple, BF16), (one, F32)],
         [pltpu.with_memory_space_constraint(x, pltpu.HBM) for x in (q, k, v, g)],
         2.0,
-        in_spec=HBM,
+        in_spec=[HBM] * 4,
         scratch=[pltpu.SemaphoreType.DMA((2, 4))],
     )
     other = swap(send, 1)
-    own, extra, part_q0 = call(
-        bind(near_body, per_owner), [(triple, BF16), (one, BF16), (one, F32)], here, 1.0
+    own, extra, part_q0, w = call(
+        bind(near_body, per_owner),
+        [(triple, BF16), (one, BF16), (one, F32), (w.shape, BF16)],
+        (*here, pltpu.with_memory_space_constraint(w, pltpu.HBM)),
+        1.0,
+        in_spec=[VMEM] * 4 + [HBM],
+        scratch=[pltpu.SemaphoreType.DMA],
     )
     chip_sums = call(bind(join_body, per_owner), [(payload, BF16)] * GROUPS, (own, other), 0.5)
     locals_ = [(twice, F32), (twice, F32), (twice, BF16), (twice, BF16)]
@@ -347,24 +373,27 @@
     )
     near = [carried[0]] + [swap(carried[j], 2 * j) for j in range(1, GROUPS)]
     far = [swap(x, 1) for x in near]
+    scale = 1.0 / math.sqrt(length)
     outs = [((rows, width), BF16)] * 3 + [((heads,) + block, F32)]
-    scale = 1.0 / math.sqrt(length)
-
-    def tail(which, part_q, other_states, payloads, before):
-        return call(
-            bind(tail_body, which, per_owner, scale),
+    halves = [((rows, width // 2), BF16)] * 3 + [((heads // 2,) + block, F32)]
+    shared = (*here, w, key_w, gram)
+    near_half = call(
+        bind(tail_near_body, per_owner, scale),
+        halves,
+        (*shared, part_q0, part_k, part_v, other, *near),
+        1.0,
+    )
+    return tuple(
+        call(
+            bind(tail_far_body, per_owner, scale),
             outs,
-            (*here, w, key_w, gram, part_q, part_k, part_v, other_states, *payloads),
-            1.6,
-            after=before,
-            scratch=[pltpu.VMEM((rows, width // 2), BF16)] * 3
-            + [pltpu.VMEM((heads // 2,) + block, F32), pltpu.SemaphoreType.DMA((4,))],
+            (*shared, part_q1, part_k, part_v, extra, *far, *near_half),
+            2.0,
+            scratch=[pltpu.VMEM(shape, dtype) for shape, dtype in halves]
+            + [pltpu.SemaphoreType.DMA((8,))],
             out_specs=[HBM] * 4,
-            aliases={11 + GROUPS + n: n for n in range(len(before))},
         )
-
-    first = tail(0, part_q0, other, near, ())
-    return tuple(tail(1, part_q1, extra, far, tuple(first)))
+    )
 
 
 def gathered(q, k, v, g, w):

time: 31.6 us -> 31 us (0.981)
  local copies, waits for them, and re-layouts: 0.51 us -> 0 us
    unnamed x2 -> x0, local copies, waits for them, and re-layouts: 0.51 us -> none
  transfers between devices with their start and end apart: 12 -> 12, of which waited for: 6 -> 7; matrix products, arithmetic and copies ran while one was open for 0% -> 0% of each run, Pallas kernels for 8% -> 8%
where the time goes in v5:
time: 31 us; the launch traced here: 30.9 us
  waiting for transfers between devices  11.6 us (37%)
  Pallas kernels  9.46 us (31%)
  starting transfers between devices  9.07 us (29%)
  between operations  0.71 us (2%)
    ppermute x12, waiting for transfers between devices, swap(): return lax.ppermute(x, 'ctx', [(i, i ^ apart) for i in range(count)])  11.6 us
    pallas_call x8, Pallas kernels, call(): pl.pallas_call(run, out_shape=[jax.ShapeDtypeStruct(shape, dtype) for sha...  9.46 us
    ppermute x12, starting transfers between devices, swap(): return lax.ppermute(x, 'ctx', [(i, i ^ apart) for i in range(count)])  9.07 us
  transfers between devices with their start and end apart: 12, of which 7 were waited for; matrix products, arithmetic and copies ran while one was open for 0% of the time, Pallas kernels for 8%

profile of v5, /device:TPU:0, one launch (start us, length us, event | category | flops | bytes accessed | tf_op | source)
XLA Modules:
  0.0 30.9 jit_solution(5429596945313876177)
XLA Ops:
  0.6 2.0 %shard_map.84 = (bf16[128,2048]{1,0:T(8,128)(2,1)S(1)}, bf16[128,2048]{1,0:T(8,128)(2,1)S(1)}, bf16[128,2048]{1,0:T(8,128)(2,1)S(1)}, bf16[128,2048]{1,0:T(8,128...) custom-call(bf16[128,2048]{1,0:T(8,128)(2,1)} %refs_0_.1, ...), custom_call_target="tpu_custom_call" | custom-call | flops 2300000000 | tf_op jit(solution)/shard_map/pallas_call | solution.py:41
  2.6 0.5 %collective-permute-start = (bf16[4,3,2,128,128]{4,3,2,1,0:T(8,128)(2,1)S(1)}, bf16[4,3,2,128,128]{4,3,2,1,0:T(8,128)(2,1)S(1)}, u32[]{:S(2)}, u32[]{:S(2)}) collective-permute-start(bf16[4,3,2,128,128]{4,3,2,1,0:T(8,128)(2,1)S(1)} %get-tuple-element.45), channel_id=1, source_target_pairs={{0,1},{1,0},{2,3},{3,2},{4,5},{5,4},{6,7},{7,6},{8,9},{9,8},{10,11... | collective-permute-start | bytes 2359304 | tf_op jit(solution)/shard_map/ppermute | solution.py:320
  3.1 1.4 %shard_map.85 = (bf16[4,3,2,128,128]{4,3,2,1,0:T(8,128)(2,1)S(1)}, bf16[4,2,128,128]{3,2,1,0:T(8,128)(2,1)S(1)}, f32[4,2,128,128]{3,2,1,0:T(8,128)S(1)}, bf16[16,128,128]{2,1,0:T(8,128)(2,1)S(1)}) custom-call(bf16[128,2048]{1,0:T(8,128)(2,1)S(1)} %get-tuple-element.39.refs_0_, bf16[128,2048]{1,0:T(8,128)(2,1)S(1)} %get-tuple-element.40.refs_1_, ...), custom_call_target="tpu_custom_call" | custom-call | flops 1150000000 | tf_op jit(solution)/shard_map/pallas_call | solution.py:41
  4.6 0.5 %collective-permute-done.refs_1_.refs_10_ = bf16[4,3,2,128,128]{4,3,2,1,0:T(8,128)(2,1)S(1)} collective-permute-done((bf16[4,3,2,128,128]{4,3,2,1,0:T(8,128)(2,1)S(1)}, bf16[4,3,2,128,128]{4,3,2,1,0:T(8,128)(2,1)S(1)}, u32[]{:S(2)}, u32[]{:S(2)}) %collective-permute-start) | collective-permute-done | bytes 786464 | tf_op jit(solution)/shard_map/ppermute | solution.py:320
  5.0 0.5 %shard_map.86 = (bf16[656,128]{1,0:T(8,128)(2,1)S(1)}, bf16[656,128]{1,0:T(8,128)(2,1)S(1)}, bf16[656,128]{1,0:T(8,128)(2,1)S(1)}, bf16[656,128]{1,0:T(8,128)(2,1)S(1)}) custom-call(bf16[4,3,2,128,128]{4,3,2,1,0:T(8,128)(2,1)S(1)} %get-tuple-element.44.refs_0_, bf16[4,3,2,128,128]{4,3,2,1,0:T(8,128)(2,1)S(1)} %collective-permute-done.refs_1_.refs_10_), custom_call_target="tpu_custom_call" | custom-call | flops 575000000 | tf_op jit(solution)/shard_map/pallas_call | solution.py:41
  5.5 1.8 %shard_map.87 = (f32[2,4,2,128,128]{4,3,2,1,0:T(8,128)S(1)}, f32[2,4,2,128,128]{4,3,2,1,0:T(8,128)S(1)}, bf16[2,4,2,128,128]{4,3,2,1,0:T(8,128)(2,1)S(1)}, bf16[2,4,2,128,128]{4,3,2,1,0:T(8,128)(2,1)S(1)}) custom-call(bf16[128,2048]{1,0:T(8,128)(2,1)S(1)} %get-tuple-element.39.refs_0_, bf16[128,2048]{1,0:T(8,128)(2,1)S(1)} %get-tuple-element.40.refs_1_, ...), custom_call_target="tpu_custom_call" | custom-call | flops 2070000000 | tf_op jit(solution)/shard_map/pallas_call | solution.py:41
  7.4 2.9 %collective-permute-start.2 = (bf16[656,128]{1,0:T(8,128)(2,1)S(1)}, bf16[656,128]{1,0:T(8,128)(2,1)S(1)}, u32[]{:S(2)}, u32[]{:S(2)}) collective-permute-start(bf16[656,128]{1,0:T(8,128)(2,1)S(1)} %get-tuple-element.62), channel_id=1, source_target_pairs={{0,2},{1,3},{2,0},{3,1},{4,6},{5,7},{6,4},{7,5},{8,10},{9,11},{10,... | collective-permute-start | bytes 503816 | tf_op jit(solution)/shard_map/ppermute | solution.py:320
  10.3 1.5 %collective-permute-start.3 = (bf16[656,128]{1,0:T(8,128)(2,1)S(1)}, bf16[656,128]{1,0:T(8,128)(2,1)S(1)}, u32[]{:S(2)}, u32[]{:S(2)}) collective-permute-start(bf16[656,128]{1,0:T(8,128)(2,1)S(1)} %get-tuple-element.63), channel_id=1, source_target_pairs={{0,4},{1,5},{2,6},{3,7},{4,0},{5,1},{6,2},{7,3},{8,12},{9,13},{10,... | collective-permute-start | bytes 503816 | tf_op jit(solution)/shard_map/ppermute | solution.py:320
  11.8 0.0 collective-permute-start.4
  11.8 3.3 %collective-permute-done.2.refs_1_ = bf16[656,128]{1,0:T(8,128)(2,1)S(1)} collective-permute-done((bf16[656,128]{1,0:T(8,128)(2,1)S(1)}, bf16[656,128]{1,0:T(8,128)(2,1)S(1)}, u32[]{:S(2)}, u32[]{:S(2)}) %collective-permute-start.2) | collective-permute-done | bytes 167968 | tf_op jit(solution)/shard_map/ppermute | solution.py:320
  15.1 3.6 %collective-permute-done.3.refs_2_ = bf16[656,128]{1,0:T(8,128)(2,1)S(1)} collective-permute-done((bf16[656,128]{1,0:T(8,128)(2,1)S(1)}, bf16[656,128]{1,0:T(8,128)(2,1)S(1)}, u32[]{:S(2)}, u32[]{:S(2)}) %collective-permute-start.3) | collective-permute-done | bytes 167968 | tf_op jit(solution)/shard_map/ppermute | solution.py:320
  18.7 0.0 collective-permute-done.4.refs_3_
  18.7 0.5 %shard_map.89 = (bf16[656,128]{1,0:T(8,128)(2,1)S(1)}, bf16[656,128]{1,0:T(8,128)(2,1)S(1)}, bf16[656,128]{1,0:T(8,128)(2,1)S(1)}, bf16[656,128]{1,0:T(8,128)(2,1)S(1)}) custom-call(bf16[656,128]{1,0:T(8,128)(2,1)S(1)} %get-tuple-element.61.refs_5_.refs_0_, bf16[656,128]{1,0:T(8,128)(2,1)S(1)} %collective-permute-done.2.refs_1_, ...), custom_call_target="tpu_custom_call" | custom-call | flops 575000000 | tf_op jit(solution)/shard_map/pallas_call | solution.py:41
  19.3 0.7 %collective-permute-start.6 = (bf16[656,128]{1,0:T(8,128)(2,1)S(1)}, bf16[656,128]{1,0:T(8,128)(2,1)S(1)}, u32[]{:S(2)}, u32[]{:S(2)}) collective-permute-start(bf16[656,128]{1,0:T(8,128)(2,1)S(1)} %get-tuple-element.66), channel_id=1, source_target_pairs={{0,2},{1,3},{2,0},{3,1},{4,6},{5,7},{6,4},{7,5},{8,10},{9,11},{10,... | collective-permute-start | bytes 503816 | tf_op jit(solution)/shard_map/ppermute | solution.py:320
  20.0 0.8 %collective-permute-start.8 = (bf16[656,128]{1,0:T(8,128)(2,1)S(1)}, bf16[656,128]{1,0:T(8,128)(2,1)S(1)}, u32[]{:S(2)}, u32[]{:S(2)}) collective-permute-start(bf16[656,128]{1,0:T(8,128)(2,1)S(1)} %get-tuple-element.67), channel_id=1, source_target_pairs={{0,4},{1,5},{2,6},{3,7},{4,0},{5,1},{6,2},{7,3},{8,12},{9,13},{10,... | collective-permute-start | bytes 503816 | tf_op jit(solution)/shard_map/ppermute | solution.py:320
  20.8 2.0 %collective-permute-start.10 = (bf16[656,128]{1,0:T(8,128)(2,1)S(1)}, bf16[656,128]{1,0:T(8,128)(2,1)S(1)}, u32[]{:S(2)}, u32[]{:S(2)}) collective-permute-start(bf16[656,128]{1,0:T(8,128)(2,1)S(1)} %get-tuple-element.68), channel_id=1, source_target_pairs={{0,6},{1,7},{2,4},{3,5},{4,2},{5,3},{6,0},{7,1},{8,14},{9,15},{10,... | collective-permute-start | bytes 503816 | tf_op jit(solution)/shard_map/ppermute | solution.py:320
  22.8 0.0 collective-permute-start.1
  22.8 0.5 %collective-permute-start.5 = (bf16[656,128]{1,0:T(8,128)(2,1)S(1)}, bf16[656,128]{1,0:T(8,128)(2,1)S(1)}, u32[]{:S(2)}, u32[]{:S(2)}) collective-permute-start(bf16[656,128]{1,0:T(8,128)(2,1)S(1)} %get-tuple-element.65.refs_11_), channel_id=1, source_target_pairs={{0,1},{1,0},{2,3},{3,2},{4,5},{5,4},{6,7},{7,6},{8,9},{9,8},{10,11... | collective-permute-start | bytes 503816 | tf_op jit(solution)/shard_map/ppermute | solution.py:320
  23.3 1.5 %collective-permute-done.6.refs_12_ = bf16[656,128]{1,0:T(8,128)(2,1)S(1)} collective-permute-done((bf16[656,128]{1,0:T(8,128)(2,1)S(1)}, bf16[656,128]{1,0:T(8,128)(2,1)S(1)}, u32[]{:S(2)}, u32[]{:S(2)}) %collective-permute-start.6) | collective-permute-done | bytes 167968 | tf_op jit(solution)/shard_map/ppermute | solution.py:320
  24.9 0.0 collective-permute-start.7
  24.9 0.5 %collective-permute-done.8.refs_13_ = bf16[656,128]{1,0:T(8,128)(2,1)S(1)} collective-permute-done((bf16[656,128]{1,0:T(8,128)(2,1)S(1)}, bf16[656,128]{1,0:T(8,128)(2,1)S(1)}, u32[]{:S(2)}, u32[]{:S(2)}) %collective-permute-start.8) | collective-permute-done | bytes 167968 | tf_op jit(solution)/shard_map/ppermute | solution.py:320
  25.3 0.0 collective-permute-start.9
  25.4 1.8 %collective-permute-done.10.refs_14_ = bf16[656,128]{1,0:T(8,128)(2,1)S(1)} collective-permute-done((bf16[656,128]{1,0:T(8,128)(2,1)S(1)}, bf16[656,128]{1,0:T(8,128)(2,1)S(1)}, u32[]{:S(2)}, u32[]{:S(2)}) %collective-permute-start.10) | collective-permute-done | bytes 167968 | tf_op jit(solution)/shard_map/ppermute | solution.py:320
  27.1 0.0 collective-permute-start.11
  27.1 0.9 %shard_map.90 = (bf16[128,1024]{1,0:T(8,128)(2,1)S(1)}, bf16[128,1024]{1,0:T(8,128)(2,1)S(1)}, bf16[128,1024]{1,0:T(8,128)(2,1)S(1)}, f32[8,128,128]{2,1,0:T(8,128)S(1)}) custom-call(bf16[128,2048]{1,0:T(8,128)(2,1)S(1)} %get-tuple-element.39.refs_0_, bf16[128,2048]{1,0:T(8,128)(2,1)S(1)} %get-tuple-element.40.refs_1_, ...), custom_call_target="tpu_custom_call" | custom-call | flops 1150000000 | tf_op jit(solution)/shard_map/pallas_call | solution.py:41
  28.1 0.0 collective-permute-done.1.refs_10_
  28.1 0.0 collective-permute-done.5.refs_11_
  28.1 0.0 collective-permute-done.7.refs_12_
  28.1 0.0 collective-permute-done.9.refs_13_
  28.1 0.4 %collective-permute-done.11.refs_14_ = bf16[656,128]{1,0:T(8,128)(2,1)S(1)} collective-permute-done((bf16[656,128]{1,0:T(8,128)(2,1)S(1)}, bf16[656,128]{1,0:T(8,128)(2,1)S(1)}, u32[]{:S(2)}, u32[]{:S(2)}) %collective-permute-start.11) | collective-permute-done | bytes 167968 | tf_op jit(solution)/shard_map/ppermute | solution.py:320
  28.5 2.3 %shard_map.91 = (bf16[128,2048]{1,0:T(8,128)(2,1)}, bf16[128,2048]{1,0:T(8,128)(2,1)}, bf16[128,2048]{1,0:T(8,128)(2,1)}, f32[16,128,128]{2,1,0:T(8,128)}) custom-call(bf16[128,2048]{1,0:T(8,128)(2,1)S(1)} %get-tuple-element.39.refs_0_, bf16[128,2048]{1,0:T(8,128)(2,1)S(1)} %get-tuple-element.40.refs_1_, bf16[128,2048]{1,0:T(8,128)(2,1)S(1)} %get-tuple-element.41.refs_2_, ...), custom_call_target="tpu_custom_call" | custom-call | flops 2300000000 | tf_op jit(solution)/shard_map/pallas_call | solution.py:41
  (1 shorter events, 0.0 us)
Async XLA Ops:
  2.6 2.4 %collective-permute-start = (bf16[4,3,2,128,128]{4,3,2,1,0:T(8,128)(2,1)S(1)}, bf16[4,3,2,128,128]{4,3,2,1,0:T(8,128)(2,1)S(1)}, u32[]{:S(2)}, u32[]{:S(2)}) collective-permute-start(bf16[4,3,2,128,128]{4,3,2,1,0:T(8,128)(2,1)S(1)} %get-tuple-element.45), channel_id=1, source_target_pairs={{0,1},{1,0},{2,3},{3,2},{4,5},{5,4},{6,7},{7,6},{8,9},{9,8},{10,11... | collective-permute-start | bytes 2359304 | tf_op jit(solution)/shard_map/ppermute | solution.py:320
  7.4 7.8 %collective-permute-start.2 = (bf16[656,128]{1,0:T(8,128)(2,1)S(1)}, bf16[656,128]{1,0:T(8,128)(2,1)S(1)}, u32[]{:S(2)}, u32[]{:S(2)}) collective-permute-start(bf16[656,128]{1,0:T(8,128)(2,1)S(1)} %get-tuple-element.62), channel_id=1, source_target_pairs={{0,2},{1,3},{2,0},{3,1},{4,6},{5,7},{6,4},{7,5},{8,10},{9,11},{10,... | collective-permute-start | bytes 503816 | tf_op jit(solution)/shard_map/ppermute | solution.py:320
  10.3 8.5 %collective-permute-start.3 = (bf16[656,128]{1,0:T(8,128)(2,1)S(1)}, bf16[656,128]{1,0:T(8,128)(2,1)S(1)}, u32[]{:S(2)}, u32[]{:S(2)}) collective-permute-start(bf16[656,128]{1,0:T(8,128)(2,1)S(1)} %get-tuple-element.63), channel_id=1, source_target_pairs={{0,4},{1,5},{2,6},{3,7},{4,0},{5,1},{6,2},{7,3},{8,12},{9,13},{10,... | collective-permute-start | bytes 503816 | tf_op jit(solution)/shard_map/ppermute | solution.py:320
  11.8 7.0 %collective-permute-start.4 = (bf16[656,128]{1,0:T(8,128)(2,1)S(1)}, bf16[656,128]{1,0:T(8,128)(2,1)S(1)}, u32[]{:S(2)}, u32[]{:S(2)}) collective-permute-start(bf16[656,128]{1,0:T(8,128)(2,1)S(1)} %get-tuple-element.64), channel_id=1, source_target_pairs={{0,6},{1,7},{2,4},{3,5},{4,2},{5,3},{6,0},{7,1},{8,14},{9,15},{10,... | collective-permute-start | bytes 503816 | tf_op jit(solution)/shard_map/ppermute | solution.py:320
  19.3 5.6 %collective-permute-start.6 = (bf16[656,128]{1,0:T(8,128)(2,1)S(1)}, bf16[656,128]{1,0:T(8,128)(2,1)S(1)}, u32[]{:S(2)}, u32[]{:S(2)}) collective-permute-start(bf16[656,128]{1,0:T(8,128)(2,1)S(1)} %get-tuple-element.66), channel_id=1, source_target_pairs={{0,2},{1,3},{2,0},{3,1},{4,6},{5,7},{6,4},{7,5},{8,10},{9,11},{10,... | collective-permute-start | bytes 503816 | tf_op jit(solution)/shard_map/ppermute | solution.py:320
  20.0 5.4 %collective-permute-start.8 = (bf16[656,128]{1,0:T(8,128)(2,1)S(1)}, bf16[656,128]{1,0:T(8,128)(2,1)S(1)}, u32[]{:S(2)}, u32[]{:S(2)}) collective-permute-start(bf16[656,128]{1,0:T(8,128)(2,1)S(1)} %get-tuple-element.67), channel_id=1, source_target_pairs={{0,4},{1,5},{2,6},{3,7},{4,0},{5,1},{6,2},{7,3},{8,12},{9,13},{10,... | collective-permute-start | bytes 503816 | tf_op jit(solution)/shard_map/ppermute | solution.py:320
  20.8 6.3 %collective-permute-start.10 = (bf16[656,128]{1,0:T(8,128)(2,1)S(1)}, bf16[656,128]{1,0:T(8,128)(2,1)S(1)}, u32[]{:S(2)}, u32[]{:S(2)}) collective-permute-start(bf16[656,128]{1,0:T(8,128)(2,1)S(1)} %get-tuple-element.68), channel_id=1, source_target_pairs={{0,6},{1,7},{2,4},{3,5},{4,2},{5,3},{6,0},{7,1},{8,14},{9,15},{10,... | collective-permute-start | bytes 503816 | tf_op jit(solution)/shard_map/ppermute | solution.py:320
  22.8 5.2 %collective-permute-start.1 = (bf16[4,2,128,128]{3,2,1,0:T(8,128)(2,1)S(1)}, bf16[4,2,128,128]{3,2,1,0:T(8,128)(2,1)S(1)}, u32[]{:S(2)}, u32[]{:S(2)}) collective-permute-start(bf16[4,2,128,128]{3,2,1,0:T(8,128)(2,1)S(1)} %get-tuple-element.60), channel_id=1, source_target_pairs={{0,1},{1,0},{2,3},{3,2},{4,5},{5,4},{6,7},{7,6},{8,9},{9,8},{10,11... | collective-permute-start | bytes 786440 | tf_op jit(solution)/shard_map/ppermute | solution.py:320
  22.8 5.2 %collective-permute-start.5 = (bf16[656,128]{1,0:T(8,128)(2,1)S(1)}, bf16[656,128]{1,0:T(8,128)(2,1)S(1)}, u32[]{:S(2)}, u32[]{:S(2)}) collective-permute-start(bf16[656,128]{1,0:T(8,128)(2,1)S(1)} %get-tuple-element.65.refs_11_), channel_id=1, source_target_pairs={{0,1},{1,0},{2,3},{3,2},{4,5},{5,4},{6,7},{7,6},{8,9},{9,8},{10,11... | collective-permute-start | bytes 503816 | tf_op jit(solution)/shard_map/ppermute | solution.py:320
  24.9 3.2 %collective-permute-start.7 = (bf16[656,128]{1,0:T(8,128)(2,1)S(1)}, bf16[656,128]{1,0:T(8,128)(2,1)S(1)}, u32[]{:S(2)}, u32[]{:S(2)}) collective-permute-start(bf16[656,128]{1,0:T(8,128)(2,1)S(1)} %collective-permute-done.6.refs_12_), channel_id=1, source_target_pairs={{0,1},{1,0},{2,3},{3,2},{4,5},{5,4},{6,7},{7,6},{8,9},{9,8},{10,11... | collective-permute-start | bytes 503816 | tf_op jit(solution)/shard_map/ppermute | solution.py:320
  25.3 2.7 %collective-permute-start.9 = (bf16[656,128]{1,0:T(8,128)(2,1)S(1)}, bf16[656,128]{1,0:T(8,128)(2,1)S(1)}, u32[]{:S(2)}, u32[]{:S(2)}) collective-permute-start(bf16[656,128]{1,0:T(8,128)(2,1)S(1)} %collective-permute-done.8.refs_13_), channel_id=1, source_target_pairs={{0,1},{1,0},{2,3},{3,2},{4,5},{5,4},{6,7},{7,6},{8,9},{9,8},{10,11... | collective-permute-start | bytes 503816 | tf_op jit(solution)/shard_map/ppermute | solution.py:320
  27.1 1.4 %collective-permute-start.11 = (bf16[656,128]{1,0:T(8,128)(2,1)S(1)}, bf16[656,128]{1,0:T(8,128)(2,1)S(1)}, u32[]{:S(2)}, u32[]{:S(2)}) collective-permute-start(bf16[656,128]{1,0:T(8,128)(2,1)S(1)} %collective-permute-done.10.refs_14_), channel_id=1, source_target_pairs={{0,1},{1,0},{2,3},{3,2},{4,5},{5,4},{6,7},{7,6},{8,9},{9,8},{10,11... | collective-permute-start | bytes 503816 | tf_op jit(solution)/shard_map/ppermute | solution.py:320

commit v6 on v4

v6 whole, which is shorter than its diff:
```python
import functools
import math

import jax
import jax.numpy as jnp
from jax import lax
from jax.experimental import pallas as pl
from jax.experimental.pallas import tpu as pltpu
from jax.sharding import PartitionSpec as P

F32 = jnp.float32
BF16 = jnp.bfloat16
VMEM = pl.BlockSpec(memory_space=pltpu.VMEM)
HBM = pl.BlockSpec(memory_space=pltpu.HBM)
ANY = pl.BlockSpec(memory_space=pl.ANY)
GROUPS = 4
FIRST = 0
EXTRA = 16


def dot_nn(a, b):
    return lax.dot_general(a, b, (((1,), (0,)), ((), ())), preferred_element_type=F32)


def dot_nt(a, b):
    return lax.dot_general(a, b, (((1,), (1,)), ((), ())), preferred_element_type=F32)


def dot_tn(a, b):
    return lax.dot_general(a, b, (((0,), (0,)), ((), ())), preferred_element_type=F32)


def call(
    body, outs, operands, cost, after=(), scratch=(), in_spec=None, out_specs=None, aliases=None, in_after=ANY
):
    count = len(operands)

    def run(*refs):
        return body(*refs[:count], *refs[count + len(after) :])

    return pl.pallas_call(
        run,
        out_shape=[jax.ShapeDtypeStruct(shape, dtype) for shape, dtype in outs],
        in_specs=(in_spec or [VMEM] * count) + [in_after] * len(after),
        out_specs=out_specs or [VMEM] * len(outs),
        scratch_shapes=list(scratch),
        input_output_aliases=aliases or {},
        cost_estimate=pl.CostEstimate(
            flops=int(cost * 1.15e9), bytes_accessed=0, transcendentals=0
        ),
        compiler_params=pltpu.CompilerParams(vmem_limit_bytes=16 * 2**20),
    )(*operands, *after)


def place():
    me = lax.axis_index("ctx")
    return lax.rem(me, 2), lax.div(me, 2)


def owned(half, chip, per_owner):
    base = half * (GROUPS * per_owner)
    return [
        (apart, i, base + (chip ^ apart) * per_owner + i)
        for apart in range(GROUPS)
        for i in range(per_owner)
    ]


def columns(head, size):
    return pl.ds(pl.multiple_of(head * size, size), size)


def triangle(size):
    rows = lax.broadcasted_iota(jnp.int32, (size, size), 0)
    cols = lax.broadcasted_iota(jnp.int32, (size, size), 1)
    return rows, cols


def load_body(per_owner, q, k, v, g, w, q_here, k_here, v_here, g_here, w_here, send, part_q, sems):
    half_width = q.shape[1] // 2
    core, chip = place()
    pairs = ((k, k_here), (v, v_here), (q, q_here), (g, g_here))
    copies = []
    for turn, half in enumerate((1 - core, core)):
        at = columns(half, half_width)
        for n, (source, target) in enumerate(pairs):
            copies.append(
                pltpu.make_async_copy(source.at[:, at], target.at[:, at], sems.at[turn, n])
            )
    copies.append(pltpu.make_async_copy(w, w_here, sems.at[2, 0]))
    for copy in copies:
        copy.start()
    for copy in copies[:4]:
        copy.wait()
    states(send, part_q, owned(1 - core, chip, per_owner), q_here, k_here, v_here, g_here)
    for copy in copies[4:]:
        copy.wait()


def states(out, part_q, heads, q, k, v, g):
    size = out.shape[-1]
    per_owner = len(heads) // GROUPS
    rows, cols = triangle(q.shape[0])
    ats = [columns(head, size) for _, _, head in heads]
    mixing = [dot_nt(g[:, at], v[:, at]) for at in ats]
    early = [dot_tn(k[:, at], v[:, at]) for at in ats]
    mixing = [jnp.where(rows >= cols, x, 0.0).astype(BF16) for x in mixing]
    mixed = [dot_nn(x, k[:, at]) for x, at in zip(mixing, ats)]
    wide = [
        dot_tn(q[:, at], jnp.concatenate([g[:, at], x.astype(BF16)], axis=1))
        for x, at in zip(mixed, ats)
    ]
    for n, (apart, i, _) in enumerate(heads):
        part_q[apart, i] = mixed[n]
        out[apart, i * size : (i + 1) * size] = early[n].astype(BF16)
        out[apart, (per_owner + i) * size : (per_owner + i + 1) * size] = wide[n][:, :size].astype(BF16)
        if i % 2:
            both, diagonal = pack(wide[n - 1][:, size:], wide[n][:, size:])
            start = 2 * per_owner * size + (i // 2) * (size + EXTRA)
            out[apart, start : start + size] = both.astype(BF16)
            out[apart, start + size : start + size + EXTRA] = diagonal.astype(BF16)


def near_body(per_owner, q, k, v, g, own, extra, part_q):
    size = own.shape[-1]
    core, chip = place()
    heads = owned(core, chip, per_owner)
    states(own, part_q, heads, q, k, v, g)
    for apart in range(GROUPS):
        early = own[apart, : per_owner * size]
        late = own[apart, per_owner * size : 2 * per_owner * size]
        extra[apart] = jnp.where(core == 0, early, late)


def pack(first, second):
    size = first.shape[0]
    rows, cols = triangle(size)
    both = jnp.where(rows >= cols, first, second)
    both += jnp.where(rows <= cols, first, second).T
    diagonal = 2.0 * jnp.sum(jnp.where(rows == cols, second, 0.0), axis=0, keepdims=True)
    return both, jnp.broadcast_to(diagonal, (EXTRA, size))


def join_body(per_owner, own, other, *outs):
    size = own.shape[-1]
    count = 2 * per_owner * size
    core, _ = place()
    last = core == 1
    totals = []
    for apart in range(GROUPS):
        for i in range(per_owner):
            ahead = slice(i * size, (i + 1) * size)
            behind = slice((per_owner + i) * size, (per_owner + i + 1) * size)
            early = jnp.where(last, other[apart, ahead], own[apart, ahead])
            late = jnp.where(last, own[apart, behind], other[apart, behind])
            totals.append(dot_nt(late, early))
    for apart in range(GROUPS):
        outs[apart][:count] = own[apart, :count] + other[apart, :count]
        for pair in range(per_owner // 2):
            both, diagonal = pack(*totals[apart * per_owner + 2 * pair :][:2])
            start = count + pair * (size + EXTRA)
            for x in (own, other):
                both += x[apart, start : start + size].astype(F32)
                diagonal += x[apart, start + size : start + size + EXTRA].astype(F32)
            outs[apart][start : start + size] = both.astype(BF16)
            outs[apart][start + size : start + size + EXTRA] = diagonal.astype(BF16)


def rest_first_body(per_owner, *refs):
    core, _ = place()

    @pl.when(core == FIRST)
    def _():
        rest(per_owner, *refs)


def rest_second_body(per_owner, *refs):
    core, _ = place()

    @pl.when(core != FIRST)
    def _():
        rest(per_owner, *refs[:5], *refs[-4:])


def rest(per_owner, q, k, v, g, w, part_k, part_v, key_w, gram):
    size = w.shape[-1]
    core, chip = place()
    rows, cols = triangle(q.shape[0])
    later = cols >= rows
    for which, half in enumerate((core, 1 - core)):
        heads = owned(half, chip, per_owner)
        ats = [columns(head, size) for _, _, head in heads]
        square = [dot_nt(w[head], w[head]).astype(BF16) for _, _, head in heads]
        mixing = [dot_nt(v[:, at], g[:, at]) for at in ats]
        mixing = [jnp.where(later, x, 0.0).astype(BF16) for x in mixing]
        keyed = [dot_nn(k[:, at], x).astype(BF16) for x, at in zip(square, ats)]
        mixed = [dot_nn(x, q[:, at]) for x, at in zip(mixing, ats)]
        scores = [dot_nt(x, q[:, at]) for x, at in zip(keyed, ats)]
        scores = [jnp.where(later, x, 0.0).astype(BF16) for x in scores]
        scored = [dot_nn(x, g[:, at]) for x, at in zip(scores, ats)]
        for n, (apart, i, _) in enumerate(heads):
            gram[which, apart, i] = square[n]
            key_w[which, apart, i] = keyed[n]
            part_k[which, apart, i] = mixed[n]
            part_v[which, apart, i] = scored[n]


def owner_body(per_owner, *refs):
    parts, outs, (placed, carried) = refs[:GROUPS], refs[GROUPS : 2 * GROUPS], refs[2 * GROUPS :]
    size = outs[0].shape[-1]
    states = 2 * per_owner * size
    _, chip = place()
    for apart, part in enumerate(parts):
        placed[chip ^ apart] = part[:states]
    totals = []
    for i in range(per_owner):
        ahead = slice(i * size, (i + 1) * size)
        behind = slice((per_owner + i) * size, (per_owner + i + 1) * size)
        early = [placed[n, ahead] for n in range(GROUPS)]
        late = [placed[n, behind] for n in range(GROUPS)]
        prefix = [jnp.zeros_like(early[0])]
        suffix = [jnp.zeros_like(late[0])]
        before, after = early[0].astype(F32), late[-1].astype(F32)
        for n in range(1, GROUPS):
            prefix.append(before.astype(BF16))
            suffix.insert(0, after.astype(BF16))
            before += early[n].astype(F32)
            after += late[GROUPS - 1 - n].astype(F32)
        cross = dot_nt(late[1], prefix[1])
        for n in range(2, GROUPS):
            cross += dot_nt(late[n], prefix[n])
        totals.append(cross)
        for n in range(GROUPS):
            carried[n, ahead] = prefix[n]
            carried[n, behind] = suffix[n]
    for apart, out in enumerate(outs):
        out[:states] = carried[chip ^ apart]
    for pair in range(per_owner // 2):
        both, diagonal = pack(totals[2 * pair], totals[2 * pair + 1])
        start = states + pair * (size + EXTRA)
        for part in parts:
            both += part[start : start + size].astype(F32)
            diagonal += part[start + size : start + size + EXTRA].astype(F32)
        for out in outs:
            out[start : start + size] = both.astype(BF16)
            out[start + size : start + size + EXTRA] = diagonal.astype(BF16)


def finish(pieces, per_owner, scale, shared, sources, outs):
    g, v, w, key_w, gram, part_q, part_k, part_v, other, extra = shared
    size = gram.shape[-1]
    core, chip = place()
    heads = []
    for piece, (which, apart) in enumerate(pieces):
        half = 1 - core if which else core
        for i in range(per_owner):
            index = piece * per_owner + i
            head = (half * GROUPS + (chip ^ apart)) * per_owner + i
            heads.append((which, apart, i, sources[piece], head, slice(index * size, (index + 1) * size)))
    ats = [columns(head[4], size) for head in heads]
    prefix, suffix = [], []
    for which, apart, i, source, *_ in heads:
        ahead = slice(i * size, (i + 1) * size)
        behind = slice((per_owner + i) * size, (per_owner + i + 1) * size)
        if which:
            early = late = extra[apart, ahead]
        else:
            early, late = other[apart, ahead], other[apart, behind]
        before, after = source[ahead], source[behind]
        prefix.append(before + jnp.where(core == 1, early, jnp.zeros_like(early)))
        suffix.append(after + jnp.where(core == 0, late, jnp.zeros_like(late)))
    raw_q = [dot_nt(g[:, at], x) for x, at in zip(prefix, ats)]
    raw_k = [dot_nt(v[:, at], x) for x, at in zip(suffix, ats)]
    raw_v = [dot_nn(key_w[h, a, i], x) for x, (h, a, i, *_) in zip(suffix, heads)]
    raw_q = [(part_q[h][a, i] + x).astype(BF16) for x, (h, a, i, *_) in zip(raw_q, heads)]
    raw_k = [(part_k[h, a, i] + x).astype(BF16) for x, (h, a, i, *_) in zip(raw_k, heads)]
    for x, (h, a, i, _, _, to) in zip(raw_v, heads):
        outs[2][:, to] = (part_v[h, a, i] + x).astype(BF16)
    done_q = [dot_nn(x, gram[h, a, i]) for x, (h, a, i, *_) in zip(raw_q, heads)]
    done_k = [dot_nn(x, gram[h, a, i]) for x, (h, a, i, *_) in zip(raw_k, heads)]
    for x, y, (*_, to) in zip(done_q, done_k, heads):
        outs[0][:, to] = x.astype(BF16)
        outs[1][:, to] = y.astype(BF16)
    rows, cols = triangle(size)
    for piece, source in enumerate(sources):
        for pair in range(per_owner // 2):
            start = 2 * per_owner * size + pair * (size + EXTRA)
            both = source[start : start + size].astype(F32)
            diagonal = source[start + size : start + size + EXTRA][:1].astype(F32)
            turned = both.T
            first = jnp.where(rows >= cols, both, turned)
            second = jnp.where(rows < cols, both, turned)
            second = jnp.where(rows == cols, diagonal, second)
            for i, whole in ((2 * pair, first), (2 * pair + 1, second)):
                index = piece * per_owner + i
                outs[3][index] = dot_nn(whole.astype(BF16), w[heads[index][4]]) * scale


def leave(pieces, per_owner, here, outs, sems):
    core, chip = place()
    size = here[3].shape[-1]
    copies = []
    for piece, (which, apart) in enumerate(pieces):
        half = 1 - core if which else core
        owner = half * GROUPS + (chip ^ apart)
        at = pl.ds(piece * per_owner * size, per_owner * size)
        ends = [(here[n].at[:, at], outs[n].at[:, columns(owner, per_owner * size)]) for n in range(3)]
        at = pl.ds(piece * per_owner, per_owner)
        ends.append((here[3].at[at], outs[3].at[pl.ds(owner * per_owner, per_owner)]))
        for n, (source, target) in enumerate(ends):
            copies.append(pltpu.make_async_copy(source, target, sems.at[piece, n]))
            copies[-1].start()
    return copies


def tail_body(pieces, ready, per_owner, scale, *refs):
    shared, refs = (*refs[:5], refs[5:7], *refs[7:11]), refs[11:]
    sources, refs = refs[: len(pieces)], refs[len(pieces) :]
    if ready is None:
        finish(pieces, per_owner, scale, shared, sources, refs)
        return
    outs, here, sems, ready_sems = refs[-10:-6], refs[-6:-2], refs[-2], refs[-1]
    copies = leave(ready, per_owner, refs[:4], outs, ready_sems) if ready else []
    finish(pieces, per_owner, scale, shared, sources, here)
    copies += leave(pieces, per_owner, here, outs, sems)
    for copy in copies:
        copy.wait()


def swap(x, apart):
    count = lax.axis_size("ctx")
    return lax.ppermute(x, "ctx", [(i, i ^ apart) for i in range(count)])


def paired(q, k, v, g, w):
    rows, width = q.shape
    heads, size = w.shape[0], w.shape[-1]
    per_owner = heads // (2 * GROUPS)
    length = rows * lax.axis_size("ctx")
    block = (size, size)
    one = (GROUPS, per_owner) + block
    twice = (2,) + one
    payload = (2 * per_owner * size + (per_owner // 2) * (size + EXTRA), size)
    payloads = (GROUPS,) + payload
    bind = functools.partial

    *here, w, send, part_q1 = call(
        bind(load_body, per_owner),
        [((rows, width), BF16)] * 4 + [(w.shape, BF16), (payloads, BF16), (one, F32)],
        [pltpu.with_memory_space_constraint(x, pltpu.HBM) for x in (q, k, v, g, w)],
        2.0,
        in_spec=[HBM] * 5,
        scratch=[pltpu.SemaphoreType.DMA((3, 4))],
    )
    other = swap(send, 1)
    own, extra, part_q0 = call(
        bind(near_body, per_owner),
        [(payloads, BF16), ((GROUPS, per_owner * size, size), BF16), (one, F32)],
        here,
        1.0,
    )
    chip_sums = call(bind(join_body, per_owner), [(payload, BF16)] * GROUPS, (own, other), 0.4)
    locals_ = [(twice, F32), (twice, F32), (twice, BF16), (twice, BF16)]
    local = list(
        call(bind(rest_first_body, per_owner), locals_, (*here, w), 1.8, after=chip_sums[:1])
    )
    held = lax.optimization_barrier((*chip_sums, local[0]))
    chip_sums, local[0] = list(held[:GROUPS]), held[GROUPS]
    parts = [chip_sums[0]] + [swap(chip_sums[j], 2 * j) for j in range(1, GROUPS)]
    extra, local[0] = lax.optimization_barrier((extra, local[0]))
    extra = swap(extra, 1)
    local = call(
        bind(rest_second_body, per_owner),
        locals_,
        (*here, w),
        1.8,
        after=tuple(local),
        aliases={5 + n: n for n in range(4)},
        in_after=VMEM,
    )
    part_k, part_v, key_w, gram = local
    carried = call(
        bind(owner_body, per_owner),
        [(payload, BF16)] * GROUPS,
        parts,
        0.5,
        after=(gram,),
        scratch=[pltpu.VMEM((GROUPS, 2 * per_owner * size, size), BF16)] * 2,
    )
    near = [carried[0]] + [swap(carried[j], 2 * j) for j in range(1, GROUPS)]
    scale = 1.0 / math.sqrt(length)
    outs = [((rows, width), BF16)] * 3 + [((heads,) + block, F32)]
    shared = (here[3], here[2], w, key_w, gram, part_q0, part_q1, part_k, part_v, other)

    def tail(pieces, payloads, ready=(), done=(), before=()):
        count = len(pieces) * per_owner
        room = [((rows, count * size), BF16)] * 3 + [((count,) + block, F32)]
        operands = (*shared, extra, *payloads, *done)
        if ready is None:
            return call(bind(tail_body, pieces, None, per_owner, scale), room, operands, 0.9)
        return call(
            bind(tail_body, pieces, ready, per_owner, scale),
            outs,
            operands,
            1.2,
            after=before,
            scratch=[pltpu.VMEM(shape, dtype) for shape, dtype in room]
            + [pltpu.SemaphoreType.DMA((max(1, len(x)), 4)) for x in (pieces, ready)],
            out_specs=[HBM] * 4,
            aliases={len(operands) + n: n for n in range(len(before))},
        )

    far = [swap(x, 1) for x in near]
    middle = [(0, n) for n in range(GROUPS)] + [(1, n) for n in range(1)]
    done = tail(middle, (*near, *far[:1]), ready=None)
    last = [(1, n) for n in range(1, GROUPS)]
    return tuple(tail(last, far[1:], ready=middle, done=done))


def gathered(q, k, v, g, w):
    rows, width = q.shape
    heads, size = w.shape[0], w.shape[-1]
    count = lax.axis_size("ctx")
    me = lax.axis_index("ctx")
    q, k, v, g = (x.reshape(rows, heads, size) for x in (q, k, v, g))

    def mul(spec, a, b):
        return jnp.einsum(spec, a, b, preferred_element_type=F32)

    query_feat = mul("thd,hde->the", q, w).astype(BF16)
    key_feat = mul("thd,hde->the", k, w).astype(BF16)
    key_state = mul("the,thv->hev", key_feat, v).astype(BF16)
    grad_state = mul("the,thv->hev", query_feat, g).astype(BF16)
    index = jnp.arange(count).reshape(count, 1, 1, 1)
    keys = lax.all_gather(key_state, "ctx").astype(F32)
    prefix = jnp.sum(jnp.where(index < me, keys, 0.0), 0).astype(BF16)
    grads = lax.all_gather(grad_state, "ctx").astype(F32)
    suffix = jnp.sum(jnp.where(index > me, grads, 0.0), 0).astype(BF16)
    row, col = triangle(rows)
    causal = row >= col
    scores = jnp.where(causal, mul("the,she->hts", query_feat, key_feat), 0.0).astype(BF16)
    mixing = jnp.where(causal, mul("thv,shv->hts", g, v), 0.0).astype(BF16)
    feat_q = mul("hts,she->the", mixing, key_feat) + mul("thv,hev->the", g, prefix)
    feat_k = mul("hts,the->she", mixing, query_feat) + mul("shv,hev->she", v, suffix)
    feat_q, feat_k = feat_q.astype(BF16), feat_k.astype(BF16)
    value_grad = mul("hts,thv->shv", scores, g) + mul("she,hev->shv", key_feat, suffix)
    query_grad = mul("the,hde->thd", feat_q, w)
    key_grad = mul("the,hde->thd", feat_k, w)
    local = mul("thd,the->hde", q, feat_q) + mul("thd,the->hde", k, feat_k)
    map_grad = lax.psum(local.astype(BF16).astype(F32), "ctx") / math.sqrt(rows * count)
    flat = (rows, width)
    return (
        query_grad.reshape(flat).astype(BF16),
        key_grad.reshape(flat).astype(BF16),
        value_grad.reshape(flat).astype(BF16),
        map_grad,
    )


def per_device(queries, key_rows, values, out_grad, feature_map):
    fits = lax.axis_size("ctx") == 2 * GROUPS and feature_map.shape[0] % (4 * GROUPS) == 0
    plan = paired if fits else gathered
    return plan(queries, key_rows, values, out_grad, feature_map)


def solution(mesh):
    rows = P(("seq", "ctx"), None)
    return jax.shard_map(
        per_device,
        mesh=mesh,
        in_specs=(rows, rows, rows, rows, P()),
        out_specs=(rows, rows, rows, P("seq", None, None)),
        check_vma=False,
    )
```

time: 31.6 us -> 30.9 us (0.978)
  waiting for transfers between devices: 11.8 us -> 12.4 us
  local copies, waits for them, and re-layouts: 0.51 us -> 0 us
  starting transfers between devices: 9.05 us -> 8.57 us
    ppermute x12, waiting for transfers between devices: 11.8 us -> 12.4 us  [swap(): return lax.ppermute(x, 'ctx', [(i, i ^ apart) for i in range(count)])]
    unnamed x2 -> x0, local copies, waits for them, and re-layouts: 0.51 us -> none
    ppermute x12, starting transfers between devices: 9.05 us -> 8.57 us  [swap(): return lax.ppermute(x, 'ctx', [(i, i ^ apart) for i in range(count)])]
  transfers between devices with their start and end apart: 12 -> 12, of which waited for: 6 -> 7; matrix products, arithmetic and copies ran while one was open for 0% -> 0% of each run, Pallas kernels for 8% -> 8%
where the time goes in v6:
time: 30.9 us; the launch traced here: 30.7 us
  waiting for transfers between devices  12.4 us (40%)
  Pallas kernels  9.05 us (29%)
  starting transfers between devices  8.57 us (28%)
  between operations  0.69 us (2%)
    ppermute x12, waiting for transfers between devices, swap(): return lax.ppermute(x, 'ctx', [(i, i ^ apart) for i in range(count)])  12.4 us
    pallas_call x8, Pallas kernels, call(): pl.pallas_call(run, out_shape=[jax.ShapeDtypeStruct(shape, dtype) for sha...  9.05 us
    ppermute x12, starting transfers between devices, swap(): return lax.ppermute(x, 'ctx', [(i, i ^ apart) for i in range(count)])  8.57 us
  transfers between devices with their start and end apart: 12, of which 7 were waited for; matrix products, arithmetic and copies ran while one was open for 0% of the time, Pallas kernels for 8%

profile of v6, /device:TPU:0, one launch (start us, length us, event | category | flops | bytes accessed | tf_op | source)
XLA Modules:
  0.0 30.7 jit_solution(509378618427467336)
XLA Ops:
  0.6 2.1 %shard_map.84 = (bf16[128,2048]{1,0:T(8,128)(2,1)S(1)}, bf16[128,2048]{1,0:T(8,128)(2,1)S(1)}, bf16[128,2048]{1,0:T(8,128)(2,1)S(1)}, bf16[128,2048]{1,0:T(8,128...) custom-call(bf16[128,2048]{1,0:T(8,128)(2,1)} %refs_0_.1, ...), custom_call_target="tpu_custom_call" | custom-call | flops 2300000000 | tf_op jit(solution)/shard_map/pallas_call | solution.py:41
  2.8 0.5 %collective-permute-start = (bf16[4,656,128]{2,1,0:T(8,128)(2,1)S(1)}, bf16[4,656,128]{2,1,0:T(8,128)(2,1)S(1)}, u32[]{:S(2)}, u32[]{:S(2)}) collective-permute-start(bf16[4,656,128]{2,1,0:T(8,128)(2,1)S(1)} %get-tuple-element.48), channel_id=1, source_target_pairs={{0,1},{1,0},{2,3},{3,2},{4,5},{5,4},{6,7},{7,6},{8,9},{9,8},{10,11... | collective-permute-start | bytes 2015240 | tf_op jit(solution)/shard_map/ppermute | solution.py:332
  3.3 0.9 %shard_map.85 = (bf16[4,656,128]{2,1,0:T(8,128)(2,1)S(1)}, bf16[4,256,128]{2,1,0:T(8,128)(2,1)S(1)}, f32[4,2,128,128]{3,2,1,0:T(8,128)S(1)}) custom-call(bf16[128,2048]{1,0:T(8,128)(2,1)S(1)} %get-tuple-element.44.refs_0_, bf16[128,2048]{1,0:T(8,128)(2,1)S(1)} %get-tuple-element.45.refs_1_, bf16[128,2048]{1,0:T(8,128)(2,1)S(1)} %get-tuple-element.42.refs_2_.refs_1_, ...), custom_call_target="tpu_custom_call" | custom-call | flops 1150000000 | tf_op jit(solution)/shard_map/pallas_call | solution.py:41
  4.2 0.9 %collective-permute-done.refs_1_.refs_9_ = bf16[4,656,128]{2,1,0:T(8,128)(2,1)S(1)} collective-permute-done((bf16[4,656,128]{2,1,0:T(8,128)(2,1)S(1)}, bf16[4,656,128]{2,1,0:T(8,128)(2,1)S(1)}, u32[]{:S(2)}, u32[]{:S(2)}) %collective-permute-start) | collective-permute-done | bytes 671776 | tf_op jit(solution)/shard_map/ppermute | solution.py:332
  5.0 0.5 %shard_map.86 = (bf16[656,128]{1,0:T(8,128)(2,1)S(1)}, bf16[656,128]{1,0:T(8,128)(2,1)S(1)}, bf16[656,128]{1,0:T(8,128)(2,1)S(1)}, bf16[656,128]{1,0:T(8,128)(2,1)S(1)}) custom-call(bf16[4,656,128]{2,1,0:T(8,128)(2,1)S(1)} %get-tuple-element.47.refs_0_, bf16[4,656,128]{2,1,0:T(8,128)(2,1)S(1)} %collective-permute-done.refs_1_.refs_9_), custom_call_target="tpu_custom_call" | custom-call | flops 460000000 | tf_op jit(solution)/shard_map/pallas_call | solution.py:41
  5.5 1.8 %shard_map.87 = (f32[2,4,2,128,128]{4,3,2,1,0:T(8,128)S(1)}, f32[2,4,2,128,128]{4,3,2,1,0:T(8,128)S(1)}, bf16[2,4,2,128,128]{4,3,2,1,0:T(8,128)(2,1)S(1)}, bf16[2,4,2,128,128]{4,3,2,1,0:T(8,128)(2,1)S(1)}) custom-call(bf16[128,2048]{1,0:T(8,128)(2,1)S(1)} %get-tuple-element.44.refs_0_, bf16[128,2048]{1,0:T(8,128)(2,1)S(1)} %get-tuple-element.45.refs_1_, ...), custom_call_target="tpu_custom_call" | custom-call | flops 2070000000 | tf_op jit(solution)/shard_map/pallas_call | solution.py:41
  7.4 2.9 %collective-permute-start.2 = (bf16[656,128]{1,0:T(8,128)(2,1)S(1)}, bf16[656,128]{1,0:T(8,128)(2,1)S(1)}, u32[]{:S(2)}, u32[]{:S(2)}) collective-permute-start(bf16[656,128]{1,0:T(8,128)(2,1)S(1)} %get-tuple-element.67), channel_id=1, source_target_pairs={{0,2},{1,3},{2,0},{3,1},{4,6},{5,7},{6,4},{7,5},{8,10},{9,11},{10,... | collective-permute-start | bytes 503816 | tf_op jit(solution)/shard_map/ppermute | solution.py:332
  10.3 1.5 %collective-permute-start.3 = (bf16[656,128]{1,0:T(8,128)(2,1)S(1)}, bf16[656,128]{1,0:T(8,128)(2,1)S(1)}, u32[]{:S(2)}, u32[]{:S(2)}) collective-permute-start(bf16[656,128]{1,0:T(8,128)(2,1)S(1)} %get-tuple-element.68), channel_id=1, source_target_pairs={{0,4},{1,5},{2,6},{3,7},{4,0},{5,1},{6,2},{7,3},{8,12},{9,13},{10,... | collective-permute-start | bytes 503816 | tf_op jit(solution)/shard_map/ppermute | solution.py:332
  11.8 0.0 collective-permute-start.4
  11.8 0.0 collective-permute-start.1
  11.8 3.3 %collective-permute-done.2.refs_1_ = bf16[656,128]{1,0:T(8,128)(2,1)S(1)} collective-permute-done((bf16[656,128]{1,0:T(8,128)(2,1)S(1)}, bf16[656,128]{1,0:T(8,128)(2,1)S(1)}, u32[]{:S(2)}, u32[]{:S(2)}) %collective-permute-start.2) | collective-permute-done | bytes 167968 | tf_op jit(solution)/shard_map/ppermute | solution.py:332
  15.1 3.6 %collective-permute-done.3.refs_2_ = bf16[656,128]{1,0:T(8,128)(2,1)S(1)} collective-permute-done((bf16[656,128]{1,0:T(8,128)(2,1)S(1)}, bf16[656,128]{1,0:T(8,128)(2,1)S(1)}, u32[]{:S(2)}, u32[]{:S(2)}) %collective-permute-start.3) | collective-permute-done | bytes 167968 | tf_op jit(solution)/shard_map/ppermute | solution.py:332
  18.7 0.0 collective-permute-done.4.refs_3_
  18.7 0.4 %shard_map.89 = (bf16[656,128]{1,0:T(8,128)(2,1)S(1)}, bf16[656,128]{1,0:T(8,128)(2,1)S(1)}, bf16[656,128]{1,0:T(8,128)(2,1)S(1)}, bf16[656,128]{1,0:T(8,128)(2,1)S(1)}) custom-call(bf16[656,128]{1,0:T(8,128)(2,1)S(1)} %get-tuple-element.66.refs_5_.refs_0_, bf16[656,128]{1,0:T(8,128)(2,1)S(1)} %collective-permute-done.2.refs_1_, ...), custom_call_target="tpu_custom_call" | custom-call | flops 575000000 | tf_op jit(solution)/shard_map/pallas_call | solution.py:41
  19.2 0.7 %collective-permute-start.5 = (bf16[656,128]{1,0:T(8,128)(2,1)S(1)}, bf16[656,128]{1,0:T(8,128)(2,1)S(1)}, u32[]{:S(2)}, u32[]{:S(2)}) collective-permute-start(bf16[656,128]{1,0:T(8,128)(2,1)S(1)} %get-tuple-element.70), channel_id=1, source_target_pairs={{0,2},{1,3},{2,0},{3,1},{4,6},{5,7},{6,4},{7,5},{8,10},{9,11},{10,... | collective-permute-start | bytes 503816 | tf_op jit(solution)/shard_map/ppermute | solution.py:332
  19.9 0.8 %collective-permute-start.7 = (bf16[656,128]{1,0:T(8,128)(2,1)S(1)}, bf16[656,128]{1,0:T(8,128)(2,1)S(1)}, u32[]{:S(2)}, u32[]{:S(2)}) collective-permute-start(bf16[656,128]{1,0:T(8,128)(2,1)S(1)} %get-tuple-element.71), channel_id=1, source_target_pairs={{0,4},{1,5},{2,6},{3,7},{4,0},{5,1},{6,2},{7,3},{8,12},{9,13},{10,... | collective-permute-start | bytes 503816 | tf_op jit(solution)/shard_map/ppermute | solution.py:332
  20.7 2.0 %collective-permute-start.9 = (bf16[656,128]{1,0:T(8,128)(2,1)S(1)}, bf16[656,128]{1,0:T(8,128)(2,1)S(1)}, u32[]{:S(2)}, u32[]{:S(2)}) collective-permute-start(bf16[656,128]{1,0:T(8,128)(2,1)S(1)} %get-tuple-element.72), channel_id=1, source_target_pairs={{0,6},{1,7},{2,4},{3,5},{4,2},{5,3},{6,0},{7,1},{8,14},{9,15},{10,... | collective-permute-start | bytes 503816 | tf_op jit(solution)/shard_map/ppermute | solution.py:332
  22.7 0.0 collective-permute-start.11
  22.7 2.0 %collective-permute-done.5.refs_12_ = bf16[656,128]{1,0:T(8,128)(2,1)S(1)} collective-permute-done((bf16[656,128]{1,0:T(8,128)(2,1)S(1)}, bf16[656,128]{1,0:T(8,128)(2,1)S(1)}, u32[]{:S(2)}, u32[]{:S(2)}) %collective-permute-start.5) | collective-permute-done | bytes 167968 | tf_op jit(solution)/shard_map/ppermute | solution.py:332
  24.8 0.0 collective-permute-start.6
  24.8 0.5 %collective-permute-done.7.refs_13_ = bf16[656,128]{1,0:T(8,128)(2,1)S(1)} collective-permute-done((bf16[656,128]{1,0:T(8,128)(2,1)S(1)}, bf16[656,128]{1,0:T(8,128)(2,1)S(1)}, u32[]{:S(2)}, u32[]{:S(2)}) %collective-permute-start.7) | collective-permute-done | bytes 167968 | tf_op jit(solution)/shard_map/ppermute | solution.py:332
  25.2 0.0 collective-permute-start.8
  25.3 1.8 %collective-permute-done.9.refs_14_ = bf16[656,128]{1,0:T(8,128)(2,1)S(1)} collective-permute-done((bf16[656,128]{1,0:T(8,128)(2,1)S(1)}, bf16[656,128]{1,0:T(8,128)(2,1)S(1)}, u32[]{:S(2)}, u32[]{:S(2)}) %collective-permute-start.9) | collective-permute-done | bytes 167968 | tf_op jit(solution)/shard_map/ppermute | solution.py:332
  27.0 0.0 collective-permute-start.10
  27.0 0.0 collective-permute-done.1.refs_10_
  27.0 0.0 collective-permute-done.11.refs_15_
  27.0 1.0 %shard_map.90 = (bf16[128,1280]{1,0:T(8,128)(2,1)S(1)}, bf16[128,1280]{1,0:T(8,128)(2,1)S(1)}, bf16[128,1280]{1,0:T(8,128)(2,1)S(1)}, f32[10,128,128]{2,1,0:T(8,128)S(1)}) custom-call(bf16[128,2048]{1,0:T(8,128)(2,1)S(1)} %get-tuple-element.41.refs_3_.refs_0_, bf16[128,2048]{1,0:T(8,128)(2,1)S(1)} %get-tuple-element.42.refs_2_.refs_1_, ...), custom_call_target="tpu_custom_call" | custom-call | flops 1035000000 | tf_op jit(solution)/shard_map/pallas_call | solution.py:41
  28.1 0.0 collective-permute-done.6.refs_11_
  28.1 0.0 collective-permute-done.8.refs_12_
  28.1 0.3 %collective-permute-done.10.refs_13_ = bf16[656,128]{1,0:T(8,128)(2,1)S(1)} collective-permute-done((bf16[656,128]{1,0:T(8,128)(2,1)S(1)}, bf16[656,128]{1,0:T(8,128)(2,1)S(1)}, u32[]{:S(2)}, u32[]{:S(2)}) %collective-permute-start.10) | collective-permute-done | bytes 167968 | tf_op jit(solution)/shard_map/ppermute | solution.py:332
  28.4 2.3 %shard_map.91 = (bf16[128,2048]{1,0:T(8,128)(2,1)}, bf16[128,2048]{1,0:T(8,128)(2,1)}, bf16[128,2048]{1,0:T(8,128)(2,1)}, f32[16,128,128]{2,1,0:T(8,128)}) custom-call(bf16[128,2048]{1,0:T(8,128)(2,1)S(1)} %get-tuple-element.41.refs_3_.refs_0_, bf16[128,2048]{1,0:T(8,128)(2,1)S(1)} %get-tuple-element.42.refs_2_.refs_1_, ...), custom_call_target="tpu_custom_call" | custom-call | flops 1380000000 | tf_op jit(solution)/shard_map/pallas_call | solution.py:41
  (1 shorter events, 0.0 us)
Async XLA Ops:
  2.8 2.3 %collective-permute-start = (bf16[4,656,128]{2,1,0:T(8,128)(2,1)S(1)}, bf16[4,656,128]{2,1,0:T(8,128)(2,1)S(1)}, u32[]{:S(2)}, u32[]{:S(2)}) collective-permute-start(bf16[4,656,128]{2,1,0:T(8,128)(2,1)S(1)} %get-tuple-element.48), channel_id=1, source_target_pairs={{0,1},{1,0},{2,3},{3,2},{4,5},{5,4},{6,7},{7,6},{8,9},{9,8},{10,11... | collective-permute-start | bytes 2015240 | tf_op jit(solution)/shard_map/ppermute | solution.py:332
  7.4 7.7 %collective-permute-start.2 = (bf16[656,128]{1,0:T(8,128)(2,1)S(1)}, bf16[656,128]{1,0:T(8,128)(2,1)S(1)}, u32[]{:S(2)}, u32[]{:S(2)}) collective-permute-start(bf16[656,128]{1,0:T(8,128)(2,1)S(1)} %get-tuple-element.67), channel_id=1, source_target_pairs={{0,2},{1,3},{2,0},{3,1},{4,6},{5,7},{6,4},{7,5},{8,10},{9,11},{10,... | collective-permute-start | bytes 503816 | tf_op jit(solution)/shard_map/ppermute | solution.py:332
  10.3 8.5 %collective-permute-start.3 = (bf16[656,128]{1,0:T(8,128)(2,1)S(1)}, bf16[656,128]{1,0:T(8,128)(2,1)S(1)}, u32[]{:S(2)}, u32[]{:S(2)}) collective-permute-start(bf16[656,128]{1,0:T(8,128)(2,1)S(1)} %get-tuple-element.68), channel_id=1, source_target_pairs={{0,4},{1,5},{2,6},{3,7},{4,0},{5,1},{6,2},{7,3},{8,12},{9,13},{10,... | collective-permute-start | bytes 503816 | tf_op jit(solution)/shard_map/ppermute | solution.py:332
  11.8 7.0 %collective-permute-start.4 = (bf16[656,128]{1,0:T(8,128)(2,1)S(1)}, bf16[656,128]{1,0:T(8,128)(2,1)S(1)}, u32[]{:S(2)}, u32[]{:S(2)}) collective-permute-start(bf16[656,128]{1,0:T(8,128)(2,1)S(1)} %get-tuple-element.69), channel_id=1, source_target_pairs={{0,6},{1,7},{2,4},{3,5},{4,2},{5,3},{6,0},{7,1},{8,14},{9,15},{10,... | collective-permute-start | bytes 503816 | tf_op jit(solution)/shard_map/ppermute | solution.py:332
  11.8 15.2 %collective-permute-start.1 = (bf16[4,256,128]{2,1,0:T(8,128)(2,1)S(1)}, bf16[4,256,128]{2,1,0:T(8,128)(2,1)S(1)}, u32[]{:S(2)}, u32[]{:S(2)}) collective-permute-start(bf16[4,256,128]{2,1,0:T(8,128)(2,1)S(1)} %get-tuple-element.65), channel_id=1, source_target_pairs={{0,1},{1,0},{2,3},{3,2},{4,5},{5,4},{6,7},{7,6},{8,9},{9,8},{10,11... | collective-permute-start | bytes 786440 | tf_op jit(solution)/shard_map/ppermute | solution.py:332
  19.2 5.6 %collective-permute-start.5 = (bf16[656,128]{1,0:T(8,128)(2,1)S(1)}, bf16[656,128]{1,0:T(8,128)(2,1)S(1)}, u32[]{:S(2)}, u32[]{:S(2)}) collective-permute-start(bf16[656,128]{1,0:T(8,128)(2,1)S(1)} %get-tuple-element.70), channel_id=1, source_target_pairs={{0,2},{1,3},{2,0},{3,1},{4,6},{5,7},{6,4},{7,5},{8,10},{9,11},{10,... | collective-permute-start | bytes 503816 | tf_op jit(solution)/shard_map/ppermute | solution.py:332
  19.9 5.4 %collective-permute-start.7 = (bf16[656,128]{1,0:T(8,128)(2,1)S(1)}, bf16[656,128]{1,0:T(8,128)(2,1)S(1)}, u32[]{:S(2)}, u32[]{:S(2)}) collective-permute-start(bf16[656,128]{1,0:T(8,128)(2,1)S(1)} %get-tuple-element.71), channel_id=1, source_target_pairs={{0,4},{1,5},{2,6},{3,7},{4,0},{5,1},{6,2},{7,3},{8,12},{9,13},{10,... | collective-permute-start | bytes 503816 | tf_op jit(solution)/shard_map/ppermute | solution.py:332
  20.7 6.3 %collective-permute-start.9 = (bf16[656,128]{1,0:T(8,128)(2,1)S(1)}, bf16[656,128]{1,0:T(8,128)(2,1)S(1)}, u32[]{:S(2)}, u32[]{:S(2)}) collective-permute-start(bf16[656,128]{1,0:T(8,128)(2,1)S(1)} %get-tuple-element.72), channel_id=1, source_target_pairs={{0,6},{1,7},{2,4},{3,5},{4,2},{5,3},{6,0},{7,1},{8,14},{9,15},{10,... | collective-permute-start | bytes 503816 | tf_op jit(solution)/shard_map/ppermute | solution.py:332
  22.7 4.3 %collective-permute-start.11 = (bf16[656,128]{1,0:T(8,128)(2,1)S(1)}, bf16[656,128]{1,0:T(8,128)(2,1)S(1)}, u32[]{:S(2)}, u32[]{:S(2)}) collective-permute-start(bf16[656,128]{1,0:T(8,128)(2,1)S(1)} %get-tuple-element.73.refs_11_), channel_id=1, source_target_pairs={{0,1},{1,0},{2,3},{3,2},{4,5},{5,4},{6,7},{7,6},{8,9},{9,8},{10,11... | collective-permute-start | bytes 503816 | tf_op jit(solution)/shard_map/ppermute | solution.py:332
  24.8 3.3 %collective-permute-start.6 = (bf16[656,128]{1,0:T(8,128)(2,1)S(1)}, bf16[656,128]{1,0:T(8,128)(2,1)S(1)}, u32[]{:S(2)}, u32[]{:S(2)}) collective-permute-start(bf16[656,128]{1,0:T(8,128)(2,1)S(1)} %collective-permute-done.5.refs_12_), channel_id=1, source_target_pairs={{0,1},{1,0},{2,3},{3,2},{4,5},{5,4},{6,7},{7,6},{8,9},{9,8},{10,11... | collective-permute-start | bytes 503816 | tf_op jit(solution)/shard_map/ppermute | solution.py:332
  25.2 2.9 %collective-permute-start.8 = (bf16[656,128]{1,0:T(8,128)(2,1)S(1)}, bf16[656,128]{1,0:T(8,128)(2,1)S(1)}, u32[]{:S(2)}, u32[]{:S(2)}) collective-permute-start(bf16[656,128]{1,0:T(8,128)(2,1)S(1)} %collective-permute-done.7.refs_13_), channel_id=1, source_target_pairs={{0,1},{1,0},{2,3},{3,2},{4,5},{5,4},{6,7},{7,6},{8,9},{9,8},{10,11... | collective-permute-start | bytes 503816 | tf_op jit(solution)/shard_map/ppermute | solution.py:332
  27.0 1.4 %collective-permute-start.10 = (bf16[656,128]{1,0:T(8,128)(2,1)S(1)}, bf16[656,128]{1,0:T(8,128)(2,1)S(1)}, u32[]{:S(2)}, u32[]{:S(2)}) collective-permute-start(bf16[656,128]{1,0:T(8,128)(2,1)S(1)} %collective-permute-done.9.refs_14_), channel_id=1, source_target_pairs={{0,1},{1,0},{2,3},{3,2},{4,5},{5,4},{6,7},{7,6},{8,9},{9,8},{10,11... | collective-permute-start | bytes 503816 | tf_op jit(solution)/shard_map/ppermute | solution.py:332

commit v7 on v6

--- a/solution.py
+++ b/solution.py
@@ -79,7 +79,7 @@
 def load_body(per_owner, q, k, v, g, w, q_here, k_here, v_here, g_here, w_here, send, part_q, sems):
     half_width = q.shape[1] // 2
     core, chip = place()
-    pairs = ((k, k_here), (v, v_here), (q, q_here), (g, g_here))
+    pairs = ((g, g_here), (v, v_here), (k, k_here), (q, q_here))
     copies = []
     for turn, half in enumerate((1 - core, core)):
         at = columns(half, half_width)
@@ -90,29 +90,35 @@
     copies.append(pltpu.make_async_copy(w, w_here, sems.at[2, 0]))
     for copy in copies:
         copy.start()
-    for copy in copies[:4]:
-        copy.wait()
-    states(send, part_q, owned(1 - core, chip, per_owner), q_here, k_here, v_here, g_here)
+    heads = owned(1 - core, chip, per_owner)
+    states(send, part_q, heads, q_here, k_here, v_here, g_here, copies[:4])
     for copy in copies[4:]:
         copy.wait()
 
 
-def states(out, part_q, heads, q, k, v, g):
+def states(out, part_q, heads, q, k, v, g, copies=()):
     size = out.shape[-1]
     per_owner = len(heads) // GROUPS
     rows, cols = triangle(q.shape[0])
     ats = [columns(head, size) for _, _, head in heads]
+    for copy in copies[:2]:
+        copy.wait()
     mixing = [dot_nt(g[:, at], v[:, at]) for at in ats]
+    mixing = [jnp.where(rows >= cols, x, 0.0).astype(BF16) for x in mixing]
+    for copy in copies[2:3]:
+        copy.wait()
+    mixed = [dot_nn(x, k[:, at]) for x, at in zip(mixing, ats)]
     early = [dot_tn(k[:, at], v[:, at]) for at in ats]
-    mixing = [jnp.where(rows >= cols, x, 0.0).astype(BF16) for x in mixing]
-    mixed = [dot_nn(x, k[:, at]) for x, at in zip(mixing, ats)]
+    for n, (apart, i, _) in enumerate(heads):
+        part_q[apart, i] = mixed[n]
+        out[apart, i * size : (i + 1) * size] = early[n].astype(BF16)
+    for copy in copies[3:]:
+        copy.wait()
     wide = [
         dot_tn(q[:, at], jnp.concatenate([g[:, at], x.astype(BF16)], axis=1))
         for x, at in zip(mixed, ats)
     ]
     for n, (apart, i, _) in enumerate(heads):
-        part_q[apart, i] = mixed[n]
-        out[apart, i * size : (i + 1) * size] = early[n].astype(BF16)
         out[apart, (per_owner + i) * size : (per_owner + i + 1) * size] = wide[n][:, :size].astype(BF16)
         if i % 2:
             both, diagonal = pack(wide[n - 1][:, size:], wide[n][:, size:])
@@ -121,15 +127,15 @@
             out[apart, start + size : start + size + EXTRA] = diagonal.astype(BF16)
 
 
-def near_body(per_owner, q, k, v, g, own, extra, part_q):
+def near_body(per_owner, q, k, v, g, own, *refs):
     size = own.shape[-1]
     core, chip = place()
     heads = owned(core, chip, per_owner)
-    states(own, part_q, heads, q, k, v, g)
+    states(own, refs[2], heads, q, k, v, g)
     for apart in range(GROUPS):
         early = own[apart, : per_owner * size]
         late = own[apart, per_owner * size : 2 * per_owner * size]
-        extra[apart] = jnp.where(core == 0, early, late)
+        refs[apart // 2][apart % 2] = jnp.where(core == 0, early, late)
 
 
 def pack(first, second):
@@ -246,7 +252,7 @@
             out[start + size : start + size + EXTRA] = diagonal.astype(BF16)
 
 
-def finish(pieces, per_owner, scale, shared, sources, outs):
+def finish(pieces, per_owner, scale, shared, sources, near, far):
     g, v, w, key_w, gram, part_q, part_k, part_v, other, extra = shared
     size = gram.shape[-1]
     core, chip = place()
@@ -254,16 +260,16 @@
     for piece, (which, apart) in enumerate(pieces):
         half = 1 - core if which else core
         for i in range(per_owner):
-            index = piece * per_owner + i
-            head = (half * GROUPS + (chip ^ apart)) * per_owner + i
-            heads.append((which, apart, i, sources[piece], head, slice(index * size, (index + 1) * size)))
+            slot = (chip ^ apart) * per_owner + i
+            head = half * GROUPS * per_owner + slot
+            heads.append((which, apart, i, sources[piece], head, slot))
     ats = [columns(head[4], size) for head in heads]
     prefix, suffix = [], []
     for which, apart, i, source, *_ in heads:
         ahead = slice(i * size, (i + 1) * size)
         behind = slice((per_owner + i) * size, (per_owner + i + 1) * size)
         if which:
-            early = late = extra[apart, ahead]
+            early = late = extra[apart // 2][apart % 2, ahead]
         else:
             early, late = other[apart, ahead], other[apart, behind]
         before, after = source[ahead], source[behind]
@@ -275,12 +281,14 @@
     raw_q = [(part_q[h][a, i] + x).astype(BF16) for x, (h, a, i, *_) in zip(raw_q, heads)]
     raw_k = [(part_k[h, a, i] + x).astype(BF16) for x, (h, a, i, *_) in zip(raw_k, heads)]
     for x, (h, a, i, _, _, to) in zip(raw_v, heads):
-        outs[2][:, to] = (part_v[h, a, i] + x).astype(BF16)
+        outs = far if h else near
+        outs[2][:, columns(to, size)] = (part_v[h, a, i] + x).astype(BF16)
     done_q = [dot_nn(x, gram[h, a, i]) for x, (h, a, i, *_) in zip(raw_q, heads)]
     done_k = [dot_nn(x, gram[h, a, i]) for x, (h, a, i, *_) in zip(raw_k, heads)]
-    for x, y, (*_, to) in zip(done_q, done_k, heads):
-        outs[0][:, to] = x.astype(BF16)
-        outs[1][:, to] = y.astype(BF16)
+    for x, y, (h, *_, to) in zip(done_q, done_k, heads):
+        outs = far if h else near
+        outs[0][:, columns(to, size)] = x.astype(BF16)
+        outs[1][:, columns(to, size)] = y.astype(BF16)
     rows, cols = triangle(size)
     for piece, source in enumerate(sources):
         for pair in range(per_owner // 2):
@@ -292,37 +300,42 @@
             second = jnp.where(rows < cols, both, turned)
             second = jnp.where(rows == cols, diagonal, second)
             for i, whole in ((2 * pair, first), (2 * pair + 1, second)):
-                index = piece * per_owner + i
-                outs[3][index] = dot_nn(whole.astype(BF16), w[heads[index][4]]) * scale
-
-
-def leave(pieces, per_owner, here, outs, sems):
+                which, _, _, _, head, slot = heads[piece * per_owner + i]
+                (far if which else near)[3][slot] = dot_nn(whole.astype(BF16), w[head]) * scale
+
+
+def leave(half, here, outs, sems):
+    width, count = here[0].shape[1], here[3].shape[0]
+    copies = []
+    for n in range(4):
+        at = outs[n].at[pl.ds(half * count, count)] if n == 3 else outs[n].at[:, columns(half, width)]
+        copies.append(pltpu.make_async_copy(here[n], at, sems.at[n]))
+        copies[-1].start()
+    return copies
+
+
+def tail_first_body(pieces, per_owner, scale, *refs):
+    shared, refs = (*refs[:5], refs[5:7], *refs[7:10], refs[10:12]), refs[12:]
+    sources, refs = refs[: len(pieces)], refs[len(pieces) :]
+    finish(pieces, per_owner, scale, shared, sources, refs[:4], refs[4:])
+
+
+def tail_last_body(pieces, per_owner, scale, *refs):
+    shared, refs = (*refs[:5], refs[5:7], *refs[7:10], refs[10:12]), refs[12:]
+    sources, refs = refs[: len(pieces)], refs[len(pieces) :]
+    near, far, outs, here, sems = refs[:4], refs[4:8], refs[8:12], refs[12:16], refs[16]
     core, chip = place()
     size = here[3].shape[-1]
-    copies = []
-    for piece, (which, apart) in enumerate(pieces):
-        half = 1 - core if which else core
-        owner = half * GROUPS + (chip ^ apart)
-        at = pl.ds(piece * per_owner * size, per_owner * size)
-        ends = [(here[n].at[:, at], outs[n].at[:, columns(owner, per_owner * size)]) for n in range(3)]
-        at = pl.ds(piece * per_owner, per_owner)
-        ends.append((here[3].at[at], outs[3].at[pl.ds(owner * per_owner, per_owner)]))
-        for n, (source, target) in enumerate(ends):
-            copies.append(pltpu.make_async_copy(source, target, sems.at[piece, n]))
-            copies[-1].start()
-    return copies
-
-
-def tail_body(pieces, ready, per_owner, scale, *refs):
-    shared, refs = (*refs[:5], refs[5:7], *refs[7:11]), refs[11:]
-    sources, refs = refs[: len(pieces)], refs[len(pieces) :]
-    if ready is None:
-        finish(pieces, per_owner, scale, shared, sources, refs)
-        return
-    outs, here, sems, ready_sems = refs[-10:-6], refs[-6:-2], refs[-2], refs[-1]
-    copies = leave(ready, per_owner, refs[:4], outs, ready_sems) if ready else []
-    finish(pieces, per_owner, scale, shared, sources, here)
-    copies += leave(pieces, per_owner, here, outs, sems)
+    copies = leave(core, near, outs, sems.at[0])
+    for apart in range(GROUPS - len(pieces)):
+        spot = chip ^ apart
+        for n in range(3):
+            at = columns(spot, per_owner * size)
+            here[n][:, at] = far[n][:, at]
+        at = pl.ds(spot * per_owner, per_owner)
+        here[3][at] = far[3][at]
+    finish(pieces, per_owner, scale, shared, sources, None, here)
+    copies += leave(1 - core, here, outs, sems.at[1])
     for copy in copies:
         copy.wait()
 
@@ -353,9 +366,9 @@
         scratch=[pltpu.SemaphoreType.DMA((3, 4))],
     )
     other = swap(send, 1)
-    own, extra, part_q0 = call(
+    own, *extra, part_q0 = call(
         bind(near_body, per_owner),
-        [(payloads, BF16), ((GROUPS, per_owner * size, size), BF16), (one, F32)],
+        [(payloads, BF16), *[((GROUPS // 2, per_owner * size, size), BF16)] * 2, (one, F32)],
         here,
         1.0,
     )
@@ -367,8 +380,6 @@
     held = lax.optimization_barrier((*chip_sums, local[0]))
     chip_sums, local[0] = list(held[:GROUPS]), held[GROUPS]
     parts = [chip_sums[0]] + [swap(chip_sums[j], 2 * j) for j in range(1, GROUPS)]
-    extra, local[0] = lax.optimization_barrier((extra, local[0]))
-    extra = swap(extra, 1)
     local = call(
         bind(rest_second_body, per_owner),
         locals_,
@@ -379,12 +390,14 @@
         in_after=VMEM,
     )
     part_k, part_v, key_w, gram = local
+    *extra, gram = lax.optimization_barrier((*extra, gram))
+    extra = [swap(x, 1) for x in extra]
     carried = call(
         bind(owner_body, per_owner),
         [(payload, BF16)] * GROUPS,
         parts,
         0.5,
-        after=(gram,),
+        after=(gram, *extra),
         scratch=[pltpu.VMEM((GROUPS, 2 * per_owner * size, size), BF16)] * 2,
     )
     near = [carried[0]] + [swap(carried[j], 2 * j) for j in range(1, GROUPS)]
@@ -392,29 +405,27 @@
     outs = [((rows, width), BF16)] * 3 + [((heads,) + block, F32)]
     shared = (here[3], here[2], w, key_w, gram, part_q0, part_q1, part_k, part_v, other)
 
-    def tail(pieces, payloads, ready=(), done=(), before=()):
-        count = len(pieces) * per_owner
-        room = [((rows, count * size), BF16)] * 3 + [((count,) + block, F32)]
-        operands = (*shared, extra, *payloads, *done)
-        if ready is None:
-            return call(bind(tail_body, pieces, None, per_owner, scale), room, operands, 0.9)
-        return call(
-            bind(tail_body, pieces, ready, per_owner, scale),
+    half = [((rows, width // 2), BF16)] * 3 + [((heads // 2,) + block, F32)]
+    far = [swap(x, 1) for x in near]
+    pieces = [(0, n) for n in range(GROUPS)] + [(1, n) for n in range(2)]
+    done = call(
+        bind(tail_first_body, pieces, per_owner, scale),
+        half * 2,
+        (*shared, *extra, *near, *far[:2]),
+        1.0,
+    )
+    pieces = [(1, n) for n in range(2, GROUPS)]
+    return tuple(
+        call(
+            bind(tail_last_body, pieces, per_owner, scale),
             outs,
-            operands,
+            (*shared, *extra, *far[2:], *done),
             1.2,
-            after=before,
-            scratch=[pltpu.VMEM(shape, dtype) for shape, dtype in room]
-            + [pltpu.SemaphoreType.DMA((max(1, len(x)), 4)) for x in (pieces, ready)],
+            scratch=[pltpu.VMEM(shape, dtype) for shape, dtype in half]
+            + [pltpu.SemaphoreType.DMA((2, 4))],
             out_specs=[HBM] * 4,
-            aliases={len(operands) + n: n for n in range(len(before))},
         )
-
-    far = [swap(x, 1) for x in near]
-    middle = [(0, n) for n in range(GROUPS)] + [(1, n) for n in range(1)]
-    done = tail(middle, (*near, *far[:1]), ready=None)
-    last = [(1, n) for n in range(1, GROUPS)]
-    return tuple(tail(last, far[1:], ready=middle, done=done))
+    )
 
 
 def gathered(q, k, v, g, w):

time: 30.9 us -> 30.7 us (level)
  waiting for transfers between devices: 12.4 us -> 11.7 us
  starting transfers between devices: 8.57 us -> 9.08 us
    ppermute x12 -> x13, waiting for transfers between devices: 12.4 us -> 11.7 us  [swap(): return lax.ppermute(x, 'ctx', [(i, i ^ apart) for i in range(count)])]
    ppermute x12 -> x13, starting transfers between devices: 8.57 us -> 9.08 us  [swap(): return lax.ppermute(x, 'ctx', [(i, i ^ apart) for i in range(count)])]
  transfers between devices with their start and end apart: 12 -> 13, of which waited for: 7 -> 9; matrix products, arithmetic and copies ran while one was open for 0% -> 0% of each run, Pallas kernels for 8% -> 7%
where the time goes in v7:
time: 30.7 us; the launch traced here: 30.5 us
  waiting for transfers between devices  11.7 us (38%)
  starting transfers between devices  9.08 us (30%)
  Pallas kernels  9.05 us (29%)
  between operations  0.68 us (2%)
    ppermute x13, waiting for transfers between devices, swap(): return lax.ppermute(x, 'ctx', [(i, i ^ apart) for i in range(count)])  11.7 us
    ppermute x13, starting transfers between devices, swap(): return lax.ppermute(x, 'ctx', [(i, i ^ apart) for i in range(count)])  9.08 us
    pallas_call x8, Pallas kernels, call(): pl.pallas_call(run, out_shape=[jax.ShapeDtypeStruct(shape, dtype) for sha...  9.05 us
  transfers between devices with their start and end apart: 13, of which 9 were waited for; matrix products, arithmetic and copies ran while one was open for 0% of the time, Pallas kernels for 7%

profile of v7, /device:TPU:0, one launch (start us, length us, event | category | flops | bytes accessed | tf_op | source)
XLA Modules:
  0.0 30.5 jit_solution(15869204455424680145)
XLA Ops:
  0.6 2.2 %shard_map.84 = (bf16[128,2048]{1,0:T(8,128)(2,1)S(1)}, bf16[128,2048]{1,0:T(8,128)(2,1)S(1)}, bf16[128,2048]{1,0:T(8,128)(2,1)S(1)}, bf16[128,2048]{1,0:T(8,128...) custom-call(bf16[128,2048]{1,0:T(8,128)(2,1)} %refs_0_.1, ...), custom_call_target="tpu_custom_call" | custom-call | flops 2300000000 | tf_op jit(solution)/shard_map/pallas_call | solution.py:41
  2.8 0.5 %collective-permute-start = (bf16[4,656,128]{2,1,0:T(8,128)(2,1)S(1)}, bf16[4,656,128]{2,1,0:T(8,128)(2,1)S(1)}, u32[]{:S(2)}, u32[]{:S(2)}) collective-permute-start(bf16[4,656,128]{2,1,0:T(8,128)(2,1)S(1)} %get-tuple-element.53), channel_id=1, source_target_pairs={{0,1},{1,0},{2,3},{3,2},{4,5},{5,4},{6,7},{7,6},{8,9},{9,8},{10,11... | collective-permute-start | bytes 2015240 | tf_op jit(solution)/shard_map/ppermute | solution.py:345
  3.4 0.8 %shard_map.85 = (bf16[4,656,128]{2,1,0:T(8,128)(2,1)S(1)}, bf16[2,256,128]{2,1,0:T(8,128)(2,1)S(1)}, bf16[2,256,128]{2,1,0:T(8,128)(2,1)S(1)}, f32[4,2,128,128]{3,2,1,0:T(8,128)S(1)}) custom-call(bf16[128,2048]{1,0:T(8,128)(2,1)S(1)} %get-tuple-element.50.refs_0_, bf16[128,2048]{1,0:T(8,128)(2,1)S(1)} %get-tuple-element.51.refs_1_, ...), custom_call_target="tpu_custom_call" | custom-call | flops 1150000000 | tf_op jit(solution)/shard_map/pallas_call | solution.py:41
  4.2 0.9 %collective-permute-done.refs_1_.refs_9_ = bf16[4,656,128]{2,1,0:T(8,128)(2,1)S(1)} collective-permute-done((bf16[4,656,128]{2,1,0:T(8,128)(2,1)S(1)}, bf16[4,656,128]{2,1,0:T(8,128)(2,1)S(1)}, u32[]{:S(2)}, u32[]{:S(2)}) %collective-permute-start) | collective-permute-done | bytes 671776 | tf_op jit(solution)/shard_map/ppermute | solution.py:345
  5.1 0.5 %shard_map.86 = (bf16[656,128]{1,0:T(8,128)(2,1)S(1)}, bf16[656,128]{1,0:T(8,128)(2,1)S(1)}, bf16[656,128]{1,0:T(8,128)(2,1)S(1)}, bf16[656,128]{1,0:T(8,128)(2,1)S(1)}) custom-call(bf16[4,656,128]{2,1,0:T(8,128)(2,1)S(1)} %get-tuple-element.52.refs_0_, bf16[4,656,128]{2,1,0:T(8,128)(2,1)S(1)} %collective-permute-done.refs_1_.refs_9_), custom_call_target="tpu_custom_call" | custom-call | flops 460000000 | tf_op jit(solution)/shard_map/pallas_call | solution.py:41
  5.6 1.8 %shard_map.87 = (f32[2,4,2,128,128]{4,3,2,1,0:T(8,128)S(1)}, f32[2,4,2,128,128]{4,3,2,1,0:T(8,128)S(1)}, bf16[2,4,2,128,128]{4,3,2,1,0:T(8,128)(2,1)S(1)}, bf16[2,4,2,128,128]{4,3,2,1,0:T(8,128)(2,1)S(1)}) custom-call(bf16[128,2048]{1,0:T(8,128)(2,1)S(1)} %get-tuple-element.50.refs_0_, bf16[128,2048]{1,0:T(8,128)(2,1)S(1)} %get-tuple-element.51.refs_1_, ...), custom_call_target="tpu_custom_call" | custom-call | flops 2070000000 | tf_op jit(solution)/shard_map/pallas_call | solution.py:41
  7.4 2.9 %collective-permute-start.3 = (bf16[656,128]{1,0:T(8,128)(2,1)S(1)}, bf16[656,128]{1,0:T(8,128)(2,1)S(1)}, u32[]{:S(2)}, u32[]{:S(2)}) collective-permute-start(bf16[656,128]{1,0:T(8,128)(2,1)S(1)} %get-tuple-element.75), channel_id=1, source_target_pairs={{0,2},{1,3},{2,0},{3,1},{4,6},{5,7},{6,4},{7,5},{8,10},{9,11},{10,... | collective-permute-start | bytes 503816 | tf_op jit(solution)/shard_map/ppermute | solution.py:345
  10.3 1.5 %collective-permute-start.4 = (bf16[656,128]{1,0:T(8,128)(2,1)S(1)}, bf16[656,128]{1,0:T(8,128)(2,1)S(1)}, u32[]{:S(2)}, u32[]{:S(2)}) collective-permute-start(bf16[656,128]{1,0:T(8,128)(2,1)S(1)} %get-tuple-element.76), channel_id=1, source_target_pairs={{0,4},{1,5},{2,6},{3,7},{4,0},{5,1},{6,2},{7,3},{8,12},{9,13},{10,... | collective-permute-start | bytes 503816 | tf_op jit(solution)/shard_map/ppermute | solution.py:345
  11.9 0.0 collective-permute-start.5
  11.9 0.0 collective-permute-start.1
  11.9 0.5 %collective-permute-start.2 = (bf16[2,256,128]{2,1,0:T(8,128)(2,1)S(1)}, bf16[2,256,128]{2,1,0:T(8,128)(2,1)S(1)}, u32[]{:S(2)}, u32[]{:S(2)}) collective-permute-start(bf16[2,256,128]{2,1,0:T(8,128)(2,1)S(1)} %get-tuple-element.73), channel_id=1, source_target_pairs={{0,1},{1,0},{2,3},{3,2},{4,5},{5,4},{6,7},{7,6},{8,9},{9,8},{10,11... | collective-permute-start | bytes 393224 | tf_op jit(solution)/shard_map/ppermute | solution.py:345
  12.4 0.8 %collective-permute-done.1.refs_5_.refs_10_ = bf16[2,256,128]{2,1,0:T(8,128)(2,1)S(1)} collective-permute-done((bf16[2,256,128]{2,1,0:T(8,128)(2,1)S(1)}, bf16[2,256,128]{2,1,0:T(8,128)(2,1)S(1)}, u32[]{:S(2)}, u32[]{:S(2)}) %collective-permute-start.1) | collective-permute-done | bytes 131104 | tf_op jit(solution)/shard_map/ppermute | solution.py:345
  13.2 0.2 collective-permute-done.2.refs_6_.refs_11_
  13.4 1.8 %collective-permute-done.3.refs_1_ = bf16[656,128]{1,0:T(8,128)(2,1)S(1)} collective-permute-done((bf16[656,128]{1,0:T(8,128)(2,1)S(1)}, bf16[656,128]{1,0:T(8,128)(2,1)S(1)}, u32[]{:S(2)}, u32[]{:S(2)}) %collective-permute-start.3) | collective-permute-done | bytes 167968 | tf_op jit(solution)/shard_map/ppermute | solution.py:345
  15.2 3.6 %collective-permute-done.4.refs_2_ = bf16[656,128]{1,0:T(8,128)(2,1)S(1)} collective-permute-done((bf16[656,128]{1,0:T(8,128)(2,1)S(1)}, bf16[656,128]{1,0:T(8,128)(2,1)S(1)}, u32[]{:S(2)}, u32[]{:S(2)}) %collective-permute-start.4) | collective-permute-done | bytes 167968 | tf_op jit(solution)/shard_map/ppermute | solution.py:345
  18.8 0.0 collective-permute-done.5.refs_3_
  18.8 0.4 %shard_map.89 = (bf16[656,128]{1,0:T(8,128)(2,1)S(1)}, bf16[656,128]{1,0:T(8,128)(2,1)S(1)}, bf16[656,128]{1,0:T(8,128)(2,1)S(1)}, bf16[656,128]{1,0:T(8,128)(2,1)S(1)}) custom-call(bf16[656,128]{1,0:T(8,128)(2,1)S(1)} %get-tuple-element.74.refs_5_.refs_0_, bf16[656,128]{1,0:T(8,128)(2,1)S(1)} %collective-permute-done.3.refs_1_, ...), custom_call_target="tpu_custom_call" | custom-call | flops 575000000 | tf_op jit(solution)/shard_map/pallas_call | solution.py:41
  19.2 0.7 %collective-permute-start.10 = (bf16[656,128]{1,0:T(8,128)(2,1)S(1)}, bf16[656,128]{1,0:T(8,128)(2,1)S(1)}, u32[]{:S(2)}, u32[]{:S(2)}) collective-permute-start(bf16[656,128]{1,0:T(8,128)(2,1)S(1)} %get-tuple-element.81), channel_id=1, source_target_pairs={{0,2},{1,3},{2,0},{3,1},{4,6},{5,7},{6,4},{7,5},{8,10},{9,11},{10,... | collective-permute-start | bytes 503816 | tf_op jit(solution)/shard_map/ppermute | solution.py:345
  19.9 0.8 %collective-permute-start.6 = (bf16[656,128]{1,0:T(8,128)(2,1)S(1)}, bf16[656,128]{1,0:T(8,128)(2,1)S(1)}, u32[]{:S(2)}, u32[]{:S(2)}) collective-permute-start(bf16[656,128]{1,0:T(8,128)(2,1)S(1)} %get-tuple-element.78), channel_id=1, source_target_pairs={{0,4},{1,5},{2,6},{3,7},{4,0},{5,1},{6,2},{7,3},{8,12},{9,13},{10,... | collective-permute-start | bytes 503816 | tf_op jit(solution)/shard_map/ppermute | solution.py:345
  20.7 2.0 %collective-permute-start.8 = (bf16[656,128]{1,0:T(8,128)(2,1)S(1)}, bf16[656,128]{1,0:T(8,128)(2,1)S(1)}, u32[]{:S(2)}, u32[]{:S(2)}) collective-permute-start(bf16[656,128]{1,0:T(8,128)(2,1)S(1)} %get-tuple-element.79), channel_id=1, source_target_pairs={{0,6},{1,7},{2,4},{3,5},{4,2},{5,3},{6,0},{7,1},{8,14},{9,15},{10,... | collective-permute-start | bytes 503816 | tf_op jit(solution)/shard_map/ppermute | solution.py:345
  22.8 0.0 collective-permute-start.11
  22.8 2.0 %collective-permute-done.10.refs_13_ = bf16[656,128]{1,0:T(8,128)(2,1)S(1)} collective-permute-done((bf16[656,128]{1,0:T(8,128)(2,1)S(1)}, bf16[656,128]{1,0:T(8,128)(2,1)S(1)}, u32[]{:S(2)}, u32[]{:S(2)}) %collective-permute-start.10) | collective-permute-done | bytes 167968 | tf_op jit(solution)/shard_map/ppermute | solution.py:345
  24.8 0.0 collective-permute-start.12
  24.8 0.5 %collective-permute-done.6.refs_14_ = bf16[656,128]{1,0:T(8,128)(2,1)S(1)} collective-permute-done((bf16[656,128]{1,0:T(8,128)(2,1)S(1)}, bf16[656,128]{1,0:T(8,128)(2,1)S(1)}, u32[]{:S(2)}, u32[]{:S(2)}) %collective-permute-start.6) | collective-permute-done | bytes 167968 | tf_op jit(solution)/shard_map/ppermute | solution.py:345
  25.3 0.0 collective-permute-start.7
  25.3 1.8 %collective-permute-done.8.refs_15_ = bf16[656,128]{1,0:T(8,128)(2,1)S(1)} collective-permute-done((bf16[656,128]{1,0:T(8,128)(2,1)S(1)}, bf16[656,128]{1,0:T(8,128)(2,1)S(1)}, u32[]{:S(2)}, u32[]{:S(2)}) %collective-permute-start.8) | collective-permute-done | bytes 167968 | tf_op jit(solution)/shard_map/ppermute | solution.py:345
  27.1 0.0 collective-permute-start.9
  27.1 0.0 collective-permute-done.11.refs_16_
  27.1 0.0 collective-permute-done.12.refs_17_
  27.1 1.3 %shard_map.90 = (bf16[128,1024]{1,0:T(8,128)(2,1)S(1)}, bf16[128,1024]{1,0:T(8,128)(2,1)S(1)}, bf16[128,1024]{1,0:T(8,128)(2,1)S(1)}, f32[8,128,128]{2,1,0:T(8,1...) custom-call(bf16[128,2048]{1,0:T(8,128)(2,1)S(1)} %get-tuple-element, ...), custom_call_target="tpu_custom_call" | custom-call | flops 1150000000 | tf_op jit(solution)/shard_map/pallas_call | solution.py:41
  28.4 0.0 collective-permute-done.7.refs_12_
  28.4 0.1 collective-permute-done.9.refs_13_
  28.5 2.0 %shard_map.91 = (bf16[128,2048]{1,0:T(8,128)(2,1)}, bf16[128,2048]{1,0:T(8,128)(2,1)}, bf16[128,2048]{1,0:T(8,128)(2,1)}, f32[16,128,128]{2,1,0:T(8,128)}) custom-call(bf16[128,2048]{1,0:T(8,128)(2,1)S(1)} %get-tuple-element.47.refs_3_.refs_0_, bf16[128,2048]{1,0:T(8,128)(2,1)S(1)} %get-tuple-element.48.refs_2_.refs_1_, ...), custom_call_target="tpu_custom_call" | custom-call | flops 1380000000 | tf_op jit(solution)/shard_map/pallas_call | solution.py:41
  (1 shorter events, 0.0 us)
Async XLA Ops:
  2.8 2.3 %collective-permute-start = (bf16[4,656,128]{2,1,0:T(8,128)(2,1)S(1)}, bf16[4,656,128]{2,1,0:T(8,128)(2,1)S(1)}, u32[]{:S(2)}, u32[]{:S(2)}) collective-permute-start(bf16[4,656,128]{2,1,0:T(8,128)(2,1)S(1)} %get-tuple-element.53), channel_id=1, source_target_pairs={{0,1},{1,0},{2,3},{3,2},{4,5},{5,4},{6,7},{7,6},{8,9},{9,8},{10,11... | collective-permute-start | bytes 2015240 | tf_op jit(solution)/shard_map/ppermute | solution.py:345
  7.4 7.8 %collective-permute-start.3 = (bf16[656,128]{1,0:T(8,128)(2,1)S(1)}, bf16[656,128]{1,0:T(8,128)(2,1)S(1)}, u32[]{:S(2)}, u32[]{:S(2)}) collective-permute-start(bf16[656,128]{1,0:T(8,128)(2,1)S(1)} %get-tuple-element.75), channel_id=1, source_target_pairs={{0,2},{1,3},{2,0},{3,1},{4,6},{5,7},{6,4},{7,5},{8,10},{9,11},{10,... | collective-permute-start | bytes 503816 | tf_op jit(solution)/shard_map/ppermute | solution.py:345
  10.3 8.5 %collective-permute-start.4 = (bf16[656,128]{1,0:T(8,128)(2,1)S(1)}, bf16[656,128]{1,0:T(8,128)(2,1)S(1)}, u32[]{:S(2)}, u32[]{:S(2)}) collective-permute-start(bf16[656,128]{1,0:T(8,128)(2,1)S(1)} %get-tuple-element.76), channel_id=1, source_target_pairs={{0,4},{1,5},{2,6},{3,7},{4,0},{5,1},{6,2},{7,3},{8,12},{9,13},{10,... | collective-permute-start | bytes 503816 | tf_op jit(solution)/shard_map/ppermute | solution.py:345
  11.9 6.9 %collective-permute-start.5 = (bf16[656,128]{1,0:T(8,128)(2,1)S(1)}, bf16[656,128]{1,0:T(8,128)(2,1)S(1)}, u32[]{:S(2)}, u32[]{:S(2)}) collective-permute-start(bf16[656,128]{1,0:T(8,128)(2,1)S(1)} %get-tuple-element.77), channel_id=1, source_target_pairs={{0,6},{1,7},{2,4},{3,5},{4,2},{5,3},{6,0},{7,1},{8,14},{9,15},{10,... | collective-permute-start | bytes 503816 | tf_op jit(solution)/shard_map/ppermute | solution.py:345
  11.9 1.3 %collective-permute-start.1 = (bf16[2,256,128]{2,1,0:T(8,128)(2,1)S(1)}, bf16[2,256,128]{2,1,0:T(8,128)(2,1)S(1)}, u32[]{:S(2)}, u32[]{:S(2)}) collective-permute-start(bf16[2,256,128]{2,1,0:T(8,128)(2,1)S(1)} %get-tuple-element.72), channel_id=1, source_target_pairs={{0,1},{1,0},{2,3},{3,2},{4,5},{5,4},{6,7},{7,6},{8,9},{9,8},{10,11... | collective-permute-start | bytes 393224 | tf_op jit(solution)/shard_map/ppermute | solution.py:345
  11.9 1.5 %collective-permute-start.2 = (bf16[2,256,128]{2,1,0:T(8,128)(2,1)S(1)}, bf16[2,256,128]{2,1,0:T(8,128)(2,1)S(1)}, u32[]{:S(2)}, u32[]{:S(2)}) collective-permute-start(bf16[2,256,128]{2,1,0:T(8,128)(2,1)S(1)} %get-tuple-element.73), channel_id=1, source_target_pairs={{0,1},{1,0},{2,3},{3,2},{4,5},{5,4},{6,7},{7,6},{8,9},{9,8},{10,11... | collective-permute-start | bytes 393224 | tf_op jit(solution)/shard_map/ppermute | solution.py:345
  19.2 5.6 %collective-permute-start.10 = (bf16[656,128]{1,0:T(8,128)(2,1)S(1)}, bf16[656,128]{1,0:T(8,128)(2,1)S(1)}, u32[]{:S(2)}, u32[]{:S(2)}) collective-permute-start(bf16[656,128]{1,0:T(8,128)(2,1)S(1)} %get-tuple-element.81), channel_id=1, source_target_pairs={{0,2},{1,3},{2,0},{3,1},{4,6},{5,7},{6,4},{7,5},{8,10},{9,11},{10,... | collective-permute-start | bytes 503816 | tf_op jit(solution)/shard_map/ppermute | solution.py:345
  19.9 5.4 %collective-permute-start.6 = (bf16[656,128]{1,0:T(8,128)(2,1)S(1)}, bf16[656,128]{1,0:T(8,128)(2,1)S(1)}, u32[]{:S(2)}, u32[]{:S(2)}) collective-permute-start(bf16[656,128]{1,0:T(8,128)(2,1)S(1)} %get-tuple-element.78), channel_id=1, source_target_pairs={{0,4},{1,5},{2,6},{3,7},{4,0},{5,1},{6,2},{7,3},{8,12},{9,13},{10,... | collective-permute-start | bytes 503816 | tf_op jit(solution)/shard_map/ppermute | solution.py:345
  20.7 6.3 %collective-permute-start.8 = (bf16[656,128]{1,0:T(8,128)(2,1)S(1)}, bf16[656,128]{1,0:T(8,128)(2,1)S(1)}, u32[]{:S(2)}, u32[]{:S(2)}) collective-permute-start(bf16[656,128]{1,0:T(8,128)(2,1)S(1)} %get-tuple-element.79), channel_id=1, source_target_pairs={{0,6},{1,7},{2,4},{3,5},{4,2},{5,3},{6,0},{7,1},{8,14},{9,15},{10,... | collective-permute-start | bytes 503816 | tf_op jit(solution)/shard_map/ppermute | solution.py:345
  22.8 4.3 %collective-permute-start.11 = (bf16[656,128]{1,0:T(8,128)(2,1)S(1)}, bf16[656,128]{1,0:T(8,128)(2,1)S(1)}, u32[]{:S(2)}, u32[]{:S(2)}) collective-permute-start(bf16[656,128]{1,0:T(8,128)(2,1)S(1)} %get-tuple-element.80.refs_12_), channel_id=1, source_target_pairs={{0,1},{1,0},{2,3},{3,2},{4,5},{5,4},{6,7},{7,6},{8,9},{9,8},{10,11... | collective-permute-start | bytes 503816 | tf_op jit(solution)/shard_map/ppermute | solution.py:345
  24.8 2.3 %collective-permute-start.12 = (bf16[656,128]{1,0:T(8,128)(2,1)S(1)}, bf16[656,128]{1,0:T(8,128)(2,1)S(1)}, u32[]{:S(2)}, u32[]{:S(2)}) collective-permute-start(bf16[656,128]{1,0:T(8,128)(2,1)S(1)} %collective-permute-done.10.refs_13_), channel_id=1, source_target_pairs={{0,1},{1,0},{2,3},{3,2},{4,5},{5,4},{6,7},{7,6},{8,9},{9,8},{10,11... | collective-permute-start | bytes 503816 | tf_op jit(solution)/shard_map/ppermute | solution.py:345
  25.3 3.1 %collective-permute-start.7 = (bf16[656,128]{1,0:T(8,128)(2,1)S(1)}, bf16[656,128]{1,0:T(8,128)(2,1)S(1)}, u32[]{:S(2)}, u32[]{:S(2)}) collective-permute-start(bf16[656,128]{1,0:T(8,128)(2,1)S(1)} %collective-permute-done.6.refs_14_), channel_id=1, source_target_pairs={{0,1},{1,0},{2,3},{3,2},{4,5},{5,4},{6,7},{7,6},{8,9},{9,8},{10,11... | collective-permute-start | bytes 503816 | tf_op jit(solution)/shard_map/ppermute | solution.py:345
  27.1 1.4 %collective-permute-start.9 = (bf16[656,128]{1,0:T(8,128)(2,1)S(1)}, bf16[656,128]{1,0:T(8,128)(2,1)S(1)}, u32[]{:S(2)}, u32[]{:S(2)}) collective-permute-start(bf16[656,128]{1,0:T(8,128)(2,1)S(1)} %collective-permute-done.8.refs_15_), channel_id=1, source_target_pairs={{0,1},{1,0},{2,3},{3,2},{4,5},{5,4},{6,7},{7,6},{8,9},{9,8},{10,11... | collective-permute-start | bytes 503816 | tf_op jit(solution)/shard_map/ppermute | solution.py:345

commit v8 on v7

--- a/solution.py
+++ b/solution.py
@@ -252,7 +252,7 @@
             out[start + size : start + size + EXTRA] = diagonal.astype(BF16)
 
 
-def finish(pieces, per_owner, scale, shared, sources, near, far):
+def finish(pieces, per_owner, scale, shared, sources, blocks):
     g, v, w, key_w, gram, part_q, part_k, part_v, other, extra = shared
     size = gram.shape[-1]
     core, chip = place()
@@ -260,8 +260,9 @@
     for piece, (which, apart) in enumerate(pieces):
         half = 1 - core if which else core
         for i in range(per_owner):
-            slot = (chip ^ apart) * per_owner + i
-            head = half * GROUPS * per_owner + slot
+            owner = chip ^ apart
+            head = (half * GROUPS + owner) * per_owner + i
+            slot = lax.rem(owner, 2) * per_owner + i
             heads.append((which, apart, i, sources[piece], head, slot))
     ats = [columns(head[4], size) for head in heads]
     prefix, suffix = [], []
@@ -281,12 +282,12 @@
     raw_q = [(part_q[h][a, i] + x).astype(BF16) for x, (h, a, i, *_) in zip(raw_q, heads)]
     raw_k = [(part_k[h, a, i] + x).astype(BF16) for x, (h, a, i, *_) in zip(raw_k, heads)]
     for x, (h, a, i, _, _, to) in zip(raw_v, heads):
-        outs = far if h else near
+        outs = blocks[h]
         outs[2][:, columns(to, size)] = (part_v[h, a, i] + x).astype(BF16)
     done_q = [dot_nn(x, gram[h, a, i]) for x, (h, a, i, *_) in zip(raw_q, heads)]
     done_k = [dot_nn(x, gram[h, a, i]) for x, (h, a, i, *_) in zip(raw_k, heads)]
     for x, y, (h, *_, to) in zip(done_q, done_k, heads):
-        outs = far if h else near
+        outs = blocks[h]
         outs[0][:, columns(to, size)] = x.astype(BF16)
         outs[1][:, columns(to, size)] = y.astype(BF16)
     rows, cols = triangle(size)
@@ -301,41 +302,47 @@
             second = jnp.where(rows == cols, diagonal, second)
             for i, whole in ((2 * pair, first), (2 * pair + 1, second)):
                 which, _, _, _, head, slot = heads[piece * per_owner + i]
-                (far if which else near)[3][slot] = dot_nn(whole.astype(BF16), w[head]) * scale
-
-
-def leave(half, here, outs, sems):
+                blocks[which][3][slot] = dot_nn(whole.astype(BF16), w[head]) * scale
+
+
+def leave(half, turn, here, outs, sems):
+    _, chip = place()
+    block = 2 * half + (lax.div(chip, 2) ^ turn)
     width, count = here[0].shape[1], here[3].shape[0]
     copies = []
     for n in range(4):
-        at = outs[n].at[pl.ds(half * count, count)] if n == 3 else outs[n].at[:, columns(half, width)]
+        at = outs[n].at[pl.ds(block * count, count)] if n == 3 else outs[n].at[:, columns(block, width)]
         copies.append(pltpu.make_async_copy(here[n], at, sems.at[n]))
         copies[-1].start()
     return copies
 
 
-def tail_first_body(pieces, per_owner, scale, *refs):
-    shared, refs = (*refs[:5], refs[5:7], *refs[7:10], refs[10:12]), refs[12:]
-    sources, refs = refs[: len(pieces)], refs[len(pieces) :]
-    finish(pieces, per_owner, scale, shared, sources, refs[:4], refs[4:])
-
-
-def tail_last_body(pieces, per_owner, scale, *refs):
-    shared, refs = (*refs[:5], refs[5:7], *refs[7:10], refs[10:12]), refs[12:]
-    sources, refs = refs[: len(pieces)], refs[len(pieces) :]
+def opened(refs, count):
+    shared = (*refs[:5], refs[5:7], *refs[7:10], refs[10:12])
+    return shared, refs[12 : 12 + count], refs[12 + count :]
+
+
+def tail_first_body(per_owner, scale, *refs):
+    shared, sources, refs = opened(refs, 2)
+    outs, here, sems = refs[:4], refs[4:8], refs[8]
+    core, _ = place()
+    finish([(0, 0), (0, 1)], per_owner, scale, shared, sources, [here, None])
+    for copy in leave(core, 0, here, outs, sems):
+        copy.wait()
+
+
+def tail_second_body(per_owner, scale, *refs):
+    shared, sources, outs = opened(refs, 4)
+    finish([(0, 2), (0, 3), (1, 0), (1, 1)], per_owner, scale, shared, sources, [outs[:4], outs[4:]])
+
+
+def tail_third_body(per_owner, scale, *refs):
+    shared, sources, refs = opened(refs, 2)
     near, far, outs, here, sems = refs[:4], refs[4:8], refs[8:12], refs[12:16], refs[16]
-    core, chip = place()
-    size = here[3].shape[-1]
-    copies = leave(core, near, outs, sems.at[0])
-    for apart in range(GROUPS - len(pieces)):
-        spot = chip ^ apart
-        for n in range(3):
-            at = columns(spot, per_owner * size)
-            here[n][:, at] = far[n][:, at]
-        at = pl.ds(spot * per_owner, per_owner)
-        here[3][at] = far[3][at]
-    finish(pieces, per_owner, scale, shared, sources, None, here)
-    copies += leave(1 - core, here, outs, sems.at[1])
+    core, _ = place()
+    copies = leave(core, 1, near, outs, sems.at[0]) + leave(1 - core, 0, far, outs, sems.at[1])
+    finish([(1, 2), (1, 3)], per_owner, scale, shared, sources, [None, here])
+    copies += leave(1 - core, 1, here, outs, sems.at[2])
     for copy in copies:
         copy.wait()
 
@@ -405,25 +412,36 @@
     outs = [((rows, width), BF16)] * 3 + [((heads,) + block, F32)]
     shared = (here[3], here[2], w, key_w, gram, part_q0, part_q1, part_k, part_v, other)
 
-    half = [((rows, width // 2), BF16)] * 3 + [((heads // 2,) + block, F32)]
+    part = [((rows, width // 4), BF16)] * 3 + [((heads // 4,) + block, F32)]
+    room = [pltpu.VMEM(shape, dtype) for shape, dtype in part]
+    done = call(
+        bind(tail_first_body, per_owner, scale),
+        outs,
+        (*shared, part_q0, part_q0, *near[:2]),
+        1.4,
+        scratch=room + [pltpu.SemaphoreType.DMA((4,))],
+        out_specs=[HBM] * 4,
+    )
+    done = list(done)
+    near[2], done[0] = lax.optimization_barrier((near[2], done[0]))
     far = [swap(x, 1) for x in near]
-    pieces = [(0, n) for n in range(GROUPS)] + [(1, n) for n in range(2)]
-    done = call(
-        bind(tail_first_body, pieces, per_owner, scale),
-        half * 2,
-        (*shared, *extra, *near, *far[:2]),
+    blocks = call(
+        bind(tail_second_body, per_owner, scale),
+        part * 2,
+        (*shared, *extra, *near[2:], *far[:2]),
         1.0,
     )
-    pieces = [(1, n) for n in range(2, GROUPS)]
+    operands = (*shared, *extra, *far[2:], *blocks)
     return tuple(
         call(
-            bind(tail_last_body, pieces, per_owner, scale),
+            bind(tail_third_body, per_owner, scale),
             outs,
-            (*shared, *extra, *far[2:], *done),
+            operands,
             1.2,
-            scratch=[pltpu.VMEM(shape, dtype) for shape, dtype in half]
-            + [pltpu.SemaphoreType.DMA((2, 4))],
+            after=tuple(done),
+            scratch=room + [pltpu.SemaphoreType.DMA((3, 4))],
             out_specs=[HBM] * 4,
+            aliases={len(operands) + n: n for n in range(4)},
         )
     )
 

time: 30.7 us -> 30.6 us (level)
  waiting for transfers between devices: 11.7 us -> 10.6 us
  Pallas kernels: 9.05 us -> 9.63 us
  starting transfers between devices: 9.08 us -> 9.56 us
    ppermute x13, waiting for transfers between devices: 11.7 us -> 10.6 us  [swap(): return lax.ppermute(x, 'ctx', [(i, i ^ apart) for i in range(count)])]
    pallas_call x8 -> x9, Pallas kernels: 9.05 us -> 9.63 us  [call(): pl.pallas_call(run, out_shape=[jax.ShapeDtypeStruct(shape, dtype) for sha...]
    ppermute x13, starting transfers between devices: 9.08 us -> 9.56 us  [swap(): return lax.ppermute(x, 'ctx', [(i, i ^ apart) for i in range(count)])]
  transfers between devices with their start and end apart: 13 -> 13, of which waited for: 9 -> 8; matrix products, arithmetic and copies ran while one was open for 0% -> 0% of each run, Pallas kernels for 7% -> 10%
where the time goes in v8:
time: 30.6 us; the launch traced here: 30.5 us
  waiting for transfers between devices  10.6 us (35%)
  Pallas kernels  9.63 us (31%)
  starting transfers between devices  9.56 us (31%)
  between operations  0.69 us (2%)
    ppermute x13, waiting for transfers between devices, swap(): return lax.ppermute(x, 'ctx', [(i, i ^ apart) for i in range(count)])  10.6 us
    pallas_call x9, Pallas kernels, call(): pl.pallas_call(run, out_shape=[jax.ShapeDtypeStruct(shape, dtype) for sha...  9.63 us
    ppermute x13, starting transfers between devices, swap(): return lax.ppermute(x, 'ctx', [(i, i ^ apart) for i in range(count)])  9.56 us
  transfers between devices with their start and end apart: 13, of which 8 were waited for; matrix products, arithmetic and copies ran while one was open for 0% of the time, Pallas kernels for 10%

profile of v8, /device:TPU:0, one launch (start us, length us, event | category | flops | bytes accessed | tf_op | source)
XLA Modules:
  0.0 30.5 jit_solution(4489002780830469713)
XLA Ops:
  0.6 2.2 %shard_map.84 = (bf16[128,2048]{1,0:T(8,128)(2,1)S(1)}, bf16[128,2048]{1,0:T(8,128)(2,1)S(1)}, bf16[128,2048]{1,0:T(8,128)(2,1)S(1)}, bf16[128,2048]{1,0:T(8,128...) custom-call(bf16[128,2048]{1,0:T(8,128)(2,1)} %refs_0_.1, ...), custom_call_target="tpu_custom_call" | custom-call | flops 2300000000 | tf_op jit(solution)/shard_map/pallas_call | solution.py:41
  2.8 0.5 %collective-permute-start = (bf16[4,656,128]{2,1,0:T(8,128)(2,1)S(1)}, bf16[4,656,128]{2,1,0:T(8,128)(2,1)S(1)}, u32[]{:S(2)}, u32[]{:S(2)}) collective-permute-start(bf16[4,656,128]{2,1,0:T(8,128)(2,1)S(1)} %get-tuple-element.59), channel_id=1, source_target_pairs={{0,1},{1,0},{2,3},{3,2},{4,5},{5,4},{6,7},{7,6},{8,9},{9,8},{10,11... | collective-permute-start | bytes 2015240 | tf_op jit(solution)/shard_map/ppermute | solution.py:352
  3.4 0.8 %shard_map.85 = (bf16[4,656,128]{2,1,0:T(8,128)(2,1)S(1)}, bf16[2,256,128]{2,1,0:T(8,128)(2,1)S(1)}, bf16[2,256,128]{2,1,0:T(8,128)(2,1)S(1)}, f32[4,2,128,128]{3,2,1,0:T(8,128)S(1)}) custom-call(bf16[128,2048]{1,0:T(8,128)(2,1)S(1)} %get-tuple-element.56.refs_0_, bf16[128,2048]{1,0:T(8,128)(2,1)S(1)} %get-tuple-element.57.refs_1_, ...), custom_call_target="tpu_custom_call" | custom-call | flops 1150000000 | tf_op jit(solution)/shard_map/pallas_call | solution.py:41
  4.2 0.9 %collective-permute-done.refs_1_.refs_9_ = bf16[4,656,128]{2,1,0:T(8,128)(2,1)S(1)} collective-permute-done((bf16[4,656,128]{2,1,0:T(8,128)(2,1)S(1)}, bf16[4,656,128]{2,1,0:T(8,128)(2,1)S(1)}, u32[]{:S(2)}, u32[]{:S(2)}) %collective-permute-start) | collective-permute-done | bytes 671776 | tf_op jit(solution)/shard_map/ppermute | solution.py:352
  5.1 0.5 %shard_map.86 = (bf16[656,128]{1,0:T(8,128)(2,1)S(1)}, bf16[656,128]{1,0:T(8,128)(2,1)S(1)}, bf16[656,128]{1,0:T(8,128)(2,1)S(1)}, bf16[656,128]{1,0:T(8,128)(2,1)S(1)}) custom-call(bf16[4,656,128]{2,1,0:T(8,128)(2,1)S(1)} %get-tuple-element.58.refs_0_, bf16[4,656,128]{2,1,0:T(8,128)(2,1)S(1)} %collective-permute-done.refs_1_.refs_9_), custom_call_target="tpu_custom_call" | custom-call | flops 460000000 | tf_op jit(solution)/shard_map/pallas_call | solution.py:41
  5.6 1.8 %shard_map.87 = (f32[2,4,2,128,128]{4,3,2,1,0:T(8,128)S(1)}, f32[2,4,2,128,128]{4,3,2,1,0:T(8,128)S(1)}, bf16[2,4,2,128,128]{4,3,2,1,0:T(8,128)(2,1)S(1)}, bf16[2,4,2,128,128]{4,3,2,1,0:T(8,128)(2,1)S(1)}) custom-call(bf16[128,2048]{1,0:T(8,128)(2,1)S(1)} %get-tuple-element.56.refs_0_, bf16[128,2048]{1,0:T(8,128)(2,1)S(1)} %get-tuple-element.57.refs_1_, ...), custom_call_target="tpu_custom_call" | custom-call | flops 2070000000 | tf_op jit(solution)/shard_map/pallas_call | solution.py:41
  7.4 2.9 %collective-permute-start.3 = (bf16[656,128]{1,0:T(8,128)(2,1)S(1)}, bf16[656,128]{1,0:T(8,128)(2,1)S(1)}, u32[]{:S(2)}, u32[]{:S(2)}) collective-permute-start(bf16[656,128]{1,0:T(8,128)(2,1)S(1)} %get-tuple-element.81), channel_id=1, source_target_pairs={{0,2},{1,3},{2,0},{3,1},{4,6},{5,7},{6,4},{7,5},{8,10},{9,11},{10,... | collective-permute-start | bytes 503816 | tf_op jit(solution)/shard_map/ppermute | solution.py:352
  10.3 1.5 %collective-permute-start.4 = (bf16[656,128]{1,0:T(8,128)(2,1)S(1)}, bf16[656,128]{1,0:T(8,128)(2,1)S(1)}, u32[]{:S(2)}, u32[]{:S(2)}) collective-permute-start(bf16[656,128]{1,0:T(8,128)(2,1)S(1)} %get-tuple-element.82), channel_id=1, source_target_pairs={{0,4},{1,5},{2,6},{3,7},{4,0},{5,1},{6,2},{7,3},{8,12},{9,13},{10,... | collective-permute-start | bytes 503816 | tf_op jit(solution)/shard_map/ppermute | solution.py:352
  11.8 0.0 collective-permute-start.5
  11.9 0.0 collective-permute-start.1
  11.9 0.5 %collective-permute-start.2 = (bf16[2,256,128]{2,1,0:T(8,128)(2,1)S(1)}, bf16[2,256,128]{2,1,0:T(8,128)(2,1)S(1)}, u32[]{:S(2)}, u32[]{:S(2)}) collective-permute-start(bf16[2,256,128]{2,1,0:T(8,128)(2,1)S(1)} %get-tuple-element.79), channel_id=1, source_target_pairs={{0,1},{1,0},{2,3},{3,2},{4,5},{5,4},{6,7},{7,6},{8,9},{9,8},{10,11... | collective-permute-start | bytes 393224 | tf_op jit(solution)/shard_map/ppermute | solution.py:352
  12.4 0.8 %collective-permute-done.1.refs_5_.refs_10_ = bf16[2,256,128]{2,1,0:T(8,128)(2,1)S(1)} collective-permute-done((bf16[2,256,128]{2,1,0:T(8,128)(2,1)S(1)}, bf16[2,256,128]{2,1,0:T(8,128)(2,1)S(1)}, u32[]{:S(2)}, u32[]{:S(2)}) %collective-permute-start.1) | collective-permute-done | bytes 131104 | tf_op jit(solution)/shard_map/ppermute | solution.py:352
  13.2 0.2 collective-permute-done.2.refs_6_.refs_11_
  13.4 1.8 %collective-permute-done.3.refs_1_ = bf16[656,128]{1,0:T(8,128)(2,1)S(1)} collective-permute-done((bf16[656,128]{1,0:T(8,128)(2,1)S(1)}, bf16[656,128]{1,0:T(8,128)(2,1)S(1)}, u32[]{:S(2)}, u32[]{:S(2)}) %collective-permute-start.3) | collective-permute-done | bytes 167968 | tf_op jit(solution)/shard_map/ppermute | solution.py:352
  15.1 3.6 %collective-permute-done.4.refs_2_ = bf16[656,128]{1,0:T(8,128)(2,1)S(1)} collective-permute-done((bf16[656,128]{1,0:T(8,128)(2,1)S(1)}, bf16[656,128]{1,0:T(8,128)(2,1)S(1)}, u32[]{:S(2)}, u32[]{:S(2)}) %collective-permute-start.4) | collective-permute-done | bytes 167968 | tf_op jit(solution)/shard_map/ppermute | solution.py:352
  18.8 0.0 collective-permute-done.5.refs_3_
  18.8 0.4 %shard_map.89 = (bf16[656,128]{1,0:T(8,128)(2,1)S(1)}, bf16[656,128]{1,0:T(8,128)(2,1)S(1)}, bf16[656,128]{1,0:T(8,128)(2,1)S(1)}, bf16[656,128]{1,0:T(8,128)(2,1)S(1)}) custom-call(bf16[656,128]{1,0:T(8,128)(2,1)S(1)} %get-tuple-element.80.refs_5_.refs_0_, bf16[656,128]{1,0:T(8,128)(2,1)S(1)} %collective-permute-done.3.refs_1_, ...), custom_call_target="tpu_custom_call" | custom-call | flops 575000000 | tf_op jit(solution)/shard_map/pallas_call | solution.py:41
  19.2 0.7 %collective-permute-start.7 = (bf16[656,128]{1,0:T(8,128)(2,1)S(1)}, bf16[656,128]{1,0:T(8,128)(2,1)S(1)}, u32[]{:S(2)}, u32[]{:S(2)}) collective-permute-start(bf16[656,128]{1,0:T(8,128)(2,1)S(1)} %get-tuple-element.86), channel_id=1, source_target_pairs={{0,2},{1,3},{2,0},{3,1},{4,6},{5,7},{6,4},{7,5},{8,10},{9,11},{10,... | collective-permute-start | bytes 503816 | tf_op jit(solution)/shard_map/ppermute | solution.py:352
  19.9 0.8 %collective-permute-start.6 = (bf16[656,128]{1,0:T(8,128)(2,1)S(1)}, bf16[656,128]{1,0:T(8,128)(2,1)S(1)}, u32[]{:S(2)}, u32[]{:S(2)}) collective-permute-start(bf16[656,128]{1,0:T(8,128)(2,1)S(1)} %get-tuple-element.84), channel_id=1, source_target_pairs={{0,4},{1,5},{2,6},{3,7},{4,0},{5,1},{6,2},{7,3},{8,12},{9,13},{10,... | collective-permute-start | bytes 503816 | tf_op jit(solution)/shard_map/ppermute | solution.py:352
  20.7 2.0 %collective-permute-start.9 = (bf16[656,128]{1,0:T(8,128)(2,1)S(1)}, bf16[656,128]{1,0:T(8,128)(2,1)S(1)}, u32[]{:S(2)}, u32[]{:S(2)}) collective-permute-start(bf16[656,128]{1,0:T(8,128)(2,1)S(1)} %get-tuple-element.89), channel_id=1, source_target_pairs={{0,6},{1,7},{2,4},{3,5},{4,2},{5,3},{6,0},{7,1},{8,14},{9,15},{10,... | collective-permute-start | bytes 503816 | tf_op jit(solution)/shard_map/ppermute | solution.py:352
  22.8 0.0 collective-permute-start.11
  22.8 2.0 %collective-permute-done.7.refs_13_ = bf16[656,128]{1,0:T(8,128)(2,1)S(1)} collective-permute-done((bf16[656,128]{1,0:T(8,128)(2,1)S(1)}, bf16[656,128]{1,0:T(8,128)(2,1)S(1)}, u32[]{:S(2)}, u32[]{:S(2)}) %collective-permute-start.7) | collective-permute-done | bytes 167968 | tf_op jit(solution)/shard_map/ppermute | solution.py:352
  24.8 0.0 collective-permute-start.12
  24.8 1.3 %shard_map.90 = (bf16[128,2048]{1,0:T(8,128)(2,1)}, bf16[128,2048]{1,0:T(8,128)(2,1)}, bf16[128,2048]{1,0:T(8,128)(2,1)}, f32[16,128,128]{2,1,0:T(8,128)}) custom-call(bf16[128,2048]{1,0:T(8,128)(2,1)S(1)} %get-tuple-element.53.refs_3_.refs_0_, bf16[128,2048]{1,0:T(8,128)(2,1)S(1)} %get-tuple-element.54.refs_2_.refs_1_, ...), custom_call_target="tpu_custom_call" | custom-call | flops 1610000000 | tf_op jit(solution)/shard_map/pallas_call | solution.py:41
  26.1 0.0 collective-permute-done.6.refs_12_
  26.1 1.0 %collective-permute-done.9.refs_13_ = bf16[656,128]{1,0:T(8,128)(2,1)S(1)} collective-permute-done((bf16[656,128]{1,0:T(8,128)(2,1)S(1)}, bf16[656,128]{1,0:T(8,128)(2,1)S(1)}, u32[]{:S(2)}, u32[]{:S(2)}) %collective-permute-start.9) | collective-permute-done | bytes 167968 | tf_op jit(solution)/shard_map/ppermute | solution.py:352
  27.1 0.0 collective-permute-start.10
  27.1 0.5 %collective-permute-start.8 = (bf16[656,128]{1,0:T(8,128)(2,1)S(1)}, bf16[656,128]{1,0:T(8,128)(2,1)S(1)}, u32[]{:S(2)}, u32[]{:S(2)}) collective-permute-start(bf16[656,128]{1,0:T(8,128)(2,1)S(1)} %collective-permute-done.6.refs_12_), channel_id=1, source_target_pairs={{0,1},{1,0},{2,3},{3,2},{4,5},{5,4},{6,7},{7,6},{8,9},{9,8},{10,11... | collective-permute-start | bytes 503816 | tf_op jit(solution)/shard_map/ppermute | solution.py:352
  27.6 0.0 collective-permute-done.11.refs_14_
  27.6 0.0 collective-permute-done.12.refs_15_
  27.6 0.8 %shard_map.91 = (bf16[128,512]{1,0:T(8,128)(2,1)S(1)}, bf16[128,512]{1,0:T(8,128)(2,1)S(1)}, bf16[128,512]{1,0:T(8,128)(2,1)S(1)}, f32[4,128,128]{2,1,0:T(8,128)...) custom-call(bf16[128,2048]{1,0:T(8,128)(2,1)S(1)} %get-tuple-element, ...), custom_call_target="tpu_custom_call" | custom-call | flops 1150000000 | tf_op jit(solution)/shard_map/pallas_call | solution.py:41
  28.4 0.0 collective-permute-done.10.refs_13_
  28.5 0.2 collective-permute-done.8.refs_12_
  28.7 1.8 %shard_map.92 = (bf16[128,2048]{1,0:T(8,128)(2,1)}, bf16[128,2048]{1,0:T(8,128)(2,1)}, bf16[128,2048]{1,0:T(8,128)(2,1)}, f32[16,128,128]{2,1,0:T(8,128)}) custom-call(bf16[128,2048]{1,0:T(8,128)(2,1)S(1)} %get-tuple-element.53.refs_3_.refs_0_, ...), custom_call_target="tpu_custom_call", output_to_operand_aliasing={{0}: (22, {}), {1}: (23, {}), {2}: (24, {}), {3}: (25, {})} | custom-call | flops 1380000000 | tf_op jit(solution)/shard_map/pallas_call | solution.py:41
  (1 shorter events, 0.0 us)
Async XLA Ops:
  2.8 2.3 %collective-permute-start = (bf16[4,656,128]{2,1,0:T(8,128)(2,1)S(1)}, bf16[4,656,128]{2,1,0:T(8,128)(2,1)S(1)}, u32[]{:S(2)}, u32[]{:S(2)}) collective-permute-start(bf16[4,656,128]{2,1,0:T(8,128)(2,1)S(1)} %get-tuple-element.59), channel_id=1, source_target_pairs={{0,1},{1,0},{2,3},{3,2},{4,5},{5,4},{6,7},{7,6},{8,9},{9,8},{10,11... | collective-permute-start | bytes 2015240 | tf_op jit(solution)/shard_map/ppermute | solution.py:352
  7.4 7.8 %collective-permute-start.3 = (bf16[656,128]{1,0:T(8,128)(2,1)S(1)}, bf16[656,128]{1,0:T(8,128)(2,1)S(1)}, u32[]{:S(2)}, u32[]{:S(2)}) collective-permute-start(bf16[656,128]{1,0:T(8,128)(2,1)S(1)} %get-tuple-element.81), channel_id=1, source_target_pairs={{0,2},{1,3},{2,0},{3,1},{4,6},{5,7},{6,4},{7,5},{8,10},{9,11},{10,... | collective-permute-start | bytes 503816 | tf_op jit(solution)/shard_map/ppermute | solution.py:352
  10.3 8.5 %collective-permute-start.4 = (bf16[656,128]{1,0:T(8,128)(2,1)S(1)}, bf16[656,128]{1,0:T(8,128)(2,1)S(1)}, u32[]{:S(2)}, u32[]{:S(2)}) collective-permute-start(bf16[656,128]{1,0:T(8,128)(2,1)S(1)} %get-tuple-element.82), channel_id=1, source_target_pairs={{0,4},{1,5},{2,6},{3,7},{4,0},{5,1},{6,2},{7,3},{8,12},{9,13},{10,... | collective-permute-start | bytes 503816 | tf_op jit(solution)/shard_map/ppermute | solution.py:352
  11.8 6.9 %collective-permute-start.5 = (bf16[656,128]{1,0:T(8,128)(2,1)S(1)}, bf16[656,128]{1,0:T(8,128)(2,1)S(1)}, u32[]{:S(2)}, u32[]{:S(2)}) collective-permute-start(bf16[656,128]{1,0:T(8,128)(2,1)S(1)} %get-tuple-element.83), channel_id=1, source_target_pairs={{0,6},{1,7},{2,4},{3,5},{4,2},{5,3},{6,0},{7,1},{8,14},{9,15},{10,... | collective-permute-start | bytes 503816 | tf_op jit(solution)/shard_map/ppermute | solution.py:352
  11.9 1.3 %collective-permute-start.1 = (bf16[2,256,128]{2,1,0:T(8,128)(2,1)S(1)}, bf16[2,256,128]{2,1,0:T(8,128)(2,1)S(1)}, u32[]{:S(2)}, u32[]{:S(2)}) collective-permute-start(bf16[2,256,128]{2,1,0:T(8,128)(2,1)S(1)} %get-tuple-element.78), channel_id=1, source_target_pairs={{0,1},{1,0},{2,3},{3,2},{4,5},{5,4},{6,7},{7,6},{8,9},{9,8},{10,11... | collective-permute-start | bytes 393224 | tf_op jit(solution)/shard_map/ppermute | solution.py:352
  11.9 1.5 %collective-permute-start.2 = (bf16[2,256,128]{2,1,0:T(8,128)(2,1)S(1)}, bf16[2,256,128]{2,1,0:T(8,128)(2,1)S(1)}, u32[]{:S(2)}, u32[]{:S(2)}) collective-permute-start(bf16[2,256,128]{2,1,0:T(8,128)(2,1)S(1)} %get-tuple-element.79), channel_id=1, source_target_pairs={{0,1},{1,0},{2,3},{3,2},{4,5},{5,4},{6,7},{7,6},{8,9},{9,8},{10,11... | collective-permute-start | bytes 393224 | tf_op jit(solution)/shard_map/ppermute | solution.py:352
  19.2 5.6 %collective-permute-start.7 = (bf16[656,128]{1,0:T(8,128)(2,1)S(1)}, bf16[656,128]{1,0:T(8,128)(2,1)S(1)}, u32[]{:S(2)}, u32[]{:S(2)}) collective-permute-start(bf16[656,128]{1,0:T(8,128)(2,1)S(1)} %get-tuple-element.86), channel_id=1, source_target_pairs={{0,2},{1,3},{2,0},{3,1},{4,6},{5,7},{6,4},{7,5},{8,10},{9,11},{10,... | collective-permute-start | bytes 503816 | tf_op jit(solution)/shard_map/ppermute | solution.py:352
  19.9 6.2 %collective-permute-start.6 = (bf16[656,128]{1,0:T(8,128)(2,1)S(1)}, bf16[656,128]{1,0:T(8,128)(2,1)S(1)}, u32[]{:S(2)}, u32[]{:S(2)}) collective-permute-start(bf16[656,128]{1,0:T(8,128)(2,1)S(1)} %get-tuple-element.84), channel_id=1, source_target_pairs={{0,4},{1,5},{2,6},{3,7},{4,0},{5,1},{6,2},{7,3},{8,12},{9,13},{10,... | collective-permute-start | bytes 503816 | tf_op jit(solution)/shard_map/ppermute | solution.py:352
  20.7 6.3 %collective-permute-start.9 = (bf16[656,128]{1,0:T(8,128)(2,1)S(1)}, bf16[656,128]{1,0:T(8,128)(2,1)S(1)}, u32[]{:S(2)}, u32[]{:S(2)}) collective-permute-start(bf16[656,128]{1,0:T(8,128)(2,1)S(1)} %get-tuple-element.89), channel_id=1, source_target_pairs={{0,6},{1,7},{2,4},{3,5},{4,2},{5,3},{6,0},{7,1},{8,14},{9,15},{10,... | collective-permute-start | bytes 503816 | tf_op jit(solution)/shard_map/ppermute | solution.py:352
  22.8 4.8 %collective-permute-start.11 = (bf16[656,128]{1,0:T(8,128)(2,1)S(1)}, bf16[656,128]{1,0:T(8,128)(2,1)S(1)}, u32[]{:S(2)}, u32[]{:S(2)}) collective-permute-start(bf16[656,128]{1,0:T(8,128)(2,1)S(1)} %get-tuple-element.85.refs_12_), channel_id=1, source_target_pairs={{0,1},{1,0},{2,3},{3,2},{4,5},{5,4},{6,7},{7,6},{8,9},{9,8},{10,11... | collective-permute-start | bytes 503816 | tf_op jit(solution)/shard_map/ppermute | solution.py:352
  24.8 2.8 %collective-permute-start.12 = (bf16[656,128]{1,0:T(8,128)(2,1)S(1)}, bf16[656,128]{1,0:T(8,128)(2,1)S(1)}, u32[]{:S(2)}, u32[]{:S(2)}) collective-permute-start(bf16[656,128]{1,0:T(8,128)(2,1)S(1)} %collective-permute-done.7.refs_13_), channel_id=1, source_target_pairs={{0,1},{1,0},{2,3},{3,2},{4,5},{5,4},{6,7},{7,6},{8,9},{9,8},{10,11... | collective-permute-start | bytes 503816 | tf_op jit(solution)/shard_map/ppermute | solution.py:352
  27.1 1.4 %collective-permute-start.10 = (bf16[656,128]{1,0:T(8,128)(2,1)S(1)}, bf16[656,128]{1,0:T(8,128)(2,1)S(1)}, u32[]{:S(2)}, u32[]{:S(2)}) collective-permute-start(bf16[656,128]{1,0:T(8,128)(2,1)S(1)} %collective-permute-done.9.refs_13_), channel_id=1, source_target_pairs={{0,1},{1,0},{2,3},{3,2},{4,5},{5,4},{6,7},{7,6},{8,9},{9,8},{10,11... | collective-permute-start | bytes 503816 | tf_op jit(solution)/shard_map/ppermute | solution.py:352
  27.1 1.6 %collective-permute-start.8 = (bf16[656,128]{1,0:T(8,128)(2,1)S(1)}, bf16[656,128]{1,0:T(8,128)(2,1)S(1)}, u32[]{:S(2)}, u32[]{:S(2)}) collective-permute-start(bf16[656,128]{1,0:T(8,128)(2,1)S(1)} %collective-permute-done.6.refs_12_), channel_id=1, source_target_pairs={{0,1},{1,0},{2,3},{3,2},{4,5},{5,4},{6,7},{7,6},{8,9},{9,8},{10,11... | collective-permute-start | bytes 503816 | tf_op jit(solution)/shard_map/ppermute | solution.py:352

commit v9 on v8

--- a/solution.py
+++ b/solution.py
@@ -66,6 +66,11 @@
     ]
 
 
+def pick(refs, apart):
+    group, place_ = ((1, 0), (0, 0), (1, 1), (0, 1))[apart]
+    return refs[group].at[place_]
+
+
 def columns(head, size):
     return pl.ds(pl.multiple_of(head * size, size), size)
 
@@ -76,7 +81,8 @@
     return rows, cols
 
 
-def load_body(per_owner, q, k, v, g, w, q_here, k_here, v_here, g_here, w_here, send, part_q, sems):
+def load_body(per_owner, q, k, v, g, w, q_here, k_here, v_here, g_here, w_here, *refs):
+    send, part_q, sems = refs[:2], refs[2], refs[3]
     half_width = q.shape[1] // 2
     core, chip = place()
     pairs = ((g, g_here), (v, v_here), (k, k_here), (q, q_here))
@@ -97,7 +103,7 @@
 
 
 def states(out, part_q, heads, q, k, v, g, copies=()):
-    size = out.shape[-1]
+    size = out[0].shape[-1]
     per_owner = len(heads) // GROUPS
     rows, cols = triangle(q.shape[0])
     ats = [columns(head, size) for _, _, head in heads]
@@ -111,7 +117,7 @@
     early = [dot_tn(k[:, at], v[:, at]) for at in ats]
     for n, (apart, i, _) in enumerate(heads):
         part_q[apart, i] = mixed[n]
-        out[apart, i * size : (i + 1) * size] = early[n].astype(BF16)
+        pick(out, apart)[i * size : (i + 1) * size] = early[n].astype(BF16)
     for copy in copies[3:]:
         copy.wait()
     wide = [
@@ -119,23 +125,25 @@
         for x, at in zip(mixed, ats)
     ]
     for n, (apart, i, _) in enumerate(heads):
-        out[apart, (per_owner + i) * size : (per_owner + i + 1) * size] = wide[n][:, :size].astype(BF16)
+        to = pick(out, apart)
+        to[(per_owner + i) * size : (per_owner + i + 1) * size] = wide[n][:, :size].astype(BF16)
         if i % 2:
             both, diagonal = pack(wide[n - 1][:, size:], wide[n][:, size:])
             start = 2 * per_owner * size + (i // 2) * (size + EXTRA)
-            out[apart, start : start + size] = both.astype(BF16)
-            out[apart, start + size : start + size + EXTRA] = diagonal.astype(BF16)
-
-
-def near_body(per_owner, q, k, v, g, own, *refs):
-    size = own.shape[-1]
+            to[start : start + size] = both.astype(BF16)
+            to[start + size : start + size + EXTRA] = diagonal.astype(BF16)
+
+
+def near_body(per_owner, q, k, v, g, *refs):
+    own, extra, part_q = refs[:2], refs[2:4], refs[4]
+    size = own[0].shape[-1]
     core, chip = place()
     heads = owned(core, chip, per_owner)
-    states(own, refs[2], heads, q, k, v, g)
+    states(own, part_q, heads, q, k, v, g)
     for apart in range(GROUPS):
-        early = own[apart, : per_owner * size]
-        late = own[apart, per_owner * size : 2 * per_owner * size]
-        refs[apart // 2][apart % 2] = jnp.where(core == 0, early, late)
+        early = pick(own, apart)[: per_owner * size]
+        late = pick(own, apart)[per_owner * size : 2 * per_owner * size]
+        extra[apart // 2][apart % 2] = jnp.where(core == 0, early, late)
 
 
 def pack(first, second):
@@ -153,14 +161,14 @@
     core, _ = place()
     last = core == 1
     totals = []
-    for apart in range(GROUPS):
+    for apart in range(len(outs)):
         for i in range(per_owner):
             ahead = slice(i * size, (i + 1) * size)
             behind = slice((per_owner + i) * size, (per_owner + i + 1) * size)
             early = jnp.where(last, other[apart, ahead], own[apart, ahead])
             late = jnp.where(last, own[apart, behind], other[apart, behind])
             totals.append(dot_nt(late, early))
-    for apart in range(GROUPS):
+    for apart in range(len(outs)):
         outs[apart][:count] = own[apart, :count] + other[apart, :count]
         for pair in range(per_owner // 2):
             both, diagonal = pack(*totals[apart * per_owner + 2 * pair :][:2])
@@ -272,7 +280,7 @@
         if which:
             early = late = extra[apart // 2][apart % 2, ahead]
         else:
-            early, late = other[apart, ahead], other[apart, behind]
+            early, late = pick(other, apart)[ahead], pick(other, apart)[behind]
         before, after = source[ahead], source[behind]
         prefix.append(before + jnp.where(core == 1, early, jnp.zeros_like(early)))
         suffix.append(after + jnp.where(core == 0, late, jnp.zeros_like(late)))
@@ -318,8 +326,8 @@
 
 
 def opened(refs, count):
-    shared = (*refs[:5], refs[5:7], *refs[7:10], refs[10:12])
-    return shared, refs[12 : 12 + count], refs[12 + count :]
+    shared = (*refs[:5], refs[5:7], *refs[7:9], refs[9:11], refs[11:13])
+    return shared, refs[13 : 13 + count], refs[13 + count :]
 
 
 def tail_first_body(per_owner, scale, *refs):
@@ -361,31 +369,35 @@
     one = (GROUPS, per_owner) + block
     twice = (2,) + one
     payload = (2 * per_owner * size + (per_owner // 2) * (size + EXTRA), size)
-    payloads = (GROUPS,) + payload
+    payloads = (GROUPS // 2,) + payload
     bind = functools.partial
 
-    *here, w, send, part_q1 = call(
+    *here, w, send_near, send_rest, part_q1 = call(
         bind(load_body, per_owner),
-        [((rows, width), BF16)] * 4 + [(w.shape, BF16), (payloads, BF16), (one, F32)],
+        [((rows, width), BF16)] * 4 + [(w.shape, BF16), (payloads, BF16), (payloads, BF16), (one, F32)],
         [pltpu.with_memory_space_constraint(x, pltpu.HBM) for x in (q, k, v, g, w)],
         2.0,
         in_spec=[HBM] * 5,
         scratch=[pltpu.SemaphoreType.DMA((3, 4))],
     )
-    other = swap(send, 1)
-    own, *extra, part_q0 = call(
+    other = [swap(x, 1) for x in (send_near, send_rest)]
+    *own, extra_a, extra_b, part_q0 = call(
         bind(near_body, per_owner),
-        [(payloads, BF16), *[((GROUPS // 2, per_owner * size, size), BF16)] * 2, (one, F32)],
+        [(payloads, BF16)] * 2
+        + [*[((GROUPS // 2, per_owner * size, size), BF16)] * 2, (one, F32)],
         here,
         1.0,
     )
-    chip_sums = call(bind(join_body, per_owner), [(payload, BF16)] * GROUPS, (own, other), 0.4)
+    extra = [extra_a, extra_b]
+    join = bind(join_body, per_owner)
+    near_sums = call(join, [(payload, BF16)] * 2, (own[0], other[0]), 0.3)
     locals_ = [(twice, F32), (twice, F32), (twice, BF16), (twice, BF16)]
     local = list(
-        call(bind(rest_first_body, per_owner), locals_, (*here, w), 1.8, after=chip_sums[:1])
-    )
-    held = lax.optimization_barrier((*chip_sums, local[0]))
-    chip_sums, local[0] = list(held[:GROUPS]), held[GROUPS]
+        call(bind(rest_first_body, per_owner), locals_, (*here, w), 1.8, after=near_sums[:1])
+    )
+    *near_sums, local[0] = lax.optimization_barrier((*near_sums, local[0]))
+    rest_sums = call(join, [(payload, BF16)] * 2, (own[1], other[1]), 0.2, after=near_sums[:1])
+    chip_sums = [rest_sums[0], near_sums[0], rest_sums[1], near_sums[1]]
     parts = [chip_sums[0]] + [swap(chip_sums[j], 2 * j) for j in range(1, GROUPS)]
     local = call(
         bind(rest_second_body, per_owner),
@@ -410,7 +422,7 @@
     near = [carried[0]] + [swap(carried[j], 2 * j) for j in range(1, GROUPS)]
     scale = 1.0 / math.sqrt(length)
     outs = [((rows, width), BF16)] * 3 + [((heads,) + block, F32)]
-    shared = (here[3], here[2], w, key_w, gram, part_q0, part_q1, part_k, part_v, other)
+    shared = (here[3], here[2], w, key_w, gram, part_q0, part_q1, part_k, part_v, *other)
 
     part = [((rows, width // 4), BF16)] * 3 + [((heads // 4,) + block, F32)]
     room = [pltpu.VMEM(shape, dtype) for shape, dtype in part]

time: 30.6 us -> 30.5 us (level)
  waiting for transfers between devices: 10.6 us -> 10.1 us
    ppermute x13 -> x14, waiting for transfers between devices: 10.6 us -> 10.1 us  [swap(): return lax.ppermute(x, 'ctx', [(i, i ^ apart) for i in range(count)])]
    pallas_call x9 -> x10, Pallas kernels: 9.63 us -> 9.83 us  [call(): pl.pallas_call(run, out_shape=[jax.ShapeDtypeStruct(shape, dtype) for sha...]
    ppermute x13 -> x14, starting transfers between devices: 9.56 us -> 9.73 us  [swap(): return lax.ppermute(x, 'ctx', [(i, i ^ apart) for i in range(count)])]
  transfers between devices with their start and end apart: 13 -> 14, of which waited for: 8 -> 7; matrix products, arithmetic and copies ran while one was open for 0% -> 0% of each run, Pallas kernels for 10% -> 18%
where the time goes in v9:
time: 30.5 us; the launch traced here: 30.4 us
  waiting for transfers between devices  10.1 us (33%)
  Pallas kernels  9.83 us (32%)
  starting transfers between devices  9.73 us (32%)
  between operations  0.69 us (2%)
    ppermute x14, waiting for transfers between devices, swap(): return lax.ppermute(x, 'ctx', [(i, i ^ apart) for i in range(count)])  10.1 us
    pallas_call x10, Pallas kernels, call(): pl.pallas_call(run, out_shape=[jax.ShapeDtypeStruct(shape, dtype) for sha...  9.83 us
    ppermute x14, starting transfers between devices, swap(): return lax.ppermute(x, 'ctx', [(i, i ^ apart) for i in range(count)])  9.73 us
  transfers between devices with their start and end apart: 14, of which 7 were waited for; matrix products, arithmetic and copies ran while one was open for 0% of the time, Pallas kernels for 18%

profile of v9, /device:TPU:0, one launch (start us, length us, event | category | flops | bytes accessed | tf_op | source)
XLA Modules:
  0.0 30.4 jit_solution(10333837305783634131)
XLA Ops:
  0.6 2.2 %shard_map.84 = (bf16[128,2048]{1,0:T(8,128)(2,1)S(1)}, bf16[128,2048]{1,0:T(8,128)(2,1)S(1)}, bf16[128,2048]{1,0:T(8,128)(2,1)S(1)}, bf16[128,2048]{1,0:T(8,128...) custom-call(bf16[128,2048]{1,0:T(8,128)(2,1)} %refs_0_.1, ...), custom_call_target="tpu_custom_call" | custom-call | flops 2300000000 | tf_op jit(solution)/shard_map/pallas_call | solution.py:41
  2.8 0.5 %collective-permute-start = (bf16[2,656,128]{2,1,0:T(8,128)(2,1)S(1)}, bf16[2,656,128]{2,1,0:T(8,128)(2,1)S(1)}, u32[]{:S(2)}, u32[]{:S(2)}) collective-permute-start(bf16[2,656,128]{2,1,0:T(8,128)(2,1)S(1)} %get-tuple-element.59), channel_id=1, source_target_pairs={{0,1},{1,0},{2,3},{3,2},{4,5},{5,4},{6,7},{7,6},{8,9},{9,8},{10,11... | collective-permute-start | bytes 1007624 | tf_op jit(solution)/shard_map/ppermute | solution.py:360
  3.4 0.1 collective-permute-start.1
  3.4 0.8 %shard_map.85 = (bf16[2,656,128]{2,1,0:T(8,128)(2,1)S(1)}, bf16[2,656,128]{2,1,0:T(8,128)(2,1)S(1)}, bf16[2,256,128]{2,1,0:T(8,128)(2,1)S(1)}, bf16[2,256,128]{2,1,0:T(8,128)(2,1)S(1)}, f32[4,2,128,128]{3,2,1,0:T(8,128)S(1)}) custom-call(bf16[128,2048]{1,0:T(8,128)(2,1)S(1)} %get-tuple-element.56.refs_0_, bf16[128,2048]{1,0:T(8,128)(2,1)S(1)} %get-tuple-element.57.refs_1_, ...), custom_call_target="tpu_custom_call" | custom-call | flops 1150000000 | tf_op jit(solution)/shard_map/pallas_call | solution.py:41
  4.2 0.4 %collective-permute-done.refs_1_.refs_9_ = bf16[2,656,128]{2,1,0:T(8,128)(2,1)S(1)} collective-permute-done((bf16[2,656,128]{2,1,0:T(8,128)(2,1)S(1)}, bf16[2,656,128]{2,1,0:T(8,128)(2,1)S(1)}, u32[]{:S(2)}, u32[]{:S(2)}) %collective-permute-start) | collective-permute-done | bytes 335904 | tf_op jit(solution)/shard_map/ppermute | solution.py:360
  4.6 0.3 %shard_map.86 = (bf16[656,128]{1,0:T(8,128)(2,1)S(1)}, bf16[656,128]{1,0:T(8,128)(2,1)S(1)}) custom-call(bf16[2,656,128]{2,1,0:T(8,128)(2,1)S(1)} %get-tuple-element.58.refs_0_, bf16[2,656,128]{2,1,0:T(8,128)(2,1)S(1)} %collective-permute-done.refs_1_.refs_9_), custom_call_target="tpu_custom_call" | custom-call | flops 345000000 | tf_op jit(solution)/shard_map/pallas_call | solution.py:41
  4.9 1.8 %shard_map.87 = (f32[2,4,2,128,128]{4,3,2,1,0:T(8,128)S(1)}, f32[2,4,2,128,128]{4,3,2,1,0:T(8,128)S(1)}, bf16[2,4,2,128,128]{4,3,2,1,0:T(8,128)(2,1)S(1)}, bf16[2,4,2,128,128]{4,3,2,1,0:T(8,128)(2,1)S(1)}) custom-call(bf16[128,2048]{1,0:T(8,128)(2,1)S(1)} %get-tuple-element.56.refs_0_, bf16[128,2048]{1,0:T(8,128)(2,1)S(1)} %get-tuple-element.57.refs_1_, ...), custom_call_target="tpu_custom_call" | custom-call | flops 2070000000 | tf_op jit(solution)/shard_map/pallas_call | solution.py:41
  6.8 2.9 %collective-permute-start.4 = (bf16[656,128]{1,0:T(8,128)(2,1)S(1)}, bf16[656,128]{1,0:T(8,128)(2,1)S(1)}, u32[]{:S(2)}, u32[]{:S(2)}) collective-permute-start(bf16[656,128]{1,0:T(8,128)(2,1)S(1)} %get-tuple-element.80.refs_5_.refs_2_), channel_id=1, source_target_pairs={{0,2},{1,3},{2,0},{3,1},{4,6},{5,7},{6,4},{7,5},{8,10},{9,11},{10,... | collective-permute-start | bytes 503816 | tf_op jit(solution)/shard_map/ppermute | solution.py:360
  9.7 0.0 collective-permute-done.1.refs_1_.refs_10_
  9.7 0.3 %shard_map.89 = (bf16[656,128]{1,0:T(8,128)(2,1)S(1)}, bf16[656,128]{1,0:T(8,128)(2,1)S(1)}) custom-call(bf16[2,656,128]{2,1,0:T(8,128)(2,1)S(1)} %get-tuple-element.79.refs_0_, bf16[2,656,128]{2,1,0:T(8,128)(2,1)S(1)} %collective-permute-done.1.refs_1_.refs_10_, bf16[656,128]{1,0:T(8,128)(2,1)S(1)} %get-tuple-element.80.refs_5_.refs_2_), custom_call_target="tpu_custom_call" | custom-call | flops 230000000 | tf_op jit(solution)/shard_map/pallas_call | solution.py:41
  10.0 1.6 %collective-permute-start.5 = (bf16[656,128]{1,0:T(8,128)(2,1)S(1)}, bf16[656,128]{1,0:T(8,128)(2,1)S(1)}, u32[]{:S(2)}, u32[]{:S(2)}) collective-permute-start(bf16[656,128]{1,0:T(8,128)(2,1)S(1)} %get-tuple-element.82), channel_id=1, source_target_pairs={{0,4},{1,5},{2,6},{3,7},{4,0},{5,1},{6,2},{7,3},{8,12},{9,13},{10,... | collective-permute-start | bytes 503816 | tf_op jit(solution)/shard_map/ppermute | solution.py:360
  11.6 0.1 collective-permute-start.6
  11.6 0.0 collective-permute-start.2
  11.6 0.5 %collective-permute-start.3 = (bf16[2,256,128]{2,1,0:T(8,128)(2,1)S(1)}, bf16[2,256,128]{2,1,0:T(8,128)(2,1)S(1)}, u32[]{:S(2)}, u32[]{:S(2)}) collective-permute-start(bf16[2,256,128]{2,1,0:T(8,128)(2,1)S(1)} %get-tuple-element.78), channel_id=1, source_target_pairs={{0,1},{1,0},{2,3},{3,2},{4,5},{5,4},{6,7},{7,6},{8,9},{9,8},{10,11... | collective-permute-start | bytes 393224 | tf_op jit(solution)/shard_map/ppermute | solution.py:360
  12.2 0.8 %collective-permute-done.2.refs_5_.refs_11_ = bf16[2,256,128]{2,1,0:T(8,128)(2,1)S(1)} collective-permute-done((bf16[2,256,128]{2,1,0:T(8,128)(2,1)S(1)}, bf16[2,256,128]{2,1,0:T(8,128)(2,1)S(1)}, u32[]{:S(2)}, u32[]{:S(2)}) %collective-permute-start.2) | collective-permute-done | bytes 131104 | tf_op jit(solution)/shard_map/ppermute | solution.py:360
  13.0 0.2 collective-permute-done.3.refs_6_.refs_12_
  13.2 5.5 %collective-permute-done.5.refs_2_ = bf16[656,128]{1,0:T(8,128)(2,1)S(1)} collective-permute-done((bf16[656,128]{1,0:T(8,128)(2,1)S(1)}, bf16[656,128]{1,0:T(8,128)(2,1)S(1)}, u32[]{:S(2)}, u32[]{:S(2)}) %collective-permute-start.5) | collective-permute-done | bytes 167968 | tf_op jit(solution)/shard_map/ppermute | solution.py:360
  18.6 0.0 collective-permute-done.6.refs_3_
  18.6 0.0 collective-permute-done.4.refs_1_
  18.7 0.4 %shard_map.90 = (bf16[656,128]{1,0:T(8,128)(2,1)S(1)}, bf16[656,128]{1,0:T(8,128)(2,1)S(1)}, bf16[656,128]{1,0:T(8,128)(2,1)S(1)}, bf16[656,128]{1,0:T(8,128)(2,1)S(1)}) custom-call(bf16[656,128]{1,0:T(8,128)(2,1)S(1)} %get-tuple-element.81.refs_0_, bf16[656,128]{1,0:T(8,128)(2,1)S(1)} %collective-permute-done.4.refs_1_, ...), custom_call_target="tpu_custom_call" | custom-call | flops 575000000 | tf_op jit(solution)/shard_map/pallas_call | solution.py:41
  19.1 0.2 collective-permute-start.8
  19.3 1.2 %collective-permute-start.7 = (bf16[656,128]{1,0:T(8,128)(2,1)S(1)}, bf16[656,128]{1,0:T(8,128)(2,1)S(1)}, u32[]{:S(2)}, u32[]{:S(2)}) collective-permute-start(bf16[656,128]{1,0:T(8,128)(2,1)S(1)} %get-tuple-element.84), channel_id=1, source_target_pairs={{0,4},{1,5},{2,6},{3,7},{4,0},{5,1},{6,2},{7,3},{8,12},{9,13},{10,... | collective-permute-start | bytes 503816 | tf_op jit(solution)/shard_map/ppermute | solution.py:360
  20.5 2.1 %collective-permute-start.10 = (bf16[656,128]{1,0:T(8,128)(2,1)S(1)}, bf16[656,128]{1,0:T(8,128)(2,1)S(1)}, u32[]{:S(2)}, u32[]{:S(2)}) collective-permute-start(bf16[656,128]{1,0:T(8,128)(2,1)S(1)} %get-tuple-element.89), channel_id=1, source_target_pairs={{0,6},{1,7},{2,4},{3,5},{4,2},{5,3},{6,0},{7,1},{8,14},{9,15},{10,... | collective-permute-start | bytes 503816 | tf_op jit(solution)/shard_map/ppermute | solution.py:360
  22.6 0.0 collective-permute-start.12
  22.6 2.4 %collective-permute-done.8.refs_14_ = bf16[656,128]{1,0:T(8,128)(2,1)S(1)} collective-permute-done((bf16[656,128]{1,0:T(8,128)(2,1)S(1)}, bf16[656,128]{1,0:T(8,128)(2,1)S(1)}, u32[]{:S(2)}, u32[]{:S(2)}) %collective-permute-start.8) | collective-permute-done | bytes 167968 | tf_op jit(solution)/shard_map/ppermute | solution.py:360
  25.1 0.0 collective-permute-start.13
  25.1 1.3 %shard_map.91 = (bf16[128,2048]{1,0:T(8,128)(2,1)}, bf16[128,2048]{1,0:T(8,128)(2,1)}, bf16[128,2048]{1,0:T(8,128)(2,1)}, f32[16,128,128]{2,1,0:T(8,128)}) custom-call(bf16[128,2048]{1,0:T(8,128)(2,1)S(1)} %get-tuple-element.53.refs_3_.refs_0_, bf16[128,2048]{1,0:T(8,128)(2,1)S(1)} %get-tuple-element.54.refs_2_.refs_1_, ...), custom_call_target="tpu_custom_call" | custom-call | flops 1610000000 | tf_op jit(solution)/shard_map/pallas_call | solution.py:41
  26.4 0.6 %collective-permute-done.7.refs_13_ = bf16[656,128]{1,0:T(8,128)(2,1)S(1)} collective-permute-done((bf16[656,128]{1,0:T(8,128)(2,1)S(1)}, bf16[656,128]{1,0:T(8,128)(2,1)S(1)}, u32[]{:S(2)}, u32[]{:S(2)}) %collective-permute-start.7) | collective-permute-done | bytes 167968 | tf_op jit(solution)/shard_map/ppermute | solution.py:360
  26.9 0.0 collective-permute-done.10.refs_14_
  26.9 0.0 collective-permute-start.11
  27.0 0.5 %collective-permute-start.9 = (bf16[656,128]{1,0:T(8,128)(2,1)S(1)}, bf16[656,128]{1,0:T(8,128)(2,1)S(1)}, u32[]{:S(2)}, u32[]{:S(2)}) collective-permute-start(bf16[656,128]{1,0:T(8,128)(2,1)S(1)} %collective-permute-done.7.refs_13_), channel_id=1, source_target_pairs={{0,1},{1,0},{2,3},{3,2},{4,5},{5,4},{6,7},{7,6},{8,9},{9,8},{10,11... | collective-permute-start | bytes 503816 | tf_op jit(solution)/shard_map/ppermute | solution.py:360
  27.5 0.0 collective-permute-done.12.refs_15_
  27.5 0.0 collective-permute-done.13.refs_16_
  27.5 0.9 %shard_map.92 = (bf16[128,512]{1,0:T(8,128)(2,1)S(1)}, bf16[128,512]{1,0:T(8,128)(2,1)S(1)}, bf16[128,512]{1,0:T(8,128)(2,1)S(1)}, f32[4,128,128]{2,1,0:T(8,128)...) custom-call(bf16[128,2048]{1,0:T(8,128)(2,1)S(1)} %get-tuple-element, ...), custom_call_target="tpu_custom_call" | custom-call | flops 1150000000 | tf_op jit(solution)/shard_map/pallas_call | solution.py:41
  28.3 0.0 collective-permute-done.11.refs_14_
  28.4 0.2 collective-permute-done.9.refs_13_
  28.6 1.8 %shard_map.93 = (bf16[128,2048]{1,0:T(8,128)(2,1)}, bf16[128,2048]{1,0:T(8,128)(2,1)}, bf16[128,2048]{1,0:T(8,128)(2,1)}, f32[16,128,128]{2,1,0:T(8,128)}) custom-call(bf16[128,2048]{1,0:T(8,128)(2,1)S(1)} %get-tuple-element.53.refs_3_.refs_0_, ...), custom_call_target="tpu_custom_call", output_to_operand_aliasing={{0}: (23, {}), {1}: (24, {}), {2}: (25, {}), {3}: (26, {})} | custom-call | flops 1380000000 | tf_op jit(solution)/shard_map/pallas_call | solution.py:41
  (1 shorter events, 0.0 us)
Async XLA Ops:
  2.8 1.8 %collective-permute-start = (bf16[2,656,128]{2,1,0:T(8,128)(2,1)S(1)}, bf16[2,656,128]{2,1,0:T(8,128)(2,1)S(1)}, u32[]{:S(2)}, u32[]{:S(2)}) collective-permute-start(bf16[2,656,128]{2,1,0:T(8,128)(2,1)S(1)} %get-tuple-element.59), channel_id=1, source_target_pairs={{0,1},{1,0},{2,3},{3,2},{4,5},{5,4},{6,7},{7,6},{8,9},{9,8},{10,11... | collective-permute-start | bytes 1007624 | tf_op jit(solution)/shard_map/ppermute | solution.py:360
  3.4 6.3 %collective-permute-start.1 = (bf16[2,656,128]{2,1,0:T(8,128)(2,1)S(1)}, bf16[2,656,128]{2,1,0:T(8,128)(2,1)S(1)}, u32[]{:S(2)}, u32[]{:S(2)}) collective-permute-start(bf16[2,656,128]{2,1,0:T(8,128)(2,1)S(1)} %get-tuple-element.76), channel_id=1, source_target_pairs={{0,1},{1,0},{2,3},{3,2},{4,5},{5,4},{6,7},{7,6},{8,9},{9,8},{10,11... | collective-permute-start | bytes 1007624 | tf_op jit(solution)/shard_map/ppermute | solution.py:360
  6.8 11.9 %collective-permute-start.4 = (bf16[656,128]{1,0:T(8,128)(2,1)S(1)}, bf16[656,128]{1,0:T(8,128)(2,1)S(1)}, u32[]{:S(2)}, u32[]{:S(2)}) collective-permute-start(bf16[656,128]{1,0:T(8,128)(2,1)S(1)} %get-tuple-element.80.refs_5_.refs_2_), channel_id=1, source_target_pairs={{0,2},{1,3},{2,0},{3,1},{4,6},{5,7},{6,4},{7,5},{8,10},{9,11},{10,... | collective-permute-start | bytes 503816 | tf_op jit(solution)/shard_map/ppermute | solution.py:360
  10.0 8.6 %collective-permute-start.5 = (bf16[656,128]{1,0:T(8,128)(2,1)S(1)}, bf16[656,128]{1,0:T(8,128)(2,1)S(1)}, u32[]{:S(2)}, u32[]{:S(2)}) collective-permute-start(bf16[656,128]{1,0:T(8,128)(2,1)S(1)} %get-tuple-element.82), channel_id=1, source_target_pairs={{0,4},{1,5},{2,6},{3,7},{4,0},{5,1},{6,2},{7,3},{8,12},{9,13},{10,... | collective-permute-start | bytes 503816 | tf_op jit(solution)/shard_map/ppermute | solution.py:360
  11.6 7.1 %collective-permute-start.6 = (bf16[656,128]{1,0:T(8,128)(2,1)S(1)}, bf16[656,128]{1,0:T(8,128)(2,1)S(1)}, u32[]{:S(2)}, u32[]{:S(2)}) collective-permute-start(bf16[656,128]{1,0:T(8,128)(2,1)S(1)} %get-tuple-element.83), channel_id=1, source_target_pairs={{0,6},{1,7},{2,4},{3,5},{4,2},{5,3},{6,0},{7,1},{8,14},{9,15},{10,... | collective-permute-start | bytes 503816 | tf_op jit(solution)/shard_map/ppermute | solution.py:360
  11.6 1.3 %collective-permute-start.2 = (bf16[2,256,128]{2,1,0:T(8,128)(2,1)S(1)}, bf16[2,256,128]{2,1,0:T(8,128)(2,1)S(1)}, u32[]{:S(2)}, u32[]{:S(2)}) collective-permute-start(bf16[2,256,128]{2,1,0:T(8,128)(2,1)S(1)} %get-tuple-element.77), channel_id=1, source_target_pairs={{0,1},{1,0},{2,3},{3,2},{4,5},{5,4},{6,7},{7,6},{8,9},{9,8},{10,11... | collective-permute-start | bytes 393224 | tf_op jit(solution)/shard_map/ppermute | solution.py:360
  11.6 1.5 %collective-permute-start.3 = (bf16[2,256,128]{2,1,0:T(8,128)(2,1)S(1)}, bf16[2,256,128]{2,1,0:T(8,128)(2,1)S(1)}, u32[]{:S(2)}, u32[]{:S(2)}) collective-permute-start(bf16[2,256,128]{2,1,0:T(8,128)(2,1)S(1)} %get-tuple-element.78), channel_id=1, source_target_pairs={{0,1},{1,0},{2,3},{3,2},{4,5},{5,4},{6,7},{7,6},{8,9},{9,8},{10,11... | collective-permute-start | bytes 393224 | tf_op jit(solution)/shard_map/ppermute | solution.py:360
  19.1 6.0 %collective-permute-start.8 = (bf16[656,128]{1,0:T(8,128)(2,1)S(1)}, bf16[656,128]{1,0:T(8,128)(2,1)S(1)}, u32[]{:S(2)}, u32[]{:S(2)}) collective-permute-start(bf16[656,128]{1,0:T(8,128)(2,1)S(1)} %get-tuple-element.86), channel_id=1, source_target_pairs={{0,2},{1,3},{2,0},{3,1},{4,6},{5,7},{6,4},{7,5},{8,10},{9,11},{10,... | collective-permute-start | bytes 503816 | tf_op jit(solution)/shard_map/ppermute | solution.py:360
  19.3 7.6 %collective-permute-start.7 = (bf16[656,128]{1,0:T(8,128)(2,1)S(1)}, bf16[656,128]{1,0:T(8,128)(2,1)S(1)}, u32[]{:S(2)}, u32[]{:S(2)}) collective-permute-start(bf16[656,128]{1,0:T(8,128)(2,1)S(1)} %get-tuple-element.84), channel_id=1, source_target_pairs={{0,4},{1,5},{2,6},{3,7},{4,0},{5,1},{6,2},{7,3},{8,12},{9,13},{10,... | collective-permute-start | bytes 503816 | tf_op jit(solution)/shard_map/ppermute | solution.py:360
  20.5 6.5 %collective-permute-start.10 = (bf16[656,128]{1,0:T(8,128)(2,1)S(1)}, bf16[656,128]{1,0:T(8,128)(2,1)S(1)}, u32[]{:S(2)}, u32[]{:S(2)}) collective-permute-start(bf16[656,128]{1,0:T(8,128)(2,1)S(1)} %get-tuple-element.89), channel_id=1, source_target_pairs={{0,6},{1,7},{2,4},{3,5},{4,2},{5,3},{6,0},{7,1},{8,14},{9,15},{10,... | collective-permute-start | bytes 503816 | tf_op jit(solution)/shard_map/ppermute | solution.py:360
  22.6 4.8 %collective-permute-start.12 = (bf16[656,128]{1,0:T(8,128)(2,1)S(1)}, bf16[656,128]{1,0:T(8,128)(2,1)S(1)}, u32[]{:S(2)}, u32[]{:S(2)}) collective-permute-start(bf16[656,128]{1,0:T(8,128)(2,1)S(1)} %get-tuple-element.85.refs_13_), channel_id=1, source_target_pairs={{0,1},{1,0},{2,3},{3,2},{4,5},{5,4},{6,7},{7,6},{8,9},{9,8},{10,11... | collective-permute-start | bytes 503816 | tf_op jit(solution)/shard_map/ppermute | solution.py:360
  25.1 2.4 %collective-permute-start.13 = (bf16[656,128]{1,0:T(8,128)(2,1)S(1)}, bf16[656,128]{1,0:T(8,128)(2,1)S(1)}, u32[]{:S(2)}, u32[]{:S(2)}) collective-permute-start(bf16[656,128]{1,0:T(8,128)(2,1)S(1)} %collective-permute-done.8.refs_14_), channel_id=1, source_target_pairs={{0,1},{1,0},{2,3},{3,2},{4,5},{5,4},{6,7},{7,6},{8,9},{9,8},{10,11... | collective-permute-start | bytes 503816 | tf_op jit(solution)/shard_map/ppermute | solution.py:360
  26.9 1.4 %collective-permute-start.11 = (bf16[656,128]{1,0:T(8,128)(2,1)S(1)}, bf16[656,128]{1,0:T(8,128)(2,1)S(1)}, u32[]{:S(2)}, u32[]{:S(2)}) collective-permute-start(bf16[656,128]{1,0:T(8,128)(2,1)S(1)} %collective-permute-done.10.refs_14_), channel_id=1, source_target_pairs={{0,1},{1,0},{2,3},{3,2},{4,5},{5,4},{6,7},{7,6},{8,9},{9,8},{10,11... | collective-permute-start | bytes 503816 | tf_op jit(solution)/shard_map/ppermute | solution.py:360
  27.0 1.6 %collective-permute-start.9 = (bf16[656,128]{1,0:T(8,128)(2,1)S(1)}, bf16[656,128]{1,0:T(8,128)(2,1)S(1)}, u32[]{:S(2)}, u32[]{:S(2)}) collective-permute-start(bf16[656,128]{1,0:T(8,128)(2,1)S(1)} %collective-permute-done.7.refs_13_), channel_id=1, source_target_pairs={{0,1},{1,0},{2,3},{3,2},{4,5},{5,4},{6,7},{7,6},{8,9},{9,8},{10,11... | collective-permute-start | bytes 503816 | tf_op jit(solution)/shard_map/ppermute | solution.py:360

commit v10 on v9

--- a/solution.py
+++ b/solution.py
@@ -155,29 +155,29 @@
     return both, jnp.broadcast_to(diagonal, (EXTRA, size))
 
 
-def join_body(per_owner, own, other, *outs):
+def join_body(places, per_owner, own, other, *outs):
     size = own.shape[-1]
     count = 2 * per_owner * size
     core, _ = place()
     last = core == 1
     totals = []
-    for apart in range(len(outs)):
+    for at in places:
         for i in range(per_owner):
             ahead = slice(i * size, (i + 1) * size)
             behind = slice((per_owner + i) * size, (per_owner + i + 1) * size)
-            early = jnp.where(last, other[apart, ahead], own[apart, ahead])
-            late = jnp.where(last, own[apart, behind], other[apart, behind])
+            early = jnp.where(last, other[at, ahead], own[at, ahead])
+            late = jnp.where(last, own[at, behind], other[at, behind])
             totals.append(dot_nt(late, early))
-    for apart in range(len(outs)):
-        outs[apart][:count] = own[apart, :count] + other[apart, :count]
+    for n, at in enumerate(places):
+        outs[n][:count] = own[at, :count] + other[at, :count]
         for pair in range(per_owner // 2):
-            both, diagonal = pack(*totals[apart * per_owner + 2 * pair :][:2])
+            both, diagonal = pack(*totals[n * per_owner + 2 * pair :][:2])
             start = count + pair * (size + EXTRA)
             for x in (own, other):
-                both += x[apart, start : start + size].astype(F32)
-                diagonal += x[apart, start + size : start + size + EXTRA].astype(F32)
-            outs[apart][start : start + size] = both.astype(BF16)
-            outs[apart][start + size : start + size + EXTRA] = diagonal.astype(BF16)
+                both += x[at, start : start + size].astype(F32)
+                diagonal += x[at, start + size : start + size + EXTRA].astype(F32)
+            outs[n][start : start + size] = both.astype(BF16)
+            outs[n][start + size : start + size + EXTRA] = diagonal.astype(BF16)
 
 
 def rest_first_body(per_owner, *refs):
@@ -389,16 +389,21 @@
         1.0,
     )
     extra = [extra_a, extra_b]
-    join = bind(join_body, per_owner)
-    near_sums = call(join, [(payload, BF16)] * 2, (own[0], other[0]), 0.3)
+
+    def join(places, group, cost, after=()):
+        body = bind(join_body, places, per_owner)
+        return call(body, [(payload, BF16)] * len(places), (own[group], other[group]), cost, after)
+
+    near_sums = join((0,), 0, 0.15)
     locals_ = [(twice, F32), (twice, F32), (twice, BF16), (twice, BF16)]
     local = list(
         call(bind(rest_first_body, per_owner), locals_, (*here, w), 1.8, after=near_sums[:1])
     )
     *near_sums, local[0] = lax.optimization_barrier((*near_sums, local[0]))
-    rest_sums = call(join, [(payload, BF16)] * 2, (own[1], other[1]), 0.2, after=near_sums[:1])
-    chip_sums = [rest_sums[0], near_sums[0], rest_sums[1], near_sums[1]]
-    parts = [chip_sums[0]] + [swap(chip_sums[j], 2 * j) for j in range(1, GROUPS)]
+    (y_sum,) = join((1,), 1, 0.15, near_sums[:1])
+    (far_sum,) = join((1,), 0, 0.15, near_sums[:1])
+    chip_sums = [None, near_sums[0], y_sum, far_sum]
+    parts = [None] + [swap(chip_sums[j], 2 * j) for j in range(1, GROUPS)]
     local = call(
         bind(rest_second_body, per_owner),
         locals_,
@@ -409,6 +414,7 @@
         in_after=VMEM,
     )
     part_k, part_v, key_w, gram = local
+    (parts[0],) = join((0,), 1, 0.15, (gram,))
     *extra, gram = lax.optimization_barrier((*extra, gram))
     extra = [swap(x, 1) for x in extra]
     carried = call(

time: 30.5 us -> 30.4 us (level)
  waiting for transfers between devices: 10.1 us -> 9.41 us
  Pallas kernels: 9.83 us -> 10.3 us
    ppermute x14, waiting for transfers between devices: 10.1 us -> 9.41 us  [swap(): return lax.ppermute(x, 'ctx', [(i, i ^ apart) for i in range(count)])]
    pallas_call x10 -> x12, Pallas kernels: 9.83 us -> 10.3 us  [call(): pl.pallas_call(run, out_shape=[jax.ShapeDtypeStruct(shape, dtype) for sha...]
  transfers between devices with their start and end apart: 14 -> 14, of which waited for: 7 -> 7; matrix products, arithmetic and copies ran while one was open for 0% -> 0% of each run, Pallas kernels for 18% -> 19%
where the time goes in v10:
time: 30.4 us; the launch traced here: 30.3 us
  Pallas kernels  10.3 us (34%)
  starting transfers between devices  9.81 us (32%)
  waiting for transfers between devices  9.41 us (31%)
  between operations  0.73 us (2%)
    pallas_call x12, Pallas kernels, call(): pl.pallas_call(run, out_shape=[jax.ShapeDtypeStruct(shape, dtype) for sha...  10.3 us
    ppermute x14, starting transfers between devices, swap(): return lax.ppermute(x, 'ctx', [(i, i ^ apart) for i in range(count)])  9.81 us
    ppermute x14, waiting for transfers between devices, swap(): return lax.ppermute(x, 'ctx', [(i, i ^ apart) for i in range(count)])  9.41 us
  transfers between devices with their start and end apart: 14, of which 7 were waited for; matrix products, arithmetic and copies ran while one was open for 0% of the time, Pallas kernels for 19%

profile of v10, /device:TPU:0, one launch (start us, length us, event | category | flops | bytes accessed | tf_op | source)
XLA Modules:
  0.0 30.3 jit_solution(7363434174243028752)
XLA Ops:
  0.6 2.2 %shard_map.84 = (bf16[128,2048]{1,0:T(8,128)(2,1)S(1)}, bf16[128,2048]{1,0:T(8,128)(2,1)S(1)}, bf16[128,2048]{1,0:T(8,128)(2,1)S(1)}, bf16[128,2048]{1,0:T(8,128...) custom-call(bf16[128,2048]{1,0:T(8,128)(2,1)} %refs_0_.1, ...), custom_call_target="tpu_custom_call" | custom-call | flops 2300000000 | tf_op jit(solution)/shard_map/pallas_call | solution.py:41
  2.8 0.5 %collective-permute-start = (bf16[2,656,128]{2,1,0:T(8,128)(2,1)S(1)}, bf16[2,656,128]{2,1,0:T(8,128)(2,1)S(1)}, u32[]{:S(2)}, u32[]{:S(2)}) collective-permute-start(bf16[2,656,128]{2,1,0:T(8,128)(2,1)S(1)} %get-tuple-element.54), channel_id=1, source_target_pairs={{0,1},{1,0},{2,3},{3,2},{4,5},{5,4},{6,7},{7,6},{8,9},{9,8},{10,11... | collective-permute-start | bytes 1007624 | tf_op jit(solution)/shard_map/ppermute | solution.py:360
  3.4 0.1 collective-permute-start.1
  3.4 0.8 %shard_map.85 = (bf16[2,656,128]{2,1,0:T(8,128)(2,1)S(1)}, bf16[2,656,128]{2,1,0:T(8,128)(2,1)S(1)}, bf16[2,256,128]{2,1,0:T(8,128)(2,1)S(1)}, bf16[2,256,128]{2,1,0:T(8,128)(2,1)S(1)}, f32[4,2,128,128]{3,2,1,0:T(8,128)S(1)}) custom-call(bf16[128,2048]{1,0:T(8,128)(2,1)S(1)} %get-tuple-element.51.refs_0_, bf16[128,2048]{1,0:T(8,128)(2,1)S(1)} %get-tuple-element.52.refs_1_, ...), custom_call_target="tpu_custom_call" | custom-call | flops 1150000000 | tf_op jit(solution)/shard_map/pallas_call | solution.py:41
  4.2 0.4 %collective-permute-done.refs_1_.refs_9_ = bf16[2,656,128]{2,1,0:T(8,128)(2,1)S(1)} collective-permute-done((bf16[2,656,128]{2,1,0:T(8,128)(2,1)S(1)}, bf16[2,656,128]{2,1,0:T(8,128)(2,1)S(1)}, u32[]{:S(2)}, u32[]{:S(2)}) %collective-permute-start) | collective-permute-done | bytes 335904 | tf_op jit(solution)/shard_map/ppermute | solution.py:360
  4.6 0.3 shard_map.86.refs_5_.refs_2_
  4.9 1.8 %shard_map.87 = (f32[2,4,2,128,128]{4,3,2,1,0:T(8,128)S(1)}, f32[2,4,2,128,128]{4,3,2,1,0:T(8,128)S(1)}, bf16[2,4,2,128,128]{4,3,2,1,0:T(8,128)(2,1)S(1)}, bf16[2,4,2,128,128]{4,3,2,1,0:T(8,128)(2,1)S(1)}) custom-call(bf16[128,2048]{1,0:T(8,128)(2,1)S(1)} %get-tuple-element.51.refs_0_, bf16[128,2048]{1,0:T(8,128)(2,1)S(1)} %get-tuple-element.52.refs_1_, ...), custom_call_target="tpu_custom_call" | custom-call | flops 2070000000 | tf_op jit(solution)/shard_map/pallas_call | solution.py:41
  6.7 2.9 %collective-permute-start.4 = (bf16[656,128]{1,0:T(8,128)(2,1)S(1)}, bf16[656,128]{1,0:T(8,128)(2,1)S(1)}, u32[]{:S(2)}, u32[]{:S(2)}) collective-permute-start(bf16[656,128]{1,0:T(8,128)(2,1)S(1)} %shard_map.86.refs_5_.refs_2_), channel_id=1, source_target_pairs={{0,2},{1,3},{2,0},{3,1},{4,6},{5,7},{6,4},{7,5},{8,10},{9,11},{10,... | collective-permute-start | bytes 503816 | tf_op jit(solution)/shard_map/ppermute | solution.py:360
  9.6 0.0 collective-permute-done.1.refs_1_.refs_10_
  9.6 0.3 shard_map.90
  9.9 1.6 %collective-permute-start.5 = (bf16[656,128]{1,0:T(8,128)(2,1)S(1)}, bf16[656,128]{1,0:T(8,128)(2,1)S(1)}, u32[]{:S(2)}, u32[]{:S(2)}) collective-permute-start(bf16[656,128]{1,0:T(8,128)(2,1)S(1)} %shard_map.90), channel_id=1, source_target_pairs={{0,4},{1,5},{2,6},{3,7},{4,0},{5,1},{6,2},{7,3},{8,12},{9,13},{10,... | collective-permute-start | bytes 503816 | tf_op jit(solution)/shard_map/ppermute | solution.py:360
  11.5 0.3 shard_map.91
  11.8 0.1 collective-permute-start.6
  11.9 0.1 collective-permute-start.2
  12.0 0.5 %collective-permute-start.3 = (bf16[2,256,128]{2,1,0:T(8,128)(2,1)S(1)}, bf16[2,256,128]{2,1,0:T(8,128)(2,1)S(1)}, u32[]{:S(2)}, u32[]{:S(2)}) collective-permute-start(bf16[2,256,128]{2,1,0:T(8,128)(2,1)S(1)} %get-tuple-element.71), channel_id=1, source_target_pairs={{0,1},{1,0},{2,3},{3,2},{4,5},{5,4},{6,7},{7,6},{8,9},{9,8},{10,11... | collective-permute-start | bytes 393224 | tf_op jit(solution)/shard_map/ppermute | solution.py:360
  12.5 0.3 shard_map.89.refs_0_
  12.7 0.6 %collective-permute-done.2.refs_5_.refs_11_ = bf16[2,256,128]{2,1,0:T(8,128)(2,1)S(1)} collective-permute-done((bf16[2,256,128]{2,1,0:T(8,128)(2,1)S(1)}, bf16[2,256,128]{2,1,0:T(8,128)(2,1)S(1)}, u32[]{:S(2)}, u32[]{:S(2)}) %collective-permute-start.2) | collective-permute-done | bytes 131104 | tf_op jit(solution)/shard_map/ppermute | solution.py:360
  13.3 0.2 collective-permute-done.3.refs_6_.refs_12_
  13.5 5.2 %collective-permute-done.5.refs_2_ = bf16[656,128]{1,0:T(8,128)(2,1)S(1)} collective-permute-done((bf16[656,128]{1,0:T(8,128)(2,1)S(1)}, bf16[656,128]{1,0:T(8,128)(2,1)S(1)}, u32[]{:S(2)}, u32[]{:S(2)}) %collective-permute-start.5) | collective-permute-done | bytes 167968 | tf_op jit(solution)/shard_map/ppermute | solution.py:360
  18.7 0.0 collective-permute-done.6.refs_3_
  18.7 0.0 collective-permute-done.4.refs_1_
  18.7 0.4 %shard_map.92 = (bf16[656,128]{1,0:T(8,128)(2,1)S(1)}, bf16[656,128]{1,0:T(8,128)(2,1)S(1)}, bf16[656,128]{1,0:T(8,128)(2,1)S(1)}, bf16[656,128]{1,0:T(8,128)(2,1)S(1)}) custom-call(bf16[656,128]{1,0:T(8,128)(2,1)S(1)} %shard_map.89.refs_0_, bf16[656,128]{1,0:T(8,128)(2,1)S(1)} %collective-permute-done.4.refs_1_, ...), custom_call_target="tpu_custom_call" | custom-call | flops 575000000 | tf_op jit(solution)/shard_map/pallas_call | solution.py:41
  19.1 0.4 %collective-permute-start.8 = (bf16[656,128]{1,0:T(8,128)(2,1)S(1)}, bf16[656,128]{1,0:T(8,128)(2,1)S(1)}, u32[]{:S(2)}, u32[]{:S(2)}) collective-permute-start(bf16[656,128]{1,0:T(8,128)(2,1)S(1)} %get-tuple-element.76), channel_id=1, source_target_pairs={{0,2},{1,3},{2,0},{3,1},{4,6},{5,7},{6,4},{7,5},{8,10},{9,11},{10,... | collective-permute-start | bytes 503816 | tf_op jit(solution)/shard_map/ppermute | solution.py:360
  19.5 0.9 %collective-permute-start.7 = (bf16[656,128]{1,0:T(8,128)(2,1)S(1)}, bf16[656,128]{1,0:T(8,128)(2,1)S(1)}, u32[]{:S(2)}, u32[]{:S(2)}) collective-permute-start(bf16[656,128]{1,0:T(8,128)(2,1)S(1)} %get-tuple-element.74), channel_id=1, source_target_pairs={{0,4},{1,5},{2,6},{3,7},{4,0},{5,1},{6,2},{7,3},{8,12},{9,13},{10,... | collective-permute-start | bytes 503816 | tf_op jit(solution)/shard_map/ppermute | solution.py:360
  20.4 2.3 %collective-permute-start.10 = (bf16[656,128]{1,0:T(8,128)(2,1)S(1)}, bf16[656,128]{1,0:T(8,128)(2,1)S(1)}, u32[]{:S(2)}, u32[]{:S(2)}) collective-permute-start(bf16[656,128]{1,0:T(8,128)(2,1)S(1)} %get-tuple-element.79), channel_id=1, source_target_pairs={{0,6},{1,7},{2,4},{3,5},{4,2},{5,3},{6,0},{7,1},{8,14},{9,15},{10,... | collective-permute-start | bytes 503816 | tf_op jit(solution)/shard_map/ppermute | solution.py:360
  22.7 0.0 collective-permute-start.12
  22.7 2.0 %collective-permute-done.8.refs_14_ = bf16[656,128]{1,0:T(8,128)(2,1)S(1)} collective-permute-done((bf16[656,128]{1,0:T(8,128)(2,1)S(1)}, bf16[656,128]{1,0:T(8,128)(2,1)S(1)}, u32[]{:S(2)}, u32[]{:S(2)}) %collective-permute-start.8) | collective-permute-done | bytes 167968 | tf_op jit(solution)/shard_map/ppermute | solution.py:360
  24.7 0.0 collective-permute-start.13
  24.7 1.3 %shard_map.93 = (bf16[128,2048]{1,0:T(8,128)(2,1)}, bf16[128,2048]{1,0:T(8,128)(2,1)}, bf16[128,2048]{1,0:T(8,128)(2,1)}, f32[16,128,128]{2,1,0:T(8,128)}) custom-call(bf16[128,2048]{1,0:T(8,128)(2,1)S(1)} %get-tuple-element.48.refs_3_.refs_0_, bf16[128,2048]{1,0:T(8,128)(2,1)S(1)} %get-tuple-element.49.refs_2_.refs_1_, ...), custom_call_target="tpu_custom_call" | custom-call | flops 1610000000 | tf_op jit(solution)/shard_map/pallas_call | solution.py:41
  26.0 0.0 collective-permute-done.7.refs_13_
  26.0 0.8 %collective-permute-done.10.refs_14_ = bf16[656,128]{1,0:T(8,128)(2,1)S(1)} collective-permute-done((bf16[656,128]{1,0:T(8,128)(2,1)S(1)}, bf16[656,128]{1,0:T(8,128)(2,1)S(1)}, u32[]{:S(2)}, u32[]{:S(2)}) %collective-permute-start.10) | collective-permute-done | bytes 167968 | tf_op jit(solution)/shard_map/ppermute | solution.py:360
  26.8 0.0 collective-permute-start.11
  26.8 0.5 %collective-permute-start.9 = (bf16[656,128]{1,0:T(8,128)(2,1)S(1)}, bf16[656,128]{1,0:T(8,128)(2,1)S(1)}, u32[]{:S(2)}, u32[]{:S(2)}) collective-permute-start(bf16[656,128]{1,0:T(8,128)(2,1)S(1)} %collective-permute-done.7.refs_13_), channel_id=1, source_target_pairs={{0,1},{1,0},{2,3},{3,2},{4,5},{5,4},{6,7},{7,6},{8,9},{9,8},{10,11... | collective-permute-start | bytes 503816 | tf_op jit(solution)/shard_map/ppermute | solution.py:360
  27.3 0.0 collective-permute-done.12.refs_15_
  27.3 0.0 collective-permute-done.13.refs_16_
  27.4 0.9 %shard_map.94 = (bf16[128,512]{1,0:T(8,128)(2,1)S(1)}, bf16[128,512]{1,0:T(8,128)(2,1)S(1)}, bf16[128,512]{1,0:T(8,128)(2,1)S(1)}, f32[4,128,128]{2,1,0:T(8,128)...) custom-call(bf16[128,2048]{1,0:T(8,128)(2,1)S(1)} %get-tuple-element, ...), custom_call_target="tpu_custom_call" | custom-call | flops 1150000000 | tf_op jit(solution)/shard_map/pallas_call | solution.py:41
  28.2 0.0 collective-permute-done.11.refs_14_
  28.3 0.2 collective-permute-done.9.refs_13_
  28.5 1.8 %shard_map.95 = (bf16[128,2048]{1,0:T(8,128)(2,1)}, bf16[128,2048]{1,0:T(8,128)(2,1)}, bf16[128,2048]{1,0:T(8,128)(2,1)}, f32[16,128,128]{2,1,0:T(8,128)}) custom-call(bf16[128,2048]{1,0:T(8,128)(2,1)S(1)} %get-tuple-element.48.refs_3_.refs_0_, ...), custom_call_target="tpu_custom_call", output_to_operand_aliasing={{0}: (23, {}), {1}: (24, {}), {2}: (25, {}), {3}: (26, {})} | custom-call | flops 1380000000 | tf_op jit(solution)/shard_map/pallas_call | solution.py:41
  (1 shorter events, 0.0 us)
Async XLA Ops:
  2.8 1.8 %collective-permute-start = (bf16[2,656,128]{2,1,0:T(8,128)(2,1)S(1)}, bf16[2,656,128]{2,1,0:T(8,128)(2,1)S(1)}, u32[]{:S(2)}, u32[]{:S(2)}) collective-permute-start(bf16[2,656,128]{2,1,0:T(8,128)(2,1)S(1)} %get-tuple-element.54), channel_id=1, source_target_pairs={{0,1},{1,0},{2,3},{3,2},{4,5},{5,4},{6,7},{7,6},{8,9},{9,8},{10,11... | collective-permute-start | bytes 1007624 | tf_op jit(solution)/shard_map/ppermute | solution.py:360
  3.4 6.3 %collective-permute-start.1 = (bf16[2,656,128]{2,1,0:T(8,128)(2,1)S(1)}, bf16[2,656,128]{2,1,0:T(8,128)(2,1)S(1)}, u32[]{:S(2)}, u32[]{:S(2)}) collective-permute-start(bf16[2,656,128]{2,1,0:T(8,128)(2,1)S(1)} %get-tuple-element.69), channel_id=1, source_target_pairs={{0,1},{1,0},{2,3},{3,2},{4,5},{5,4},{6,7},{7,6},{8,9},{9,8},{10,11... | collective-permute-start | bytes 1007624 | tf_op jit(solution)/shard_map/ppermute | solution.py:360
  6.7 12.0 %collective-permute-start.4 = (bf16[656,128]{1,0:T(8,128)(2,1)S(1)}, bf16[656,128]{1,0:T(8,128)(2,1)S(1)}, u32[]{:S(2)}, u32[]{:S(2)}) collective-permute-start(bf16[656,128]{1,0:T(8,128)(2,1)S(1)} %shard_map.86.refs_5_.refs_2_), channel_id=1, source_target_pairs={{0,2},{1,3},{2,0},{3,1},{4,6},{5,7},{6,4},{7,5},{8,10},{9,11},{10,... | collective-permute-start | bytes 503816 | tf_op jit(solution)/shard_map/ppermute | solution.py:360
  9.9 8.8 %collective-permute-start.5 = (bf16[656,128]{1,0:T(8,128)(2,1)S(1)}, bf16[656,128]{1,0:T(8,128)(2,1)S(1)}, u32[]{:S(2)}, u32[]{:S(2)}) collective-permute-start(bf16[656,128]{1,0:T(8,128)(2,1)S(1)} %shard_map.90), channel_id=1, source_target_pairs={{0,4},{1,5},{2,6},{3,7},{4,0},{5,1},{6,2},{7,3},{8,12},{9,13},{10,... | collective-permute-start | bytes 503816 | tf_op jit(solution)/shard_map/ppermute | solution.py:360
  11.8 6.9 %collective-permute-start.6 = (bf16[656,128]{1,0:T(8,128)(2,1)S(1)}, bf16[656,128]{1,0:T(8,128)(2,1)S(1)}, u32[]{:S(2)}, u32[]{:S(2)}) collective-permute-start(bf16[656,128]{1,0:T(8,128)(2,1)S(1)} %shard_map.91), channel_id=1, source_target_pairs={{0,6},{1,7},{2,4},{3,5},{4,2},{5,3},{6,0},{7,1},{8,14},{9,15},{10,... | collective-permute-start | bytes 503816 | tf_op jit(solution)/shard_map/ppermute | solution.py:360
  11.9 1.4 %collective-permute-start.2 = (bf16[2,256,128]{2,1,0:T(8,128)(2,1)S(1)}, bf16[2,256,128]{2,1,0:T(8,128)(2,1)S(1)}, u32[]{:S(2)}, u32[]{:S(2)}) collective-permute-start(bf16[2,256,128]{2,1,0:T(8,128)(2,1)S(1)} %get-tuple-element.70), channel_id=1, source_target_pairs={{0,1},{1,0},{2,3},{3,2},{4,5},{5,4},{6,7},{7,6},{8,9},{9,8},{10,11... | collective-permute-start | bytes 393224 | tf_op jit(solution)/shard_map/ppermute | solution.py:360
  12.0 1.5 %collective-permute-start.3 = (bf16[2,256,128]{2,1,0:T(8,128)(2,1)S(1)}, bf16[2,256,128]{2,1,0:T(8,128)(2,1)S(1)}, u32[]{:S(2)}, u32[]{:S(2)}) collective-permute-start(bf16[2,256,128]{2,1,0:T(8,128)(2,1)S(1)} %get-tuple-element.71), channel_id=1, source_target_pairs={{0,1},{1,0},{2,3},{3,2},{4,5},{5,4},{6,7},{7,6},{8,9},{9,8},{10,11... | collective-permute-start | bytes 393224 | tf_op jit(solution)/shard_map/ppermute | solution.py:360
  19.1 5.6 %collective-permute-start.8 = (bf16[656,128]{1,0:T(8,128)(2,1)S(1)}, bf16[656,128]{1,0:T(8,128)(2,1)S(1)}, u32[]{:S(2)}, u32[]{:S(2)}) collective-permute-start(bf16[656,128]{1,0:T(8,128)(2,1)S(1)} %get-tuple-element.76), channel_id=1, source_target_pairs={{0,2},{1,3},{2,0},{3,1},{4,6},{5,7},{6,4},{7,5},{8,10},{9,11},{10,... | collective-permute-start | bytes 503816 | tf_op jit(solution)/shard_map/ppermute | solution.py:360
  19.5 6.4 %collective-permute-start.7 = (bf16[656,128]{1,0:T(8,128)(2,1)S(1)}, bf16[656,128]{1,0:T(8,128)(2,1)S(1)}, u32[]{:S(2)}, u32[]{:S(2)}) collective-permute-start(bf16[656,128]{1,0:T(8,128)(2,1)S(1)} %get-tuple-element.74), channel_id=1, source_target_pairs={{0,4},{1,5},{2,6},{3,7},{4,0},{5,1},{6,2},{7,3},{8,12},{9,13},{10,... | collective-permute-start | bytes 503816 | tf_op jit(solution)/shard_map/ppermute | solution.py:360
  20.4 6.4 %collective-permute-start.10 = (bf16[656,128]{1,0:T(8,128)(2,1)S(1)}, bf16[656,128]{1,0:T(8,128)(2,1)S(1)}, u32[]{:S(2)}, u32[]{:S(2)}) collective-permute-start(bf16[656,128]{1,0:T(8,128)(2,1)S(1)} %get-tuple-element.79), channel_id=1, source_target_pairs={{0,6},{1,7},{2,4},{3,5},{4,2},{5,3},{6,0},{7,1},{8,14},{9,15},{10,... | collective-permute-start | bytes 503816 | tf_op jit(solution)/shard_map/ppermute | solution.py:360
  22.7 4.7 %collective-permute-start.12 = (bf16[656,128]{1,0:T(8,128)(2,1)S(1)}, bf16[656,128]{1,0:T(8,128)(2,1)S(1)}, u32[]{:S(2)}, u32[]{:S(2)}) collective-permute-start(bf16[656,128]{1,0:T(8,128)(2,1)S(1)} %get-tuple-element.75.refs_13_), channel_id=1, source_target_pairs={{0,1},{1,0},{2,3},{3,2},{4,5},{5,4},{6,7},{7,6},{8,9},{9,8},{10,11... | collective-permute-start | bytes 503816 | tf_op jit(solution)/shard_map/ppermute | solution.py:360
  24.7 2.7 %collective-permute-start.13 = (bf16[656,128]{1,0:T(8,128)(2,1)S(1)}, bf16[656,128]{1,0:T(8,128)(2,1)S(1)}, u32[]{:S(2)}, u32[]{:S(2)}) collective-permute-start(bf16[656,128]{1,0:T(8,128)(2,1)S(1)} %collective-permute-done.8.refs_14_), channel_id=1, source_target_pairs={{0,1},{1,0},{2,3},{3,2},{4,5},{5,4},{6,7},{7,6},{8,9},{9,8},{10,11... | collective-permute-start | bytes 503816 | tf_op jit(solution)/shard_map/ppermute | solution.py:360
  26.8 1.4 %collective-permute-start.11 = (bf16[656,128]{1,0:T(8,128)(2,1)S(1)}, bf16[656,128]{1,0:T(8,128)(2,1)S(1)}, u32[]{:S(2)}, u32[]{:S(2)}) collective-permute-start(bf16[656,128]{1,0:T(8,128)(2,1)S(1)} %collective-permute-done.10.refs_14_), channel_id=1, source_target_pairs={{0,1},{1,0},{2,3},{3,2},{4,5},{5,4},{6,7},{7,6},{8,9},{9,8},{10,11... | collective-permute-start | bytes 503816 | tf_op jit(solution)/shard_map/ppermute | solution.py:360
  26.8 1.6 %collective-permute-start.9 = (bf16[656,128]{1,0:T(8,128)(2,1)S(1)}, bf16[656,128]{1,0:T(8,128)(2,1)S(1)}, u32[]{:S(2)}, u32[]{:S(2)}) collective-permute-start(bf16[656,128]{1,0:T(8,128)(2,1)S(1)} %collective-permute-done.7.refs_13_), channel_id=1, source_target_pairs={{0,1},{1,0},{2,3},{3,2},{4,5},{5,4},{6,7},{7,6},{8,9},{9,8},{10,11... | collective-permute-start | bytes 503816 | tf_op jit(solution)/shard_map/ppermute | solution.py:360

commit v11 on v10

--- a/solution.py
+++ b/solution.py
@@ -67,7 +67,7 @@
 
 
 def pick(refs, apart):
-    group, place_ = ((1, 0), (0, 0), (1, 1), (0, 1))[apart]
+    group, place_ = ((1, 0), (0, 0), (0, 1), (1, 1))[apart]
     return refs[group].at[place_]
 
 
@@ -400,8 +400,8 @@
         call(bind(rest_first_body, per_owner), locals_, (*here, w), 1.8, after=near_sums[:1])
     )
     *near_sums, local[0] = lax.optimization_barrier((*near_sums, local[0]))
-    (y_sum,) = join((1,), 1, 0.15, near_sums[:1])
-    (far_sum,) = join((1,), 0, 0.15, near_sums[:1])
+    (y_sum,) = join((1,), 0, 0.15, near_sums[:1])
+    (far_sum,) = join((1,), 1, 0.15, (y_sum,))
     chip_sums = [None, near_sums[0], y_sum, far_sum]
     parts = [None] + [swap(chip_sums[j], 2 * j) for j in range(1, GROUPS)]
     local = call(

time: 30.4 us -> 30.4 us (level)
  transfers between devices with their start and end apart: 14 -> 14, of which waited for: 7 -> 8; matrix products, arithmetic and copies ran while one was open for 0% -> 0% of each run, Pallas kernels for 19% -> 19%
where the time goes in v11:
time: 30.4 us; the launch traced here: 30.2 us
  Pallas kernels  10.3 us (34%)
  starting transfers between devices  9.81 us (32%)
  waiting for transfers between devices  9.42 us (31%)
  between operations  0.73 us (2%)
    pallas_call x12, Pallas kernels, call(): pl.pallas_call(run, out_shape=[jax.ShapeDtypeStruct(shape, dtype) for sha...  10.3 us
    ppermute x14, starting transfers between devices, swap(): return lax.ppermute(x, 'ctx', [(i, i ^ apart) for i in range(count)])  9.81 us
    ppermute x14, waiting for transfers between devices, swap(): return lax.ppermute(x, 'ctx', [(i, i ^ apart) for i in range(count)])  9.42 us
  transfers between devices with their start and end apart: 14, of which 8 were waited for; matrix products, arithmetic and copies ran while one was open for 0% of the time, Pallas kernels for 19%

profile of v11, /device:TPU:0, one launch (start us, length us, event | category | flops | bytes accessed | tf_op | source)
XLA Modules:
  0.0 30.2 jit_solution(16049432961677605746)
XLA Ops:
  0.6 2.2 %shard_map.84 = (bf16[128,2048]{1,0:T(8,128)(2,1)S(1)}, bf16[128,2048]{1,0:T(8,128)(2,1)S(1)}, bf16[128,2048]{1,0:T(8,128)(2,1)S(1)}, bf16[128,2048]{1,0:T(8,128...) custom-call(bf16[128,2048]{1,0:T(8,128)(2,1)} %refs_0_.1, ...), custom_call_target="tpu_custom_call" | custom-call | flops 2300000000 | tf_op jit(solution)/shard_map/pallas_call | solution.py:41
  2.8 0.5 %collective-permute-start = (bf16[2,656,128]{2,1,0:T(8,128)(2,1)S(1)}, bf16[2,656,128]{2,1,0:T(8,128)(2,1)S(1)}, u32[]{:S(2)}, u32[]{:S(2)}) collective-permute-start(bf16[2,656,128]{2,1,0:T(8,128)(2,1)S(1)} %get-tuple-element.54), channel_id=1, source_target_pairs={{0,1},{1,0},{2,3},{3,2},{4,5},{5,4},{6,7},{7,6},{8,9},{9,8},{10,11... | collective-permute-start | bytes 1007624 | tf_op jit(solution)/shard_map/ppermute | solution.py:360
  3.4 0.1 collective-permute-start.1
  3.4 0.8 %shard_map.85 = (bf16[2,656,128]{2,1,0:T(8,128)(2,1)S(1)}, bf16[2,656,128]{2,1,0:T(8,128)(2,1)S(1)}, bf16[2,256,128]{2,1,0:T(8,128)(2,1)S(1)}, bf16[2,256,128]{2,1,0:T(8,128)(2,1)S(1)}, f32[4,2,128,128]{3,2,1,0:T(8,128)S(1)}) custom-call(bf16[128,2048]{1,0:T(8,128)(2,1)S(1)} %get-tuple-element.51.refs_0_, bf16[128,2048]{1,0:T(8,128)(2,1)S(1)} %get-tuple-element.52.refs_1_, ...), custom_call_target="tpu_custom_call" | custom-call | flops 1150000000 | tf_op jit(solution)/shard_map/pallas_call | solution.py:41
  4.2 0.4 %collective-permute-done.refs_1_.refs_9_ = bf16[2,656,128]{2,1,0:T(8,128)(2,1)S(1)} collective-permute-done((bf16[2,656,128]{2,1,0:T(8,128)(2,1)S(1)}, bf16[2,656,128]{2,1,0:T(8,128)(2,1)S(1)}, u32[]{:S(2)}, u32[]{:S(2)}) %collective-permute-start) | collective-permute-done | bytes 335904 | tf_op jit(solution)/shard_map/ppermute | solution.py:360
  4.6 0.3 shard_map.86.refs_5_.refs_2_
  4.9 1.8 %shard_map.87 = (f32[2,4,2,128,128]{4,3,2,1,0:T(8,128)S(1)}, f32[2,4,2,128,128]{4,3,2,1,0:T(8,128)S(1)}, bf16[2,4,2,128,128]{4,3,2,1,0:T(8,128)(2,1)S(1)}, bf16[2,4,2,128,128]{4,3,2,1,0:T(8,128)(2,1)S(1)}) custom-call(bf16[128,2048]{1,0:T(8,128)(2,1)S(1)} %get-tuple-element.51.refs_0_, bf16[128,2048]{1,0:T(8,128)(2,1)S(1)} %get-tuple-element.52.refs_1_, ...), custom_call_target="tpu_custom_call" | custom-call | flops 2070000000 | tf_op jit(solution)/shard_map/pallas_call | solution.py:41
  6.7 2.9 %collective-permute-start.4 = (bf16[656,128]{1,0:T(8,128)(2,1)S(1)}, bf16[656,128]{1,0:T(8,128)(2,1)S(1)}, u32[]{:S(2)}, u32[]{:S(2)}) collective-permute-start(bf16[656,128]{1,0:T(8,128)(2,1)S(1)} %shard_map.86.refs_5_.refs_2_), channel_id=1, source_target_pairs={{0,2},{1,3},{2,0},{3,1},{4,6},{5,7},{6,4},{7,5},{8,10},{9,11},{10,... | collective-permute-start | bytes 503816 | tf_op jit(solution)/shard_map/ppermute | solution.py:360
  9.6 0.3 shard_map.90.refs_2_
  9.9 1.6 %collective-permute-start.5 = (bf16[656,128]{1,0:T(8,128)(2,1)S(1)}, bf16[656,128]{1,0:T(8,128)(2,1)S(1)}, u32[]{:S(2)}, u32[]{:S(2)}) collective-permute-start(bf16[656,128]{1,0:T(8,128)(2,1)S(1)} %shard_map.90.refs_2_), channel_id=1, source_target_pairs={{0,4},{1,5},{2,6},{3,7},{4,0},{5,1},{6,2},{7,3},{8,12},{9,13},{10,... | collective-permute-start | bytes 503816 | tf_op jit(solution)/shard_map/ppermute | solution.py:360
  11.5 0.0 collective-permute-done.1.refs_1_.refs_10_
  11.5 0.3 shard_map.91
  11.8 0.1 collective-permute-start.6
  11.9 0.1 collective-permute-start.2
  11.9 0.5 %collective-permute-start.3 = (bf16[2,256,128]{2,1,0:T(8,128)(2,1)S(1)}, bf16[2,256,128]{2,1,0:T(8,128)(2,1)S(1)}, u32[]{:S(2)}, u32[]{:S(2)}) collective-permute-start(bf16[2,256,128]{2,1,0:T(8,128)(2,1)S(1)} %get-tuple-element.71), channel_id=1, source_target_pairs={{0,1},{1,0},{2,3},{3,2},{4,5},{5,4},{6,7},{7,6},{8,9},{9,8},{10,11... | collective-permute-start | bytes 393224 | tf_op jit(solution)/shard_map/ppermute | solution.py:360
  12.4 0.3 shard_map.89.refs_0_
  12.7 0.6 %collective-permute-done.2.refs_5_.refs_11_ = bf16[2,256,128]{2,1,0:T(8,128)(2,1)S(1)} collective-permute-done((bf16[2,256,128]{2,1,0:T(8,128)(2,1)S(1)}, bf16[2,256,128]{2,1,0:T(8,128)(2,1)S(1)}, u32[]{:S(2)}, u32[]{:S(2)}) %collective-permute-start.2) | collective-permute-done | bytes 131104 | tf_op jit(solution)/shard_map/ppermute | solution.py:360
  13.3 0.2 collective-permute-done.3.refs_6_.refs_12_
  13.5 4.7 %collective-permute-done.6.refs_3_ = bf16[656,128]{1,0:T(8,128)(2,1)S(1)} collective-permute-done((bf16[656,128]{1,0:T(8,128)(2,1)S(1)}, bf16[656,128]{1,0:T(8,128)(2,1)S(1)}, u32[]{:S(2)}, u32[]{:S(2)}) %collective-permute-start.6) | collective-permute-done | bytes 167968 | tf_op jit(solution)/shard_map/ppermute | solution.py:360
  18.2 0.5 %collective-permute-done.5.refs_2_ = bf16[656,128]{1,0:T(8,128)(2,1)S(1)} collective-permute-done((bf16[656,128]{1,0:T(8,128)(2,1)S(1)}, bf16[656,128]{1,0:T(8,128)(2,1)S(1)}, u32[]{:S(2)}, u32[]{:S(2)}) %collective-permute-start.5) | collective-permute-done | bytes 167968 | tf_op jit(solution)/shard_map/ppermute | solution.py:360
  18.7 0.0 collective-permute-done.4.refs_1_
  18.7 0.4 %shard_map.92 = (bf16[656,128]{1,0:T(8,128)(2,1)S(1)}, bf16[656,128]{1,0:T(8,128)(2,1)S(1)}, bf16[656,128]{1,0:T(8,128)(2,1)S(1)}, bf16[656,128]{1,0:T(8,128)(2,1)S(1)}) custom-call(bf16[656,128]{1,0:T(8,128)(2,1)S(1)} %shard_map.89.refs_0_, bf16[656,128]{1,0:T(8,128)(2,1)S(1)} %collective-permute-done.4.refs_1_, ...), custom_call_target="tpu_custom_call" | custom-call | flops 575000000 | tf_op jit(solution)/shard_map/pallas_call | solution.py:41
  19.1 0.4 %collective-permute-start.8 = (bf16[656,128]{1,0:T(8,128)(2,1)S(1)}, bf16[656,128]{1,0:T(8,128)(2,1)S(1)}, u32[]{:S(2)}, u32[]{:S(2)}) collective-permute-start(bf16[656,128]{1,0:T(8,128)(2,1)S(1)} %get-tuple-element.76), channel_id=1, source_target_pairs={{0,2},{1,3},{2,0},{3,1},{4,6},{5,7},{6,4},{7,5},{8,10},{9,11},{10,... | collective-permute-start | bytes 503816 | tf_op jit(solution)/shard_map/ppermute | solution.py:360
  19.5 0.8 %collective-permute-start.7 = (bf16[656,128]{1,0:T(8,128)(2,1)S(1)}, bf16[656,128]{1,0:T(8,128)(2,1)S(1)}, u32[]{:S(2)}, u32[]{:S(2)}) collective-permute-start(bf16[656,128]{1,0:T(8,128)(2,1)S(1)} %get-tuple-element.74), channel_id=1, source_target_pairs={{0,4},{1,5},{2,6},{3,7},{4,0},{5,1},{6,2},{7,3},{8,12},{9,13},{10,... | collective-permute-start | bytes 503816 | tf_op jit(solution)/shard_map/ppermute | solution.py:360
  20.4 2.3 %collective-permute-start.10 = (bf16[656,128]{1,0:T(8,128)(2,1)S(1)}, bf16[656,128]{1,0:T(8,128)(2,1)S(1)}, u32[]{:S(2)}, u32[]{:S(2)}) collective-permute-start(bf16[656,128]{1,0:T(8,128)(2,1)S(1)} %get-tuple-element.79), channel_id=1, source_target_pairs={{0,6},{1,7},{2,4},{3,5},{4,2},{5,3},{6,0},{7,1},{8,14},{9,15},{10,... | collective-permute-start | bytes 503816 | tf_op jit(solution)/shard_map/ppermute | solution.py:360
  22.7 0.0 collective-permute-start.12
  22.7 2.0 %collective-permute-done.8.refs_14_ = bf16[656,128]{1,0:T(8,128)(2,1)S(1)} collective-permute-done((bf16[656,128]{1,0:T(8,128)(2,1)S(1)}, bf16[656,128]{1,0:T(8,128)(2,1)S(1)}, u32[]{:S(2)}, u32[]{:S(2)}) %collective-permute-start.8) | collective-permute-done | bytes 167968 | tf_op jit(solution)/shard_map/ppermute | solution.py:360
  24.7 0.0 collective-permute-start.13
  24.7 1.3 %shard_map.93 = (bf16[128,2048]{1,0:T(8,128)(2,1)}, bf16[128,2048]{1,0:T(8,128)(2,1)}, bf16[128,2048]{1,0:T(8,128)(2,1)}, f32[16,128,128]{2,1,0:T(8,128)}) custom-call(bf16[128,2048]{1,0:T(8,128)(2,1)S(1)} %get-tuple-element.48.refs_3_.refs_0_, bf16[128,2048]{1,0:T(8,128)(2,1)S(1)} %get-tuple-element.49.refs_2_.refs_1_, ...), custom_call_target="tpu_custom_call" | custom-call | flops 1610000000 | tf_op jit(solution)/shard_map/pallas_call | solution.py:41
  26.0 0.0 collective-permute-done.7.refs_13_
  26.0 0.8 %collective-permute-done.10.refs_14_ = bf16[656,128]{1,0:T(8,128)(2,1)S(1)} collective-permute-done((bf16[656,128]{1,0:T(8,128)(2,1)S(1)}, bf16[656,128]{1,0:T(8,128)(2,1)S(1)}, u32[]{:S(2)}, u32[]{:S(2)}) %collective-permute-start.10) | collective-permute-done | bytes 167968 | tf_op jit(solution)/shard_map/ppermute | solution.py:360
  26.8 0.0 collective-permute-start.11
  26.8 0.5 %collective-permute-start.9 = (bf16[656,128]{1,0:T(8,128)(2,1)S(1)}, bf16[656,128]{1,0:T(8,128)(2,1)S(1)}, u32[]{:S(2)}, u32[]{:S(2)}) collective-permute-start(bf16[656,128]{1,0:T(8,128)(2,1)S(1)} %collective-permute-done.7.refs_13_), channel_id=1, source_target_pairs={{0,1},{1,0},{2,3},{3,2},{4,5},{5,4},{6,7},{7,6},{8,9},{9,8},{10,11... | collective-permute-start | bytes 503816 | tf_op jit(solution)/shard_map/ppermute | solution.py:360
  27.3 0.0 collective-permute-done.12.refs_15_
  27.3 0.0 collective-permute-done.13.refs_16_
  27.3 0.9 %shard_map.94 = (bf16[128,512]{1,0:T(8,128)(2,1)S(1)}, bf16[128,512]{1,0:T(8,128)(2,1)S(1)}, bf16[128,512]{1,0:T(8,128)(2,1)S(1)}, f32[4,128,128]{2,1,0:T(8,128)...) custom-call(bf16[128,2048]{1,0:T(8,128)(2,1)S(1)} %get-tuple-element, ...), custom_call_target="tpu_custom_call" | custom-call | flops 1150000000 | tf_op jit(solution)/shard_map/pallas_call | solution.py:41
  28.2 0.0 collective-permute-done.11.refs_14_
  28.2 0.2 collective-permute-done.9.refs_13_
  28.5 1.8 %shard_map.95 = (bf16[128,2048]{1,0:T(8,128)(2,1)}, bf16[128,2048]{1,0:T(8,128)(2,1)}, bf16[128,2048]{1,0:T(8,128)(2,1)}, f32[16,128,128]{2,1,0:T(8,128)}) custom-call(bf16[128,2048]{1,0:T(8,128)(2,1)S(1)} %get-tuple-element.48.refs_3_.refs_0_, ...), custom_call_target="tpu_custom_call", output_to_operand_aliasing={{0}: (23, {}), {1}: (24, {}), {2}: (25, {}), {3}: (26, {})} | custom-call | flops 1380000000 | tf_op jit(solution)/shard_map/pallas_call | solution.py:41
  (1 shorter events, 0.0 us)
Async XLA Ops:
  2.8 1.8 %collective-permute-start = (bf16[2,656,128]{2,1,0:T(8,128)(2,1)S(1)}, bf16[2,656,128]{2,1,0:T(8,128)(2,1)S(1)}, u32[]{:S(2)}, u32[]{:S(2)}) collective-permute-start(bf16[2,656,128]{2,1,0:T(8,128)(2,1)S(1)} %get-tuple-element.54), channel_id=1, source_target_pairs={{0,1},{1,0},{2,3},{3,2},{4,5},{5,4},{6,7},{7,6},{8,9},{9,8},{10,11... | collective-permute-start | bytes 1007624 | tf_op jit(solution)/shard_map/ppermute | solution.py:360
  3.4 8.1 %collective-permute-start.1 = (bf16[2,656,128]{2,1,0:T(8,128)(2,1)S(1)}, bf16[2,656,128]{2,1,0:T(8,128)(2,1)S(1)}, u32[]{:S(2)}, u32[]{:S(2)}) collective-permute-start(bf16[2,656,128]{2,1,0:T(8,128)(2,1)S(1)} %get-tuple-element.69), channel_id=1, source_target_pairs={{0,1},{1,0},{2,3},{3,2},{4,5},{5,4},{6,7},{7,6},{8,9},{9,8},{10,11... | collective-permute-start | bytes 1007624 | tf_op jit(solution)/shard_map/ppermute | solution.py:360
  6.7 12.0 %collective-permute-start.4 = (bf16[656,128]{1,0:T(8,128)(2,1)S(1)}, bf16[656,128]{1,0:T(8,128)(2,1)S(1)}, u32[]{:S(2)}, u32[]{:S(2)}) collective-permute-start(bf16[656,128]{1,0:T(8,128)(2,1)S(1)} %shard_map.86.refs_5_.refs_2_), channel_id=1, source_target_pairs={{0,2},{1,3},{2,0},{3,1},{4,6},{5,7},{6,4},{7,5},{8,10},{9,11},{10,... | collective-permute-start | bytes 503816 | tf_op jit(solution)/shard_map/ppermute | solution.py:360
  9.9 8.8 %collective-permute-start.5 = (bf16[656,128]{1,0:T(8,128)(2,1)S(1)}, bf16[656,128]{1,0:T(8,128)(2,1)S(1)}, u32[]{:S(2)}, u32[]{:S(2)}) collective-permute-start(bf16[656,128]{1,0:T(8,128)(2,1)S(1)} %shard_map.90.refs_2_), channel_id=1, source_target_pairs={{0,4},{1,5},{2,6},{3,7},{4,0},{5,1},{6,2},{7,3},{8,12},{9,13},{10,... | collective-permute-start | bytes 503816 | tf_op jit(solution)/shard_map/ppermute | solution.py:360
  11.8 6.4 %collective-permute-start.6 = (bf16[656,128]{1,0:T(8,128)(2,1)S(1)}, bf16[656,128]{1,0:T(8,128)(2,1)S(1)}, u32[]{:S(2)}, u32[]{:S(2)}) collective-permute-start(bf16[656,128]{1,0:T(8,128)(2,1)S(1)} %shard_map.91), channel_id=1, source_target_pairs={{0,6},{1,7},{2,4},{3,5},{4,2},{5,3},{6,0},{7,1},{8,14},{9,15},{10,... | collective-permute-start | bytes 503816 | tf_op jit(solution)/shard_map/ppermute | solution.py:360
  11.9 1.4 %collective-permute-start.2 = (bf16[2,256,128]{2,1,0:T(8,128)(2,1)S(1)}, bf16[2,256,128]{2,1,0:T(8,128)(2,1)S(1)}, u32[]{:S(2)}, u32[]{:S(2)}) collective-permute-start(bf16[2,256,128]{2,1,0:T(8,128)(2,1)S(1)} %get-tuple-element.70), channel_id=1, source_target_pairs={{0,1},{1,0},{2,3},{3,2},{4,5},{5,4},{6,7},{7,6},{8,9},{9,8},{10,11... | collective-permute-start | bytes 393224 | tf_op jit(solution)/shard_map/ppermute | solution.py:360
  11.9 1.5 %collective-permute-start.3 = (bf16[2,256,128]{2,1,0:T(8,128)(2,1)S(1)}, bf16[2,256,128]{2,1,0:T(8,128)(2,1)S(1)}, u32[]{:S(2)}, u32[]{:S(2)}) collective-permute-start(bf16[2,256,128]{2,1,0:T(8,128)(2,1)S(1)} %get-tuple-element.71), channel_id=1, source_target_pairs={{0,1},{1,0},{2,3},{3,2},{4,5},{5,4},{6,7},{7,6},{8,9},{9,8},{10,11... | collective-permute-start | bytes 393224 | tf_op jit(solution)/shard_map/ppermute | solution.py:360
  19.1 5.6 %collective-permute-start.8 = (bf16[656,128]{1,0:T(8,128)(2,1)S(1)}, bf16[656,128]{1,0:T(8,128)(2,1)S(1)}, u32[]{:S(2)}, u32[]{:S(2)}) collective-permute-start(bf16[656,128]{1,0:T(8,128)(2,1)S(1)} %get-tuple-element.76), channel_id=1, source_target_pairs={{0,2},{1,3},{2,0},{3,1},{4,6},{5,7},{6,4},{7,5},{8,10},{9,11},{10,... | collective-permute-start | bytes 503816 | tf_op jit(solution)/shard_map/ppermute | solution.py:360
  19.5 6.4 %collective-permute-start.7 = (bf16[656,128]{1,0:T(8,128)(2,1)S(1)}, bf16[656,128]{1,0:T(8,128)(2,1)S(1)}, u32[]{:S(2)}, u32[]{:S(2)}) collective-permute-start(bf16[656,128]{1,0:T(8,128)(2,1)S(1)} %get-tuple-element.74), channel_id=1, source_target_pairs={{0,4},{1,5},{2,6},{3,7},{4,0},{5,1},{6,2},{7,3},{8,12},{9,13},{10,... | collective-permute-start | bytes 503816 | tf_op jit(solution)/shard_map/ppermute | solution.py:360
  20.4 6.4 %collective-permute-start.10 = (bf16[656,128]{1,0:T(8,128)(2,1)S(1)}, bf16[656,128]{1,0:T(8,128)(2,1)S(1)}, u32[]{:S(2)}, u32[]{:S(2)}) collective-permute-start(bf16[656,128]{1,0:T(8,128)(2,1)S(1)} %get-tuple-element.79), channel_id=1, source_target_pairs={{0,6},{1,7},{2,4},{3,5},{4,2},{5,3},{6,0},{7,1},{8,14},{9,15},{10,... | collective-permute-start | bytes 503816 | tf_op jit(solution)/shard_map/ppermute | solution.py:360
  22.7 4.7 %collective-permute-start.12 = (bf16[656,128]{1,0:T(8,128)(2,1)S(1)}, bf16[656,128]{1,0:T(8,128)(2,1)S(1)}, u32[]{:S(2)}, u32[]{:S(2)}) collective-permute-start(bf16[656,128]{1,0:T(8,128)(2,1)S(1)} %get-tuple-element.75.refs_13_), channel_id=1, source_target_pairs={{0,1},{1,0},{2,3},{3,2},{4,5},{5,4},{6,7},{7,6},{8,9},{9,8},{10,11... | collective-permute-start | bytes 503816 | tf_op jit(solution)/shard_map/ppermute | solution.py:360
  24.7 2.7 %collective-permute-start.13 = (bf16[656,128]{1,0:T(8,128)(2,1)S(1)}, bf16[656,128]{1,0:T(8,128)(2,1)S(1)}, u32[]{:S(2)}, u32[]{:S(2)}) collective-permute-start(bf16[656,128]{1,0:T(8,128)(2,1)S(1)} %collective-permute-done.8.refs_14_), channel_id=1, source_target_pairs={{0,1},{1,0},{2,3},{3,2},{4,5},{5,4},{6,7},{7,6},{8,9},{9,8},{10,11... | collective-permute-start | bytes 503816 | tf_op jit(solution)/shard_map/ppermute | solution.py:360
  26.8 1.4 %collective-permute-start.11 = (bf16[656,128]{1,0:T(8,128)(2,1)S(1)}, bf16[656,128]{1,0:T(8,128)(2,1)S(1)}, u32[]{:S(2)}, u32[]{:S(2)}) collective-permute-start(bf16[656,128]{1,0:T(8,128)(2,1)S(1)} %collective-permute-done.10.refs_14_), channel_id=1, source_target_pairs={{0,1},{1,0},{2,3},{3,2},{4,5},{5,4},{6,7},{7,6},{8,9},{9,8},{10,11... | collective-permute-start | bytes 503816 | tf_op jit(solution)/shard_map/ppermute | solution.py:360
  26.8 1.6 %collective-permute-start.9 = (bf16[656,128]{1,0:T(8,128)(2,1)S(1)}, bf16[656,128]{1,0:T(8,128)(2,1)S(1)}, u32[]{:S(2)}, u32[]{:S(2)}) collective-permute-start(bf16[656,128]{1,0:T(8,128)(2,1)S(1)} %collective-permute-done.7.refs_13_), channel_id=1, source_target_pairs={{0,1},{1,0},{2,3},{3,2},{4,5},{5,4},{6,7},{7,6},{8,9},{9,8},{10,11... | collective-permute-start | bytes 503816 | tf_op jit(solution)/shard_map/ppermute | solution.py:360

commit v12 on v11

--- a/solution.py
+++ b/solution.py
@@ -401,7 +401,7 @@
     )
     *near_sums, local[0] = lax.optimization_barrier((*near_sums, local[0]))
     (y_sum,) = join((1,), 0, 0.15, near_sums[:1])
-    (far_sum,) = join((1,), 1, 0.15, (y_sum,))
+    (far_sum,) = join((1,), 1, 0.15, near_sums[:1])
     chip_sums = [None, near_sums[0], y_sum, far_sum]
     parts = [None] + [swap(chip_sums[j], 2 * j) for j in range(1, GROUPS)]
     local = call(

time: 30.4 us -> 31.8 us (1.046)
  waiting for transfers between devices: 9.42 us -> 10.8 us
    ppermute x14, waiting for transfers between devices: 9.42 us -> 10.8 us  [swap(): return lax.ppermute(x, 'ctx', [(i, i ^ apart) for i in range(count)])]
where the time goes in v12:
time: 31.8 us; the launch traced here: 31.7 us
  waiting for transfers between devices  10.8 us (34%)
  Pallas kernels  10.3 us (32%)
  starting transfers between devices  9.82 us (31%)
  between operations  0.71 us (2%)
    ppermute x14, waiting for transfers between devices, swap(): return lax.ppermute(x, 'ctx', [(i, i ^ apart) for i in range(count)])  10.8 us
    pallas_call x12, Pallas kernels, call(): pl.pallas_call(run, out_shape=[jax.ShapeDtypeStruct(shape, dtype) for sha...  10.3 us
    ppermute x14, starting transfers between devices, swap(): return lax.ppermute(x, 'ctx', [(i, i ^ apart) for i in range(count)])  9.82 us
  transfers between devices with their start and end apart: 14, of which 8 were waited for; matrix products, arithmetic and copies ran while one was open for 0% of the time, Pallas kernels for 19%

profile of v12, /device:TPU:0, one launch (start us, length us, event | category | flops | bytes accessed | tf_op | source)
XLA Modules:
  0.0 31.7 jit_solution(9687831407386141461)
XLA Ops:
  0.6 2.2 %shard_map.84 = (bf16[128,2048]{1,0:T(8,128)(2,1)S(1)}, bf16[128,2048]{1,0:T(8,128)(2,1)S(1)}, bf16[128,2048]{1,0:T(8,128)(2,1)S(1)}, bf16[128,2048]{1,0:T(8,128...) custom-call(bf16[128,2048]{1,0:T(8,128)(2,1)} %refs_0_.1, ...), custom_call_target="tpu_custom_call" | custom-call | flops 2300000000 | tf_op jit(solution)/shard_map/pallas_call | solution.py:41
  2.8 0.5 %collective-permute-start = (bf16[2,656,128]{2,1,0:T(8,128)(2,1)S(1)}, bf16[2,656,128]{2,1,0:T(8,128)(2,1)S(1)}, u32[]{:S(2)}, u32[]{:S(2)}) collective-permute-start(bf16[2,656,128]{2,1,0:T(8,128)(2,1)S(1)} %get-tuple-element.54), channel_id=1, source_target_pairs={{0,1},{1,0},{2,3},{3,2},{4,5},{5,4},{6,7},{7,6},{8,9},{9,8},{10,11... | collective-permute-start | bytes 1007624 | tf_op jit(solution)/shard_map/ppermute | solution.py:360
  3.4 0.1 collective-permute-start.1
  3.4 0.8 %shard_map.85 = (bf16[2,656,128]{2,1,0:T(8,128)(2,1)S(1)}, bf16[2,656,128]{2,1,0:T(8,128)(2,1)S(1)}, bf16[2,256,128]{2,1,0:T(8,128)(2,1)S(1)}, bf16[2,256,128]{2,1,0:T(8,128)(2,1)S(1)}, f32[4,2,128,128]{3,2,1,0:T(8,128)S(1)}) custom-call(bf16[128,2048]{1,0:T(8,128)(2,1)S(1)} %get-tuple-element.51.refs_0_, bf16[128,2048]{1,0:T(8,128)(2,1)S(1)} %get-tuple-element.52.refs_1_, ...), custom_call_target="tpu_custom_call" | custom-call | flops 1150000000 | tf_op jit(solution)/shard_map/pallas_call | solution.py:41
  4.2 0.4 %collective-permute-done.refs_1_.refs_9_ = bf16[2,656,128]{2,1,0:T(8,128)(2,1)S(1)} collective-permute-done((bf16[2,656,128]{2,1,0:T(8,128)(2,1)S(1)}, bf16[2,656,128]{2,1,0:T(8,128)(2,1)S(1)}, u32[]{:S(2)}, u32[]{:S(2)}) %collective-permute-start) | collective-permute-done | bytes 335904 | tf_op jit(solution)/shard_map/ppermute | solution.py:360
  4.6 0.3 shard_map.86.refs_5_.refs_2_
  4.9 1.8 %shard_map.87 = (f32[2,4,2,128,128]{4,3,2,1,0:T(8,128)S(1)}, f32[2,4,2,128,128]{4,3,2,1,0:T(8,128)S(1)}, bf16[2,4,2,128,128]{4,3,2,1,0:T(8,128)(2,1)S(1)}, bf16[2,4,2,128,128]{4,3,2,1,0:T(8,128)(2,1)S(1)}) custom-call(bf16[128,2048]{1,0:T(8,128)(2,1)S(1)} %get-tuple-element.51.refs_0_, bf16[128,2048]{1,0:T(8,128)(2,1)S(1)} %get-tuple-element.52.refs_1_, ...), custom_call_target="tpu_custom_call" | custom-call | flops 2070000000 | tf_op jit(solution)/shard_map/pallas_call | solution.py:41
  6.7 2.9 %collective-permute-start.4 = (bf16[656,128]{1,0:T(8,128)(2,1)S(1)}, bf16[656,128]{1,0:T(8,128)(2,1)S(1)}, u32[]{:S(2)}, u32[]{:S(2)}) collective-permute-start(bf16[656,128]{1,0:T(8,128)(2,1)S(1)} %shard_map.86.refs_5_.refs_2_), channel_id=1, source_target_pairs={{0,2},{1,3},{2,0},{3,1},{4,6},{5,7},{6,4},{7,5},{8,10},{9,11},{10,... | collective-permute-start | bytes 503816 | tf_op jit(solution)/shard_map/ppermute | solution.py:360
  9.6 0.0 collective-permute-done.1.refs_1_.refs_10_
  9.6 0.3 shard_map.91
  9.9 1.6 %collective-permute-start.6 = (bf16[656,128]{1,0:T(8,128)(2,1)S(1)}, bf16[656,128]{1,0:T(8,128)(2,1)S(1)}, u32[]{:S(2)}, u32[]{:S(2)}) collective-permute-start(bf16[656,128]{1,0:T(8,128)(2,1)S(1)} %shard_map.91), channel_id=1, source_target_pairs={{0,6},{1,7},{2,4},{3,5},{4,2},{5,3},{6,0},{7,1},{8,14},{9,15},{10,... | collective-permute-start | bytes 503816 | tf_op jit(solution)/shard_map/ppermute | solution.py:360
  11.5 0.3 shard_map.90
  11.7 0.1 collective-permute-start.5
  11.8 0.1 collective-permute-start.2
  11.9 0.5 %collective-permute-start.3 = (bf16[2,256,128]{2,1,0:T(8,128)(2,1)S(1)}, bf16[2,256,128]{2,1,0:T(8,128)(2,1)S(1)}, u32[]{:S(2)}, u32[]{:S(2)}) collective-permute-start(bf16[2,256,128]{2,1,0:T(8,128)(2,1)S(1)} %get-tuple-element.71), channel_id=1, source_target_pairs={{0,1},{1,0},{2,3},{3,2},{4,5},{5,4},{6,7},{7,6},{8,9},{9,8},{10,11... | collective-permute-start | bytes 393224 | tf_op jit(solution)/shard_map/ppermute | solution.py:360
  12.4 0.3 shard_map.89.refs_0_
  12.7 0.6 %collective-permute-done.2.refs_5_.refs_11_ = bf16[2,256,128]{2,1,0:T(8,128)(2,1)S(1)} collective-permute-done((bf16[2,256,128]{2,1,0:T(8,128)(2,1)S(1)}, bf16[2,256,128]{2,1,0:T(8,128)(2,1)S(1)}, u32[]{:S(2)}, u32[]{:S(2)}) %collective-permute-start.2) | collective-permute-done | bytes 131104 | tf_op jit(solution)/shard_map/ppermute | solution.py:360
  13.3 0.2 collective-permute-done.3.refs_6_.refs_12_
  13.4 3.9 %collective-permute-done.6.refs_3_ = bf16[656,128]{1,0:T(8,128)(2,1)S(1)} collective-permute-done((bf16[656,128]{1,0:T(8,128)(2,1)S(1)}, bf16[656,128]{1,0:T(8,128)(2,1)S(1)}, u32[]{:S(2)}, u32[]{:S(2)}) %collective-permute-start.6) | collective-permute-done | bytes 167968 | tf_op jit(solution)/shard_map/ppermute | solution.py:360
  17.3 1.7 %collective-permute-done.5.refs_2_ = bf16[656,128]{1,0:T(8,128)(2,1)S(1)} collective-permute-done((bf16[656,128]{1,0:T(8,128)(2,1)S(1)}, bf16[656,128]{1,0:T(8,128)(2,1)S(1)}, u32[]{:S(2)}, u32[]{:S(2)}) %collective-permute-start.5) | collective-permute-done | bytes 167968 | tf_op jit(solution)/shard_map/ppermute | solution.py:360
  19.0 0.0 collective-permute-done.4.refs_1_
  19.0 0.4 %shard_map.92 = (bf16[656,128]{1,0:T(8,128)(2,1)S(1)}, bf16[656,128]{1,0:T(8,128)(2,1)S(1)}, bf16[656,128]{1,0:T(8,128)(2,1)S(1)}, bf16[656,128]{1,0:T(8,128)(2,1)S(1)}) custom-call(bf16[656,128]{1,0:T(8,128)(2,1)S(1)} %shard_map.89.refs_0_, bf16[656,128]{1,0:T(8,128)(2,1)S(1)} %collective-permute-done.4.refs_1_, ...), custom_call_target="tpu_custom_call" | custom-call | flops 575000000 | tf_op jit(solution)/shard_map/pallas_call | solution.py:41
  19.5 1.6 %collective-permute-start.8 = (bf16[656,128]{1,0:T(8,128)(2,1)S(1)}, bf16[656,128]{1,0:T(8,128)(2,1)S(1)}, u32[]{:S(2)}, u32[]{:S(2)}) collective-permute-start(bf16[656,128]{1,0:T(8,128)(2,1)S(1)} %get-tuple-element.76), channel_id=1, source_target_pairs={{0,2},{1,3},{2,0},{3,1},{4,6},{5,7},{6,4},{7,5},{8,10},{9,11},{10,... | collective-permute-start | bytes 503816 | tf_op jit(solution)/shard_map/ppermute | solution.py:360
  21.1 0.5 %collective-permute-start.7 = (bf16[656,128]{1,0:T(8,128)(2,1)S(1)}, bf16[656,128]{1,0:T(8,128)(2,1)S(1)}, u32[]{:S(2)}, u32[]{:S(2)}) collective-permute-start(bf16[656,128]{1,0:T(8,128)(2,1)S(1)} %get-tuple-element.74), channel_id=1, source_target_pairs={{0,4},{1,5},{2,6},{3,7},{4,0},{5,1},{6,2},{7,3},{8,12},{9,13},{10,... | collective-permute-start | bytes 503816 | tf_op jit(solution)/shard_map/ppermute | solution.py:360
  21.5 1.5 %collective-permute-start.10 = (bf16[656,128]{1,0:T(8,128)(2,1)S(1)}, bf16[656,128]{1,0:T(8,128)(2,1)S(1)}, u32[]{:S(2)}, u32[]{:S(2)}) collective-permute-start(bf16[656,128]{1,0:T(8,128)(2,1)S(1)} %get-tuple-element.79), channel_id=1, source_target_pairs={{0,6},{1,7},{2,4},{3,5},{4,2},{5,3},{6,0},{7,1},{8,14},{9,15},{10,... | collective-permute-start | bytes 503816 | tf_op jit(solution)/shard_map/ppermute | solution.py:360
  23.0 0.0 collective-permute-start.12
  23.0 1.9 %collective-permute-done.8.refs_14_ = bf16[656,128]{1,0:T(8,128)(2,1)S(1)} collective-permute-done((bf16[656,128]{1,0:T(8,128)(2,1)S(1)}, bf16[656,128]{1,0:T(8,128)(2,1)S(1)}, u32[]{:S(2)}, u32[]{:S(2)}) %collective-permute-start.8) | collective-permute-done | bytes 167968 | tf_op jit(solution)/shard_map/ppermute | solution.py:360
  24.9 0.0 collective-permute-start.13
  24.9 1.3 %shard_map.93 = (bf16[128,2048]{1,0:T(8,128)(2,1)}, bf16[128,2048]{1,0:T(8,128)(2,1)}, bf16[128,2048]{1,0:T(8,128)(2,1)}, f32[16,128,128]{2,1,0:T(8,128)}) custom-call(bf16[128,2048]{1,0:T(8,128)(2,1)S(1)} %get-tuple-element.48.refs_3_.refs_0_, bf16[128,2048]{1,0:T(8,128)(2,1)S(1)} %get-tuple-element.49.refs_2_.refs_1_, ...), custom_call_target="tpu_custom_call" | custom-call | flops 1610000000 | tf_op jit(solution)/shard_map/pallas_call | solution.py:41
  26.2 2.0 %collective-permute-done.7.refs_13_ = bf16[656,128]{1,0:T(8,128)(2,1)S(1)} collective-permute-done((bf16[656,128]{1,0:T(8,128)(2,1)S(1)}, bf16[656,128]{1,0:T(8,128)(2,1)S(1)}, u32[]{:S(2)}, u32[]{:S(2)}) %collective-permute-start.7) | collective-permute-done | bytes 167968 | tf_op jit(solution)/shard_map/ppermute | solution.py:360
  28.2 0.0 collective-permute-done.10.refs_14_
  28.2 0.0 collective-permute-start.11
  28.2 0.5 %collective-permute-start.9 = (bf16[656,128]{1,0:T(8,128)(2,1)S(1)}, bf16[656,128]{1,0:T(8,128)(2,1)S(1)}, u32[]{:S(2)}, u32[]{:S(2)}) collective-permute-start(bf16[656,128]{1,0:T(8,128)(2,1)S(1)} %collective-permute-done.7.refs_13_), channel_id=1, source_target_pairs={{0,1},{1,0},{2,3},{3,2},{4,5},{5,4},{6,7},{7,6},{8,9},{9,8},{10,11... | collective-permute-start | bytes 503816 | tf_op jit(solution)/shard_map/ppermute | solution.py:360
  28.7 0.0 collective-permute-done.12.refs_15_
  28.7 0.0 collective-permute-done.13.refs_16_
  28.7 0.9 %shard_map.94 = (bf16[128,512]{1,0:T(8,128)(2,1)S(1)}, bf16[128,512]{1,0:T(8,128)(2,1)S(1)}, bf16[128,512]{1,0:T(8,128)(2,1)S(1)}, f32[4,128,128]{2,1,0:T(8,128)...) custom-call(bf16[128,2048]{1,0:T(8,128)(2,1)S(1)} %get-tuple-element, ...), custom_call_target="tpu_custom_call" | custom-call | flops 1150000000 | tf_op jit(solution)/shard_map/pallas_call | solution.py:41
  29.6 0.0 collective-permute-done.11.refs_14_
  29.6 0.2 collective-permute-done.9.refs_13_
  29.9 1.8 %shard_map.95 = (bf16[128,2048]{1,0:T(8,128)(2,1)}, bf16[128,2048]{1,0:T(8,128)(2,1)}, bf16[128,2048]{1,0:T(8,128)(2,1)}, f32[16,128,128]{2,1,0:T(8,128)}) custom-call(bf16[128,2048]{1,0:T(8,128)(2,1)S(1)} %get-tuple-element.48.refs_3_.refs_0_, ...), custom_call_target="tpu_custom_call", output_to_operand_aliasing={{0}: (23, {}), {1}: (24, {}), {2}: (25, {}), {3}: (26, {})} | custom-call | flops 1380000000 | tf_op jit(solution)/shard_map/pallas_call | solution.py:41
  (1 shorter events, 0.0 us)
Async XLA Ops:
  2.8 1.8 %collective-permute-start = (bf16[2,656,128]{2,1,0:T(8,128)(2,1)S(1)}, bf16[2,656,128]{2,1,0:T(8,128)(2,1)S(1)}, u32[]{:S(2)}, u32[]{:S(2)}) collective-permute-start(bf16[2,656,128]{2,1,0:T(8,128)(2,1)S(1)} %get-tuple-element.54), channel_id=1, source_target_pairs={{0,1},{1,0},{2,3},{3,2},{4,5},{5,4},{6,7},{7,6},{8,9},{9,8},{10,11... | collective-permute-start | bytes 1007624 | tf_op jit(solution)/shard_map/ppermute | solution.py:360
  3.4 6.3 %collective-permute-start.1 = (bf16[2,656,128]{2,1,0:T(8,128)(2,1)S(1)}, bf16[2,656,128]{2,1,0:T(8,128)(2,1)S(1)}, u32[]{:S(2)}, u32[]{:S(2)}) collective-permute-start(bf16[2,656,128]{2,1,0:T(8,128)(2,1)S(1)} %get-tuple-element.69), channel_id=1, source_target_pairs={{0,1},{1,0},{2,3},{3,2},{4,5},{5,4},{6,7},{7,6},{8,9},{9,8},{10,11... | collective-permute-start | bytes 1007624 | tf_op jit(solution)/shard_map/ppermute | solution.py:360
  6.7 12.3 %collective-permute-start.4 = (bf16[656,128]{1,0:T(8,128)(2,1)S(1)}, bf16[656,128]{1,0:T(8,128)(2,1)S(1)}, u32[]{:S(2)}, u32[]{:S(2)}) collective-permute-start(bf16[656,128]{1,0:T(8,128)(2,1)S(1)} %shard_map.86.refs_5_.refs_2_), channel_id=1, source_target_pairs={{0,2},{1,3},{2,0},{3,1},{4,6},{5,7},{6,4},{7,5},{8,10},{9,11},{10,... | collective-permute-start | bytes 503816 | tf_op jit(solution)/shard_map/ppermute | solution.py:360
  9.9 7.4 %collective-permute-start.6 = (bf16[656,128]{1,0:T(8,128)(2,1)S(1)}, bf16[656,128]{1,0:T(8,128)(2,1)S(1)}, u32[]{:S(2)}, u32[]{:S(2)}) collective-permute-start(bf16[656,128]{1,0:T(8,128)(2,1)S(1)} %shard_map.91), channel_id=1, source_target_pairs={{0,6},{1,7},{2,4},{3,5},{4,2},{5,3},{6,0},{7,1},{8,14},{9,15},{10,... | collective-permute-start | bytes 503816 | tf_op jit(solution)/shard_map/ppermute | solution.py:360
  11.7 7.3 %collective-permute-start.5 = (bf16[656,128]{1,0:T(8,128)(2,1)S(1)}, bf16[656,128]{1,0:T(8,128)(2,1)S(1)}, u32[]{:S(2)}, u32[]{:S(2)}) collective-permute-start(bf16[656,128]{1,0:T(8,128)(2,1)S(1)} %shard_map.90), channel_id=1, source_target_pairs={{0,4},{1,5},{2,6},{3,7},{4,0},{5,1},{6,2},{7,3},{8,12},{9,13},{10,... | collective-permute-start | bytes 503816 | tf_op jit(solution)/shard_map/ppermute | solution.py:360
  11.8 1.4 %collective-permute-start.2 = (bf16[2,256,128]{2,1,0:T(8,128)(2,1)S(1)}, bf16[2,256,128]{2,1,0:T(8,128)(2,1)S(1)}, u32[]{:S(2)}, u32[]{:S(2)}) collective-permute-start(bf16[2,256,128]{2,1,0:T(8,128)(2,1)S(1)} %get-tuple-element.70), channel_id=1, source_target_pairs={{0,1},{1,0},{2,3},{3,2},{4,5},{5,4},{6,7},{7,6},{8,9},{9,8},{10,11... | collective-permute-start | bytes 393224 | tf_op jit(solution)/shard_map/ppermute | solution.py:360
  11.9 1.5 %collective-permute-start.3 = (bf16[2,256,128]{2,1,0:T(8,128)(2,1)S(1)}, bf16[2,256,128]{2,1,0:T(8,128)(2,1)S(1)}, u32[]{:S(2)}, u32[]{:S(2)}) collective-permute-start(bf16[2,256,128]{2,1,0:T(8,128)(2,1)S(1)} %get-tuple-element.71), channel_id=1, source_target_pairs={{0,1},{1,0},{2,3},{3,2},{4,5},{5,4},{6,7},{7,6},{8,9},{9,8},{10,11... | collective-permute-start | bytes 393224 | tf_op jit(solution)/shard_map/ppermute | solution.py:360
  19.5 5.4 %collective-permute-start.8 = (bf16[656,128]{1,0:T(8,128)(2,1)S(1)}, bf16[656,128]{1,0:T(8,128)(2,1)S(1)}, u32[]{:S(2)}, u32[]{:S(2)}) collective-permute-start(bf16[656,128]{1,0:T(8,128)(2,1)S(1)} %get-tuple-element.76), channel_id=1, source_target_pairs={{0,2},{1,3},{2,0},{3,1},{4,6},{5,7},{6,4},{7,5},{8,10},{9,11},{10,... | collective-permute-start | bytes 503816 | tf_op jit(solution)/shard_map/ppermute | solution.py:360
  21.1 7.2 %collective-permute-start.7 = (bf16[656,128]{1,0:T(8,128)(2,1)S(1)}, bf16[656,128]{1,0:T(8,128)(2,1)S(1)}, u32[]{:S(2)}, u32[]{:S(2)}) collective-permute-start(bf16[656,128]{1,0:T(8,128)(2,1)S(1)} %get-tuple-element.74), channel_id=1, source_target_pairs={{0,4},{1,5},{2,6},{3,7},{4,0},{5,1},{6,2},{7,3},{8,12},{9,13},{10,... | collective-permute-start | bytes 503816 | tf_op jit(solution)/shard_map/ppermute | solution.py:360
  21.5 6.7 %collective-permute-start.10 = (bf16[656,128]{1,0:T(8,128)(2,1)S(1)}, bf16[656,128]{1,0:T(8,128)(2,1)S(1)}, u32[]{:S(2)}, u32[]{:S(2)}) collective-permute-start(bf16[656,128]{1,0:T(8,128)(2,1)S(1)} %get-tuple-element.79), channel_id=1, source_target_pairs={{0,6},{1,7},{2,4},{3,5},{4,2},{5,3},{6,0},{7,1},{8,14},{9,15},{10,... | collective-permute-start | bytes 503816 | tf_op jit(solution)/shard_map/ppermute | solution.py:360
  23.0 5.7 %collective-permute-start.12 = (bf16[656,128]{1,0:T(8,128)(2,1)S(1)}, bf16[656,128]{1,0:T(8,128)(2,1)S(1)}, u32[]{:S(2)}, u32[]{:S(2)}) collective-permute-start(bf16[656,128]{1,0:T(8,128)(2,1)S(1)} %get-tuple-element.75.refs_13_), channel_id=1, source_target_pairs={{0,1},{1,0},{2,3},{3,2},{4,5},{5,4},{6,7},{7,6},{8,9},{9,8},{10,11... | collective-permute-start | bytes 503816 | tf_op jit(solution)/shard_map/ppermute | solution.py:360
  24.9 3.8 %collective-permute-start.13 = (bf16[656,128]{1,0:T(8,128)(2,1)S(1)}, bf16[656,128]{1,0:T(8,128)(2,1)S(1)}, u32[]{:S(2)}, u32[]{:S(2)}) collective-permute-start(bf16[656,128]{1,0:T(8,128)(2,1)S(1)} %collective-permute-done.8.refs_14_), channel_id=1, source_target_pairs={{0,1},{1,0},{2,3},{3,2},{4,5},{5,4},{6,7},{7,6},{8,9},{9,8},{10,11... | collective-permute-start | bytes 503816 | tf_op jit(solution)/shard_map/ppermute | solution.py:360
  28.2 1.4 %collective-permute-start.11 = (bf16[656,128]{1,0:T(8,128)(2,1)S(1)}, bf16[656,128]{1,0:T(8,128)(2,1)S(1)}, u32[]{:S(2)}, u32[]{:S(2)}) collective-permute-start(bf16[656,128]{1,0:T(8,128)(2,1)S(1)} %collective-permute-done.10.refs_14_), channel_id=1, source_target_pairs={{0,1},{1,0},{2,3},{3,2},{4,5},{5,4},{6,7},{7,6},{8,9},{9,8},{10,11... | collective-permute-start | bytes 503816 | tf_op jit(solution)/shard_map/ppermute | solution.py:360
  28.2 1.6 %collective-permute-start.9 = (bf16[656,128]{1,0:T(8,128)(2,1)S(1)}, bf16[656,128]{1,0:T(8,128)(2,1)S(1)}, u32[]{:S(2)}, u32[]{:S(2)}) collective-permute-start(bf16[656,128]{1,0:T(8,128)(2,1)S(1)} %collective-permute-done.7.refs_13_), channel_id=1, source_target_pairs={{0,1},{1,0},{2,3},{3,2},{4,5},{5,4},{6,7},{7,6},{8,9},{9,8},{10,11... | collective-permute-start | bytes 503816 | tf_op jit(solution)/shard_map/ppermute | solution.py:360
